TPU v7x, 32 devices: a whole 2x2x4 slice. The times are simulated.
32 devices in a mesh: ctx: 2 (over core), head: 16 (over z, y, x).
Axes of the slice: x: 2, y: 2, z: 4, core: 2. Of those that a mesh axis runs over, the one named last changes fastest.
Arguments:
- queries: bfloat16 [2048, 64, 128], P(('ctx', 'head')), may hold values from -6 to 6
- keys: bfloat16 [2048, 8, 128], P(('ctx', 'head')), may hold values from -6 to 6
- values: bfloat16 [2048, 8, 128], P(('ctx', 'head')), may hold values from -6 to 6
- outputs: bfloat16 [2048, 64, 128], P(('ctx', 'head')), may hold values from -6 to 6
- out_grads: bfloat16 [2048, 64, 128], P(('ctx', 'head')), may hold values from -1.5 to 1.5
- log_norms: float32 [2048, 64], P(('ctx', 'head')), may hold values from 1 to 4
- block_doc: int32 [16], replicated, may hold values from 0 to 5, never falling along the last dimension, each value on 1 to 8 neighbouring positions
Outputs:
- query_grads: bfloat16 [2048, 64, 128], P(('ctx', 'head'))
- key_grads: bfloat16 [2048, 8, 128], P(('ctx', 'head'))
- value_grads: bfloat16 [2048, 8, 128], P(('ctx', 'head'))
Inputs may be any that keep to these rules, and one draw needn't show every extreme that they name: `block_doc`: block ids never fall; each document covers 1 to 8 blocks, and one covers exactly 8.
All inputs are finite; a program needn't handle non-finite values.
Results may differ from a plain program's by a relative error of at most 0.0058.
Values may be sent and summed in bfloat16 or wider, within the bound.
No kernel may reach another device: no remote copies, remote signals or barrier semaphores. Data moves between devices by JAX's collectives and lax.ppermute only.
A program may use at most 64 MiB of HBM per device.

v0:
```python
import jax
import jax.numpy as jnp
from jax import lax
from jax.sharding import PartitionSpec as P

BLK = 128


def shifted(value, axis, steps):
    count = lax.axis_size(axis)
    initial, last = (max(0, -steps), min(count, count - steps))
    return lax.ppermute(value, axis, [(source, source + steps) for source in range(initial, last)])


def tile_pass(q_tile, grad_tile, norm_tile, delta_tile, key_tile, value_tile, visible):
    scale_factor = q_tile.shape[-1] ** (-0.5)
    scores = (
        jnp.einsum("qhd,khd->hqk", q_tile, key_tile, preferred_element_type=jnp.float32)
        * scale_factor
    )
    soft_probs = jnp.where(visible[None], jnp.exp(scores - norm_tile.T[:, :, None]), 0.0)
    grad_probs = jnp.einsum(
        "qhd,khd->hqk", grad_tile, value_tile, preferred_element_type=jnp.float32
    )
    grad_scores = (soft_probs * (grad_probs - delta_tile.T[:, :, None])).astype(jnp.bfloat16)
    query_part = None
    key_part = None
    value_part = None
    query_part = (
        jnp.einsum("hqk,khd->qhd", grad_scores, key_tile, preferred_element_type=jnp.float32)
        * scale_factor
    )
    key_part = (
        jnp.einsum("hqk,qhd->khd", grad_scores, q_tile, preferred_element_type=jnp.float32)
        * scale_factor
    )
    value_part = jnp.einsum(
        "hqk,qhd->khd",
        soft_probs.astype(jnp.bfloat16),
        grad_tile,
        preferred_element_type=jnp.float32,
    )
    return (query_part, key_part, value_part)


def add_rows(accum, start, tile_rows, addend):
    return lax.dynamic_update_slice_in_dim(
        accum, lax.dynamic_slice_in_dim(accum, start, tile_rows, 0) + addend, start, 0
    )


def accumulate(
    carried, query_side, key_side, docs_query, docs_key, row_index, col_index, tile_rows, causal
):
    q_start = row_index * tile_rows
    k_start = col_index * tile_rows
    rows_docs = lax.dynamic_slice_in_dim(docs_query, q_start, tile_rows, 0)
    cols_docs = lax.dynamic_slice_in_dim(docs_key, k_start, tile_rows, 0)
    visible = rows_docs[:, None] == cols_docs[None, :]
    if causal:
        offsets = jnp.arange(tile_rows, dtype=jnp.int32)
        visible = visible & ((q_start + offsets)[:, None] >= (k_start + offsets)[None, :])

    def update(current):
        query_acc, key_acc, value_acc = current
        query_parts = [
            lax.dynamic_slice_in_dim(member, q_start, tile_rows, 0) for member in query_side
        ]
        key_parts = [lax.dynamic_slice_in_dim(member, k_start, tile_rows, 0) for member in key_side]
        query_part, key_part, value_part = tile_pass(
            query_parts[0],
            query_parts[1],
            query_parts[2],
            query_parts[3],
            key_parts[0],
            key_parts[1],
            visible,
        )
        query_acc = add_rows(query_acc, q_start, tile_rows, query_part)
        key_acc = add_rows(key_acc, k_start, tile_rows, key_part)
        value_acc = add_rows(value_acc, k_start, tile_rows, value_part)
        return (query_acc, key_acc, value_acc)

    return lax.cond(jnp.any(visible), update, lambda current: current, carried)


def own_sweep(carried, query_side, key_side, own_docs, tile_rows, tile_count):

    def outer_step(row_index, current):

        def inner_step(col_index, inner_state):
            return accumulate(
                inner_state,
                query_side,
                key_side,
                own_docs,
                own_docs,
                row_index,
                col_index,
                tile_rows,
                True,
            )

        return lax.fori_loop(0, row_index + 1, inner_step, current)

    return lax.fori_loop(0, tile_count, outer_step, carried)


def cross_sweep(carried, query_side, key_side, docs_query, docs_key, tile_rows, tile_count):

    def visit(flat_index, current):
        return accumulate(
            current,
            query_side,
            key_side,
            docs_query,
            docs_key,
            flat_index // tile_count,
            flat_index % tile_count,
            tile_rows,
            False,
        )

    return lax.fori_loop(0, tile_count * tile_count, visit, carried)


def per_device(queries, keys, values, outputs, out_grads, log_norms, block_doc):
    heads_all = queries.shape[1]
    kv_heads = keys.shape[1]
    query_group_factor = heads_all // kv_heads
    keys_wide = jnp.repeat(keys, query_group_factor, axis=1)
    values_wide = jnp.repeat(values, query_group_factor, axis=1)
    q_here, k_here, v_here, grad_here, out_here = (
        lax.all_to_all(queries, "head", split_axis=1, concat_axis=0, tiled=True),
        lax.all_to_all(keys_wide, "head", split_axis=1, concat_axis=0, tiled=True),
        lax.all_to_all(values_wide, "head", split_axis=1, concat_axis=0, tiled=True),
        lax.all_to_all(out_grads, "head", split_axis=1, concat_axis=0, tiled=True),
        lax.all_to_all(outputs, "head", split_axis=1, concat_axis=0, tiled=True),
    )
    norms_here = lax.all_to_all(log_norms, "head", split_axis=1, concat_axis=0, tiled=True)
    deltas_here = jnp.sum(grad_here.astype(jnp.float32) * out_here.astype(jnp.float32), axis=-1)
    group_len = q_here.shape[0]
    tile_rows = min(512, group_len)
    tile_count = group_len // tile_rows
    group_blocks = group_len // BLK
    ctx_index = lax.axis_index("ctx")

    def docs_of(range_index):
        return jnp.repeat(
            lax.dynamic_slice_in_dim(block_doc, range_index * group_blocks, group_blocks, 0), BLK
        )

    own_docs = docs_of(ctx_index)
    prior_docs = jnp.where(ctx_index > 0, docs_of(jnp.maximum(ctx_index - 1, 0)), -1)
    query_side = (q_here, grad_here, norms_here, deltas_here)
    key_side = (k_here, v_here)
    zero_rows = jnp.zeros(q_here.shape, jnp.float32)
    own_state = own_sweep(
        (zero_rows, zero_rows, zero_rows), query_side, key_side, own_docs, tile_rows, tile_count
    )
    prior_pair = shifted((k_here, v_here), "ctx", 1)
    query_acc, side_keys, side_values = cross_sweep(
        (own_state[0], zero_rows, zero_rows),
        query_side,
        prior_pair,
        own_docs,
        prior_docs,
        tile_rows,
        tile_count,
    )
    later_keys, later_values = shifted((side_keys, side_values), "ctx", -1)
    key_acc = own_state[1] + later_keys
    value_acc = own_state[2] + later_values
    query_grads, key_head_count, value_head_count = (
        lax.all_to_all(
            query_acc.astype(jnp.bfloat16), "head", split_axis=0, concat_axis=1, tiled=True
        ),
        lax.all_to_all(
            key_acc.astype(jnp.bfloat16), "head", split_axis=0, concat_axis=1, tiled=True
        ),
        lax.all_to_all(
            value_acc.astype(jnp.bfloat16), "head", split_axis=0, concat_axis=1, tiled=True
        ),
    )
    tok_rows = query_grads.shape[0]
    head_dim = query_grads.shape[2]
    key_grads = jnp.sum(
        key_head_count.astype(jnp.float32).reshape(
            tok_rows, kv_heads, query_group_factor, head_dim
        ),
        axis=2,
    ).astype(jnp.bfloat16)
    value_grads = jnp.sum(
        value_head_count.astype(jnp.float32).reshape(
            tok_rows, kv_heads, query_group_factor, head_dim
        ),
        axis=2,
    ).astype(jnp.bfloat16)
    return (query_grads, key_grads, value_grads)


def solution(mesh):
    in_specs = (
        P(("ctx", "head"), None, None),
        P(("ctx", "head"), None, None),
        P(("ctx", "head"), None, None),
        P(("ctx", "head"), None, None),
        P(("ctx", "head"), None, None),
        P(("ctx", "head"), None),
        P(),
    )
    out_specs = (
        P(("ctx", "head"), None, None),
        P(("ctx", "head"), None, None),
        P(("ctx", "head"), None, None),
    )
    return jax.shard_map(
        per_device, mesh=mesh, in_specs=in_specs, out_specs=out_specs, check_vma=False
    )
```

profile of v0, /device:TPU:1, one launch (start us, length us, event | category | flops | bytes accessed | tf_op | source)
XLA Modules:
  0.0 353.0 jit_solution(14886439524547921475)
XLA Ops:
  2.2 7.4 %all-to-all-start.2 = ((f32[16,1,256]{2,1,0:T(1,128)}), f32[16,1,256]{2,1,0:T(1,128)S(1)}, u32[]{:S(2)}, u32[]{:S(2)}) async-start(f32[16,1,256]{2,1,0:T(1,128)} %reshape.57), calls=%async_computation.2 | async-start | bytes 32768 | tf_op jit(solution)/shard_map/all_to_all | solution.py:140
  10.6 5.3 %all-to-all-done.2 = f32[16,1,256]{2,1,0:T(1,128)S(1)} async-done(((f32[16,1,256]{2,1,0:T(1,128)}), f32[16,1,256]{2,1,0:T(1,128)S(1)}, u32[]{:S(2)}, u32[]{:S(2)}) %all-to-all-start.2) | async-done | bytes 16416 | tf_op jit(solution)/shard_map/all_to_all | solution.py:140
  17.0 3.7 %all-to-all-start.4 = ((bf16[64,64,128]{2,0,1:T(8,128)(2,1)}), bf16[64,64,128]{2,0,1:T(8,128)(2,1)S(1)}, u32[]{:S(2)}, u32[]{:S(2)}) async-start(bf16[64,64,128]{2,0,1:T(8,128)(2,1)} %bitcast.23), calls=%async_computation.4 | async-start | bytes 2097152 | tf_op jit(solution)/shard_map/all_to_all | solution.py:136
  20.8 22.0 %all-to-all-done.4 = bf16[64,64,128]{2,0,1:T(8,128)(2,1)S(1)} async-done(((bf16[64,64,128]{2,0,1:T(8,128)(2,1)}), bf16[64,64,128]{2,0,1:T(8,128)(2,1)S(1)}, u32[]{:S(2)}, u32[]{:S(2)}) %all-to-all-start.4) | async-done | bytes 1048608 | tf_op jit(solution)/shard_map/all_to_all | solution.py:136
  44.0 6.6 %all-to-all-start = ((bf16[64,64,128]{2,0,1:T(8,128)(2,1)}), bf16[64,64,128]{2,0,1:T(8,128)(2,1)S(1)}, u32[]{:S(2)}, u32[]{:S(2)}) async-start(bf16[64,64,128]{2,0,1:T(8,128)(2,1)} %bitcast.11), calls=%async_computation | async-start | bytes 2097152 | tf_op jit(solution)/shard_map/all_to_all | solution.py:135
  50.6 1.7 copy.179
  52.3 20.5 %all-to-all-done = bf16[64,64,128]{2,0,1:T(8,128)(2,1)S(1)} async-done(((bf16[64,64,128]{2,0,1:T(8,128)(2,1)}), bf16[64,64,128]{2,0,1:T(8,128)(2,1)S(1)}, u32[]{:S(2)}, u32[]{:S(2)}) %all-to-all-start) | async-done | bytes 1048608 | tf_op jit(solution)/shard_map/all_to_all | solution.py:135
  72.7 6.7 %all-to-all-start.1 = ((bf16[64,64,128]{2,0,1:T(8,128)(2,1)}), bf16[64,64,128]{2,0,1:T(8,128)(2,1)S(1)}, u32[]{:S(2)}, u32[]{:S(2)}) async-start(bf16[64,64,128]{2,0,1:T(8,128)(2,1)} %copy.179), calls=%async_computation.1 | async-start | bytes 2097152 | tf_op jit(solution)/shard_map/all_to_all | solution.py:134
  79.5 2.9 copy.183
  82.4 19.3 %all-to-all-done.1 = bf16[64,64,128]{2,0,1:T(8,128)(2,1)S(1)} async-done(((bf16[64,64,128]{2,0,1:T(8,128)(2,1)}), bf16[64,64,128]{2,0,1:T(8,128)(2,1)S(1)}, u32[]{:S(2)}, u32[]{:S(2)}) %all-to-all-start.1) | async-done | bytes 1048608 | tf_op jit(solution)/shard_map/all_to_all | solution.py:134
  102.6 6.7 %all-to-all-start.3 = ((bf16[64,64,128]{2,0,1:T(8,128)(2,1)}), bf16[64,64,128]{2,0,1:T(8,128)(2,1)S(1)}, u32[]{:S(2)}, u32[]{:S(2)}) async-start(bf16[64,64,128]{2,0,1:T(8,128)(2,1)} %copy.183), calls=%async_computation.3 | async-start | bytes 2097152 | tf_op jit(solution)/shard_map/all_to_all | solution.py:137
  109.4 2.9 copy.187
  112.2 19.3 %all-to-all-done.3 = bf16[64,64,128]{2,0,1:T(8,128)(2,1)S(1)} async-done(((bf16[64,64,128]{2,0,1:T(8,128)(2,1)}), bf16[64,64,128]{2,0,1:T(8,128)(2,1)S(1)}, u32[]{:S(2)}, u32[]{:S(2)}) %all-to-all-start.3) | async-done | bytes 1048608 | tf_op jit(solution)/shard_map/all_to_all | solution.py:137
  131.5 6.8 %all-to-all-start.5 = ((bf16[64,64,128]{2,0,1:T(8,128)(2,1)}), bf16[64,64,128]{2,0,1:T(8,128)(2,1)}, u32[]{:S(2)}, u32[]{:S(2)}) async-start(bf16[64,64,128]{2,0,1:T(8,128)(2,1)} %copy.187), calls=%async_computation.5 | async-start | bytes 2097152 | tf_op jit(solution)/shard_map/all_to_all | solution.py:138
  143.8 16.7 %all-to-all-done.5 = bf16[64,64,128]{2,0,1:T(8,128)(2,1)} async-done(((bf16[64,64,128]{2,0,1:T(8,128)(2,1)}), bf16[64,64,128]{2,0,1:T(8,128)(2,1)}, u32[]{:S(2)}, u32[]{:S(2)}) %all-to-all-start.5) | async-done | bytes 1048608 | tf_op jit(solution)/shard_map/all_to_all | solution.py:138
  160.5 1.8 fusion.71
  168.7 35.1 %while.67 = (s32[]{:T(128)}, f32[1024,4,128]{0,2,1:T(8,128)S(1)}, f32[1024,4,128]{0,2,1:T(8,128)}, f32[1024,4,128]{0,2,1:T(8,128)}, s32[1024]{0:T(1024)S(1)}, /*...) while((s32[]{:T(128)}, f32[1024,4,128]{0,2,1:T(8,128)S(1)}, ...), condition=%wide.region_7.8_spmd, body=%wide.region_1.7_spmd.sunk | while | flops 1355023360 | bytes 67449840 | solution.py:106
  168.8 11.6 %while.69 = (s32[]{:T(128)}, f32[1024,4,128]{0,2,1:T(8,128)S(1)}, f32[1024,4,128]{0,2,1:T(8,128)}, f32[1024,4,128]{0,2,1:T(8,128)}, s32[]{:T(128)}, /*index=5*/s...) while((s32[]{:T(128)}, f32[1024,4,128]{0,2,1:T(8,128)S(1)}, ...), condition=%wide.region_6.6_spmd, body=%wide.region_2.5_spmd.sunk | while | flops 1355023360 | bytes 67445368 | solution.py:104
  170.5 10.0 %conditional.5 = ((f32[1024,4,128]{0,2,1:T(8,128)S(1)}, f32[1024,4,128]{0,2,1:T(8,128)}, f32[1024,4,128]{0,2,1:T(8,128)})) conditional(s32[]{:T(128)} %convert_element_type.107, (f32[1024,4,128]{0,2,1:T(8,128)S(1)}, f32[1024,4,128]{0,2,1:T(8,128)}, f32[1024,4,128]{0,2,1:T(8,128)}) %tuple.125, (s32[]{:T(128)}, f32[1024,4,128]{0,2,1:T(8,128)S(1)}, ...), branch_computations={%region_4.3_spmd, %region_5.4_spmd} | conditional | flops 1353973760 | bytes 67166496 | solution.py:84
  170.5 1.8 fusion.26
  172.4 2.8 multiply_convert_fusion
  178.1 2.3 fusion.15
  180.6 23.3 %while.69 = (s32[]{:T(128)}, f32[1024,4,128]{0,2,1:T(8,128)S(1)}, f32[1024,4,128]{0,2,1:T(8,128)}, f32[1024,4,128]{0,2,1:T(8,128)}, s32[]{:T(128)}, /*index=5*/s...) while((s32[]{:T(128)}, f32[1024,4,128]{0,2,1:T(8,128)S(1)}, ...), condition=%wide.region_6.6_spmd, body=%wide.region_2.5_spmd.sunk | while | flops 1355023360 | bytes 67445368 | solution.py:104
  182.2 10.0 %conditional.5 = ((f32[1024,4,128]{0,2,1:T(8,128)S(1)}, f32[1024,4,128]{0,2,1:T(8,128)}, f32[1024,4,128]{0,2,1:T(8,128)})) conditional(s32[]{:T(128)} %convert_element_type.107, (f32[1024,4,128]{0,2,1:T(8,128)S(1)}, f32[1024,4,128]{0,2,1:T(8,128)}, f32[1024,4,128]{0,2,1:T(8,128)}) %tuple.125, (s32[]{:T(128)}, f32[1024,4,128]{0,2,1:T(8,128)S(1)}, ...), branch_computations={%region_4.3_spmd, %region_5.4_spmd} | conditional | flops 1353973760 | bytes 67166496 | solution.py:84
  182.3 1.8 fusion.26
  184.1 2.8 multiply_convert_fusion
  189.9 2.3 fusion.15
  193.8 10.0 %conditional.5 = ((f32[1024,4,128]{0,2,1:T(8,128)S(1)}, f32[1024,4,128]{0,2,1:T(8,128)}, f32[1024,4,128]{0,2,1:T(8,128)})) conditional(s32[]{:T(128)} %convert_element_type.107, (f32[1024,4,128]{0,2,1:T(8,128)S(1)}, f32[1024,4,128]{0,2,1:T(8,128)}, f32[1024,4,128]{0,2,1:T(8,128)}) %tuple.125, (s32[]{:T(128)}, f32[1024,4,128]{0,2,1:T(8,128)S(1)}, ...), branch_computations={%region_4.3_spmd, %region_5.4_spmd} | conditional | flops 1353973760 | bytes 67166496 | solution.py:84
  193.9 1.8 fusion.26
  195.8 2.8 multiply_convert_fusion
  201.5 2.3 fusion.15
  205.4 1.7 broadcast_in_dim.59
  207.1 60.3 %while.68 = (s32[]{:T(128)}, f32[1024,4,128]{0,2,1:T(8,128)S(1)}, f32[1024,4,128]{0,2,1:T(8,128)}, f32[1024,4,128]{0,2,1:T(8,128)}, s32[1024]{0:T(1024)S(1)}, /*...) while((s32[]{:T(128)}, f32[1024,4,128]{0,2,1:T(8,128)S(1)}, ...), condition=%wide.region_12.13_spmd, body=%wide.region_8.12_spmd.sunk | while | flops 1354498048 | bytes 56955632 | solution.py:124
  210.6 26.7 %conditional.4 = ((f32[1024,4,128]{0,2,1:T(8,128)S(1)}, f32[1024,4,128]{0,2,1:T(8,128)}, f32[1024,4,128]{0,2,1:T(8,128)})) conditional(s32[]{:T(128)} %convert_element_type.106, (f32[1024,4,128]{0,2,1:T(8,128)S(1)}, f32[1024,4,128]{0,2,1:T(8,128)}, f32[1024,4,128]{0,2,1:T(8,128)}) %tuple.120, (s32[]{:T(128)}, f32[1024,4,128]{0,2,1:T(8,128)S(1)}, ...), branch_computations={%region_10.10_spmd, %region_11.11_spmd} | conditional | flops 1353973760 | bytes 56680688 | solution.py:84
  210.7 1.9 fusion.58
  212.6 3.0 multiply_convert_fusion.1
  215.6 2.3 fusion.51
  219.5 2.7 fusion.50
  222.2 4.4 %dynamic_update_slice.15 = f32[1024,4,128]{0,2,1:T(8,128)S(1)} dynamic-update-slice(f32[1024,4,128]{0,2,1:T(8,128)S(1)} %get-tuple-element.720, f32[512,4,128]{0,2,1:T(8,128)} %fusion.50, s32[]{:T(128)S(6)} %select_n.108, s32[]{:T(128)} %constant.154.clone, s32[]{:T(128)} %constant.154.clone) | dynamic-update-slice | bytes 2097156 | tf_op jit(solution)/shard_map/while/body/eval_jaxpr/cond/branch_1_fun/dynamic_update_slice | solution.py:47
  226.6 5.3 %dynamic_update_slice.16 = f32[1024,4,128]{0,2,1:T(8,128)} dynamic-update-slice(f32[1024,4,128]{0,2,1:T(8,128)} %get-tuple-element.730, f32[512,4,128]{0,2,1:T(8,128)} %fusion.48, s32[]{:T(128)S(6)} %select_n.109, s32[]{:T(128)} %constant.154.clone, s32[]{:T(128)} %constant.154.clone) | dynamic-update-slice | bytes 2097156 | tf_op jit(solution)/shard_map/while/body/eval_jaxpr/cond/branch_1_fun/dynamic_update_slice | solution.py:47
  232.0 5.3 %dynamic_update_slice.17 = f32[1024,4,128]{0,2,1:T(8,128)} dynamic-update-slice(f32[1024,4,128]{0,2,1:T(8,128)} %get-tuple-element.731, f32[512,4,128]{0,2,1:T(8,128)} %fusion.51, s32[]{:T(128)S(6)} %select_n.109, s32[]{:T(128)} %constant.154.clone, s32[]{:T(128)} %constant.154.clone) | dynamic-update-slice | bytes 2097156 | tf_op jit(solution)/shard_map/while/body/eval_jaxpr/cond/branch_1_fun/dynamic_update_slice | solution.py:47
  240.8 26.7 %conditional.4 = ((f32[1024,4,128]{0,2,1:T(8,128)S(1)}, f32[1024,4,128]{0,2,1:T(8,128)}, f32[1024,4,128]{0,2,1:T(8,128)})) conditional(s32[]{:T(128)} %convert_element_type.106, (f32[1024,4,128]{0,2,1:T(8,128)S(1)}, f32[1024,4,128]{0,2,1:T(8,128)}, f32[1024,4,128]{0,2,1:T(8,128)}) %tuple.120, (s32[]{:T(128)}, f32[1024,4,128]{0,2,1:T(8,128)S(1)}, ...), branch_computations={%region_10.10_spmd, %region_11.11_spmd} | conditional | flops 1353973760 | bytes 56680688 | solution.py:84
  240.9 1.9 fusion.58
  242.7 3.0 multiply_convert_fusion.1
  245.7 2.3 fusion.51
  249.6 2.7 fusion.50
  252.4 4.4 %dynamic_update_slice.15 = f32[1024,4,128]{0,2,1:T(8,128)S(1)} dynamic-update-slice(f32[1024,4,128]{0,2,1:T(8,128)S(1)} %get-tuple-element.720, f32[512,4,128]{0,2,1:T(8,128)} %fusion.50, s32[]{:T(128)S(6)} %select_n.108, s32[]{:T(128)} %constant.154.clone, s32[]{:T(128)} %constant.154.clone) | dynamic-update-slice | bytes 2097156 | tf_op jit(solution)/shard_map/while/body/eval_jaxpr/cond/branch_1_fun/dynamic_update_slice | solution.py:47
  256.8 5.3 %dynamic_update_slice.16 = f32[1024,4,128]{0,2,1:T(8,128)} dynamic-update-slice(f32[1024,4,128]{0,2,1:T(8,128)} %get-tuple-element.730, f32[512,4,128]{0,2,1:T(8,128)} %fusion.48, s32[]{:T(128)S(6)} %select_n.109, s32[]{:T(128)} %constant.154.clone, s32[]{:T(128)} %constant.154.clone) | dynamic-update-slice | bytes 2097156 | tf_op jit(solution)/shard_map/while/body/eval_jaxpr/cond/branch_1_fun/dynamic_update_slice | solution.py:47
  262.1 5.3 %dynamic_update_slice.17 = f32[1024,4,128]{0,2,1:T(8,128)} dynamic-update-slice(f32[1024,4,128]{0,2,1:T(8,128)} %get-tuple-element.731, f32[512,4,128]{0,2,1:T(8,128)} %fusion.51, s32[]{:T(128)S(6)} %select_n.109, s32[]{:T(128)} %constant.154.clone, s32[]{:T(128)} %constant.154.clone) | dynamic-update-slice | bytes 2097156 | tf_op jit(solution)/shard_map/while/body/eval_jaxpr/cond/branch_1_fun/dynamic_update_slice | solution.py:47
  267.4 2.9 copy.192
  270.3 2.7 collective-permute-start.2
  273.0 1.7 copy.189
  274.7 6.7 %all-to-all-start.6 = ((bf16[1024,4,128]{2,1,0:T(4,128)(2,1)}), bf16[1024,4,128]{2,1,0:T(4,128)(2,1)S(1)}, u32[]{:S(2)}, u32[]{:S(2)}) async-start(bf16[1024,4,128]{2,1,0:T(4,128)(2,1)} %copy.189), calls=%async_computation.6 | async-start | bytes 2097152 | tf_op jit(solution)/shard_map/all_to_all | solution.py:175
  281.5 3.1 copy.197
  284.6 2.6 collective-permute-start.3
  287.1 1.9 copy.193
  289.0 3.8 %add_convert_fusion.1 = bf16[1024,4,128]{2,1,0:T(4,128)(2,1)} fusion(f32[1024,4,128]{2,1,0:T(4,128)} %copy.193, f32[1024,4,128]{2,1,0:T(4,128)} %collective-permute-done.2), kind=kLoop, calls=%fused_computation.80 | loop fusion | flops 1048576 | bytes 5242880 | tf_op jit(solution)/shard_map/convert_element_type | solution.py:179
  292.8 6.3 %all-to-all-done.6 = bf16[1024,4,128]{2,1,0:T(4,128)(2,1)S(1)} async-done(((bf16[1024,4,128]{2,1,0:T(4,128)(2,1)}), bf16[1024,4,128]{2,1,0:T(4,128)(2,1)S(1)}, u32[]{:S(2)}, u32[]{:S(2)}) %all-to-all-start.6) | async-done | bytes 1048608 | tf_op jit(solution)/shard_map/all_to_all | solution.py:175
  299.1 9.9 %all-to-all-start.7 = ((bf16[1024,4,128]{2,1,0:T(4,128)(2,1)}), bf16[1024,4,128]{2,1,0:T(4,128)(2,1)}, u32[]{:S(2)}, u32[]{:S(2)}) async-start(bf16[1024,4,128]{2,1,0:T(4,128)(2,1)} %add_convert_fusion.1), calls=%async_computation.7 | async-start | bytes 2097152 | tf_op jit(solution)/shard_map/all_to_all | solution.py:178
  309.0 1.9 copy.198
  310.8 3.8 %add_convert_fusion = bf16[1024,4,128]{2,1,0:T(4,128)(2,1)} fusion(f32[1024,4,128]{2,1,0:T(4,128)} %copy.198, f32[1024,4,128]{2,1,0:T(4,128)} %collective-permute-done.3), kind=kLoop, calls=%fused_computation.78 | loop fusion | flops 1048576 | bytes 5242880 | tf_op jit(solution)/shard_map/convert_element_type | solution.py:182
  314.6 15.5 %all-to-all-done.7 = bf16[1024,4,128]{2,1,0:T(4,128)(2,1)} async-done(((bf16[1024,4,128]{2,1,0:T(4,128)(2,1)}), bf16[1024,4,128]{2,1,0:T(4,128)(2,1)}, u32[]{:S(2)}, u32[]{:S(2)}) %all-to-all-start.7) | async-done | bytes 1048608 | tf_op jit(solution)/shard_map/all_to_all | solution.py:178
  330.1 7.6 %all-to-all-start.8 = ((bf16[1024,4,128]{2,1,0:T(4,128)(2,1)}), bf16[1024,4,128]{2,1,0:T(4,128)(2,1)S(1)}, u32[]{:S(2)}, u32[]{:S(2)}) async-start(bf16[1024,4,128]{2,1,0:T(4,128)(2,1)} %add_convert_fusion), calls=%async_computation.8 | async-start | bytes 2097152 | tf_op jit(solution)/shard_map/all_to_all | solution.py:181
  341.7 10.4 %all-to-all-done.8 = bf16[1024,4,128]{2,1,0:T(4,128)(2,1)S(1)} async-done(((bf16[1024,4,128]{2,1,0:T(4,128)(2,1)}), bf16[1024,4,128]{2,1,0:T(4,128)(2,1)S(1)}, u32[]{:S(2)}, u32[]{:S(2)}) %all-to-all-start.8) | async-done | bytes 1048608 | tf_op jit(solution)/shard_map/all_to_all | solution.py:181
  (135 shorter events, 43.9 us)
Async XLA Ops:
  0.6 20.1 %copy-start.13 = (bf16[64,8,128]{2,1,0:T(8,128)(2,1)S(1)}, bf16[64,8,128]{2,1,0:T(8,128)(2,1)}, u32[]{:S(2)}) copy-start(bf16[64,8,128]{2,1,0:T(8,128)(2,1)} %param.18) | copy-start | bytes 393220
  2.2 13.6 %all-to-all-start.2 = ((f32[16,1,256]{2,1,0:T(1,128)}), f32[16,1,256]{2,1,0:T(1,128)S(1)}, u32[]{:S(2)}, u32[]{:S(2)}) async-start(f32[16,1,256]{2,1,0:T(1,128)} %reshape.57), calls=%async_computation.2 | async-start | bytes 32768 | tf_op jit(solution)/shard_map/all_to_all | solution.py:140
  17.0 25.8 %all-to-all-start.4 = ((bf16[64,64,128]{2,0,1:T(8,128)(2,1)}), bf16[64,64,128]{2,0,1:T(8,128)(2,1)S(1)}, u32[]{:S(2)}, u32[]{:S(2)}) async-start(bf16[64,64,128]{2,0,1:T(8,128)(2,1)} %bitcast.23), calls=%async_computation.4 | async-start | bytes 2097152 | tf_op jit(solution)/shard_map/all_to_all | solution.py:136
  20.7 29.9 %copy-start.10 = (bf16[64,64,128]{2,1,0:T(8,128)(2,1)S(1)}, bf16[64,64,128]{2,1,0:T(8,128)(2,1)}, u32[]{:S(2)}) copy-start(bf16[64,64,128]{2,1,0:T(8,128)(2,1)} %param.17) | copy-start | bytes 3145732
  44.0 28.7 %all-to-all-start = ((bf16[64,64,128]{2,0,1:T(8,128)(2,1)}), bf16[64,64,128]{2,0,1:T(8,128)(2,1)S(1)}, u32[]{:S(2)}, u32[]{:S(2)}) async-start(bf16[64,64,128]{2,0,1:T(8,128)(2,1)} %bitcast.11), calls=%async_computation | async-start | bytes 2097152 | tf_op jit(solution)/shard_map/all_to_all | solution.py:135
  72.7 28.9 %all-to-all-start.1 = ((bf16[64,64,128]{2,0,1:T(8,128)(2,1)}), bf16[64,64,128]{2,0,1:T(8,128)(2,1)S(1)}, u32[]{:S(2)}, u32[]{:S(2)}) async-start(bf16[64,64,128]{2,0,1:T(8,128)(2,1)} %copy.179), calls=%async_computation.1 | async-start | bytes 2097152 | tf_op jit(solution)/shard_map/all_to_all | solution.py:134
  101.6 1.0 copy-start.8
  102.6 28.9 %all-to-all-start.3 = ((bf16[64,64,128]{2,0,1:T(8,128)(2,1)}), bf16[64,64,128]{2,0,1:T(8,128)(2,1)S(1)}, u32[]{:S(2)}, u32[]{:S(2)}) async-start(bf16[64,64,128]{2,0,1:T(8,128)(2,1)} %copy.183), calls=%async_computation.3 | async-start | bytes 2097152 | tf_op jit(solution)/shard_map/all_to_all | solution.py:137
  109.4 28.9 %copy-start.15 = (s32[16]{0:T(128)S(1)}, s32[16]{0:T(128)}, u32[]{:S(2)}) copy-start(s32[16]{0:T(128)} %param.23) | copy-start | bytes 196
  131.5 29.0 %all-to-all-start.5 = ((bf16[64,64,128]{2,0,1:T(8,128)(2,1)}), bf16[64,64,128]{2,0,1:T(8,128)(2,1)}, u32[]{:S(2)}, u32[]{:S(2)}) async-start(bf16[64,64,128]{2,0,1:T(8,128)(2,1)} %copy.187), calls=%async_computation.5 | async-start | bytes 2097152 | tf_op jit(solution)/shard_map/all_to_all | solution.py:138
  140.5 2.1 copy-start.9
  162.4 41.4 %collective-permute-start = (bf16[1024,4,128]{2,0,1:T(8,128)(2,1)}, bf16[1024,4,128]{2,0,1:T(8,128)(2,1)}, u32[]{:S(2)}, u32[]{:S(2)}) collective-permute-start(bf16[1024,4,128]{2,0,1:T(8,128)(2,1)} %bitcast.14), channel_id=1, source_target_pairs={{0,16},{1,17},{2,18},{3,19},{4,20},{5,21},{6,22},{7,23},{8,24},{9,... | collective-permute-start | bytes 3145736 | tf_op jit(solution)/shard_map/ppermute | solution.py:12
  163.7 40.1 %collective-permute-start.1 = (bf16[1024,4,128]{2,0,1:T(8,128)(2,1)}, bf16[1024,4,128]{2,0,1:T(8,128)(2,1)}, u32[]{:S(2)}, u32[]{:S(2)}) collective-permute-start(bf16[1024,4,128]{2,0,1:T(8,128)(2,1)} %bitcast.26), channel_id=1, source_target_pairs={{0,16},{1,17},{2,18},{3,19},{4,20},{5,21},{6,22},{7,23},{8,24},{9,... | collective-permute-start | bytes 3145736 | tf_op jit(solution)/shard_map/ppermute | solution.py:12
  170.5 1.9 copy-start.11
  172.4 2.8 copy-start.4
  175.2 1.6 copy-start
  176.8 1.4 copy-start.5
  178.1 2.3 copy-start.1
  182.2 1.9 copy-start.11
  184.1 2.8 copy-start.4
  186.9 1.6 copy-start
  188.5 1.4 copy-start.5
  189.9 2.3 copy-start.1
  193.9 1.9 copy-start.11
  195.8 2.8 copy-start.4
  198.6 1.6 copy-start
  200.2 1.4 copy-start.5
  201.5 2.3 copy-start.1
  203.9 3.2 copy-start.14
  210.7 1.9 copy-start.12
  212.6 3.0 copy-start.7
  215.6 2.3 copy-start.3
  240.9 1.9 copy-start.12
  242.7 3.0 copy-start.7
  245.7 2.3 copy-start.3
  270.3 18.7 %collective-permute-start.2 = (f32[1024,4,128]{2,1,0:T(4,128)}, f32[1024,4,128]{2,1,0:T(4,128)}, u32[]{:S(2)}, u32[]{:S(2)}) collective-permute-start(f32[1024,4,128]{2,1,0:T(4,128)} %copy.192), channel_id=1, source_target_pairs={{16,0},{17,1},{18,2},{19,3},{20,4},{21,5},{22,6},{23,7},{24,8},{25... | collective-permute-start | bytes 6291464 | tf_op jit(solution)/shard_map/ppermute | solution.py:12
  274.7 24.3 %all-to-all-start.6 = ((bf16[1024,4,128]{2,1,0:T(4,128)(2,1)}), bf16[1024,4,128]{2,1,0:T(4,128)(2,1)S(1)}, u32[]{:S(2)}, u32[]{:S(2)}) async-start(bf16[1024,4,128]{2,1,0:T(4,128)(2,1)} %copy.189), calls=%async_computation.6 | async-start | bytes 2097152 | tf_op jit(solution)/shard_map/all_to_all | solution.py:175
  281.5 5.7 %copy-start.2 = (f32[1024,4,128]{0,2,1:T(8,128)S(1)}, f32[1024,4,128]{0,2,1:T(8,128)}, u32[]{:S(2)}) copy-start(f32[1024,4,128]{0,2,1:T(8,128)} %get-tuple-element.759) | copy-start | bytes 6291460
  284.6 26.3 %collective-permute-start.3 = (f32[1024,4,128]{2,1,0:T(4,128)}, f32[1024,4,128]{2,1,0:T(4,128)}, u32[]{:S(2)}, u32[]{:S(2)}) collective-permute-start(f32[1024,4,128]{2,1,0:T(4,128)} %copy.197), channel_id=1, source_target_pairs={{16,0},{17,1},{18,2},{19,3},{20,4},{21,5},{22,6},{23,7},{24,8},{25... | collective-permute-start | bytes 6291464 | tf_op jit(solution)/shard_map/ppermute | solution.py:12
  292.8 16.2 %copy-start.6 = (f32[1024,4,128]{0,2,1:T(8,128)S(1)}, f32[1024,4,128]{0,2,1:T(8,128)}, u32[]{:S(2)}) copy-start(f32[1024,4,128]{0,2,1:T(8,128)} %get-tuple-element.761) | copy-start | bytes 6291460
  299.1 31.0 %all-to-all-start.7 = ((bf16[1024,4,128]{2,1,0:T(4,128)(2,1)}), bf16[1024,4,128]{2,1,0:T(4,128)(2,1)}, u32[]{:S(2)}, u32[]{:S(2)}) async-start(bf16[1024,4,128]{2,1,0:T(4,128)(2,1)} %add_convert_fusion.1), calls=%async_computation.7 | async-start | bytes 2097152 | tf_op jit(solution)/shard_map/all_to_all | solution.py:178
  330.1 22.1 %all-to-all-start.8 = ((bf16[1024,4,128]{2,1,0:T(4,128)(2,1)}), bf16[1024,4,128]{2,1,0:T(4,128)(2,1)S(1)}, u32[]{:S(2)}, u32[]{:S(2)}) async-start(bf16[1024,4,128]{2,1,0:T(4,128)(2,1)} %add_convert_fusion), calls=%async_computation.8 | async-start | bytes 2097152 | tf_op jit(solution)/shard_map/all_to_all | solution.py:181
where the time goes:
time: 356 us; the launch traced here: 353 us
  waiting for transfers between devices  135 us (38%)
  local copies, waits for them, and re-layouts  74.4 us (21%)
  starting transfers between devices  70.1 us (20%)
  matrix products  48.9 us (14%)
  other arithmetic  18.1 us (5%)
  loops' own time  5.23 us (1%)
    dynamic_update_slice x6, local copies, waits for them, and re-layouts, add_rows(): lax.dynamic_update_slice_in_dim(accum, lax.dynamic_slice_in_dim(accum, st...  30.1 us
    all_to_all x1, waiting for transfers between devices, per_device(): lax.all_to_all(values_wide, 'head', split_axis=1, concat_axis=0, tiled=True)  22 us
    all_to_all x1, waiting for transfers between devices, per_device(): lax.all_to_all(keys_wide, 'head', split_axis=1, concat_axis=0, tiled=True)  20.5 us
    all_to_all x1, waiting for transfers between devices, per_device(): lax.all_to_all(queries, 'head', split_axis=1, concat_axis=0, tiled=True)  19.3 us
    all_to_all x1, waiting for transfers between devices, per_device(): lax.all_to_all(out_grads, 'head', split_axis=1, concat_axis=0, tiled=True)  19.3 us
    all_to_all x1, waiting for transfers between devices, per_device(): lax.all_to_all(outputs, 'head', split_axis=1, concat_axis=0, tiled=True)  16.7 us
    all_to_all x1, waiting for transfers between devices, per_device(): lax.all_to_all(key_acc.astype(jnp.bfloat16), 'head', split_axis=0, concat...  15.5 us
    dot_general x5, matrix products, tile_pass(): jnp.einsum('qhd,khd->hqk', grad_tile, value_tile, preferred_element_type=...  14.3 us
  transfers between devices with their start and end apart: 13, of which 9 were waited for; matrix products, arithmetic and copies ran while one was open for 19% of the time, Pallas kernels for 0%

commit v1 on v0

v1 whole, which is shorter than its diff:
```python
import functools

import jax
import jax.numpy as jnp
from jax import lax
from jax.experimental import pallas as pl
from jax.experimental.pallas import tpu as pltpu
from jax.sharding import PartitionSpec as P

BLK = 128
LOG2E = 1.4426950408889634
STAT_ROWS = 32


def block_steps(meta, pkg, kv, dq, dk_acc, dv_acc, dq_acc, rows, tok, q_blocks, scale):
    sources = BLK // tok
    wide = sources * rows
    group = rows // tok
    dk_acc[...] = jnp.zeros_like(dk_acc)
    dv_acc[...] = jnp.zeros_like(dv_acc)

    def over_queries(i, _):
        last, first = meta[i], meta[q_blocks + i]
        mine = pl.ds(sources * i, sources)
        q = pkg[mine, 0:rows, :].reshape(wide, 128)
        g = pkg[mine, rows : 2 * rows, :].reshape(wide, 128)
        stats = pkg[mine, 2 * rows :, :].astype(jnp.float32)
        chunks = rows // 128
        lse3, delta3 = (
            stats[:, base : base + chunks]
            + stats[:, base + chunks : base + 2 * chunks]
            + stats[:, base + 2 * chunks : base + 3 * chunks]
            for base in (0, 3 * chunks)
        )
        flat = [(s, c) for s in range(sources) for c in range(chunks)]
        lse = jnp.concatenate([lse3[s, c : c + 1, :] for s, c in flat], axis=1) * LOG2E
        delta = jnp.concatenate([delta3[s, c : c + 1, :] for s, c in flat], axis=1)
        dq_acc[...] = jnp.zeros_like(dq_acc)

        def step(j, masked):
            k = kv[pl.ds(sources * j, sources), 0].reshape(BLK, 128)
            v = kv[pl.ds(sources * j, sources), 1].reshape(BLK, 128)
            s = lax.dot_general(k, q, (((1,), (1,)), ((), ())), preferred_element_type=jnp.float32)
            p = jnp.exp2(s * (scale * LOG2E) - lse)
            if masked:
                key_at = lax.broadcasted_iota(jnp.int32, (BLK, wide), 0)
                query_at = lax.broadcasted_iota(jnp.int32, (BLK, wide), 1) // group
                p = jnp.where(query_at >= key_at, p, 0.0)
            dp = lax.dot_general(v, g, (((1,), (1,)), ((), ())), preferred_element_type=jnp.float32)
            ds = (p * (dp - delta)).astype(jnp.bfloat16)
            at = pl.ds(pl.multiple_of(j * BLK, BLK), BLK)
            dv_acc[at, :] += jnp.dot(p.astype(jnp.bfloat16), g, preferred_element_type=jnp.float32)
            dk_acc[at, :] += jnp.dot(ds, q, preferred_element_type=jnp.float32)
            dq_acc[...] += lax.dot_general(
                ds, k, (((0,), (0,)), ((), ())), preferred_element_type=jnp.float32
            )

        def inner(j, _):
            step(j, False)
            return 0

        lax.fori_loop(first, last, inner, 0)
        step(last, True)
        dq[mine] = (dq_acc[...] * scale).astype(jnp.bfloat16).reshape(sources, rows, 128)
        return 0

    lax.fori_loop(0, q_blocks, over_queries, 0)


def whole_kernel(meta, pkg, kv, dq, dkv, dk_acc, dv_acc, dq_acc, *, rows, tok, q_blocks, scale):
    block_steps(meta, pkg, kv, dq, dk_acc, dv_acc, dq_acc, rows, tok, q_blocks, scale)
    shards = dkv.shape[0]
    dkv[:, 0] = (dk_acc[...] * scale).astype(jnp.bfloat16).reshape(shards, tok, 128)
    dkv[:, 1] = dv_acc[...].astype(jnp.bfloat16).reshape(shards, tok, 128)


def planes_kernel(meta, pkg, *refs, rows, tok, q_blocks, scale, planes):
    near, (dq, *near_grads) = refs[:planes], refs[planes : 2 * planes + 1]
    kv, dkv, dk_acc, dv_acc, dq_acc, sems = refs[2 * planes + 1 :]
    team = pkg.shape[0]
    slots = team // 2
    plane = meta[2 * q_blocks]

    def place(d, b):
        return pl.ds((b * planes + (plane ^ d)) * slots, slots)

    loads = [
        pltpu.make_async_copy(near[d].at[b * slots : (b + 1) * slots], kv.at[place(d, b)], sems.at[d, b])
        for d in range(planes)
        for b in range(2)
    ]
    for copy in loads:
        copy.start()
    for copy in loads:
        copy.wait()
    block_steps(meta, pkg, kv, dq, dk_acc, dv_acc, dq_acc, rows, tok, q_blocks, scale)
    shards = dkv.shape[0]
    dkv[:, 0] = (dk_acc[...] * scale).astype(jnp.bfloat16).reshape(shards, tok, 128)
    dkv[:, 1] = dv_acc[...].astype(jnp.bfloat16).reshape(shards, tok, 128)
    stores = [
        pltpu.make_async_copy(dkv.at[place(d, b)], near_grads[d].at[b * slots : (b + 1) * slots], sems.at[d, b])
        for d in range(planes)
        for b in range(2)
    ]
    for copy in stores:
        copy.start()
    for copy in stores:
        copy.wait()


def attention(meta, pkg, kv, rows, scale):
    by_plane = isinstance(kv, tuple)
    planes = len(kv) if by_plane else 1
    first = kv[0] if by_plane else kv
    shards, _, tok, head_dim = first.shape
    shards = shards * planes
    team = pkg.shape[0]
    q_blocks = team * tok // BLK
    wide = rows * (BLK // tok)
    vmem = pl.BlockSpec(memory_space=pltpu.VMEM)
    anywhere = pl.BlockSpec(memory_space=pl.ANY)
    sizes = dict(rows=rows, tok=tok, q_blocks=q_blocks, scale=scale)
    totals = [
        pltpu.VMEM((shards * tok, head_dim), jnp.float32),
        pltpu.VMEM((shards * tok, head_dim), jnp.float32),
        pltpu.VMEM((wide, head_dim), jnp.float32),
    ]
    dq_shape = jax.ShapeDtypeStruct((team, rows, head_dim), jnp.bfloat16)
    params = pltpu.CompilerParams(vmem_limit_bytes=56 * 1024 * 1024)
    if not by_plane:
        return pl.pallas_call(
            functools.partial(whole_kernel, **sizes),
            out_shape=(dq_shape, jax.ShapeDtypeStruct(kv.shape, jnp.bfloat16)),
            in_specs=[pl.BlockSpec(memory_space=pltpu.SMEM), vmem, vmem],
            out_specs=(vmem, vmem),
            scratch_shapes=totals,
            compiler_params=params,
            name="attention_grads",
        )(meta, pkg, kv)
    whole_kv = pltpu.VMEM((shards, 2, tok, head_dim), jnp.bfloat16)
    dq, *grads = pl.pallas_call(
        functools.partial(planes_kernel, planes=planes, **sizes),
        out_shape=(dq_shape,) + (jax.ShapeDtypeStruct(first.shape, jnp.bfloat16),) * planes,
        in_specs=[pl.BlockSpec(memory_space=pltpu.SMEM), vmem] + [anywhere] * planes,
        out_specs=(vmem,) + (anywhere,) * planes,
        scratch_shapes=[whole_kv, whole_kv] + totals + [pltpu.SemaphoreType.DMA((planes, 2))],
        compiler_params=params,
        name="attention_grads_planes",
    )(meta, pkg, *kv)
    return dq, grads


def pieces(x):
    high = lax.reduce_precision(x, 8, 7)
    rest = x - high
    mid = lax.reduce_precision(rest, 8, 7)
    low = rest - mid
    return [part.astype(jnp.bfloat16) for part in (high, mid, low)]


def per_device(queries, keys, values, outputs, out_grads, log_norms, block_doc):
    tok, heads, head_dim = queries.shape
    kv_heads = keys.shape[1]
    fan = heads // kv_heads
    n_ctx, n_head = lax.axis_size("ctx"), lax.axis_size("head")
    slots = kv_heads // 2
    planes = n_head // slots
    rows = tok * fan
    scale = head_dim**-0.5
    ctx, head = lax.axis_index("ctx"), lax.axis_index("head")
    both = ("ctx", "head")
    teams = [
        [(2 * c + b) * n_head + z * slots + r for b in range(2) for r in range(slots)]
        for c in range(n_ctx // 2)
        for z in range(planes)
    ]
    pairs = [
        [(2 * c + b) * n_head + h for b in range(2) for h in range(n_head)]
        for c in range(n_ctx // 2)
    ]

    by_plane = n_ctx == 2 and planes == 4

    def across(x, distance):
        step = distance * slots
        return lax.ppermute(x, "head", [(h, h ^ step) for h in range(n_head)])

    kv = jnp.stack([keys, values], axis=0).transpose(2, 0, 1, 3)
    if by_plane:
        kv = lax.all_to_all(kv, both, 0, 0, axis_index_groups=teams, tiled=True)
        second, first = across(kv, 2), across(kv, 1)
        kv = (kv, first, second, across(second, 1))
    else:
        kv = kv.reshape(2, 1, slots, 2, tok, head_dim)
        kv = jnp.broadcast_to(kv, (2, planes, slots, 2, tok, head_dim))
        kv = kv.reshape(2 * n_head, 2, tok, head_dim)
        kv = lax.all_to_all(kv, both, 0, 0, axis_index_groups=pairs, tiled=True)

    deltas = jnp.sum(out_grads.astype(jnp.float32) * outputs.astype(jnp.float32), axis=-1)
    stats = jnp.stack(pieces(log_norms) + pieces(deltas), axis=0)
    stats = stats.reshape(6, tok, kv_heads, fan).transpose(2, 0, 1, 3)
    stats = stats.reshape(kv_heads, 6 * rows // 128, 128)
    stats = jnp.pad(stats, ((0, 0), (0, STAT_ROWS - stats.shape[1]), (0, 0)))

    def by_group(x):
        return x.reshape(tok, kv_heads, fan, head_dim).transpose(1, 0, 2, 3).reshape(kv_heads, rows, head_dim)

    pkg = jnp.concatenate([by_group(queries), by_group(out_grads), stats], axis=1)
    pkg = lax.all_to_all(pkg, both, 0, 0, axis_index_groups=teams, tiled=True)

    pair, plane = ctx // 2, head // slots
    range_blocks = n_head * tok // BLK
    team_blocks = slots * tok // BLK
    at = jnp.stack(
        [(2 * pair + b) * range_blocks + plane * team_blocks + j for b in range(2) for j in range(team_blocks)]
    )
    first_block = jnp.sum(block_doc[None, :] < block_doc[at][:, None], axis=1, dtype=jnp.int32)
    ranges_before = 1 if n_ctx > 2 else 0
    base = (2 * pair - ranges_before) * range_blocks
    meta = jnp.concatenate([at - base, first_block - base, plane[None]]).astype(jnp.int32)

    if ranges_before:
        prior = lax.ppermute(kv[n_head:], "ctx", [(c, c + 2) for c in range(n_ctx - 2)])
        kv = jnp.concatenate([prior, kv], axis=0)
    dq, dkv = attention(meta, pkg, kv, rows, scale)
    if ranges_before:
        later = lax.ppermute(dkv[:n_head], "ctx", [(c + 2, c) for c in range(n_ctx - 2)])
        last = (dkv[2 * n_head :].astype(jnp.float32) + later.astype(jnp.float32)).astype(jnp.bfloat16)
        dkv = jnp.concatenate([dkv[n_head : 2 * n_head], last], axis=0)

    if by_plane:
        wider = lambda x: x.astype(jnp.float32)
        relayed = across(dkv[3], 1)
        far = (wider(dkv[2]) + wider(relayed)).astype(jnp.bfloat16)
        far, close = across(far, 2), across(dkv[1], 1)
        dkv = (wider(dkv[0]) + wider(far) + wider(close)).astype(jnp.bfloat16)
        dq = lax.all_to_all(dq, both, 0, 0, axis_index_groups=teams, tiled=True)
        dkv = lax.all_to_all(dkv, both, 0, 0, axis_index_groups=teams, tiled=True)
    else:
        dkv = lax.all_to_all(dkv, both, 0, 0, axis_index_groups=pairs, tiled=True)
        dq = lax.all_to_all(dq, both, 0, 0, axis_index_groups=teams, tiled=True)
        dkv = dkv.reshape(2, planes, slots, 2, tok, head_dim).astype(jnp.float32).sum(axis=1)
        dkv = dkv.astype(jnp.bfloat16).reshape(kv_heads, 2, tok, head_dim)
    dkv = dkv.transpose(1, 2, 0, 3)
    dq = dq.reshape(kv_heads, tok, fan, head_dim).transpose(1, 0, 2, 3).reshape(tok, heads, head_dim)
    return dq, dkv[0], dkv[1]


def solution(mesh):
    tokens = P(("ctx", "head"), None, None)
    return jax.shard_map(
        per_device,
        mesh=mesh,
        in_specs=(tokens,) * 5 + (P(("ctx", "head"), None), P()),
        out_specs=(tokens,) * 3,
        check_vma=False,
    )
```

time: 356 us -> 115 us (0.32)
  the two profiles are of different devices: /device:TPU:1 before, /device:TPU:0 now
where the time goes in v1:
time: 115 us; the launch traced here: 114 us
  waiting for transfers between devices  54.7 us (48%)
  starting transfers between devices  22 us (19%)
  Pallas kernels  11.5 us (10%)
  local copies, waits for them, and re-layouts  9.04 us (8%)
  blocking collectives  8.99 us (8%)
  other arithmetic  7.16 us (6%)
    ppermute x6, waiting for transfers between devices, across(): return lax.ppermute(x, 'head', [(h, h ^ step) for h in range(n_head)])  37.5 us
    all_to_all x1, waiting for transfers between devices, per_device(): dq = lax.all_to_all(dq, both, 0, 0, axis_index_groups=teams, tiled=True)  13.3 us
    pallas_call x1, Pallas kernels, attention(): pl.pallas_call(functools.partial(planes_kernel, planes=planes, **sizes),...  11.5 us
    ppermute x6, starting transfers between devices, across(): return lax.ppermute(x, 'head', [(h, h ^ step) for h in range(n_head)])  9.67 us
    all_to_all x1, blocking collectives, per_device(): dkv = lax.all_to_all(dkv, both, 0, 0, axis_index_groups=teams, tiled=True)  8.99 us
    all_to_all x1, starting transfers between devices, per_device(): kv = lax.all_to_all(kv, both, 0, 0, axis_index_groups=teams, tiled=True)  5.17 us
    unnamed x15, local copies, waits for them, and re-layouts  4.39 us
    all_to_all x1, starting transfers between devices, per_device(): pkg = lax.all_to_all(pkg, both, 0, 0, axis_index_groups=teams, tiled=True)  3.63 us
  transfers between devices with their start and end apart: 9, of which 8 were waited for; matrix products, arithmetic and copies ran while one was open for 9% of the time, Pallas kernels for 0%

profile of v1, /device:TPU:0, one launch (start us, length us, event | category | flops | bytes accessed | tf_op | source)
XLA Modules:
  0.0 114.2 jit_solution(442125111407070241)
XLA Ops:
  0.6 0.0 copy-start
  0.6 0.0 copy-start.3
  0.7 1.2 %copy_bitcast_fusion.3 = (bf16[1,64,8,128]{3,1,0,2:T(8,128)(2,1)S(1)}, bf16[1,64,8,128]{3,1,0,2:T(8,128)(2,1)S(1)}) fusion(bf16[64,8,128]{2,1,0:T(8,128)(2,1)} %param.9, bf16[64,8,128]{2,1,0:T(8,128)(2,1)} %param.8), kind=kLoop, calls=%fused_computation.13 | loop fusion | bytes 524288 | tf_op jit(solution)/shard_map/stack | solution.py:188
  1.8 0.7 maximum_bitcast_fusion
  2.5 5.2 %all-to-all-start.1 = ((bf16[8,2,64,128]{3,2,1,0:T(8,128)(2,1)}), bf16[8,2,64,128]{3,2,1,0:T(8,128)(2,1)S(1)}, u32[]{:S(2)}, u32[]{:S(2)}) async-start(bf16[8,2,64,128]{3,2,1,0:T(8,128)(2,1)} %maximum_bitcast_fusion), calls=%async_computation.1 | async-start | bytes 524288 | tf_op jit(solution)/shard_map/all_to_all | solution.py:190
  7.7 0.8 copy.43
  8.6 0.0 copy-done.3
  8.6 1.8 %multiply_reduce_fusion = f32[64,64]{1,0:T(8,128)S(1)} fusion(bf16[64,64,128]{2,1,0:T(8,128)(2,1)} %param.10, bf16[64,64,128]{2,1,0:T(8,128)(2,1)S(1)} %copy-done.3), kind=kLoop, calls=%fused_computation.4 | loop fusion | flops 2093056 | bytes 2113536 | tf_op jit(solution)/shard_map/reduce_sum | solution.py:199
  10.5 0.1 copy.45
  10.6 0.4 copy.46
  11.0 0.8 reshape.252
  11.7 0.0 copy-done
  11.7 0.4 copy_bitcast_fusion.1
  12.1 1.5 %fusion.1 = bf16[8,1056,128]{2,1,0:T(8,128)(2,1)} fusion(bf16[8,24,128]{2,1,0:T(8,128)(2,1)S(1)} %reshape.252, bf16[8,512,128]{2,1,0:T(8,128)(2,1)S(1)} %get-tuple-element.29, bf16[8,512,128]{2,1,0:T(8,128)(2,1)S(1)} %get-tuple-element.30), kind=kLoop, calls=%fused_computation.3 | loop fusion | flops 8650752 | bytes 4308992 | tf_op jit(solution)/shard_map/concatenate | solution.py:208
  13.6 0.0 copy-start.1
  13.6 0.7 all-to-all-done.1.refs_0_
  14.3 0.0 copy-start.4
  14.3 3.6 %all-to-all-start = ((bf16[8,1056,128]{2,1,0:T(8,128)(2,1)}), bf16[8,1056,128]{2,1,0:T(8,128)(2,1)S(1)}, u32[]{:S(2)}, u32[]{:S(2)}) async-start(bf16[8,1056,128]{2,1,0:T(8,128)(2,1)} %fusion.1), calls=%async_computation | async-start | bytes 4325376 | tf_op jit(solution)/shard_map/all_to_all | solution.py:209
  18.0 2.7 %collective-permute-start.1 = (bf16[8,2,64,128]{3,2,1,0:T(8,128)(2,1)S(1)}, bf16[8,2,64,128]{3,2,1,0:T(8,128)(2,1)}, u32[]{:S(2)}, u32[]{:S(2)}) collective-permute-start(bf16[8,2,64,128]{3,2,1,0:T(8,128)(2,1)S(1)} %all-to-all-done.1.refs_0_), channel_id=1, source_target_pairs={{0,8},{1,9},{2,10},{3,11},{4,12},{5,13},{6,14},{7,15},{8,0},{9,1},... | collective-permute-start | bytes 786440 | tf_op jit(solution)/shard_map/ppermute | solution.py:186
  20.6 0.1 fusion.13
  20.7 0.0 copy-done.1
  20.7 0.6 gather_fusion
  21.3 0.2 convert_reduce_fusion
  21.5 0.0 copy-done.4
  21.5 1.6 %collective-permute-start = (bf16[8,2,64,128]{3,2,1,0:T(8,128)(2,1)S(1)}, bf16[8,2,64,128]{3,2,1,0:T(8,128)(2,1)S(1)}, u32[]{:S(2)}, u32[]{:S(2)}) collective-permute-start(bf16[8,2,64,128]{3,2,1,0:T(8,128)(2,1)S(1)} %all-to-all-done.1.refs_0_), channel_id=1, source_target_pairs={{0,4},{1,5},{2,6},{3,7},{4,0},{5,1},{6,2},{7,3},{8,12},{9,13},{10,... | collective-permute-start | bytes 786440 | tf_op jit(solution)/shard_map/ppermute | solution.py:186
  23.2 10.2 %collective-permute-done.1.refs_2_ = bf16[8,2,64,128]{3,2,1,0:T(8,128)(2,1)} collective-permute-done((bf16[8,2,64,128]{3,2,1,0:T(8,128)(2,1)S(1)}, bf16[8,2,64,128]{3,2,1,0:T(8,128)(2,1)}, u32[]{:S(2)}, u32[]{:S(2)}) %collective-permute-start.1) | collective-permute-done | bytes 262176 | tf_op jit(solution)/shard_map/ppermute | solution.py:186
  33.4 0.5 collective-permute-start.2
  33.9 0.1 add_subtract_fusion
  34.0 0.6 pad_add_fusion.meta
  34.6 0.0 collective-permute-done.refs_1_
  34.6 0.0 copy-start.5
  34.6 0.7 copy-done.5
  35.3 6.2 %collective-permute-done.2.refs_3_ = bf16[8,2,64,128]{3,2,1,0:T(8,128)(2,1)} collective-permute-done((bf16[8,2,64,128]{3,2,1,0:T(8,128)(2,1)}, bf16[8,2,64,128]{3,2,1,0:T(8,128)(2,1)}, u32[]{:S(2)}, u32[]{:S(2)}) %collective-permute-start.2) | collective-permute-done | bytes 262176 | tf_op jit(solution)/shard_map/ppermute | solution.py:186
  41.5 3.2 %all-to-all-done.pkg = bf16[8,1056,128]{2,1,0:T(8,128)(2,1)S(1)} async-done(((bf16[8,1056,128]{2,1,0:T(8,128)(2,1)}), bf16[8,1056,128]{2,1,0:T(8,128)(2,1)S(1)}, u32[]{:S(2)}, u32[]{:S(2)}) %all-to-all-start) | async-done | bytes 2162720 | tf_op jit(solution)/shard_map/all_to_all | solution.py:209
  44.8 0.0 copy-start.2
  44.8 1.4 %copy-done.2 = bf16[8,1056,128]{2,1,0:T(8,128)(2,1)} copy-done((bf16[8,1056,128]{2,1,0:T(8,128)(2,1)}, bf16[8,1056,128]{2,1,0:T(8,128)(2,1)S(1)}, u32[]{:S(2)}) %copy-start.2) | copy-done | bytes 2162712
  46.1 11.5 %attention_grads_planes.1 = (bf16[8,512,128]{2,1,0:T(8,128)(2,1)}, bf16[8,2,64,128]{3,2,1,0:T(8,128)(2,1)}, bf16[8,2,64,128]{3,2,1,0:T(8,128)(2,1)}, bf16[8,2,64...) custom-call(s32[9]{0:T(128)} %pad_add_fusion.meta, bf16[8,1056,128]{2,1,0:T(8,128)(2,1)} %copy-done.2, ...), custom_call_target="tpu_custom_call" | custom-call | tf_op jit(solution)/shard_map/attention_grads_planes/pallas_call | solution.py:141
  57.6 4.3 %collective-permute-start.3 = (bf16[8,2,64,128]{3,2,1,0:T(8,128)(2,1)}, bf16[8,2,64,128]{3,2,1,0:T(8,128)(2,1)S(1)}, u32[]{:S(2)}, u32[]{:S(2)}) collective-permute-start(bf16[8,2,64,128]{3,2,1,0:T(8,128)(2,1)} %get-tuple-element.11), channel_id=1, source_target_pairs={{0,4},{1,5},{2,6},{3,7},{4,0},{5,1},{6,2},{7,3},{8,12},{9,13},{10,... | collective-permute-start | bytes 786440 | tf_op jit(solution)/shard_map/ppermute | solution.py:186
  61.9 0.1 collective-permute-start.5
  62.0 7.2 %collective-permute-done.3 = bf16[8,2,64,128]{3,2,1,0:T(8,128)(2,1)S(1)} collective-permute-done((bf16[8,2,64,128]{3,2,1,0:T(8,128)(2,1)}, bf16[8,2,64,128]{3,2,1,0:T(8,128)(2,1)S(1)}, u32[]{:S(2)}, u32[]{:S(2)}) %collective-permute-start.3) | collective-permute-done | bytes 262176 | tf_op jit(solution)/shard_map/ppermute | solution.py:186
  69.2 1.0 add_convert_fusion.1
  70.2 0.5 collective-permute-start.4
  70.7 4.8 %collective-permute-done.5 = bf16[8,2,64,128]{3,2,1,0:T(8,128)(2,1)S(1)} collective-permute-done((bf16[8,2,64,128]{3,2,1,0:T(8,128)(2,1)}, bf16[8,2,64,128]{3,2,1,0:T(8,128)(2,1)S(1)}, u32[]{:S(2)}, u32[]{:S(2)}) %collective-permute-start.5) | collective-permute-done | bytes 262176 | tf_op jit(solution)/shard_map/ppermute | solution.py:186
  75.4 9.1 %collective-permute-done.4 = bf16[8,2,64,128]{3,2,1,0:T(8,128)(2,1)S(1)} collective-permute-done((bf16[8,2,64,128]{3,2,1,0:T(8,128)(2,1)S(1)}, bf16[8,2,64,128]{3,2,1,0:T(8,128)(2,1)S(1)}, u32[]{:S(2)}, u32[]{:S(2)}) %collective-permute-start.4) | collective-permute-done | bytes 262176 | tf_op jit(solution)/shard_map/ppermute | solution.py:186
  84.5 1.1 add_convert_fusion
  85.6 9.0 %all_to_all.20 = bf16[8,2,64,128]{3,2,1,0:T(8,128)(2,1)S(1)} all-to-all(bf16[8,2,64,128]{3,2,1,0:T(8,128)(2,1)S(1)} %add_convert_fusion), channel_id=1, replica_groups={{0,1,2,3,16,17,18,19},{4,5,6,7,20,21,22,23},{8,9,10,11,24,25,26,27},{12..., dimensions={0} | all-to-all | bytes 524288 | tf_op jit(solution)/shard_map/all_to_all | solution.py:238
  94.6 3.6 %all-to-all-start.2 = ((bf16[8,512,128]{2,1,0:T(8,128)(2,1)}), bf16[8,512,128]{2,1,0:T(8,128)(2,1)S(1)}, u32[]{:S(2)}, u32[]{:S(2)}) async-start(bf16[8,512,128]{2,1,0:T(8,128)(2,1)} %get-tuple-element.8), calls=%async_computation.2 | async-start | bytes 2097152 | tf_op jit(solution)/shard_map/all_to_all | solution.py:237
  98.2 0.7 copy.50
  98.9 0.7 copy.51
  99.6 13.3 %all-to-all-done.2 = bf16[8,512,128]{2,1,0:T(8,128)(2,1)S(1)} async-done(((bf16[8,512,128]{2,1,0:T(8,128)(2,1)}), bf16[8,512,128]{2,1,0:T(8,128)(2,1)S(1)}, u32[]{:S(2)}, u32[]{:S(2)}) %all-to-all-start.2) | async-done | bytes 1048608 | tf_op jit(solution)/shard_map/all_to_all | solution.py:237
  112.9 1.3 %copy_bitcast_fusion = bf16[64,64,128]{2,1,0:T(8,128)(2,1)} fusion(bf16[8,512,128]{2,1,0:T(8,128)(2,1)S(1)} %all-to-all-done.2), kind=kLoop, calls=%fused_computation.5 | loop fusion | bytes 2097152 | tf_op jit(solution)/shard_map/reshape | solution.py:245
  (8 shorter events, 0.1 us)
Async XLA Ops:
  0.6 11.1 %copy-start = (bf16[64,64,128]{2,1,0:T(8,128)(2,1)S(1)}, bf16[64,64,128]{2,1,0:T(8,128)(2,1)}, u32[]{:S(2)}) copy-start(bf16[64,64,128]{2,1,0:T(8,128)(2,1)} %param.7) | copy-start | bytes 3145732
  0.6 8.0 %copy-start.3 = (bf16[64,64,128]{2,1,0:T(8,128)(2,1)S(1)}, bf16[64,64,128]{2,1,0:T(8,128)(2,1)}, u32[]{:S(2)}) copy-start(bf16[64,64,128]{2,1,0:T(8,128)(2,1)} %param.11) | copy-start | bytes 3145732
  2.5 11.8 %all-to-all-start.1 = ((bf16[8,2,64,128]{3,2,1,0:T(8,128)(2,1)}), bf16[8,2,64,128]{3,2,1,0:T(8,128)(2,1)S(1)}, u32[]{:S(2)}, u32[]{:S(2)}) async-start(bf16[8,2,64,128]{3,2,1,0:T(8,128)(2,1)} %maximum_bitcast_fusion), calls=%async_computation.1 | async-start | bytes 524288 | tf_op jit(solution)/shard_map/all_to_all | solution.py:190
  13.6 7.1 %copy-start.1 = (s32[16]{0:T(128)S(1)}, s32[16]{0:T(128)}, u32[]{:S(2)}) copy-start(s32[16]{0:T(128)} %param.13) | copy-start | bytes 196
  14.3 7.2 %copy-start.4 = (bf16[8,2,64,128]{3,2,1,0:T(8,128)(2,1)}, bf16[8,2,64,128]{3,2,1,0:T(8,128)(2,1)S(1)}, u32[]{:S(2)}) copy-start(bf16[8,2,64,128]{3,2,1,0:T(8,128)(2,1)S(1)} %all-to-all-done.1.refs_0_) | copy-start | bytes 786436
  14.3 30.5 %all-to-all-start = ((bf16[8,1056,128]{2,1,0:T(8,128)(2,1)}), bf16[8,1056,128]{2,1,0:T(8,128)(2,1)S(1)}, u32[]{:S(2)}, u32[]{:S(2)}) async-start(bf16[8,1056,128]{2,1,0:T(8,128)(2,1)} %fusion.1), calls=%async_computation | async-start | bytes 4325376 | tf_op jit(solution)/shard_map/all_to_all | solution.py:209
  18.0 15.4 %collective-permute-start.1 = (bf16[8,2,64,128]{3,2,1,0:T(8,128)(2,1)S(1)}, bf16[8,2,64,128]{3,2,1,0:T(8,128)(2,1)}, u32[]{:S(2)}, u32[]{:S(2)}) collective-permute-start(bf16[8,2,64,128]{3,2,1,0:T(8,128)(2,1)S(1)} %all-to-all-done.1.refs_0_), channel_id=1, source_target_pairs={{0,8},{1,9},{2,10},{3,11},{4,12},{5,13},{6,14},{7,15},{8,0},{9,1},... | collective-permute-start | bytes 786440 | tf_op jit(solution)/shard_map/ppermute | solution.py:186
  21.5 13.1 %collective-permute-start = (bf16[8,2,64,128]{3,2,1,0:T(8,128)(2,1)S(1)}, bf16[8,2,64,128]{3,2,1,0:T(8,128)(2,1)S(1)}, u32[]{:S(2)}, u32[]{:S(2)}) collective-permute-start(bf16[8,2,64,128]{3,2,1,0:T(8,128)(2,1)S(1)} %all-to-all-done.1.refs_0_), channel_id=1, source_target_pairs={{0,4},{1,5},{2,6},{3,7},{4,0},{5,1},{6,2},{7,3},{8,12},{9,13},{10,... | collective-permute-start | bytes 786440 | tf_op jit(solution)/shard_map/ppermute | solution.py:186
  33.4 8.1 %collective-permute-start.2 = (bf16[8,2,64,128]{3,2,1,0:T(8,128)(2,1)}, bf16[8,2,64,128]{3,2,1,0:T(8,128)(2,1)}, u32[]{:S(2)}, u32[]{:S(2)}) collective-permute-start(bf16[8,2,64,128]{3,2,1,0:T(8,128)(2,1)} %collective-permute-done.1.refs_2_), channel_id=1, source_target_pairs={{0,4},{1,5},{2,6},{3,7},{4,0},{5,1},{6,2},{7,3},{8,12},{9,13},{10,... | collective-permute-start | bytes 786440 | tf_op jit(solution)/shard_map/ppermute | solution.py:186
  34.6 0.7 copy-start.5
  44.8 1.4 %copy-start.2 = (bf16[8,1056,128]{2,1,0:T(8,128)(2,1)}, bf16[8,1056,128]{2,1,0:T(8,128)(2,1)S(1)}, u32[]{:S(2)}) copy-start(bf16[8,1056,128]{2,1,0:T(8,128)(2,1)S(1)} %all-to-all-done.pkg) | copy-start | bytes 6488068
  57.6 11.6 %collective-permute-start.3 = (bf16[8,2,64,128]{3,2,1,0:T(8,128)(2,1)}, bf16[8,2,64,128]{3,2,1,0:T(8,128)(2,1)S(1)}, u32[]{:S(2)}, u32[]{:S(2)}) collective-permute-start(bf16[8,2,64,128]{3,2,1,0:T(8,128)(2,1)} %get-tuple-element.11), channel_id=1, source_target_pairs={{0,4},{1,5},{2,6},{3,7},{4,0},{5,1},{6,2},{7,3},{8,12},{9,13},{10,... | collective-permute-start | bytes 786440 | tf_op jit(solution)/shard_map/ppermute | solution.py:186
  61.9 13.5 %collective-permute-start.5 = (bf16[8,2,64,128]{3,2,1,0:T(8,128)(2,1)}, bf16[8,2,64,128]{3,2,1,0:T(8,128)(2,1)S(1)}, u32[]{:S(2)}, u32[]{:S(2)}) collective-permute-start(bf16[8,2,64,128]{3,2,1,0:T(8,128)(2,1)} %get-tuple-element.12), channel_id=1, source_target_pairs={{0,4},{1,5},{2,6},{3,7},{4,0},{5,1},{6,2},{7,3},{8,12},{9,13},{10,... | collective-permute-start | bytes 786440 | tf_op jit(solution)/shard_map/ppermute | solution.py:186
  70.2 14.3 %collective-permute-start.4 = (bf16[8,2,64,128]{3,2,1,0:T(8,128)(2,1)S(1)}, bf16[8,2,64,128]{3,2,1,0:T(8,128)(2,1)S(1)}, u32[]{:S(2)}, u32[]{:S(2)}) collective-permute-start(bf16[8,2,64,128]{3,2,1,0:T(8,128)(2,1)S(1)} %add_convert_fusion.1), channel_id=1, source_target_pairs={{0,8},{1,9},{2,10},{3,11},{4,12},{5,13},{6,14},{7,15},{8,0},{9,1},... | collective-permute-start | bytes 786440 | tf_op jit(solution)/shard_map/ppermute | solution.py:186
  94.6 18.4 %all-to-all-start.2 = ((bf16[8,512,128]{2,1,0:T(8,128)(2,1)}), bf16[8,512,128]{2,1,0:T(8,128)(2,1)S(1)}, u32[]{:S(2)}, u32[]{:S(2)}) async-start(bf16[8,512,128]{2,1,0:T(8,128)(2,1)} %get-tuple-element.8), calls=%async_computation.2 | async-start | bytes 2097152 | tf_op jit(solution)/shard_map/all_to_all | solution.py:237

commit v2 on v1

v2 whole, which is shorter than its diff:
```python
import functools

import jax
import jax.numpy as jnp
from jax import lax
from jax.experimental import pallas as pl
from jax.experimental.pallas import tpu as pltpu
from jax.sharding import PartitionSpec as P

BLK = 128
LOG2E = 1.4426950408889634
STAT_ROWS = 32


def stats_of(stats, sources, chunks):
    stats = stats.astype(jnp.float32)
    sums = (
        stats[:, base : base + chunks]
        + stats[:, base + chunks : base + 2 * chunks]
        + stats[:, base + 2 * chunks : base + 3 * chunks]
        for base in (0, 3 * chunks)
    )
    lse, delta = (
        jnp.concatenate([x[s, c : c + 1, :] for s in range(sources) for c in range(chunks)], axis=1)
        for x in sums
    )
    return lse * LOG2E, delta


def block_pair(q, g, lse, delta, k, v, group, scale, masked):
    s = lax.dot_general(k, q, (((1,), (1,)), ((), ())), preferred_element_type=jnp.float32)
    p = jnp.exp2(s * (scale * LOG2E) - lse)
    if masked:
        key_at = lax.broadcasted_iota(jnp.int32, p.shape, 0)
        query_at = lax.broadcasted_iota(jnp.int32, p.shape, 1) // group
        p = jnp.where(query_at >= key_at, p, 0.0)
    dp = lax.dot_general(v, g, (((1,), (1,)), ((), ())), preferred_element_type=jnp.float32)
    ds = (p * (dp - delta)).astype(jnp.bfloat16)
    dv = jnp.dot(p.astype(jnp.bfloat16), g, preferred_element_type=jnp.float32)
    dk = jnp.dot(ds, q, preferred_element_type=jnp.float32)
    dq = lax.dot_general(ds, k, (((0,), (0,)), ((), ())), preferred_element_type=jnp.float32)
    return dq, dk, dv


def whole_kernel(meta, pkg, kv, dq, dkv, dk_acc, dv_acc, dq_acc, *, rows, tok, q_blocks, scale):
    sources = BLK // tok
    wide = sources * rows
    dk_acc[...] = jnp.zeros_like(dk_acc)
    dv_acc[...] = jnp.zeros_like(dv_acc)

    def over_queries(i, _):
        last, first = meta[i], meta[q_blocks + i]
        mine = pl.ds(sources * i, sources)
        q = pkg[mine, 0:rows, :].reshape(wide, 128)
        g = pkg[mine, rows : 2 * rows, :].reshape(wide, 128)
        lse, delta = stats_of(pkg[mine, 2 * rows :, :], sources, rows // 128)
        dq_acc[...] = jnp.zeros_like(dq_acc)

        def step(j, masked):
            k = kv[pl.ds(sources * j, sources), 0].reshape(BLK, 128)
            v = kv[pl.ds(sources * j, sources), 1].reshape(BLK, 128)
            dq_part, dk, dv = block_pair(q, g, lse, delta, k, v, rows // tok, scale, masked)
            at = pl.ds(pl.multiple_of(j * BLK, BLK), BLK)
            dv_acc[at, :] += dv
            dk_acc[at, :] += dk
            dq_acc[...] += dq_part

        def inner(j, _):
            step(j, False)
            return 0

        lax.fori_loop(first, last, inner, 0)
        step(last, True)
        dq[mine] = (dq_acc[...] * scale).astype(jnp.bfloat16).reshape(sources, rows, 128)
        return 0

    lax.fori_loop(0, q_blocks, over_queries, 0)
    shards = dkv.shape[0]
    dkv[:, 0] = (dk_acc[...] * scale).astype(jnp.bfloat16).reshape(shards, tok, 128)
    dkv[:, 1] = dv_acc[...].astype(jnp.bfloat16).reshape(shards, tok, 128)


def planes_kernel(meta, pkg, *refs, rows, tok, q_blocks, scale, distances, planes):
    count = len(distances)
    ends = 0 in distances
    near, refs = refs[:count], refs[count:]
    if ends:
        dq_before, refs = refs[0], refs[1:]
    dq, near_grads, (kv, dk_acc, dv_acc, dq_acc, sems) = refs[0], refs[1 : 1 + count], refs[1 + count :]
    team = pkg.shape[0]
    sources = BLK // tok
    wide = sources * rows
    plane = meta[2 * q_blocks]
    team_blocks = team // 2 // sources
    range_blocks = team_blocks * planes
    loads = [
        pltpu.make_async_copy(near[n], kv.at[n * team : (n + 1) * team], sems.at[n]) for n in range(count)
    ]
    for copy in loads:
        copy.start()
    dk_acc[...] = jnp.zeros_like(dk_acc)
    dv_acc[...] = jnp.zeros_like(dv_acc)
    for copy in loads:
        copy.wait()

    def over_queries(i, _):
        last, first = meta[i], meta[q_blocks + i]
        mine = pl.ds(sources * i, sources)
        q = pkg[mine, 0:rows, :].reshape(wide, 128)
        g = pkg[mine, rows : 2 * rows, :].reshape(wide, 128)
        lse, delta = stats_of(pkg[mine, 2 * rows :, :], sources, rows // 128)
        if ends:
            dq_acc[...] = dq_before[i]
        else:
            dq_acc[...] = jnp.zeros_like(dq_acc)

        def step(j, distance, masked):
            within = (j // range_blocks) * team_blocks + j % team_blocks
            block = (distance - distances[0]) * (2 * team_blocks) + within
            at_shards = pl.ds(sources * block, sources)
            k = kv[at_shards, 0].reshape(BLK, 128)
            v = kv[at_shards, 1].reshape(BLK, 128)
            dq_part, dk, dv = block_pair(q, g, lse, delta, k, v, rows // tok, scale, masked)
            at = pl.ds(pl.multiple_of(block * BLK, BLK), BLK)
            dv_acc[at, :] += dv
            dk_acc[at, :] += dk
            dq_acc[...] += dq_part

        def inner(j, _):
            distance = ((j % range_blocks) // team_blocks) ^ plane

            @pl.when((distance >= distances[0]) & (distance <= distances[-1]))
            def _():
                step(j, distance, False)

            return 0

        lax.fori_loop(first, last, inner, 0)
        if ends:
            step(last, 0, True)
            dq[mine] = (dq_acc[...] * scale).astype(jnp.bfloat16).reshape(sources, rows, 128)
        else:
            dq[i] = dq_acc[...]
        return 0

    lax.fori_loop(0, q_blocks, over_queries, 0)
    for n in range(count):
        at = pl.ds(n * team * tok, team * tok)
        near_grads[n][:, 0] = (dk_acc[at, :] * scale).astype(jnp.bfloat16).reshape(team, tok, 128)
        near_grads[n][:, 1] = dv_acc[at, :].astype(jnp.bfloat16).reshape(team, tok, 128)


VMEM = pl.BlockSpec(memory_space=pltpu.VMEM)
SMEM = pl.BlockSpec(memory_space=pltpu.SMEM)


def totals(shards, tok, wide, head_dim):
    return [
        pltpu.VMEM((shards * tok, head_dim), jnp.float32),
        pltpu.VMEM((shards * tok, head_dim), jnp.float32),
        pltpu.VMEM((wide, head_dim), jnp.float32),
    ]


def attention(meta, pkg, kv, rows, scale):
    shards, _, tok, head_dim = kv.shape
    team = pkg.shape[0]
    q_blocks = team * tok // BLK
    return pl.pallas_call(
        functools.partial(whole_kernel, rows=rows, tok=tok, q_blocks=q_blocks, scale=scale),
        out_shape=(
            jax.ShapeDtypeStruct((team, rows, head_dim), jnp.bfloat16),
            jax.ShapeDtypeStruct(kv.shape, jnp.bfloat16),
        ),
        in_specs=[SMEM, VMEM, VMEM],
        out_specs=(VMEM, VMEM),
        scratch_shapes=totals(shards, tok, rows * (BLK // tok), head_dim),
        compiler_params=pltpu.CompilerParams(vmem_limit_bytes=56 * 1024 * 1024),
        name="attention_grads",
    )(meta, pkg, kv)


def attention_part(meta, pkg, kv, distances, dq_before, rows, scale, planes):
    team, _, tok, head_dim = kv[0].shape
    count = len(distances)
    q_blocks = team * tok // BLK
    wide = rows * (BLK // tok)
    ends = 0 in distances
    if ends:
        dq_shape = jax.ShapeDtypeStruct((team, rows, head_dim), jnp.bfloat16)
    else:
        dq_shape = jax.ShapeDtypeStruct((q_blocks, wide, head_dim), jnp.float32)
    pairs = 2 * q_blocks * count
    dq, *grads = pl.pallas_call(
        functools.partial(
            planes_kernel, rows=rows, tok=tok, q_blocks=q_blocks, scale=scale, distances=distances, planes=planes
        ),
        out_shape=(dq_shape,) + (jax.ShapeDtypeStruct(kv[0].shape, jnp.bfloat16),) * count,
        in_specs=[SMEM, VMEM] + [pl.BlockSpec(memory_space=pl.ANY)] * count + [VMEM] * ends,
        out_specs=(VMEM,) * (1 + count),
        scratch_shapes=[pltpu.VMEM((count * team, 2, tok, head_dim), jnp.bfloat16)]
        + totals(count * team, tok, wide, head_dim)
        + [pltpu.SemaphoreType.DMA((count,))],
        compiler_params=pltpu.CompilerParams(vmem_limit_bytes=32 * 1024 * 1024),
        cost_estimate=pl.CostEstimate(
            flops=pairs * 10 * BLK * wide * head_dim,
            bytes_accessed=4 * 1024 * 1024,
            transcendentals=pairs * BLK * wide,
        ),
        name="attention_part_" + "_".join(str(d) for d in distances),
    )(meta, pkg, *kv, *([dq_before] if ends else []))
    return dq, grads


def pieces(x):
    high = lax.reduce_precision(x, 8, 7)
    rest = x - high
    mid = lax.reduce_precision(rest, 8, 7)
    low = rest - mid
    return [part.astype(jnp.bfloat16) for part in (high, mid, low)]


def add(*terms):
    return sum(x.astype(jnp.float32) for x in terms).astype(jnp.bfloat16)


def exchange(x, slots):
    n_ctx, n_head = lax.axis_size("ctx"), lax.axis_size("head")
    me = (lax.axis_index("ctx") % 2) * slots + lax.axis_index("head") % slots
    order = me ^ jnp.arange(2 * slots)
    x = x[order]
    arrived = [x[0]]
    for d in range(1, 2 * slots):
        db, dr = divmod(d, slots)
        moves = [
            (c * n_head + h, (c ^ db) * n_head + (h ^ dr)) for c in range(n_ctx) for h in range(n_head)
        ]
        arrived.append(lax.ppermute(x[d], ("ctx", "head"), moves))
    return jnp.stack(arrived)[order]


def by_token(dq, dkv, kv_heads, fan):
    _, _, tok, head_dim = dkv.shape
    dq = dq.reshape(kv_heads, tok, fan, head_dim).transpose(1, 0, 2, 3).reshape(tok, kv_heads * fan, head_dim)
    dkv = dkv.transpose(1, 2, 0, 3)
    return dq, dkv[0], dkv[1]


def per_device(queries, keys, values, outputs, out_grads, log_norms, block_doc):
    tok, heads, head_dim = queries.shape
    kv_heads = keys.shape[1]
    fan = heads // kv_heads
    n_ctx, n_head = lax.axis_size("ctx"), lax.axis_size("head")
    slots = kv_heads // 2
    planes = n_head // slots
    rows = tok * fan
    scale = head_dim**-0.5
    ctx, head = lax.axis_index("ctx"), lax.axis_index("head")
    both = ("ctx", "head")
    teams = [
        [(2 * c + b) * n_head + z * slots + r for b in range(2) for r in range(slots)]
        for c in range(n_ctx // 2)
        for z in range(planes)
    ]
    pairs = [
        [(2 * c + b) * n_head + h for b in range(2) for h in range(n_head)]
        for c in range(n_ctx // 2)
    ]

    by_plane = n_ctx == 2 and planes == 4

    def across(x, distance):
        step = distance * slots
        return lax.ppermute(x, "head", [(h, h ^ step) for h in range(n_head)])

    kv = jnp.stack([keys, values], axis=0).transpose(2, 0, 1, 3)
    if by_plane:
        kv = lax.all_to_all(kv, both, 0, 0, axis_index_groups=teams, tiled=True)
        second, first = across(kv, 2), across(kv, 1)
        kv = (kv, first, second, across(second, 1))
    else:
        kv = kv.reshape(2, 1, slots, 2, tok, head_dim)
        kv = jnp.broadcast_to(kv, (2, planes, slots, 2, tok, head_dim))
        kv = kv.reshape(2 * n_head, 2, tok, head_dim)
        kv = lax.all_to_all(kv, both, 0, 0, axis_index_groups=pairs, tiled=True)

    deltas = jnp.sum(out_grads.astype(jnp.float32) * outputs.astype(jnp.float32), axis=-1)
    stats = jnp.stack(pieces(log_norms) + pieces(deltas), axis=0)
    stats = stats.reshape(6, tok, kv_heads, fan).transpose(2, 0, 1, 3)
    stats = stats.reshape(kv_heads, 6 * rows // 128, 128)
    stats = jnp.pad(stats, ((0, 0), (0, STAT_ROWS - stats.shape[1]), (0, 0)))

    def by_group(x):
        return x.reshape(tok, kv_heads, fan, head_dim).transpose(1, 0, 2, 3).reshape(kv_heads, rows, head_dim)

    pkg = jnp.concatenate([by_group(queries), by_group(out_grads), stats], axis=1)
    pkg = lax.all_to_all(pkg, both, 0, 0, axis_index_groups=teams, tiled=True)

    pair, plane = ctx // 2, head // slots
    range_blocks = n_head * tok // BLK
    team_blocks = slots * tok // BLK
    at = jnp.stack(
        [(2 * pair + b) * range_blocks + plane * team_blocks + j for b in range(2) for j in range(team_blocks)]
    )
    first_block = jnp.sum(block_doc[None, :] < block_doc[at][:, None], axis=1, dtype=jnp.int32)
    ranges_before = 1 if n_ctx > 2 else 0
    base = (2 * pair - ranges_before) * range_blocks
    meta = jnp.concatenate([at - base, first_block - base, plane[None]]).astype(jnp.int32)

    if by_plane:
        dq_before, (grads_3,) = attention_part(meta, pkg, kv[3:], (3,), None, rows, scale, planes)
        relayed = across(grads_3, 1)
        dq, (grads_0, grads_1, grads_2) = attention_part(
            meta, pkg, kv[:3], (0, 1, 2), dq_before, rows, scale, planes
        )
        close = across(grads_1, 1)
        far = across(add(grads_2, relayed), 2)
        dq = lax.all_to_all(dq, both, 0, 0, axis_index_groups=teams, tiled=True)
        dkv = exchange(add(grads_0, close, far), slots)
        return by_token(dq, dkv, kv_heads, fan)

    if ranges_before:
        prior = lax.ppermute(kv[n_head:], "ctx", [(c, c + 2) for c in range(n_ctx - 2)])
        kv = jnp.concatenate([prior, kv], axis=0)
    dq, dkv = attention(meta, pkg, kv, rows, scale)
    if ranges_before:
        later = lax.ppermute(dkv[:n_head], "ctx", [(c + 2, c) for c in range(n_ctx - 2)])
        dkv = jnp.concatenate([dkv[n_head : 2 * n_head], add(dkv[2 * n_head :], later)], axis=0)

    dkv = lax.all_to_all(dkv, both, 0, 0, axis_index_groups=pairs, tiled=True)
    dq = lax.all_to_all(dq, both, 0, 0, axis_index_groups=teams, tiled=True)
    dkv = dkv.reshape(2, planes, slots, 2, tok, head_dim).astype(jnp.float32).sum(axis=1)
    dkv = dkv.astype(jnp.bfloat16).reshape(kv_heads, 2, tok, head_dim)
    return by_token(dq, dkv, kv_heads, fan)


def solution(mesh):
    tokens = P(("ctx", "head"), None, None)
    return jax.shard_map(
        per_device,
        mesh=mesh,
        in_specs=(tokens,) * 5 + (P(("ctx", "head"), None), P()),
        out_specs=(tokens,) * 3,
        check_vma=False,
    )
```

time: 115 us -> 108 us (0.939)
  starting transfers between devices: 22 us -> 33.9 us
  blocking collectives: 8.99 us -> 0 us
  waiting for transfers between devices: 54.7 us -> 46.4 us
  other arithmetic: 7.16 us -> 5.74 us
    ppermute x0 -> x7, waiting for transfers between devices: none -> 13.8 us  [exchange(): arrived.append(lax.ppermute(x[d], ('ctx', 'head'), moves))]
    all_to_all x1, waiting for transfers between devices: 13.3 us -> 0.01 us  [per_device(): dq = lax.all_to_all(dq, both, 0, 0, axis_index_groups=teams, tiled=True)]
    all_to_all x1 -> x0, blocking collectives: 8.99 us -> none  [per_device(): dkv = lax.all_to_all(dkv, both, 0, 0, axis_index_groups=teams, tiled=True)]
    ppermute x6, waiting for transfers between devices: 37.5 us -> 29.5 us  [across(): return lax.ppermute(x, 'head', [(h, h ^ step) for h in range(n_head)])]
    ppermute x0 -> x7, starting transfers between devices: none -> 6.96 us  [exchange(): arrived.append(lax.ppermute(x[d], ('ctx', 'head'), moves))]
    ppermute x6, starting transfers between devices: 9.67 us -> 14.4 us  [across(): return lax.ppermute(x, 'head', [(h, h ^ step) for h in range(n_head)])]
    gather x0 -> x2, local copies, waits for them, and re-layouts: none -> 1.19 us  [the longest x1 0.6 us: exchange(): x = x[order]]
    pallas_call x1 -> x2, Pallas kernels: 11.5 us -> 10.4 us  [attention_part(): pl.pallas_call(functools.partial(planes_kernel, rows=rows, tok=tok, q_blo...]
  transfers between devices with their start and end apart: 9 -> 16, of which waited for: 8 -> 7; matrix products, arithmetic and copies ran while one was open for 9% -> 9% of each run, Pallas kernels for 0% -> 10%
where the time goes in v2:
time: 108 us; the launch traced here: 107 us
  waiting for transfers between devices  46.4 us (43%)
  starting transfers between devices  33.9 us (31%)
  Pallas kernels  10.4 us (10%)
  local copies, waits for them, and re-layouts  10.1 us (9%)
  other arithmetic  5.74 us (5%)
    ppermute x6, waiting for transfers between devices, across(): return lax.ppermute(x, 'head', [(h, h ^ step) for h in range(n_head)])  29.5 us
    ppermute x6, starting transfers between devices, across(): return lax.ppermute(x, 'head', [(h, h ^ step) for h in range(n_head)])  14.4 us
    ppermute x7, waiting for transfers between devices, exchange(): arrived.append(lax.ppermute(x[d], ('ctx', 'head'), moves))  13.8 us
    pallas_call x2, Pallas kernels, attention_part(): pl.pallas_call(functools.partial(planes_kernel, rows=rows, tok=tok, q_blo...  10.4 us
    ppermute x7, starting transfers between devices, exchange(): arrived.append(lax.ppermute(x[d], ('ctx', 'head'), moves))  6.96 us
    all_to_all x1, starting transfers between devices, per_device(): kv = lax.all_to_all(kv, both, 0, 0, axis_index_groups=teams, tiled=True)  5.17 us
    unnamed x21, local copies, waits for them, and re-layouts  4.05 us
    all_to_all x1, starting transfers between devices, per_device(): pkg = lax.all_to_all(pkg, both, 0, 0, axis_index_groups=teams, tiled=True)  3.78 us
  transfers between devices with their start and end apart: 16, of which 7 were waited for; matrix products, arithmetic and copies ran while one was open for 9% of the time, Pallas kernels for 10%

profile of v2, /device:TPU:0, one launch (start us, length us, event | category | flops | bytes accessed | tf_op | source)
XLA Modules:
  0.0 107.5 jit_solution(12046286945814226767)
XLA Ops:
  0.6 0.0 copy-start
  0.6 0.0 copy-start.5
  0.7 1.2 %copy_bitcast_fusion.3 = (bf16[1,64,8,128]{3,1,0,2:T(8,128)(2,1)S(1)}, bf16[1,64,8,128]{3,1,0,2:T(8,128)(2,1)S(1)}) fusion(bf16[64,8,128]{2,1,0:T(8,128)(2,1)} %param.9, bf16[64,8,128]{2,1,0:T(8,128)(2,1)} %param.8), kind=kLoop, calls=%fused_computation.15 | loop fusion | bytes 524288 | tf_op jit(solution)/shard_map/stack | solution.py:276
  1.8 0.7 maximum_bitcast_fusion
  2.5 5.2 %all-to-all-start.1 = ((bf16[8,2,64,128]{3,2,1,0:T(8,128)(2,1)}), bf16[8,2,64,128]{3,2,1,0:T(8,128)(2,1)S(1)}, u32[]{:S(2)}, u32[]{:S(2)}) async-start(bf16[8,2,64,128]{3,2,1,0:T(8,128)(2,1)} %maximum_bitcast_fusion), calls=%async_computation.1 | async-start | bytes 524288 | tf_op jit(solution)/shard_map/all_to_all | solution.py:278
  7.7 0.8 copy.43
  8.6 0.0 copy-done.5
  8.6 1.8 %multiply_reduce_fusion = f32[64,64]{1,0:T(8,128)S(1)} fusion(bf16[64,64,128]{2,1,0:T(8,128)(2,1)} %param.10, bf16[64,64,128]{2,1,0:T(8,128)(2,1)S(1)} %copy-done.5), kind=kLoop, calls=%fused_computation.6 | loop fusion | flops 2093056 | bytes 2113536 | tf_op jit(solution)/shard_map/reduce_sum | solution.py:287
  10.5 0.1 copy.45
  10.6 0.4 copy.46
  11.0 0.8 reshape.268
  11.7 0.0 copy-done
  11.7 0.5 copy_bitcast_fusion.1
  12.2 1.5 %fusion.1 = bf16[8,1056,128]{2,1,0:T(8,128)(2,1)} fusion(bf16[8,24,128]{2,1,0:T(8,128)(2,1)S(1)} %reshape.268, bf16[8,512,128]{2,1,0:T(8,128)(2,1)S(1)} %get-tuple-element.39, bf16[8,512,128]{2,1,0:T(8,128)(2,1)S(1)} %get-tuple-element.40), kind=kLoop, calls=%fused_computation.5 | loop fusion | flops 8650752 | bytes 4308992 | tf_op jit(solution)/shard_map/concatenate | solution.py:296
  13.8 0.6 all-to-all-done.1.refs_0_
  14.3 3.8 %all-to-all-start = ((bf16[8,1056,128]{2,1,0:T(8,128)(2,1)}), bf16[8,1056,128]{2,1,0:T(8,128)(2,1)S(1)}, u32[]{:S(2)}, u32[]{:S(2)}) async-start(bf16[8,1056,128]{2,1,0:T(8,128)(2,1)} %fusion.1), calls=%async_computation | async-start | bytes 4325376 | tf_op jit(solution)/shard_map/all_to_all | solution.py:297
  18.1 2.6 %collective-permute-start.1 = (bf16[8,2,64,128]{3,2,1,0:T(8,128)(2,1)S(1)}, bf16[8,2,64,128]{3,2,1,0:T(8,128)(2,1)}, u32[]{:S(2)}, u32[]{:S(2)}) collective-permute-start(bf16[8,2,64,128]{3,2,1,0:T(8,128)(2,1)S(1)} %all-to-all-done.1.refs_0_), channel_id=1, source_target_pairs={{0,8},{1,9},{2,10},{3,11},{4,12},{5,13},{6,14},{7,15},{8,0},{9,1},... | collective-permute-start | bytes 786440 | tf_op jit(solution)/shard_map/ppermute | solution.py:274
  20.7 0.1 fusion.7
  20.8 0.0 copy-done.4
  20.8 0.6 gather_fusion
  21.4 0.2 convert_reduce_fusion
  21.6 1.6 %collective-permute-start = (bf16[8,2,64,128]{3,2,1,0:T(8,128)(2,1)S(1)}, bf16[8,2,64,128]{3,2,1,0:T(8,128)(2,1)}, u32[]{:S(2)}, u32[]{:S(2)}) collective-permute-start(bf16[8,2,64,128]{3,2,1,0:T(8,128)(2,1)S(1)} %all-to-all-done.1.refs_0_), channel_id=1, source_target_pairs={{0,4},{1,5},{2,6},{3,7},{4,0},{5,1},{6,2},{7,3},{8,12},{9,13},{10,... | collective-permute-start | bytes 786440 | tf_op jit(solution)/shard_map/ppermute | solution.py:274
  23.2 10.3 %collective-permute-done.1.refs_2_ = bf16[8,2,64,128]{3,2,1,0:T(8,128)(2,1)} collective-permute-done((bf16[8,2,64,128]{3,2,1,0:T(8,128)(2,1)S(1)}, bf16[8,2,64,128]{3,2,1,0:T(8,128)(2,1)}, u32[]{:S(2)}, u32[]{:S(2)}) %collective-permute-start.1) | collective-permute-done | bytes 262176 | tf_op jit(solution)/shard_map/ppermute | solution.py:274
  33.5 0.5 collective-permute-start.2
  34.1 0.1 add_subtract_fusion
  34.1 0.1 pad_add_fusion.meta
  34.2 7.4 %collective-permute-done.2.refs_0_ = bf16[8,2,64,128]{3,2,1,0:T(8,128)(2,1)S(1)} collective-permute-done((bf16[8,2,64,128]{3,2,1,0:T(8,128)(2,1)}, bf16[8,2,64,128]{3,2,1,0:T(8,128)(2,1)S(1)}, u32[]{:S(2)}, u32[]{:S(2)}) %collective-permute-start.2) | collective-permute-done | bytes 262176 | tf_op jit(solution)/shard_map/ppermute | solution.py:274
  41.6 0.7 copy-done.2
  42.3 2.6 %all-to-all-done.pkg = bf16[8,1056,128]{2,1,0:T(8,128)(2,1)S(1)} async-done(((bf16[8,1056,128]{2,1,0:T(8,128)(2,1)}), bf16[8,1056,128]{2,1,0:T(8,128)(2,1)S(1)}, u32[]{:S(2)}, u32[]{:S(2)}) %all-to-all-start) | async-done | bytes 2162720 | tf_op jit(solution)/shard_map/all_to_all | solution.py:297
  44.9 0.9 copy-done.3
  45.9 2.4 %attention_part_3.1 = (f32[4,1024,128]{2,1,0:T(8,128)S(1)}, bf16[8,2,64,128]{3,2,1,0:T(8,128)(2,1)S(1)}) custom-call(s32[9]{0:T(128)S(1)} %pad_add_fusion.meta, bf16[8,1056,128]{2,1,0:T(8,128)(2,1)S(1)} %all-to-all-done.pkg, bf16[8,2,64,128]{3,2,1,0:T(8,128)(2,1)S(1)} %copy-done.3), custom_call_target="tpu_custom_call" | custom-call | flops 1342177280 | bytes 4194304 | tf_op jit(solution)/shard_map/attention_part_3/pallas_call | solution.py:194
  48.3 0.5 collective-permute-start.4
  48.8 0.0 collective-permute-done.refs_1_
  48.8 8.0 %attention_part_0_1_2.1 = (bf16[8,512,128]{2,1,0:T(8,128)(2,1)}, bf16[8,2,64,128]{3,2,1,0:T(8,128)(2,1)S(1)}, bf16[8,2,64,128]{3,2,1,0:T(8,128)(2,1)}, bf16[8,2,64,128]{3,2,1,0:T(8,128)(2,1)S(1)}) custom-call(s32[9]{0:T(128)S(1)} %pad_add_fusion.meta, bf16[8,1056,128]{2,1,0:T(8,128)(2,1)S(1)} %all-to-all-done.pkg, ...), custom_call_target="tpu_custom_call" | custom-call | flops 4026531840 | bytes 4194304 | tf_op jit(solution)/shard_map/attention_part_0_1_2/pallas_call | solution.py:194
  56.8 0.0 copy-start.1
  56.8 1.0 collective-permute-start.3
  57.8 0.0 collective-permute-done.4
  57.8 0.1 add_convert_fusion.1
  57.9 0.0 copy-done.1
  57.9 8.1 %collective-permute-start.5 = (bf16[8,2,64,128]{3,2,1,0:T(8,128)(2,1)S(1)}, bf16[8,2,64,128]{3,2,1,0:T(8,128)(2,1)S(1)}, u32[]{:S(2)}, u32[]{:S(2)}) collective-permute-start(bf16[8,2,64,128]{3,2,1,0:T(8,128)(2,1)S(1)} %add_convert_fusion.1), channel_id=1, source_target_pairs={{0,8},{1,9},{2,10},{3,11},{4,12},{5,13},{6,14},{7,15},{8,0},{9,1},... | collective-permute-start | bytes 786440 | tf_op jit(solution)/shard_map/ppermute | solution.py:274
  66.1 0.0 collective-permute-done.3
  66.1 11.8 %collective-permute-done.5 = bf16[8,2,64,128]{3,2,1,0:T(8,128)(2,1)S(1)} collective-permute-done((bf16[8,2,64,128]{3,2,1,0:T(8,128)(2,1)S(1)}, bf16[8,2,64,128]{3,2,1,0:T(8,128)(2,1)S(1)}, u32[]{:S(2)}, u32[]{:S(2)}) %collective-permute-start.5) | collective-permute-done | bytes 262176 | tf_op jit(solution)/shard_map/ppermute | solution.py:274
  77.9 1.1 add_convert_fusion
  79.0 0.6 gather_fusion.1
  79.6 0.9 collective-permute-start.6
  80.5 3.6 %all-to-all-start.2 = ((bf16[8,512,128]{2,1,0:T(8,128)(2,1)}), bf16[8,512,128]{2,1,0:T(8,128)(2,1)S(1)}, u32[]{:S(2)}, u32[]{:S(2)}) async-start(bf16[8,512,128]{2,1,0:T(8,128)(2,1)} %get-tuple-element.10), calls=%async_computation.2 | async-start | bytes 2097152 | tf_op jit(solution)/shard_map/all_to_all | solution.py:318
  84.1 1.9 %collective-permute-start.7 = (bf16[2,64,128]{2,1,0:T(8,128)(2,1)S(1)}, bf16[2,64,128]{2,1,0:T(8,128)(2,1)S(1)}, u32[]{:S(2)}, u32[]{:S(2)}) collective-permute-start(bf16[2,64,128]{2,1,0:T(8,128)(2,1)S(1)} %get-tuple-element.34), channel_id=1, source_target_pairs={{0,2},{1,3},{2,0},{3,1},{4,6},{5,7},{6,4},{7,5},{8,10},{9,11},{10,... | collective-permute-start | bytes 98312 | tf_op jit(solution)/shard_map/ppermute | solution.py:238
  86.0 1.5 %collective-permute-start.8 = (bf16[2,64,128]{2,1,0:T(8,128)(2,1)S(1)}, bf16[2,64,128]{2,1,0:T(8,128)(2,1)S(1)}, u32[]{:S(2)}, u32[]{:S(2)}) collective-permute-start(bf16[2,64,128]{2,1,0:T(8,128)(2,1)S(1)} %get-tuple-element.33), channel_id=1, source_target_pairs={{0,3},{1,2},{2,1},{3,0},{4,7},{5,6},{6,5},{7,4},{8,11},{9,10},{10,... | collective-permute-start | bytes 98312 | tf_op jit(solution)/shard_map/ppermute | solution.py:238
  87.4 0.0 collective-permute-start.9
  87.4 0.3 collective-permute-start.10
  87.7 0.0 collective-permute-done.6
  87.7 1.5 %collective-permute-start.11 = (bf16[2,64,128]{2,1,0:T(8,128)(2,1)S(1)}, bf16[2,64,128]{2,1,0:T(8,128)(2,1)S(1)}, u32[]{:S(2)}, u32[]{:S(2)}) collective-permute-start(bf16[2,64,128]{2,1,0:T(8,128)(2,1)S(1)} %get-tuple-element.30), channel_id=1, source_target_pairs={{0,18},{1,19},{2,16},{3,17},{4,22},{5,23},{6,20},{7,21},{8,26},{9,... | collective-permute-start | bytes 98312 | tf_op jit(solution)/shard_map/ppermute | solution.py:238
  89.2 10.6 %collective-permute-done.7 = bf16[2,64,128]{2,1,0:T(8,128)(2,1)S(1)} collective-permute-done((bf16[2,64,128]{2,1,0:T(8,128)(2,1)S(1)}, bf16[2,64,128]{2,1,0:T(8,128)(2,1)S(1)}, u32[]{:S(2)}, u32[]{:S(2)}) %collective-permute-start.7) | collective-permute-done | bytes 32800 | tf_op jit(solution)/shard_map/ppermute | solution.py:238
  99.8 1.0 collective-permute-start.12
  100.8 0.0 collective-permute-done.8
  100.8 0.0 collective-permute-done.9
  100.8 0.0 collective-permute-done.10
  100.8 0.0 collective-permute-done.11
  100.9 3.2 %collective-permute-done.12 = bf16[2,64,128]{2,1,0:T(8,128)(2,1)S(1)} collective-permute-done((bf16[2,64,128]{2,1,0:T(8,128)(2,1)S(1)}, bf16[2,64,128]{2,1,0:T(8,128)(2,1)S(1)}, u32[]{:S(2)}, u32[]{:S(2)}) %collective-permute-start.12) | collective-permute-done | bytes 32800 | tf_op jit(solution)/shard_map/ppermute | solution.py:238
  104.1 0.6 gather_fusion.2
  104.7 0.7 copy.50
  105.4 0.7 copy.51
  106.2 0.0 all-to-all-done.2
  106.2 1.3 %copy_bitcast_fusion = bf16[64,64,128]{2,1,0:T(8,128)(2,1)} fusion(bf16[8,512,128]{2,1,0:T(8,128)(2,1)S(1)} %all-to-all-done.2), kind=kLoop, calls=%fused_computation.7 | loop fusion | bytes 2097152 | tf_op jit(solution)/shard_map/reshape | solution.py:244
  (21 shorter events, 0.2 us)
Async XLA Ops:
  0.6 11.1 %copy-start = (bf16[64,64,128]{2,1,0:T(8,128)(2,1)S(1)}, bf16[64,64,128]{2,1,0:T(8,128)(2,1)}, u32[]{:S(2)}) copy-start(bf16[64,64,128]{2,1,0:T(8,128)(2,1)} %param.7) | copy-start | bytes 3145732
  0.6 8.0 %copy-start.5 = (bf16[64,64,128]{2,1,0:T(8,128)(2,1)S(1)}, bf16[64,64,128]{2,1,0:T(8,128)(2,1)}, u32[]{:S(2)}) copy-start(bf16[64,64,128]{2,1,0:T(8,128)(2,1)} %param.11) | copy-start | bytes 3145732
  2.5 11.8 %all-to-all-start.1 = ((bf16[8,2,64,128]{3,2,1,0:T(8,128)(2,1)}), bf16[8,2,64,128]{3,2,1,0:T(8,128)(2,1)S(1)}, u32[]{:S(2)}, u32[]{:S(2)}) async-start(bf16[8,2,64,128]{3,2,1,0:T(8,128)(2,1)} %maximum_bitcast_fusion), calls=%async_computation.1 | async-start | bytes 524288 | tf_op jit(solution)/shard_map/all_to_all | solution.py:278
  13.8 7.0 %copy-start.4 = (s32[16]{0:T(128)S(1)}, s32[16]{0:T(128)}, u32[]{:S(2)}) copy-start(s32[16]{0:T(128)} %param.13) | copy-start | bytes 196
  14.3 30.6 %all-to-all-start = ((bf16[8,1056,128]{2,1,0:T(8,128)(2,1)}), bf16[8,1056,128]{2,1,0:T(8,128)(2,1)S(1)}, u32[]{:S(2)}, u32[]{:S(2)}) async-start(bf16[8,1056,128]{2,1,0:T(8,128)(2,1)} %fusion.1), calls=%async_computation | async-start | bytes 4325376 | tf_op jit(solution)/shard_map/all_to_all | solution.py:297
  18.1 15.4 %collective-permute-start.1 = (bf16[8,2,64,128]{3,2,1,0:T(8,128)(2,1)S(1)}, bf16[8,2,64,128]{3,2,1,0:T(8,128)(2,1)}, u32[]{:S(2)}, u32[]{:S(2)}) collective-permute-start(bf16[8,2,64,128]{3,2,1,0:T(8,128)(2,1)S(1)} %all-to-all-done.1.refs_0_), channel_id=1, source_target_pairs={{0,8},{1,9},{2,10},{3,11},{4,12},{5,13},{6,14},{7,15},{8,0},{9,1},... | collective-permute-start | bytes 786440 | tf_op jit(solution)/shard_map/ppermute | solution.py:274
  21.6 27.2 %collective-permute-start = (bf16[8,2,64,128]{3,2,1,0:T(8,128)(2,1)S(1)}, bf16[8,2,64,128]{3,2,1,0:T(8,128)(2,1)}, u32[]{:S(2)}, u32[]{:S(2)}) collective-permute-start(bf16[8,2,64,128]{3,2,1,0:T(8,128)(2,1)S(1)} %all-to-all-done.1.refs_0_), channel_id=1, source_target_pairs={{0,4},{1,5},{2,6},{3,7},{4,0},{5,1},{6,2},{7,3},{8,12},{9,13},{10,... | collective-permute-start | bytes 786440 | tf_op jit(solution)/shard_map/ppermute | solution.py:274
  33.5 8.1 %collective-permute-start.2 = (bf16[8,2,64,128]{3,2,1,0:T(8,128)(2,1)}, bf16[8,2,64,128]{3,2,1,0:T(8,128)(2,1)S(1)}, u32[]{:S(2)}, u32[]{:S(2)}) collective-permute-start(bf16[8,2,64,128]{3,2,1,0:T(8,128)(2,1)} %collective-permute-done.1.refs_2_), channel_id=1, source_target_pairs={{0,4},{1,5},{2,6},{3,7},{4,0},{5,1},{6,2},{7,3},{8,12},{9,13},{10,... | collective-permute-start | bytes 786440 | tf_op jit(solution)/shard_map/ppermute | solution.py:274
  41.6 0.7 copy-start.2
  44.9 1.0 copy-start.3
  48.3 9.6 %collective-permute-start.4 = (bf16[8,2,64,128]{3,2,1,0:T(8,128)(2,1)S(1)}, bf16[8,2,64,128]{3,2,1,0:T(8,128)(2,1)S(1)}, u32[]{:S(2)}, u32[]{:S(2)}) collective-permute-start(bf16[8,2,64,128]{3,2,1,0:T(8,128)(2,1)S(1)} %get-tuple-element.14), channel_id=1, source_target_pairs={{0,4},{1,5},{2,6},{3,7},{4,0},{5,1},{6,2},{7,3},{8,12},{9,13},{10,... | collective-permute-start | bytes 786440 | tf_op jit(solution)/shard_map/ppermute | solution.py:274
  56.8 1.1 %copy-start.1 = (bf16[8,2,64,128]{3,2,1,0:T(8,128)(2,1)}, bf16[8,2,64,128]{3,2,1,0:T(8,128)(2,1)S(1)}, u32[]{:S(2)}) copy-start(bf16[8,2,64,128]{3,2,1,0:T(8,128)(2,1)S(1)} %get-tuple-element.11) | copy-start | bytes 786436
  56.8 9.3 %collective-permute-start.3 = (bf16[8,2,64,128]{3,2,1,0:T(8,128)(2,1)}, bf16[8,2,64,128]{3,2,1,0:T(8,128)(2,1)S(1)}, u32[]{:S(2)}, u32[]{:S(2)}) collective-permute-start(bf16[8,2,64,128]{3,2,1,0:T(8,128)(2,1)} %get-tuple-element.12), channel_id=1, source_target_pairs={{0,4},{1,5},{2,6},{3,7},{4,0},{5,1},{6,2},{7,3},{8,12},{9,13},{10,... | collective-permute-start | bytes 786440 | tf_op jit(solution)/shard_map/ppermute | solution.py:274
  57.9 20.0 %collective-permute-start.5 = (bf16[8,2,64,128]{3,2,1,0:T(8,128)(2,1)S(1)}, bf16[8,2,64,128]{3,2,1,0:T(8,128)(2,1)S(1)}, u32[]{:S(2)}, u32[]{:S(2)}) collective-permute-start(bf16[8,2,64,128]{3,2,1,0:T(8,128)(2,1)S(1)} %add_convert_fusion.1), channel_id=1, source_target_pairs={{0,8},{1,9},{2,10},{3,11},{4,12},{5,13},{6,14},{7,15},{8,0},{9,1},... | collective-permute-start | bytes 786440 | tf_op jit(solution)/shard_map/ppermute | solution.py:274
  79.6 8.1 %collective-permute-start.6 = (bf16[2,64,128]{2,1,0:T(8,128)(2,1)S(1)}, bf16[2,64,128]{2,1,0:T(8,128)(2,1)S(1)}, u32[]{:S(2)}, u32[]{:S(2)}) collective-permute-start(bf16[2,64,128]{2,1,0:T(8,128)(2,1)S(1)} %get-tuple-element.35), channel_id=1, source_target_pairs={{0,1},{1,0},{2,3},{3,2},{4,5},{5,4},{6,7},{7,6},{8,9},{9,8},{10,11... | collective-permute-start | bytes 98312 | tf_op jit(solution)/shard_map/ppermute | solution.py:238
  80.5 25.7 %all-to-all-start.2 = ((bf16[8,512,128]{2,1,0:T(8,128)(2,1)}), bf16[8,512,128]{2,1,0:T(8,128)(2,1)S(1)}, u32[]{:S(2)}, u32[]{:S(2)}) async-start(bf16[8,512,128]{2,1,0:T(8,128)(2,1)} %get-tuple-element.10), calls=%async_computation.2 | async-start | bytes 2097152 | tf_op jit(solution)/shard_map/all_to_all | solution.py:318
  84.1 15.8 %collective-permute-start.7 = (bf16[2,64,128]{2,1,0:T(8,128)(2,1)S(1)}, bf16[2,64,128]{2,1,0:T(8,128)(2,1)S(1)}, u32[]{:S(2)}, u32[]{:S(2)}) collective-permute-start(bf16[2,64,128]{2,1,0:T(8,128)(2,1)S(1)} %get-tuple-element.34), channel_id=1, source_target_pairs={{0,2},{1,3},{2,0},{3,1},{4,6},{5,7},{6,4},{7,5},{8,10},{9,11},{10,... | collective-permute-start | bytes 98312 | tf_op jit(solution)/shard_map/ppermute | solution.py:238
  86.0 14.8 %collective-permute-start.8 = (bf16[2,64,128]{2,1,0:T(8,128)(2,1)S(1)}, bf16[2,64,128]{2,1,0:T(8,128)(2,1)S(1)}, u32[]{:S(2)}, u32[]{:S(2)}) collective-permute-start(bf16[2,64,128]{2,1,0:T(8,128)(2,1)S(1)} %get-tuple-element.33), channel_id=1, source_target_pairs={{0,3},{1,2},{2,1},{3,0},{4,7},{5,6},{6,5},{7,4},{8,11},{9,10},{10,... | collective-permute-start | bytes 98312 | tf_op jit(solution)/shard_map/ppermute | solution.py:238
  87.4 13.4 %collective-permute-start.9 = (bf16[2,64,128]{2,1,0:T(8,128)(2,1)S(1)}, bf16[2,64,128]{2,1,0:T(8,128)(2,1)S(1)}, u32[]{:S(2)}, u32[]{:S(2)}) collective-permute-start(bf16[2,64,128]{2,1,0:T(8,128)(2,1)S(1)} %get-tuple-element.32), channel_id=1, source_target_pairs={{0,16},{1,17},{2,18},{3,19},{4,20},{5,21},{6,22},{7,23},{8,24},{9,... | collective-permute-start | bytes 98312 | tf_op jit(solution)/shard_map/ppermute | solution.py:238
  87.4 13.4 %collective-permute-start.10 = (bf16[2,64,128]{2,1,0:T(8,128)(2,1)S(1)}, bf16[2,64,128]{2,1,0:T(8,128)(2,1)S(1)}, u32[]{:S(2)}, u32[]{:S(2)}) collective-permute-start(bf16[2,64,128]{2,1,0:T(8,128)(2,1)S(1)} %get-tuple-element.31), channel_id=1, source_target_pairs={{0,17},{1,16},{2,19},{3,18},{4,21},{5,20},{6,23},{7,22},{8,25},{9,... | collective-permute-start | bytes 98312 | tf_op jit(solution)/shard_map/ppermute | solution.py:238
  87.7 13.1 %collective-permute-start.11 = (bf16[2,64,128]{2,1,0:T(8,128)(2,1)S(1)}, bf16[2,64,128]{2,1,0:T(8,128)(2,1)S(1)}, u32[]{:S(2)}, u32[]{:S(2)}) collective-permute-start(bf16[2,64,128]{2,1,0:T(8,128)(2,1)S(1)} %get-tuple-element.30), channel_id=1, source_target_pairs={{0,18},{1,19},{2,16},{3,17},{4,22},{5,23},{6,20},{7,21},{8,26},{9,... | collective-permute-start | bytes 98312 | tf_op jit(solution)/shard_map/ppermute | solution.py:238
  99.8 4.2 %collective-permute-start.12 = (bf16[2,64,128]{2,1,0:T(8,128)(2,1)S(1)}, bf16[2,64,128]{2,1,0:T(8,128)(2,1)S(1)}, u32[]{:S(2)}, u32[]{:S(2)}) collective-permute-start(bf16[2,64,128]{2,1,0:T(8,128)(2,1)S(1)} %get-tuple-element.29), channel_id=1, source_target_pairs={{0,19},{1,18},{2,17},{3,16},{4,23},{5,22},{6,21},{7,20},{8,27},{9,... | collective-permute-start | bytes 98312 | tf_op jit(solution)/shard_map/ppermute | solution.py:238

commit v3 on v2

--- a/solution.py
+++ b/solution.py
@@ -80,21 +80,23 @@
     dkv[:, 1] = dv_acc[...].astype(jnp.bfloat16).reshape(shards, tok, 128)
 
 
-def planes_kernel(meta, pkg, *refs, rows, tok, q_blocks, scale, distances, planes):
-    count = len(distances)
-    ends = 0 in distances
-    near, refs = refs[:count], refs[count:]
-    if ends:
+def planes_kernel(meta, pkg, *refs, rows, tok, q_blocks, scale, odd, planes):
+    halves = planes // 2
+    team = pkg.shape[0]
+    near, refs = refs[:halves], refs[halves:]
+    if odd:
+        dq, grads, kv, dk_acc, dv_acc, dq_acc, sems = refs
+    else:
         dq_before, refs = refs[0], refs[1:]
-    dq, near_grads, (kv, dk_acc, dv_acc, dq_acc, sems) = refs[0], refs[1 : 1 + count], refs[1 + count :]
-    team = pkg.shape[0]
+        dq_out, (grads, kv, dk_acc, dv_acc, dq_acc, sems, dq, dq_sems) = refs[:team], refs[team:]
     sources = BLK // tok
     wide = sources * rows
-    plane = meta[2 * q_blocks]
+    plane, place = meta[2 * q_blocks], meta[2 * q_blocks + 1]
     team_blocks = team // 2 // sources
     range_blocks = team_blocks * planes
     loads = [
-        pltpu.make_async_copy(near[n], kv.at[n * team : (n + 1) * team], sems.at[n]) for n in range(count)
+        pltpu.make_async_copy(near[n], kv.at[pl.ds(((plane // 2) ^ n) * team, team)], sems.at[n])
+        for n in range(halves)
     ]
     for copy in loads:
         copy.start()
@@ -109,14 +111,14 @@
         q = pkg[mine, 0:rows, :].reshape(wide, 128)
         g = pkg[mine, rows : 2 * rows, :].reshape(wide, 128)
         lse, delta = stats_of(pkg[mine, 2 * rows :, :], sources, rows // 128)
-        if ends:
+        if odd:
+            dq_acc[...] = jnp.zeros_like(dq_acc)
+        else:
             dq_acc[...] = dq_before[i]
-        else:
-            dq_acc[...] = jnp.zeros_like(dq_acc)
-
-        def step(j, distance, masked):
+
+        def step(j, half, masked):
             within = (j // range_blocks) * team_blocks + j % team_blocks
-            block = (distance - distances[0]) * (2 * team_blocks) + within
+            block = half * (2 * team_blocks) + within
             at_shards = pl.ds(sources * block, sources)
             k = kv[at_shards, 0].reshape(BLK, 128)
             v = kv[at_shards, 1].reshape(BLK, 128)
@@ -127,27 +129,34 @@
             dq_acc[...] += dq_part
 
         def inner(j, _):
-            distance = ((j % range_blocks) // team_blocks) ^ plane
-
-            @pl.when((distance >= distances[0]) & (distance <= distances[-1]))
+            key_plane = (j % range_blocks) // team_blocks
+
+            @pl.when((key_plane ^ plane) & 1 == odd)
             def _():
-                step(j, distance, False)
+                step(j, key_plane // 2, False)
 
             return 0
 
         lax.fori_loop(first, last, inner, 0)
-        if ends:
-            step(last, 0, True)
+        if odd:
+            dq[i] = dq_acc[...]
+        else:
+            step(last, plane // 2, True)
             dq[mine] = (dq_acc[...] * scale).astype(jnp.bfloat16).reshape(sources, rows, 128)
-        else:
-            dq[i] = dq_acc[...]
         return 0
 
     lax.fori_loop(0, q_blocks, over_queries, 0)
-    for n in range(count):
-        at = pl.ds(n * team * tok, team * tok)
-        near_grads[n][:, 0] = (dk_acc[at, :] * scale).astype(jnp.bfloat16).reshape(team, tok, 128)
-        near_grads[n][:, 1] = dv_acc[at, :].astype(jnp.bfloat16).reshape(team, tok, 128)
+    if not odd:
+        stores = [pltpu.make_async_copy(dq.at[place ^ d], dq_out[d], dq_sems.at[d]) for d in range(team)]
+        for copy in stores:
+            copy.start()
+    for half in range(halves):
+        at = pl.ds(half * team * tok, team * tok)
+        grads[half, :, 0] = (dk_acc[at, :] * scale).astype(jnp.bfloat16).reshape(team, tok, 128)
+        grads[half, :, 1] = dv_acc[at, :].astype(jnp.bfloat16).reshape(team, tok, 128)
+    if not odd:
+        for copy in stores:
+            copy.wait()
 
 
 VMEM = pl.BlockSpec(memory_space=pltpu.VMEM)
@@ -180,36 +189,57 @@
     )(meta, pkg, kv)
 
 
-def attention_part(meta, pkg, kv, distances, dq_before, rows, scale, planes):
+def attention_part(meta, pkg, kv, dq_before, rows, scale, planes):
     team, _, tok, head_dim = kv[0].shape
-    count = len(distances)
+    halves = planes // 2
     q_blocks = team * tok // BLK
     wide = rows * (BLK // tok)
-    ends = 0 in distances
-    if ends:
-        dq_shape = jax.ShapeDtypeStruct((team, rows, head_dim), jnp.bfloat16)
+    odd = dq_before is None
+    if odd:
+        dq_shapes = (jax.ShapeDtypeStruct((q_blocks, wide, head_dim), jnp.float32),)
     else:
-        dq_shape = jax.ShapeDtypeStruct((q_blocks, wide, head_dim), jnp.float32)
-    pairs = 2 * q_blocks * count
-    dq, *grads = pl.pallas_call(
+        dq_shapes = (jax.ShapeDtypeStruct((rows, head_dim), jnp.bfloat16),) * team
+    pairs = 2 * q_blocks * halves
+    anywhere = pl.BlockSpec(memory_space=pl.ANY)
+    *dq, grads = pl.pallas_call(
         functools.partial(
-            planes_kernel, rows=rows, tok=tok, q_blocks=q_blocks, scale=scale, distances=distances, planes=planes
+            planes_kernel, rows=rows, tok=tok, q_blocks=q_blocks, scale=scale, odd=int(odd), planes=planes
         ),
-        out_shape=(dq_shape,) + (jax.ShapeDtypeStruct(kv[0].shape, jnp.bfloat16),) * count,
-        in_specs=[SMEM, VMEM] + [pl.BlockSpec(memory_space=pl.ANY)] * count + [VMEM] * ends,
-        out_specs=(VMEM,) * (1 + count),
-        scratch_shapes=[pltpu.VMEM((count * team, 2, tok, head_dim), jnp.bfloat16)]
-        + totals(count * team, tok, wide, head_dim)
-        + [pltpu.SemaphoreType.DMA((count,))],
+        out_shape=dq_shapes + (jax.ShapeDtypeStruct((halves,) + kv[0].shape, jnp.bfloat16),),
+        in_specs=[SMEM, VMEM] + [anywhere] * halves + ([] if odd else [VMEM]),
+        out_specs=((VMEM,) if odd else (anywhere,) * team) + (VMEM,),
+        scratch_shapes=[pltpu.VMEM((halves * team, 2, tok, head_dim), jnp.bfloat16)]
+        + totals(halves * team, tok, wide, head_dim)
+        + [pltpu.SemaphoreType.DMA((halves,))]
+        + ([] if odd else [pltpu.VMEM((team, rows, head_dim), jnp.bfloat16), pltpu.SemaphoreType.DMA((team,))]),
         compiler_params=pltpu.CompilerParams(vmem_limit_bytes=32 * 1024 * 1024),
         cost_estimate=pl.CostEstimate(
             flops=pairs * 10 * BLK * wide * head_dim,
             bytes_accessed=4 * 1024 * 1024,
             transcendentals=pairs * BLK * wide,
         ),
-        name="attention_part_" + "_".join(str(d) for d in distances),
-    )(meta, pkg, *kv, *([dq_before] if ends else []))
-    return dq, grads
+        name="attention_odd" if odd else "attention_even",
+    )(meta, pkg, *kv, *([] if odd else [dq_before]))
+    return (dq[0] if odd else dq), grads
+
+
+def place_kernel(place, *refs):
+    *arrived, out = refs
+    for d, block in enumerate(arrived):
+        out[:, place[0] ^ d] = block[...]
+
+
+def place_blocks(place, arrived, tok):
+    rows, head_dim = arrived[0].shape
+    fan = rows // tok
+    out = pl.pallas_call(
+        place_kernel,
+        out_shape=jax.ShapeDtypeStruct((tok, len(arrived), fan, head_dim), jnp.bfloat16),
+        in_specs=[SMEM] + [VMEM] * len(arrived),
+        out_specs=VMEM,
+        name="place_dq",
+    )(place, *[x.reshape(tok, fan, head_dim) for x in arrived])
+    return out.reshape(tok, len(arrived) * fan, head_dim)
 
 
 def pieces(x):
@@ -224,26 +254,26 @@
     return sum(x.astype(jnp.float32) for x in terms).astype(jnp.bfloat16)
 
 
-def exchange(x, slots):
+def exchange(blocks, slots):
     n_ctx, n_head = lax.axis_size("ctx"), lax.axis_size("head")
-    me = (lax.axis_index("ctx") % 2) * slots + lax.axis_index("head") % slots
-    order = me ^ jnp.arange(2 * slots)
-    x = x[order]
-    arrived = [x[0]]
+    arrived = [blocks[0]]
     for d in range(1, 2 * slots):
         db, dr = divmod(d, slots)
         moves = [
             (c * n_head + h, (c ^ db) * n_head + (h ^ dr)) for c in range(n_ctx) for h in range(n_head)
         ]
-        arrived.append(lax.ppermute(x[d], ("ctx", "head"), moves))
-    return jnp.stack(arrived)[order]
-
-
-def by_token(dq, dkv, kv_heads, fan):
-    _, _, tok, head_dim = dkv.shape
-    dq = dq.reshape(kv_heads, tok, fan, head_dim).transpose(1, 0, 2, 3).reshape(tok, kv_heads * fan, head_dim)
-    dkv = dkv.transpose(1, 2, 0, 3)
-    return dq, dkv[0], dkv[1]
+        arrived.append(lax.ppermute(blocks[d], ("ctx", "head"), moves))
+    return arrived
+
+
+def dq_by_token(dq, tok, fan):
+    kv_heads, _, head_dim = dq.shape
+    return dq.reshape(kv_heads, tok, fan, head_dim).transpose(1, 0, 2, 3).reshape(tok, kv_heads * fan, head_dim)
+
+
+def dkv_by_token(parts):
+    dkv = parts.astype(jnp.float32).sum(axis=0).astype(jnp.bfloat16).transpose(1, 2, 0, 3)
+    return dkv[0], dkv[1]
 
 
 def per_device(queries, keys, values, outputs, out_grads, log_norms, block_doc):
@@ -273,6 +303,17 @@
         step = distance * slots
         return lax.ppermute(x, "head", [(h, h ^ step) for h in range(n_head)])
 
+    alternate = [
+        [
+            (2 * c + b) * n_head + z * slots + r
+            for z in range(parity, planes, 2)
+            for b in range(2)
+            for r in range(slots)
+        ]
+        for c in range(n_ctx // 2)
+        for parity in range(2)
+    ]
+
     kv = jnp.stack([keys, values], axis=0).transpose(2, 0, 1, 3)
     if by_plane:
         kv = lax.all_to_all(kv, both, 0, 0, axis_index_groups=teams, tiled=True)
@@ -305,19 +346,17 @@
     first_block = jnp.sum(block_doc[None, :] < block_doc[at][:, None], axis=1, dtype=jnp.int32)
     ranges_before = 1 if n_ctx > 2 else 0
     base = (2 * pair - ranges_before) * range_blocks
-    meta = jnp.concatenate([at - base, first_block - base, plane[None]]).astype(jnp.int32)
+    place = (ctx % 2) * slots + head % slots
+    meta = jnp.concatenate([at - base, first_block - base, plane[None], place[None]]).astype(jnp.int32)
 
     if by_plane:
-        dq_before, (grads_3,) = attention_part(meta, pkg, kv[3:], (3,), None, rows, scale, planes)
-        relayed = across(grads_3, 1)
-        dq, (grads_0, grads_1, grads_2) = attention_part(
-            meta, pkg, kv[:3], (0, 1, 2), dq_before, rows, scale, planes
-        )
-        close = across(grads_1, 1)
-        far = across(add(grads_2, relayed), 2)
-        dq = lax.all_to_all(dq, both, 0, 0, axis_index_groups=teams, tiled=True)
-        dkv = exchange(add(grads_0, close, far), slots)
-        return by_token(dq, dkv, kv_heads, fan)
+        dq_before, odd_grads = attention_part(meta, pkg, (kv[1], kv[3]), None, rows, scale, planes)
+        arrived = across(odd_grads, 1)
+        dq, even_grads = attention_part(meta, pkg, (kv[0], kv[2]), dq_before, rows, scale, planes)
+        dkv = add(arrived, even_grads).reshape(planes // 2 * kv_heads, 2, tok, head_dim)
+        dkv = lax.all_to_all(dkv, both, 0, 0, axis_index_groups=alternate, tiled=True)
+        dq = place_blocks(place[None], exchange(dq, slots), tok)
+        return (dq,) + dkv_by_token(dkv.reshape(planes // 2, kv_heads, 2, tok, head_dim))
 
     if ranges_before:
         prior = lax.ppermute(kv[n_head:], "ctx", [(c, c + 2) for c in range(n_ctx - 2)])
@@ -329,9 +368,8 @@
 
     dkv = lax.all_to_all(dkv, both, 0, 0, axis_index_groups=pairs, tiled=True)
     dq = lax.all_to_all(dq, both, 0, 0, axis_index_groups=teams, tiled=True)
-    dkv = dkv.reshape(2, planes, slots, 2, tok, head_dim).astype(jnp.float32).sum(axis=1)
-    dkv = dkv.astype(jnp.bfloat16).reshape(kv_heads, 2, tok, head_dim)
-    return by_token(dq, dkv, kv_heads, fan)
+    dkv = dkv.reshape(2, planes, slots, 2, tok, head_dim).transpose(1, 0, 2, 3, 4, 5)
+    return (dq_by_token(dq, tok, fan),) + dkv_by_token(dkv.reshape(planes, kv_heads, 2, tok, head_dim))
 
 
 def solution(mesh):

time: 108 us -> 97.3 us (0.901)
  waiting for transfers between devices: 46.4 us -> 37.4 us
  starting transfers between devices: 33.9 us -> 28.8 us
  Pallas kernels: 10.4 us -> 13.4 us
    ppermute x6 -> x4, starting transfers between devices: 14.4 us -> 5.8 us  [across(): return lax.ppermute(x, 'head', [(h, h ^ step) for h in range(n_head)])]
    ppermute x6 -> x4, waiting for transfers between devices: 29.5 us -> 22.7 us  [across(): return lax.ppermute(x, 'head', [(h, h ^ step) for h in range(n_head)])]
    pallas_call x0 -> x1, Pallas kernels: none -> 2.55 us  [place_blocks(): pl.pallas_call(place_kernel, out_shape=jax.ShapeDtypeStruct((tok, len(arr...]
    ppermute x7, waiting for transfers between devices: 13.8 us -> 11.5 us  [exchange(): arrived.append(lax.ppermute(blocks[d], ('ctx', 'head'), moves))]
    unnamed x21 -> x47, local copies, waits for them, and re-layouts: 4.05 us -> 6.32 us
    ppermute x7, starting transfers between devices: 6.96 us -> 8.86 us  [exchange(): arrived.append(lax.ppermute(blocks[d], ('ctx', 'head'), moves))]
    all_to_all x1, starting transfers between devices: 3.56 us -> 5.22 us  [per_device(): lax.all_to_all(dkv, both, 0, 0, axis_index_groups=alternate, tiled=True)]
    reshape x1 -> x0, local copies, waits for them, and re-layouts: 1.27 us -> none  [by_token(): dq.reshape(kv_heads, tok, fan, head_dim).transpose(1, 0, 2, 3)]
  transfers between devices with their start and end apart: 16 -> 14, of which waited for: 7 -> 12; matrix products, arithmetic and copies ran while one was open for 9% -> 7% of each run, Pallas kernels for 10% -> 10%
where the time goes in v3:
time: 97.3 us; the launch traced here: 96.1 us
  waiting for transfers between devices  37.4 us (38%)
  starting transfers between devices  28.8 us (30%)
  Pallas kernels  13.4 us (14%)
  local copies, waits for them, and re-layouts  9.83 us (10%)
  other arithmetic  5.7 us (6%)
    ppermute x4, waiting for transfers between devices, across(): return lax.ppermute(x, 'head', [(h, h ^ step) for h in range(n_head)])  22.7 us
    ppermute x7, waiting for transfers between devices, exchange(): arrived.append(lax.ppermute(blocks[d], ('ctx', 'head'), moves))  11.5 us
    pallas_call x2, Pallas kernels, attention_part(): pl.pallas_call(functools.partial(planes_kernel, rows=rows, tok=tok, q_blo...  10.9 us
    ppermute x7, starting transfers between devices, exchange(): arrived.append(lax.ppermute(blocks[d], ('ctx', 'head'), moves))  8.86 us
    unnamed x47, local copies, waits for them, and re-layouts  6.32 us
    ppermute x4, starting transfers between devices, across(): return lax.ppermute(x, 'head', [(h, h ^ step) for h in range(n_head)])  5.8 us
    all_to_all x1, starting transfers between devices, per_device(): lax.all_to_all(dkv, both, 0, 0, axis_index_groups=alternate, tiled=True)  5.22 us
    all_to_all x1, starting transfers between devices, per_device(): kv = lax.all_to_all(kv, both, 0, 0, axis_index_groups=teams, tiled=True)  5.17 us
  transfers between devices with their start and end apart: 14, of which 12 were waited for; matrix products, arithmetic and copies ran while one was open for 7% of the time, Pallas kernels for 10%

profile of v3, /device:TPU:0, one launch (start us, length us, event | category | flops | bytes accessed | tf_op | source)
XLA Modules:
  0.0 96.1 jit_solution(10975247245337873337)
XLA Ops:
  0.6 0.0 copy-start
  0.6 0.0 copy-start.14
  0.7 1.2 %copy_bitcast_fusion.2 = (bf16[1,64,8,128]{3,1,0,2:T(8,128)(2,1)S(1)}, bf16[1,64,8,128]{3,1,0,2:T(8,128)(2,1)S(1)}) fusion(bf16[64,8,128]{2,1,0:T(8,128)(2,1)} %param.9, bf16[64,8,128]{2,1,0:T(8,128)(2,1)} %param.8), kind=kLoop, calls=%fused_computation.11 | loop fusion | bytes 524288 | tf_op jit(solution)/shard_map/stack | solution.py:317
  1.8 0.7 maximum_bitcast_fusion
  2.5 5.2 %all-to-all-start.1 = ((bf16[8,2,64,128]{3,2,1,0:T(8,128)(2,1)}), bf16[8,2,64,128]{3,2,1,0:T(8,128)(2,1)S(1)}, u32[]{:S(2)}, u32[]{:S(2)}) async-start(bf16[8,2,64,128]{3,2,1,0:T(8,128)(2,1)} %maximum_bitcast_fusion), calls=%async_computation.1 | async-start | bytes 524288 | tf_op jit(solution)/shard_map/all_to_all | solution.py:319
  7.7 0.8 copy.36
  8.6 0.0 copy-done.14
  8.6 1.8 %multiply_reduce_fusion = f32[64,64]{1,0:T(8,128)S(1)} fusion(bf16[64,64,128]{2,1,0:T(8,128)(2,1)} %param.10, bf16[64,64,128]{2,1,0:T(8,128)(2,1)S(1)} %copy-done.14), kind=kLoop, calls=%fused_computation.4 | loop fusion | flops 2093056 | bytes 2113536 | tf_op jit(solution)/shard_map/reduce_sum | solution.py:328
  10.4 0.1 copy.38
  10.6 0.4 copy.39
  11.0 0.8 reshape.279
  11.7 0.0 copy-done
  11.7 0.5 copy_bitcast_fusion
  12.2 1.5 %fusion.1 = bf16[8,1056,128]{2,1,0:T(8,128)(2,1)} fusion(bf16[8,24,128]{2,1,0:T(8,128)(2,1)S(1)} %reshape.279, bf16[8,512,128]{2,1,0:T(8,128)(2,1)S(1)} %get-tuple-element.35, bf16[8,512,128]{2,1,0:T(8,128)(2,1)S(1)} %get-tuple-element.36), kind=kLoop, calls=%fused_computation.3 | loop fusion | flops 8650752 | bytes 4308992 | tf_op jit(solution)/shard_map/concatenate | solution.py:337
  13.8 0.5 all-to-all-done.1.refs_0_
  14.3 3.8 %all-to-all-start = ((bf16[8,1056,128]{2,1,0:T(8,128)(2,1)}), bf16[8,1056,128]{2,1,0:T(8,128)(2,1)S(1)}, u32[]{:S(2)}, u32[]{:S(2)}) async-start(bf16[8,1056,128]{2,1,0:T(8,128)(2,1)} %fusion.1), calls=%async_computation | async-start | bytes 4325376 | tf_op jit(solution)/shard_map/all_to_all | solution.py:338
  18.1 2.6 %collective-permute-start = (bf16[8,2,64,128]{3,2,1,0:T(8,128)(2,1)S(1)}, bf16[8,2,64,128]{3,2,1,0:T(8,128)(2,1)}, u32[]{:S(2)}, u32[]{:S(2)}) collective-permute-start(bf16[8,2,64,128]{3,2,1,0:T(8,128)(2,1)S(1)} %all-to-all-done.1.refs_0_), channel_id=1, source_target_pairs={{0,8},{1,9},{2,10},{3,11},{4,12},{5,13},{6,14},{7,15},{8,0},{9,1},... | collective-permute-start | bytes 786440 | tf_op jit(solution)/shard_map/ppermute | solution.py:304
  20.7 0.1 fusion.13
  20.8 0.0 copy-done.13
  20.8 0.6 gather_fusion
  21.4 0.2 convert_reduce_fusion
  21.6 1.6 %collective-permute-start.1 = (bf16[8,2,64,128]{3,2,1,0:T(8,128)(2,1)S(1)}, bf16[8,2,64,128]{3,2,1,0:T(8,128)(2,1)S(1)}, u32[]{:S(2)}, u32[]{:S(2)}) collective-permute-start(bf16[8,2,64,128]{3,2,1,0:T(8,128)(2,1)S(1)} %all-to-all-done.1.refs_0_), channel_id=1, source_target_pairs={{0,4},{1,5},{2,6},{3,7},{4,0},{5,1},{6,2},{7,3},{8,12},{9,13},{10,... | collective-permute-start | bytes 786440 | tf_op jit(solution)/shard_map/ppermute | solution.py:304
  23.2 10.3 %collective-permute-done.refs_1_ = bf16[8,2,64,128]{3,2,1,0:T(8,128)(2,1)} collective-permute-done((bf16[8,2,64,128]{3,2,1,0:T(8,128)(2,1)S(1)}, bf16[8,2,64,128]{3,2,1,0:T(8,128)(2,1)}, u32[]{:S(2)}, u32[]{:S(2)}) %collective-permute-start) | collective-permute-done | bytes 262176 | tf_op jit(solution)/shard_map/ppermute | solution.py:304
  33.5 0.5 collective-permute-start.2
  34.1 0.1 add_subtract_fusion
  34.1 0.1 pad_add_fusion.meta
  34.2 0.4 collective-permute-done.1.refs_0_
  34.6 0.7 copy-done.2
  35.3 6.3 %collective-permute-done.2.refs_1_ = bf16[8,2,64,128]{3,2,1,0:T(8,128)(2,1)S(1)} collective-permute-done((bf16[8,2,64,128]{3,2,1,0:T(8,128)(2,1)}, bf16[8,2,64,128]{3,2,1,0:T(8,128)(2,1)S(1)}, u32[]{:S(2)}, u32[]{:S(2)}) %collective-permute-start.2) | collective-permute-done | bytes 262176 | tf_op jit(solution)/shard_map/ppermute | solution.py:304
  41.6 0.7 copy-done.4
  42.3 2.6 %all-to-all-done.pkg = bf16[8,1056,128]{2,1,0:T(8,128)(2,1)S(1)} async-done(((bf16[8,1056,128]{2,1,0:T(8,128)(2,1)}), bf16[8,1056,128]{2,1,0:T(8,128)(2,1)S(1)}, u32[]{:S(2)}, u32[]{:S(2)}) %all-to-all-start) | async-done | bytes 2162720 | tf_op jit(solution)/shard_map/all_to_all | solution.py:338
  44.9 0.9 copy-done.3
  45.9 0.9 copy-done.5
  46.8 3.6 %attention_odd.1 = (f32[4,1024,128]{2,1,0:T(8,128)S(1)}, bf16[2,8,2,64,128]{4,3,2,1,0:T(8,128)(2,1)S(1)}) custom-call(s32[10]{0:T(128)S(1)} %pad_add_fusion.meta, bf16[8,1056,128]{2,1,0:T(8,128)(2,1)S(1)} %all-to-all-done.pkg, bf16[8,2,64,128]{3,2,1,0:T(8,128)(2,1)S(1)} %copy-done.3, bf16[8,2,64,128]{3,2,1,0:T(8,128)(2,1)S(1)} %copy-done.5), custom_call_target="tpu_custom_call" | custom-call | flops 2684354560 | bytes 4194304 | tf_op jit(solution)/shard_map/attention_odd/pallas_call | solution.py:204
  50.4 1.0 %collective-permute-start.10 = (bf16[2,8,2,64,128]{4,3,2,1,0:T(8,128)(2,1)S(1)}, bf16[2,8,2,64,128]{4,3,2,1,0:T(8,128)(2,1)S(1)}, u32[]{:S(2)}, u32[]{:S(2)}) collective-permute-start(bf16[2,8,2,64,128]{4,3,2,1,0:T(8,128)(2,1)S(1)} %get-tuple-element.23), channel_id=1, source_target_pairs={{0,4},{1,5},{2,6},{3,7},{4,0},{5,1},{6,2},{7,3},{8,12},{9,13},{10,... | collective-permute-start | bytes 1572872 | tf_op jit(solution)/shard_map/ppermute | solution.py:304
  51.4 7.3 %attention_even.1 = (bf16[512,128]{1,0:T(8,128)(2,1)S(1)}, bf16[512,128]{1,0:T(8,128)(2,1)S(1)}, bf16[512,128]{1,0:T(8,128)(2,1)S(1)}, bf16[512,128]{1,0:T(8,128...) custom-call(s32[10]{0:T(128)S(1)} %pad_add_fusion.meta, ...), custom_call_target="tpu_custom_call" | custom-call | flops 2684354560 | bytes 4194304 | tf_op jit(solution)/shard_map/attention_even/pallas_call | solution.py:204
  58.7 0.0 copy-start.1
  58.8 0.0 copy-start.6
  58.8 0.0 copy-start.11
  58.8 0.0 copy-start.12
  58.8 5.7 %collective-permute-done.10 = bf16[2,8,2,64,128]{4,3,2,1,0:T(8,128)(2,1)S(1)} collective-permute-done((bf16[2,8,2,64,128]{4,3,2,1,0:T(8,128)(2,1)S(1)}, bf16[2,8,2,64,128]{4,3,2,1,0:T(8,128)(2,1)S(1)}, u32[]{:S(2)}, u32[]{:S(2)}) %collective-permute-start.10) | collective-permute-done | bytes 524320 | tf_op jit(solution)/shard_map/ppermute | solution.py:304
  64.6 1.0 %add_convert_fusion = bf16[2,8,2,64,128]{4,3,2,1,0:T(8,128)(2,1)} fusion(bf16[2,8,2,64,128]{4,3,2,1,0:T(8,128)(2,1)S(1)} %get-tuple-element.24, bf16[2,8,2,64,128]{4,3,2,1,0:T(8,128)(2,1)S(1)} %collective-permute-done.10), kind=kLoop, calls=%fused_computation.7 | loop fusion | flops 1048576 | bytes 1572864 | tf_op jit(solution)/shard_map/convert_element_type | solution.py:254
  65.6 5.2 %all-to-all-start.2 = ((bf16[16,2,64,128]{3,2,1,0:T(8,128)(2,1)}), bf16[16,2,64,128]{3,2,1,0:T(8,128)(2,1)S(1)}, u32[]{:S(2)}, u32[]{:S(2)}) async-start(bf16[16,2,64,128]{3,2,1,0:T(8,128)(2,1)} %bitcast.34), calls=%async_computation.2 | async-start | bytes 1048576 | tf_op jit(solution)/shard_map/all_to_all | solution.py:357
  70.9 1.9 %collective-permute-start.3 = (bf16[512,128]{1,0:T(8,128)(2,1)}, bf16[512,128]{1,0:T(8,128)(2,1)S(1)}, u32[]{:S(2)}, u32[]{:S(2)}) collective-permute-start(bf16[512,128]{1,0:T(8,128)(2,1)} %copy-done.12), channel_id=1, source_target_pairs={{0,1},{1,0},{2,3},{3,2},{4,5},{5,4},{6,7},{7,6},{8,9},{9,8},{10,11... | collective-permute-start | bytes 393224 | tf_op jit(solution)/shard_map/ppermute | solution.py:265
  72.8 1.5 %collective-permute-start.4 = (bf16[512,128]{1,0:T(8,128)(2,1)}, bf16[512,128]{1,0:T(8,128)(2,1)S(1)}, u32[]{:S(2)}, u32[]{:S(2)}) collective-permute-start(bf16[512,128]{1,0:T(8,128)(2,1)} %copy-done.11), channel_id=1, source_target_pairs={{0,2},{1,3},{2,0},{3,1},{4,6},{5,7},{6,4},{7,5},{8,10},{9,11},{10,... | collective-permute-start | bytes 393224 | tf_op jit(solution)/shard_map/ppermute | solution.py:265
  74.2 0.2 collective-permute-start.5
  74.4 0.0 collective-permute-start.6
  74.4 2.0 %collective-permute-start.7 = (bf16[512,128]{1,0:T(8,128)(2,1)}, bf16[512,128]{1,0:T(8,128)(2,1)S(1)}, u32[]{:S(2)}, u32[]{:S(2)}) collective-permute-start(bf16[512,128]{1,0:T(8,128)(2,1)} %copy-done.8), channel_id=1, source_target_pairs={{0,17},{1,16},{2,19},{3,18},{4,21},{5,20},{6,23},{7,22},{8,25},{9,... | collective-permute-start | bytes 393224 | tf_op jit(solution)/shard_map/ppermute | solution.py:265
  76.4 3.7 %collective-permute-done.3 = bf16[512,128]{1,0:T(8,128)(2,1)S(1)} collective-permute-done((bf16[512,128]{1,0:T(8,128)(2,1)}, bf16[512,128]{1,0:T(8,128)(2,1)S(1)}, u32[]{:S(2)}, u32[]{:S(2)}) %collective-permute-start.3) | collective-permute-done | bytes 131104 | tf_op jit(solution)/shard_map/ppermute | solution.py:265
  80.1 0.2 collective-permute-start.8
  80.3 0.3 collective-permute-done.4
  80.6 3.1 %collective-permute-start.9 = (bf16[512,128]{1,0:T(8,128)(2,1)}, bf16[512,128]{1,0:T(8,128)(2,1)S(1)}, u32[]{:S(2)}, u32[]{:S(2)}) collective-permute-start(bf16[512,128]{1,0:T(8,128)(2,1)} %copy-done.6), channel_id=1, source_target_pairs={{0,19},{1,18},{2,17},{3,16},{4,23},{5,22},{6,21},{7,20},{8,27},{9,... | collective-permute-start | bytes 393224 | tf_op jit(solution)/shard_map/ppermute | solution.py:265
  83.7 0.2 collective-permute-done.5
  83.9 0.0 collective-permute-done.6
  83.9 3.7 %collective-permute-done.7 = bf16[512,128]{1,0:T(8,128)(2,1)S(1)} collective-permute-done((bf16[512,128]{1,0:T(8,128)(2,1)}, bf16[512,128]{1,0:T(8,128)(2,1)S(1)}, u32[]{:S(2)}, u32[]{:S(2)}) %collective-permute-start.7) | collective-permute-done | bytes 131104 | tf_op jit(solution)/shard_map/ppermute | solution.py:265
  87.6 0.9 collective-permute-done.8
  88.4 2.8 %collective-permute-done.9 = bf16[512,128]{1,0:T(8,128)(2,1)S(1)} collective-permute-done((bf16[512,128]{1,0:T(8,128)(2,1)}, bf16[512,128]{1,0:T(8,128)(2,1)S(1)}, u32[]{:S(2)}, u32[]{:S(2)}) %collective-permute-start.9) | collective-permute-done | bytes 131104 | tf_op jit(solution)/shard_map/ppermute | solution.py:265
  91.3 0.0 copy-done.15
  91.3 0.6 copy-done.21
  91.9 2.6 %place_dq.1 = bf16[64,8,8,128]{3,2,1,0:T(8,128)(2,1)} custom-call(s32[1]{0:T(128)} %bitcast.place, bf16[64,8,128]{2,1,0:T(8,128)(2,1)} %bitcast.76, bf16[64,8,128]{2,1,0:T(8,128)(2,1)} %bitcast.81, bf16[64,8,128]{2,1,0:T(8,128)(2,1)} %bitcast.82, bf16[64,8,128]{2,1,0:T(8,128)(2,1)} %bitcast.83, bf16[64,8,128]{2,1,0:T(8,128)(2,1)} %bitcast.84, ...), custom_call_target="tpu_custom_call" | custom-call | tf_op jit(solution)/shard_map/place_dq/pallas_call | solution.py:235
  94.5 0.0 all-to-all-done.2
  94.5 0.1 reduce_sum.35
  94.6 0.7 copy.43
  95.3 0.7 copy.42
  (37 shorter events, 0.2 us)
Async XLA Ops:
  0.6 11.1 %copy-start = (bf16[64,64,128]{2,1,0:T(8,128)(2,1)S(1)}, bf16[64,64,128]{2,1,0:T(8,128)(2,1)}, u32[]{:S(2)}) copy-start(bf16[64,64,128]{2,1,0:T(8,128)(2,1)} %param.7) | copy-start | bytes 3145732
  0.6 7.9 %copy-start.14 = (bf16[64,64,128]{2,1,0:T(8,128)(2,1)S(1)}, bf16[64,64,128]{2,1,0:T(8,128)(2,1)}, u32[]{:S(2)}) copy-start(bf16[64,64,128]{2,1,0:T(8,128)(2,1)} %param.11) | copy-start | bytes 3145732
  2.5 11.8 %all-to-all-start.1 = ((bf16[8,2,64,128]{3,2,1,0:T(8,128)(2,1)}), bf16[8,2,64,128]{3,2,1,0:T(8,128)(2,1)S(1)}, u32[]{:S(2)}, u32[]{:S(2)}) async-start(bf16[8,2,64,128]{3,2,1,0:T(8,128)(2,1)} %maximum_bitcast_fusion), calls=%async_computation.1 | async-start | bytes 524288 | tf_op jit(solution)/shard_map/all_to_all | solution.py:319
  13.8 7.0 %copy-start.13 = (s32[16]{0:T(128)S(1)}, s32[16]{0:T(128)}, u32[]{:S(2)}) copy-start(s32[16]{0:T(128)} %param.13) | copy-start | bytes 196
  14.3 30.6 %all-to-all-start = ((bf16[8,1056,128]{2,1,0:T(8,128)(2,1)}), bf16[8,1056,128]{2,1,0:T(8,128)(2,1)S(1)}, u32[]{:S(2)}, u32[]{:S(2)}) async-start(bf16[8,1056,128]{2,1,0:T(8,128)(2,1)} %fusion.1), calls=%async_computation | async-start | bytes 4325376 | tf_op jit(solution)/shard_map/all_to_all | solution.py:338
  18.1 15.4 %collective-permute-start = (bf16[8,2,64,128]{3,2,1,0:T(8,128)(2,1)S(1)}, bf16[8,2,64,128]{3,2,1,0:T(8,128)(2,1)}, u32[]{:S(2)}, u32[]{:S(2)}) collective-permute-start(bf16[8,2,64,128]{3,2,1,0:T(8,128)(2,1)S(1)} %all-to-all-done.1.refs_0_), channel_id=1, source_target_pairs={{0,8},{1,9},{2,10},{3,11},{4,12},{5,13},{6,14},{7,15},{8,0},{9,1},... | collective-permute-start | bytes 786440 | tf_op jit(solution)/shard_map/ppermute | solution.py:304
  21.6 13.0 %collective-permute-start.1 = (bf16[8,2,64,128]{3,2,1,0:T(8,128)(2,1)S(1)}, bf16[8,2,64,128]{3,2,1,0:T(8,128)(2,1)S(1)}, u32[]{:S(2)}, u32[]{:S(2)}) collective-permute-start(bf16[8,2,64,128]{3,2,1,0:T(8,128)(2,1)S(1)} %all-to-all-done.1.refs_0_), channel_id=1, source_target_pairs={{0,4},{1,5},{2,6},{3,7},{4,0},{5,1},{6,2},{7,3},{8,12},{9,13},{10,... | collective-permute-start | bytes 786440 | tf_op jit(solution)/shard_map/ppermute | solution.py:304
  33.5 8.1 %collective-permute-start.2 = (bf16[8,2,64,128]{3,2,1,0:T(8,128)(2,1)}, bf16[8,2,64,128]{3,2,1,0:T(8,128)(2,1)S(1)}, u32[]{:S(2)}, u32[]{:S(2)}) collective-permute-start(bf16[8,2,64,128]{3,2,1,0:T(8,128)(2,1)} %collective-permute-done.refs_1_), channel_id=1, source_target_pairs={{0,4},{1,5},{2,6},{3,7},{4,0},{5,1},{6,2},{7,3},{8,12},{9,13},{10,... | collective-permute-start | bytes 786440 | tf_op jit(solution)/shard_map/ppermute | solution.py:304
  34.6 0.7 copy-start.2
  41.6 0.7 copy-start.4
  44.9 1.0 copy-start.3
  45.9 0.9 copy-start.5
  50.4 14.2 %collective-permute-start.10 = (bf16[2,8,2,64,128]{4,3,2,1,0:T(8,128)(2,1)S(1)}, bf16[2,8,2,64,128]{4,3,2,1,0:T(8,128)(2,1)S(1)}, u32[]{:S(2)}, u32[]{:S(2)}) collective-permute-start(bf16[2,8,2,64,128]{4,3,2,1,0:T(8,128)(2,1)S(1)} %get-tuple-element.23), channel_id=1, source_target_pairs={{0,4},{1,5},{2,6},{3,7},{4,0},{5,1},{6,2},{7,3},{8,12},{9,13},{10,... | collective-permute-start | bytes 1572872 | tf_op jit(solution)/shard_map/ppermute | solution.py:304
  58.7 6.8 %copy-start.1 = (bf16[512,128]{1,0:T(8,128)(2,1)}, bf16[512,128]{1,0:T(8,128)(2,1)S(1)}, u32[]{:S(2)}) copy-start(bf16[512,128]{1,0:T(8,128)(2,1)S(1)} %get-tuple-element.15) | copy-start | bytes 393220
  58.8 6.8 %copy-start.6 = (bf16[512,128]{1,0:T(8,128)(2,1)}, bf16[512,128]{1,0:T(8,128)(2,1)S(1)}, u32[]{:S(2)}) copy-start(bf16[512,128]{1,0:T(8,128)(2,1)S(1)} %get-tuple-element.22) | copy-start | bytes 393220
  58.8 6.8 %copy-start.7 = (bf16[512,128]{1,0:T(8,128)(2,1)}, bf16[512,128]{1,0:T(8,128)(2,1)S(1)}, u32[]{:S(2)}) copy-start(bf16[512,128]{1,0:T(8,128)(2,1)S(1)} %get-tuple-element.21) | copy-start | bytes 393220
  58.8 6.8 %copy-start.8 = (bf16[512,128]{1,0:T(8,128)(2,1)}, bf16[512,128]{1,0:T(8,128)(2,1)S(1)}, u32[]{:S(2)}) copy-start(bf16[512,128]{1,0:T(8,128)(2,1)S(1)} %get-tuple-element.20) | copy-start | bytes 393220
  58.8 6.8 %copy-start.9 = (bf16[512,128]{1,0:T(8,128)(2,1)}, bf16[512,128]{1,0:T(8,128)(2,1)S(1)}, u32[]{:S(2)}) copy-start(bf16[512,128]{1,0:T(8,128)(2,1)S(1)} %get-tuple-element.19) | copy-start | bytes 393220
  58.8 6.8 %copy-start.10 = (bf16[512,128]{1,0:T(8,128)(2,1)}, bf16[512,128]{1,0:T(8,128)(2,1)S(1)}, u32[]{:S(2)}) copy-start(bf16[512,128]{1,0:T(8,128)(2,1)S(1)} %get-tuple-element.18) | copy-start | bytes 393220
  58.8 6.8 %copy-start.11 = (bf16[512,128]{1,0:T(8,128)(2,1)}, bf16[512,128]{1,0:T(8,128)(2,1)S(1)}, u32[]{:S(2)}) copy-start(bf16[512,128]{1,0:T(8,128)(2,1)S(1)} %get-tuple-element.17) | copy-start | bytes 393220
  58.8 6.8 %copy-start.12 = (bf16[512,128]{1,0:T(8,128)(2,1)}, bf16[512,128]{1,0:T(8,128)(2,1)S(1)}, u32[]{:S(2)}) copy-start(bf16[512,128]{1,0:T(8,128)(2,1)S(1)} %get-tuple-element.16) | copy-start | bytes 393220
  65.6 28.8 %all-to-all-start.2 = ((bf16[16,2,64,128]{3,2,1,0:T(8,128)(2,1)}), bf16[16,2,64,128]{3,2,1,0:T(8,128)(2,1)S(1)}, u32[]{:S(2)}, u32[]{:S(2)}) async-start(bf16[16,2,64,128]{3,2,1,0:T(8,128)(2,1)} %bitcast.34), calls=%async_computation.2 | async-start | bytes 1048576 | tf_op jit(solution)/shard_map/all_to_all | solution.py:357
  70.9 9.2 %collective-permute-start.3 = (bf16[512,128]{1,0:T(8,128)(2,1)}, bf16[512,128]{1,0:T(8,128)(2,1)S(1)}, u32[]{:S(2)}, u32[]{:S(2)}) collective-permute-start(bf16[512,128]{1,0:T(8,128)(2,1)} %copy-done.12), channel_id=1, source_target_pairs={{0,1},{1,0},{2,3},{3,2},{4,5},{5,4},{6,7},{7,6},{8,9},{9,8},{10,11... | collective-permute-start | bytes 393224 | tf_op jit(solution)/shard_map/ppermute | solution.py:265
  72.8 7.8 %collective-permute-start.4 = (bf16[512,128]{1,0:T(8,128)(2,1)}, bf16[512,128]{1,0:T(8,128)(2,1)S(1)}, u32[]{:S(2)}, u32[]{:S(2)}) collective-permute-start(bf16[512,128]{1,0:T(8,128)(2,1)} %copy-done.11), channel_id=1, source_target_pairs={{0,2},{1,3},{2,0},{3,1},{4,6},{5,7},{6,4},{7,5},{8,10},{9,11},{10,... | collective-permute-start | bytes 393224 | tf_op jit(solution)/shard_map/ppermute | solution.py:265
  74.2 9.6 %collective-permute-start.5 = (bf16[512,128]{1,0:T(8,128)(2,1)}, bf16[512,128]{1,0:T(8,128)(2,1)S(1)}, u32[]{:S(2)}, u32[]{:S(2)}) collective-permute-start(bf16[512,128]{1,0:T(8,128)(2,1)} %copy-done.10), channel_id=1, source_target_pairs={{0,3},{1,2},{2,1},{3,0},{4,7},{5,6},{6,5},{7,4},{8,11},{9,10},{10,... | collective-permute-start | bytes 393224 | tf_op jit(solution)/shard_map/ppermute | solution.py:265
  74.4 9.5 %collective-permute-start.6 = (bf16[512,128]{1,0:T(8,128)(2,1)}, bf16[512,128]{1,0:T(8,128)(2,1)S(1)}, u32[]{:S(2)}, u32[]{:S(2)}) collective-permute-start(bf16[512,128]{1,0:T(8,128)(2,1)} %copy-done.9), channel_id=1, source_target_pairs={{0,16},{1,17},{2,18},{3,19},{4,20},{5,21},{6,22},{7,23},{8,24},{9,... | collective-permute-start | bytes 393224 | tf_op jit(solution)/shard_map/ppermute | solution.py:265
  74.4 13.1 %collective-permute-start.7 = (bf16[512,128]{1,0:T(8,128)(2,1)}, bf16[512,128]{1,0:T(8,128)(2,1)S(1)}, u32[]{:S(2)}, u32[]{:S(2)}) collective-permute-start(bf16[512,128]{1,0:T(8,128)(2,1)} %copy-done.8), channel_id=1, source_target_pairs={{0,17},{1,16},{2,19},{3,18},{4,21},{5,20},{6,23},{7,22},{8,25},{9,... | collective-permute-start | bytes 393224 | tf_op jit(solution)/shard_map/ppermute | solution.py:265
  80.1 11.2 %copy-start.15 = (bf16[512,128]{1,0:T(8,128)(2,1)}, bf16[512,128]{1,0:T(8,128)(2,1)S(1)}, u32[]{:S(2)}) copy-start(bf16[512,128]{1,0:T(8,128)(2,1)S(1)} %collective-permute-done.3) | copy-start | bytes 393220
  80.1 8.4 %collective-permute-start.8 = (bf16[512,128]{1,0:T(8,128)(2,1)}, bf16[512,128]{1,0:T(8,128)(2,1)S(1)}, u32[]{:S(2)}, u32[]{:S(2)}) collective-permute-start(bf16[512,128]{1,0:T(8,128)(2,1)} %copy-done.7), channel_id=1, source_target_pairs={{0,18},{1,19},{2,16},{3,17},{4,22},{5,23},{6,20},{7,21},{8,26},{9,... | collective-permute-start | bytes 393224 | tf_op jit(solution)/shard_map/ppermute | solution.py:265
  80.6 10.7 %copy-start.16 = (bf16[512,128]{1,0:T(8,128)(2,1)}, bf16[512,128]{1,0:T(8,128)(2,1)S(1)}, u32[]{:S(2)}) copy-start(bf16[512,128]{1,0:T(8,128)(2,1)S(1)} %collective-permute-done.4) | copy-start | bytes 393220
  80.6 10.7 %collective-permute-start.9 = (bf16[512,128]{1,0:T(8,128)(2,1)}, bf16[512,128]{1,0:T(8,128)(2,1)S(1)}, u32[]{:S(2)}, u32[]{:S(2)}) collective-permute-start(bf16[512,128]{1,0:T(8,128)(2,1)} %copy-done.6), channel_id=1, source_target_pairs={{0,19},{1,18},{2,17},{3,16},{4,23},{5,22},{6,21},{7,20},{8,27},{9,... | collective-permute-start | bytes 393224 | tf_op jit(solution)/shard_map/ppermute | solution.py:265
  83.9 7.4 %copy-start.17 = (bf16[512,128]{1,0:T(8,128)(2,1)}, bf16[512,128]{1,0:T(8,128)(2,1)S(1)}, u32[]{:S(2)}) copy-start(bf16[512,128]{1,0:T(8,128)(2,1)S(1)} %collective-permute-done.5) | copy-start | bytes 393220
  83.9 7.4 %copy-start.18 = (bf16[512,128]{1,0:T(8,128)(2,1)}, bf16[512,128]{1,0:T(8,128)(2,1)S(1)}, u32[]{:S(2)}) copy-start(bf16[512,128]{1,0:T(8,128)(2,1)S(1)} %collective-permute-done.6) | copy-start | bytes 393220
  87.6 3.7 %copy-start.19 = (bf16[512,128]{1,0:T(8,128)(2,1)}, bf16[512,128]{1,0:T(8,128)(2,1)S(1)}, u32[]{:S(2)}) copy-start(bf16[512,128]{1,0:T(8,128)(2,1)S(1)} %collective-permute-done.7) | copy-start | bytes 393220
  88.4 2.9 %copy-start.20 = (bf16[512,128]{1,0:T(8,128)(2,1)}, bf16[512,128]{1,0:T(8,128)(2,1)S(1)}, u32[]{:S(2)}) copy-start(bf16[512,128]{1,0:T(8,128)(2,1)S(1)} %collective-permute-done.8) | copy-start | bytes 393220
  91.3 0.6 copy-start.21

commit v4 on v3

--- a/solution.py
+++ b/solution.py
@@ -10,6 +10,9 @@
 BLK = 128
 LOG2E = 1.4426950408889634
 STAT_ROWS = 32
+LIMIT = 56 * 1024 * 1024
+PART_LIMIT = 24 * 1024 * 1024
+SMALL_LIMIT = 6 * 1024 * 1024
 
 
 def stats_of(stats, sources, chunks):
@@ -80,30 +83,21 @@
     dkv[:, 1] = dv_acc[...].astype(jnp.bfloat16).reshape(shards, tok, 128)
 
 
-def planes_kernel(meta, pkg, *refs, rows, tok, q_blocks, scale, odd, planes):
+def planes_kernel(meta, pkg, kv, *refs, rows, tok, q_blocks, scale, odd, planes):
     halves = planes // 2
     team = pkg.shape[0]
-    near, refs = refs[:halves], refs[halves:]
     if odd:
-        dq, grads, kv, dk_acc, dv_acc, dq_acc, sems = refs
+        dq, grads, dk_acc, dv_acc, dq_acc = refs
     else:
         dq_before, refs = refs[0], refs[1:]
-        dq_out, (grads, kv, dk_acc, dv_acc, dq_acc, sems, dq, dq_sems) = refs[:team], refs[team:]
+        dq_out, (grads, dk_acc, dv_acc, dq_acc, dq, out_sems) = refs[:team], refs[team:]
     sources = BLK // tok
     wide = sources * rows
     plane, place = meta[2 * q_blocks], meta[2 * q_blocks + 1]
     team_blocks = team // 2 // sources
     range_blocks = team_blocks * planes
-    loads = [
-        pltpu.make_async_copy(near[n], kv.at[pl.ds(((plane // 2) ^ n) * team, team)], sems.at[n])
-        for n in range(halves)
-    ]
-    for copy in loads:
-        copy.start()
     dk_acc[...] = jnp.zeros_like(dk_acc)
     dv_acc[...] = jnp.zeros_like(dv_acc)
-    for copy in loads:
-        copy.wait()
 
     def over_queries(i, _):
         last, first = meta[i], meta[q_blocks + i]
@@ -117,7 +111,7 @@
             dq_acc[...] = dq_before[i]
 
         def step(j, half, masked):
-            within = (j // range_blocks) * team_blocks + j % team_blocks
+            within = lax.div(j, range_blocks) * team_blocks + lax.rem(j, team_blocks)
             block = half * (2 * team_blocks) + within
             at_shards = pl.ds(sources * block, sources)
             k = kv[at_shards, 0].reshape(BLK, 128)
@@ -129,7 +123,7 @@
             dq_acc[...] += dq_part
 
         def inner(j, _):
-            key_plane = (j % range_blocks) // team_blocks
+            key_plane = lax.div(lax.rem(j, range_blocks), team_blocks)
 
             @pl.when((key_plane ^ plane) & 1 == odd)
             def _():
@@ -147,7 +141,7 @@
 
     lax.fori_loop(0, q_blocks, over_queries, 0)
     if not odd:
-        stores = [pltpu.make_async_copy(dq.at[place ^ d], dq_out[d], dq_sems.at[d]) for d in range(team)]
+        stores = [pltpu.make_async_copy(dq.at[place ^ d], dq_out[d], out_sems.at[d]) for d in range(team)]
         for copy in stores:
             copy.start()
     for half in range(halves):
@@ -184,13 +178,14 @@
         in_specs=[SMEM, VMEM, VMEM],
         out_specs=(VMEM, VMEM),
         scratch_shapes=totals(shards, tok, rows * (BLK // tok), head_dim),
-        compiler_params=pltpu.CompilerParams(vmem_limit_bytes=56 * 1024 * 1024),
+        compiler_params=pltpu.CompilerParams(vmem_limit_bytes=LIMIT),
         name="attention_grads",
     )(meta, pkg, kv)
 
 
 def attention_part(meta, pkg, kv, dq_before, rows, scale, planes):
-    team, _, tok, head_dim = kv[0].shape
+    shards, _, tok, head_dim = kv.shape
+    team = pkg.shape[0]
     halves = planes // 2
     q_blocks = team * tok // BLK
     wide = rows * (BLK // tok)
@@ -200,46 +195,70 @@
     else:
         dq_shapes = (jax.ShapeDtypeStruct((rows, head_dim), jnp.bfloat16),) * team
     pairs = 2 * q_blocks * halves
-    anywhere = pl.BlockSpec(memory_space=pl.ANY)
     *dq, grads = pl.pallas_call(
         functools.partial(
             planes_kernel, rows=rows, tok=tok, q_blocks=q_blocks, scale=scale, odd=int(odd), planes=planes
         ),
-        out_shape=dq_shapes + (jax.ShapeDtypeStruct((halves,) + kv[0].shape, jnp.bfloat16),),
-        in_specs=[SMEM, VMEM] + [anywhere] * halves + ([] if odd else [VMEM]),
-        out_specs=((VMEM,) if odd else (anywhere,) * team) + (VMEM,),
-        scratch_shapes=[pltpu.VMEM((halves * team, 2, tok, head_dim), jnp.bfloat16)]
-        + totals(halves * team, tok, wide, head_dim)
-        + [pltpu.SemaphoreType.DMA((halves,))]
-        + ([] if odd else [pltpu.VMEM((team, rows, head_dim), jnp.bfloat16), pltpu.SemaphoreType.DMA((team,))]),
-        compiler_params=pltpu.CompilerParams(vmem_limit_bytes=32 * 1024 * 1024),
+        out_shape=dq_shapes + (jax.ShapeDtypeStruct((halves, team, 2, tok, head_dim), jnp.bfloat16),),
+        in_specs=[SMEM] + [VMEM] * (2 + (not odd)),
+        out_specs=((VMEM,) if odd else (pl.BlockSpec(memory_space=pl.ANY),) * team) + (VMEM,),
+        scratch_shapes=totals(shards, tok, wide, head_dim)
+        + (
+            []
+            if odd
+            else [pltpu.VMEM((team, rows, head_dim), jnp.bfloat16), pltpu.SemaphoreType.DMA((team,))]
+        ),
+        compiler_params=pltpu.CompilerParams(vmem_limit_bytes=PART_LIMIT),
         cost_estimate=pl.CostEstimate(
             flops=pairs * 10 * BLK * wide * head_dim,
             bytes_accessed=4 * 1024 * 1024,
             transcendentals=pairs * BLK * wide,
         ),
         name="attention_odd" if odd else "attention_even",
-    )(meta, pkg, *kv, *([] if odd else [dq_before]))
+    )(meta, pkg, kv, *([] if odd else [dq_before]))
     return (dq[0] if odd else dq), grads
 
 
-def place_kernel(place, *refs):
+def place_dq_kernel(place, *refs):
     *arrived, out = refs
     for d, block in enumerate(arrived):
         out[:, place[0] ^ d] = block[...]
 
 
-def place_blocks(place, arrived, tok):
+def place_dq(place, arrived, tok):
     rows, head_dim = arrived[0].shape
     fan = rows // tok
     out = pl.pallas_call(
-        place_kernel,
+        place_dq_kernel,
         out_shape=jax.ShapeDtypeStruct((tok, len(arrived), fan, head_dim), jnp.bfloat16),
         in_specs=[SMEM] + [VMEM] * len(arrived),
         out_specs=VMEM,
+        compiler_params=pltpu.CompilerParams(vmem_limit_bytes=SMALL_LIMIT),
         name="place_dq",
     )(place, *[x.reshape(tok, fan, head_dim) for x in arrived])
     return out.reshape(tok, len(arrived) * fan, head_dim)
+
+
+def place_dkv_kernel(parts, dk, dv, wide):
+    halves, kv_heads = parts.shape[:2]
+    for n, out in enumerate((dk, dv)):
+        for h in range(kv_heads):
+            wide[:, h, :] = sum(parts[p, h, n].astype(jnp.float32) for p in range(halves))
+        out[...] = wide[...].astype(jnp.bfloat16)
+
+
+def place_dkv(parts):
+    _, kv_heads, _, tok, head_dim = parts.shape
+    shape = (tok, kv_heads, head_dim)
+    return pl.pallas_call(
+        place_dkv_kernel,
+        out_shape=(jax.ShapeDtypeStruct(shape, jnp.bfloat16),) * 2,
+        in_specs=[VMEM],
+        out_specs=(VMEM, VMEM),
+        scratch_shapes=[pltpu.VMEM(shape, jnp.float32)],
+        compiler_params=pltpu.CompilerParams(vmem_limit_bytes=SMALL_LIMIT),
+        name="place_dkv",
+    )(parts)
 
 
 def pieces(x):
@@ -254,16 +273,11 @@
     return sum(x.astype(jnp.float32) for x in terms).astype(jnp.bfloat16)
 
 
-def exchange(blocks, slots):
+def to_member(block, d, slots):
     n_ctx, n_head = lax.axis_size("ctx"), lax.axis_size("head")
-    arrived = [blocks[0]]
-    for d in range(1, 2 * slots):
-        db, dr = divmod(d, slots)
-        moves = [
-            (c * n_head + h, (c ^ db) * n_head + (h ^ dr)) for c in range(n_ctx) for h in range(n_head)
-        ]
-        arrived.append(lax.ppermute(blocks[d], ("ctx", "head"), moves))
-    return arrived
+    db, dr = divmod(d, slots)
+    moves = [(c * n_head + h, (c ^ db) * n_head + (h ^ dr)) for c in range(n_ctx) for h in range(n_head)]
+    return lax.ppermute(block, ("ctx", "head"), moves)
 
 
 def dq_by_token(dq, tok, fan):
@@ -325,19 +339,18 @@
         kv = kv.reshape(2 * n_head, 2, tok, head_dim)
         kv = lax.all_to_all(kv, both, 0, 0, axis_index_groups=pairs, tiled=True)
 
+    def by_group(x):
+        return x.reshape(tok, kv_heads, fan, head_dim).transpose(1, 0, 2, 3).reshape(kv_heads, rows, head_dim)
+
     deltas = jnp.sum(out_grads.astype(jnp.float32) * outputs.astype(jnp.float32), axis=-1)
     stats = jnp.stack(pieces(log_norms) + pieces(deltas), axis=0)
     stats = stats.reshape(6, tok, kv_heads, fan).transpose(2, 0, 1, 3)
     stats = stats.reshape(kv_heads, 6 * rows // 128, 128)
     stats = jnp.pad(stats, ((0, 0), (0, STAT_ROWS - stats.shape[1]), (0, 0)))
-
-    def by_group(x):
-        return x.reshape(tok, kv_heads, fan, head_dim).transpose(1, 0, 2, 3).reshape(kv_heads, rows, head_dim)
-
     pkg = jnp.concatenate([by_group(queries), by_group(out_grads), stats], axis=1)
     pkg = lax.all_to_all(pkg, both, 0, 0, axis_index_groups=teams, tiled=True)
 
-    pair, plane = ctx // 2, head // slots
+    pair, plane = lax.div(ctx, 2), lax.div(head, slots)
     range_blocks = n_head * tok // BLK
     team_blocks = slots * tok // BLK
     at = jnp.stack(
@@ -346,17 +359,24 @@
     first_block = jnp.sum(block_doc[None, :] < block_doc[at][:, None], axis=1, dtype=jnp.int32)
     ranges_before = 1 if n_ctx > 2 else 0
     base = (2 * pair - ranges_before) * range_blocks
-    place = (ctx % 2) * slots + head % slots
+    place = lax.rem(ctx, 2) * slots + lax.rem(head, slots)
     meta = jnp.concatenate([at - base, first_block - base, plane[None], place[None]]).astype(jnp.int32)
 
     if by_plane:
-        dq_before, odd_grads = attention_part(meta, pkg, (kv[1], kv[3]), None, rows, scale, planes)
+        upper = plane // 2 == 1
+
+        def in_order(near, far):
+            return jnp.where(upper, jnp.concatenate([far, near]), jnp.concatenate([near, far]))
+
+        dq_before, odd_grads = attention_part(meta, pkg, in_order(kv[1], kv[3]), None, rows, scale, planes)
         arrived = across(odd_grads, 1)
-        dq, even_grads = attention_part(meta, pkg, (kv[0], kv[2]), dq_before, rows, scale, planes)
+        dq, even_grads = attention_part(meta, pkg, in_order(kv[0], kv[2]), dq_before, rows, scale, planes)
         dkv = add(arrived, even_grads).reshape(planes // 2 * kv_heads, 2, tok, head_dim)
         dkv = lax.all_to_all(dkv, both, 0, 0, axis_index_groups=alternate, tiled=True)
-        dq = place_blocks(place[None], exchange(dq, slots), tok)
-        return (dq,) + dkv_by_token(dkv.reshape(planes // 2, kv_heads, 2, tok, head_dim))
+        dq = [dq[0]] + [to_member(dq[d], d, slots) for d in range(1, kv_heads)]
+        dk, dv = place_dkv(dkv.reshape(planes // 2, kv_heads, 2, tok, head_dim))
+        dk, dv, *dq = lax.optimization_barrier((dk, dv, *dq))
+        return place_dq(place[None], dq, tok), dk, dv
 
     if ranges_before:
         prior = lax.ppermute(kv[n_head:], "ctx", [(c, c + 2) for c in range(n_ctx - 2)])

time: 97.3 us -> 93 us (0.956); the launches traced: 96.1 us -> 92.8 us
  local copies, waits for them, and re-layouts: 9.83 us -> 5.41 us
  other arithmetic: 5.7 us -> 7.77 us
  Pallas kernels: 13.4 us -> 12.1 us
  starting transfers between devices: 28.8 us -> 30.1 us
    unnamed x47 -> x21, local copies, waits for them, and re-layouts: 6.32 us -> 1.92 us
    ppermute x7, waiting for transfers between devices: 11.5 us -> 7.56 us  [to_member(): return lax.ppermute(block, ('ctx', 'head'), moves)]
    all_to_all x1, waiting for transfers between devices: 0.01 us -> 2.98 us  [per_device(): lax.all_to_all(dkv, both, 0, 0, axis_index_groups=alternate, tiled=True)]
    select_n x0 -> x2, other arithmetic: none -> 2.18 us  [in_order(): jnp.where(upper, jnp.concatenate([far, near]), jnp.concatenate([near, far]))]
    all_to_all x1, starting transfers between devices: 5.22 us -> 6.49 us  [per_device(): lax.all_to_all(dkv, both, 0, 0, axis_index_groups=alternate, tiled=True)]
    pallas_call x2, Pallas kernels: 10.9 us -> 9.81 us  [attention_part(): pl.pallas_call(functools.partial(planes_kernel, rows=rows, tok=tok, q_blo...]
    pallas_call x1 -> x2, Pallas kernels: 2.55 us -> 2.27 us  [the longest x1 1.27 us: place_dq(): pl.pallas_call(place_dq_kernel, out_shape=jax.ShapeDtypeStruct((tok, len(...]
  transfers between devices with their start and end apart: 14 -> 14, of which waited for: 12 -> 11; matrix products, arithmetic and copies ran while one was open for 7% -> 10% of each run, Pallas kernels for 10% -> 8%
where the time goes in v4:
time: 93 us; the launch traced here: 92.8 us
  waiting for transfers between devices  36.7 us (39%)
  starting transfers between devices  30.1 us (32%)
  Pallas kernels  12.1 us (13%)
  other arithmetic  7.77 us (8%)
  local copies, waits for them, and re-layouts  5.41 us (6%)
    ppermute x4, waiting for transfers between devices, across(): return lax.ppermute(x, 'head', [(h, h ^ step) for h in range(n_head)])  23.5 us
    pallas_call x2, Pallas kernels, attention_part(): pl.pallas_call(functools.partial(planes_kernel, rows=rows, tok=tok, q_blo...  9.81 us
    ppermute x7, starting transfers between devices, to_member(): return lax.ppermute(block, ('ctx', 'head'), moves)  8.86 us
    ppermute x7, waiting for transfers between devices, to_member(): return lax.ppermute(block, ('ctx', 'head'), moves)  7.56 us
    all_to_all x1, starting transfers between devices, per_device(): lax.all_to_all(dkv, both, 0, 0, axis_index_groups=alternate, tiled=True)  6.49 us
    ppermute x4, starting transfers between devices, across(): return lax.ppermute(x, 'head', [(h, h ^ step) for h in range(n_head)])  5.87 us
    all_to_all x1, starting transfers between devices, per_device(): kv = lax.all_to_all(kv, both, 0, 0, axis_index_groups=teams, tiled=True)  5.17 us
    all_to_all x1, starting transfers between devices, per_device(): pkg = lax.all_to_all(pkg, both, 0, 0, axis_index_groups=teams, tiled=True)  3.67 us
  transfers between devices with their start and end apart: 14, of which 11 were waited for; matrix products, arithmetic and copies ran while one was open for 10% of the time, Pallas kernels for 8%

profile of v4, /device:TPU:0, one launch (start us, length us, event | category | flops | bytes accessed | tf_op | source)
XLA Modules:
  0.0 92.8 jit_solution(16042003781505116470)
XLA Ops:
  0.6 0.0 copy-start
  0.6 0.0 copy-start.9
  0.7 1.2 %copy_bitcast_fusion.2 = (bf16[1,64,8,128]{3,1,0,2:T(8,128)(2,1)S(1)}, bf16[1,64,8,128]{3,1,0,2:T(8,128)(2,1)S(1)}) fusion(bf16[64,8,128]{2,1,0:T(8,128)(2,1)} %param.9, bf16[64,8,128]{2,1,0:T(8,128)(2,1)} %param.8), kind=kLoop, calls=%fused_computation.11 | loop fusion | bytes 524288 | tf_op jit(solution)/shard_map/stack | solution.py:331
  1.8 0.7 maximum_bitcast_fusion
  2.5 5.2 %all-to-all-start.1 = ((bf16[8,2,64,128]{3,2,1,0:T(8,128)(2,1)}), bf16[8,2,64,128]{3,2,1,0:T(8,128)(2,1)}, u32[]{:S(2)}, u32[]{:S(2)}) async-start(bf16[8,2,64,128]{3,2,1,0:T(8,128)(2,1)} %maximum_bitcast_fusion), calls=%async_computation.1 | async-start | bytes 524288 | tf_op jit(solution)/shard_map/all_to_all | solution.py:333
  7.7 0.8 copy.34
  8.6 0.0 copy-done.9
  8.6 1.8 %multiply_reduce_fusion = f32[64,64]{1,0:T(8,128)S(1)} fusion(bf16[64,64,128]{2,1,0:T(8,128)(2,1)} %param.10, bf16[64,64,128]{2,1,0:T(8,128)(2,1)S(1)} %copy-done.9), kind=kLoop, calls=%fused_computation.4 | loop fusion | flops 2093056 | bytes 2113536 | tf_op jit(solution)/shard_map/reduce_sum | solution.py:345
  10.4 0.1 copy.36
  10.6 0.4 copy.37
  11.0 0.8 reshape.279
  11.7 0.0 copy-done
  11.7 0.5 copy_bitcast_fusion
  12.2 1.5 %fusion.1 = bf16[8,1056,128]{2,1,0:T(8,128)(2,1)} fusion(bf16[8,24,128]{2,1,0:T(8,128)(2,1)S(1)} %reshape.279, bf16[8,512,128]{2,1,0:T(8,128)(2,1)S(1)} %get-tuple-element.51, bf16[8,512,128]{2,1,0:T(8,128)(2,1)S(1)} %get-tuple-element.52), kind=kLoop, calls=%fused_computation.3 | loop fusion | flops 8650752 | bytes 4308992 | tf_op jit(solution)/shard_map/concatenate | solution.py:350
  13.7 0.7 all-to-all-done.1
  14.4 3.7 %all-to-all-start = ((bf16[8,1056,128]{2,1,0:T(8,128)(2,1)}), bf16[8,1056,128]{2,1,0:T(8,128)(2,1)S(1)}, u32[]{:S(2)}, u32[]{:S(2)}) async-start(bf16[8,1056,128]{2,1,0:T(8,128)(2,1)} %fusion.1), calls=%async_computation | async-start | bytes 4325376 | tf_op jit(solution)/shard_map/all_to_all | solution.py:351
  18.1 2.8 %collective-permute-start = (bf16[8,2,64,128]{3,2,1,0:T(8,128)(2,1)}, bf16[8,2,64,128]{3,2,1,0:T(8,128)(2,1)}, u32[]{:S(2)}, u32[]{:S(2)}) collective-permute-start(bf16[8,2,64,128]{3,2,1,0:T(8,128)(2,1)} %all-to-all-done.1), channel_id=1, source_target_pairs={{0,8},{1,9},{2,10},{3,11},{4,12},{5,13},{6,14},{7,15},{8,0},{9,1},... | collective-permute-start | bytes 786440 | tf_op jit(solution)/shard_map/ppermute | solution.py:318
  20.9 0.1 fusion.13
  21.0 0.0 copy-done.8
  21.0 0.6 gather_fusion
  21.7 0.2 convert_reduce_fusion
  21.8 1.6 %collective-permute-start.2 = (bf16[8,2,64,128]{3,2,1,0:T(8,128)(2,1)}, bf16[8,2,64,128]{3,2,1,0:T(8,128)(2,1)S(1)}, u32[]{:S(2)}, u32[]{:S(2)}) collective-permute-start(bf16[8,2,64,128]{3,2,1,0:T(8,128)(2,1)} %all-to-all-done.1), channel_id=1, source_target_pairs={{0,4},{1,5},{2,6},{3,7},{4,0},{5,1},{6,2},{7,3},{8,12},{9,13},{10,... | collective-permute-start | bytes 786440 | tf_op jit(solution)/shard_map/ppermute | solution.py:318
  23.5 10.4 %collective-permute-done = bf16[8,2,64,128]{3,2,1,0:T(8,128)(2,1)} collective-permute-done((bf16[8,2,64,128]{3,2,1,0:T(8,128)(2,1)}, bf16[8,2,64,128]{3,2,1,0:T(8,128)(2,1)}, u32[]{:S(2)}, u32[]{:S(2)}) %collective-permute-start) | collective-permute-done | bytes 262176 | tf_op jit(solution)/shard_map/ppermute | solution.py:318
  33.9 0.7 collective-permute-start.1
  34.6 0.1 add_subtract_fusion
  34.6 0.1 pad_add_fusion.meta
  34.7 0.2 collective-permute-done.2
  35.0 7.2 %collective-permute-done.1 = bf16[8,2,64,128]{3,2,1,0:T(8,128)(2,1)S(1)} collective-permute-done((bf16[8,2,64,128]{3,2,1,0:T(8,128)(2,1)}, bf16[8,2,64,128]{3,2,1,0:T(8,128)(2,1)S(1)}, u32[]{:S(2)}, u32[]{:S(2)}) %collective-permute-start.1) | collective-permute-done | bytes 262176 | tf_op jit(solution)/shard_map/ppermute | solution.py:318
  42.1 0.9 maximum_select_fusion.kv
  43.0 1.9 %all-to-all-done.pkg = bf16[8,1056,128]{2,1,0:T(8,128)(2,1)S(1)} async-done(((bf16[8,1056,128]{2,1,0:T(8,128)(2,1)}), bf16[8,1056,128]{2,1,0:T(8,128)(2,1)S(1)}, u32[]{:S(2)}, u32[]{:S(2)}) %all-to-all-start) | async-done | bytes 2162720 | tf_op jit(solution)/shard_map/all_to_all | solution.py:351
  44.9 1.0 %copy-done.1 = bf16[16,2,64,128]{3,2,1,0:T(8,128)(2,1)S(1)} copy-done((bf16[16,2,64,128]{3,2,1,0:T(8,128)(2,1)S(1)}, bf16[16,2,64,128]{3,2,1,0:T(8,128)(2,1)}, u32[]{:S(2)}) %copy-start.1) | copy-done | bytes 524312
  45.9 3.5 %attention_odd.1 = (f32[4,1024,128]{2,1,0:T(8,128)S(1)}, bf16[2,8,2,64,128]{4,3,2,1,0:T(8,128)(2,1)S(1)}) custom-call(s32[10]{0:T(128)S(1)} %pad_add_fusion.meta, bf16[8,1056,128]{2,1,0:T(8,128)(2,1)S(1)} %all-to-all-done.pkg, bf16[16,2,64,128]{3,2,1,0:T(8,128)(2,1)S(1)} %copy-done.1), custom_call_target="tpu_custom_call" | custom-call | flops 2684354560 | bytes 4194304 | tf_op jit(solution)/shard_map/attention_odd/pallas_call | solution.py:198
  49.4 0.7 collective-permute-start.3
  50.1 1.3 %maximum_select_fusion.1.kv = bf16[16,2,64,128]{3,2,1,0:T(8,128)(2,1)S(1)} fusion(bf16[8,2,64,128]{3,2,1,0:T(8,128)(2,1)} %all-to-all-done.1, bf16[8,2,64,128]{3,2,1,0:T(8,128)(2,1)} %collective-permute-done, pred[]{:T(512)S(6)} %eq.3), kind=kLoop, calls=%fused_computation.9 | loop fusion | flops 786432 | bytes 1048577 | tf_op jit(solution)/shard_map/jit(_where)/select_n | solution.py:369
  51.4 6.3 %attention_even.1 = (bf16[512,128]{1,0:T(8,128)(2,1)S(1)}, bf16[512,128]{1,0:T(8,128)(2,1)S(1)}, bf16[512,128]{1,0:T(8,128)(2,1)S(1)}, bf16[512,128]{1,0:T(8,128...) custom-call(s32[10]{0:T(128)S(1)} %pad_add_fusion.meta, ...), custom_call_target="tpu_custom_call" | custom-call | flops 2684354560 | bytes 4194304 | tf_op jit(solution)/shard_map/attention_even/pallas_call | solution.py:198
  57.8 0.0 copy-start.2
  57.8 0.0 copy-start.3
  57.8 0.0 copy-start.4
  57.8 0.0 copy-start.5
  57.8 0.0 copy-start.6
  57.9 0.0 copy-start.7
  57.9 5.7 %collective-permute-done.3 = bf16[2,8,2,64,128]{4,3,2,1,0:T(8,128)(2,1)S(1)} collective-permute-done((bf16[2,8,2,64,128]{4,3,2,1,0:T(8,128)(2,1)S(1)}, bf16[2,8,2,64,128]{4,3,2,1,0:T(8,128)(2,1)S(1)}, u32[]{:S(2)}, u32[]{:S(2)}) %collective-permute-start.3) | collective-permute-done | bytes 524320 | tf_op jit(solution)/shard_map/ppermute | solution.py:318
  63.6 1.0 %add_convert_fusion = bf16[2,8,2,64,128]{4,3,2,1,0:T(8,128)(2,1)} fusion(bf16[2,8,2,64,128]{4,3,2,1,0:T(8,128)(2,1)S(1)} %get-tuple-element.28, bf16[2,8,2,64,128]{4,3,2,1,0:T(8,128)(2,1)S(1)} %collective-permute-done.3), kind=kLoop, calls=%fused_computation.7 | loop fusion | flops 1048576 | bytes 1572864 | tf_op jit(solution)/shard_map/convert_element_type | solution.py:273
  64.6 0.0 copy-done.2
  64.6 0.0 copy-done.3
  64.6 0.0 copy-done.4
  64.6 6.5 %all-to-all-start.2 = ((bf16[16,2,64,128]{3,2,1,0:T(8,128)(2,1)}), bf16[16,2,64,128]{3,2,1,0:T(8,128)(2,1)S(1)}, u32[]{:S(2)}, u32[]{:S(2)}) async-start(bf16[16,2,64,128]{3,2,1,0:T(8,128)(2,1)} %bitcast.25), calls=%async_computation.2 | async-start | bytes 1048576 | tf_op jit(solution)/shard_map/all_to_all | solution.py:375
  71.1 1.9 %collective-permute-start.4 = (bf16[512,128]{1,0:T(8,128)(2,1)}, bf16[512,128]{1,0:T(8,128)(2,1)S(1)}, u32[]{:S(2)}, u32[]{:S(2)}) collective-permute-start(bf16[512,128]{1,0:T(8,128)(2,1)} %copy-done.7), channel_id=1, source_target_pairs={{0,1},{1,0},{2,3},{3,2},{4,5},{5,4},{6,7},{7,6},{8,9},{9,8},{10,11... | collective-permute-start | bytes 393224 | tf_op jit(solution)/shard_map/ppermute | solution.py:280
  73.1 1.5 %collective-permute-start.5 = (bf16[512,128]{1,0:T(8,128)(2,1)}, bf16[512,128]{1,0:T(8,128)(2,1)S(1)}, u32[]{:S(2)}, u32[]{:S(2)}) collective-permute-start(bf16[512,128]{1,0:T(8,128)(2,1)} %copy-done.6), channel_id=1, source_target_pairs={{0,2},{1,3},{2,0},{3,1},{4,6},{5,7},{6,4},{7,5},{8,10},{9,11},{10,... | collective-permute-start | bytes 393224 | tf_op jit(solution)/shard_map/ppermute | solution.py:280
  74.5 0.2 collective-permute-start.6
  74.7 0.0 collective-permute-start.7
  74.7 2.0 %collective-permute-start.8 = (bf16[512,128]{1,0:T(8,128)(2,1)}, bf16[512,128]{1,0:T(8,128)(2,1)S(1)}, u32[]{:S(2)}, u32[]{:S(2)}) collective-permute-start(bf16[512,128]{1,0:T(8,128)(2,1)} %copy-done.3), channel_id=1, source_target_pairs={{0,17},{1,16},{2,19},{3,18},{4,21},{5,20},{6,23},{7,22},{8,25},{9,... | collective-permute-start | bytes 393224 | tf_op jit(solution)/shard_map/ppermute | solution.py:280
  76.7 3.7 %collective-permute-done.4 = bf16[512,128]{1,0:T(8,128)(2,1)S(1)} collective-permute-done((bf16[512,128]{1,0:T(8,128)(2,1)}, bf16[512,128]{1,0:T(8,128)(2,1)S(1)}, u32[]{:S(2)}, u32[]{:S(2)}) %collective-permute-start.4) | collective-permute-done | bytes 131104 | tf_op jit(solution)/shard_map/ppermute | solution.py:280
  80.4 0.2 collective-permute-start.9
  80.6 0.3 collective-permute-done.5
  80.9 3.1 %collective-permute-start.10 = (bf16[512,128]{1,0:T(8,128)(2,1)S(1)}, bf16[512,128]{1,0:T(8,128)(2,1)S(1)}, u32[]{:S(2)}, u32[]{:S(2)}) collective-permute-start(bf16[512,128]{1,0:T(8,128)(2,1)S(1)} %get-tuple-element.38), channel_id=1, source_target_pairs={{0,19},{1,18},{2,17},{3,16},{4,23},{5,22},{6,21},{7,20},{8,27},{9,... | collective-permute-start | bytes 393224 | tf_op jit(solution)/shard_map/ppermute | solution.py:280
  83.9 3.0 %all-to-all-done.2 = bf16[16,2,64,128]{3,2,1,0:T(8,128)(2,1)S(1)} async-done(((bf16[16,2,64,128]{3,2,1,0:T(8,128)(2,1)}), bf16[16,2,64,128]{3,2,1,0:T(8,128)(2,1)S(1)}, u32[]{:S(2)}, u32[]{:S(2)}) %all-to-all-start.2) | async-done | bytes 524320 | tf_op jit(solution)/shard_map/all_to_all | solution.py:375
  86.9 1.0 %place_dkv.1 = (bf16[64,8,128]{2,1,0:T(8,128)(2,1)}, bf16[64,8,128]{2,1,0:T(8,128)(2,1)}) custom-call(bf16[2,8,2,64,128]{4,3,2,1,0:T(8,128)(2,1)S(1)} %bitcast.71), custom_call_target="tpu_custom_call" | custom-call | tf_op jit(solution)/shard_map/place_dkv/pallas_call | solution.py:253
  87.9 0.0 collective-permute-done.6
  87.9 0.0 collective-permute-done.7
  87.9 0.0 collective-permute-done.8
  87.9 0.8 collective-permute-done.9
  88.7 2.8 %collective-permute-done.10 = bf16[512,128]{1,0:T(8,128)(2,1)S(1)} collective-permute-done((bf16[512,128]{1,0:T(8,128)(2,1)S(1)}, bf16[512,128]{1,0:T(8,128)(2,1)S(1)}, u32[]{:S(2)}, u32[]{:S(2)}) %collective-permute-start.10) | collective-permute-done | bytes 131104 | tf_op jit(solution)/shard_map/ppermute | solution.py:280
  91.5 1.3 %place_dq.1 = bf16[64,8,8,128]{3,2,1,0:T(8,128)(2,1)} custom-call(s32[1]{0:T(128)} %bitcast.place, bf16[64,8,128]{2,1,0:T(8,128)(2,1)S(1)} %bitcast.72, bf16[64,8,128]{2,1,0:T(8,128)(2,1)S(1)} %bitcast.73, bf16[64,8,128]{2,1,0:T(8,128)(2,1)S(1)} %bitcast.74, bf16[64,8,128]{2,1,0:T(8,128)(2,1)S(1)} %bitcast.75, bf16[64,8,128]{2,1,0:T(8,128)(2,1)S(1)} %bitcast.76, ...), custom_call_target="tpu_custom_call" | custom-call | tf_op jit(solution)/shard_map/place_dq/pallas_call | solution.py:231
  (12 shorter events, 0.1 us)
Async XLA Ops:
  0.6 11.1 %copy-start = (bf16[64,64,128]{2,1,0:T(8,128)(2,1)S(1)}, bf16[64,64,128]{2,1,0:T(8,128)(2,1)}, u32[]{:S(2)}) copy-start(bf16[64,64,128]{2,1,0:T(8,128)(2,1)} %param.7) | copy-start | bytes 3145732
  0.6 7.9 %copy-start.9 = (bf16[64,64,128]{2,1,0:T(8,128)(2,1)S(1)}, bf16[64,64,128]{2,1,0:T(8,128)(2,1)}, u32[]{:S(2)}) copy-start(bf16[64,64,128]{2,1,0:T(8,128)(2,1)} %param.11) | copy-start | bytes 3145732
  2.5 11.9 %all-to-all-start.1 = ((bf16[8,2,64,128]{3,2,1,0:T(8,128)(2,1)}), bf16[8,2,64,128]{3,2,1,0:T(8,128)(2,1)}, u32[]{:S(2)}, u32[]{:S(2)}) async-start(bf16[8,2,64,128]{3,2,1,0:T(8,128)(2,1)} %maximum_bitcast_fusion), calls=%async_computation.1 | async-start | bytes 524288 | tf_op jit(solution)/shard_map/all_to_all | solution.py:333
  13.7 7.3 %copy-start.8 = (s32[16]{0:T(128)S(1)}, s32[16]{0:T(128)}, u32[]{:S(2)}) copy-start(s32[16]{0:T(128)} %param.13) | copy-start | bytes 196
  14.4 30.5 %all-to-all-start = ((bf16[8,1056,128]{2,1,0:T(8,128)(2,1)}), bf16[8,1056,128]{2,1,0:T(8,128)(2,1)S(1)}, u32[]{:S(2)}, u32[]{:S(2)}) async-start(bf16[8,1056,128]{2,1,0:T(8,128)(2,1)} %fusion.1), calls=%async_computation | async-start | bytes 4325376 | tf_op jit(solution)/shard_map/all_to_all | solution.py:351
  18.1 15.8 %collective-permute-start = (bf16[8,2,64,128]{3,2,1,0:T(8,128)(2,1)}, bf16[8,2,64,128]{3,2,1,0:T(8,128)(2,1)}, u32[]{:S(2)}, u32[]{:S(2)}) collective-permute-start(bf16[8,2,64,128]{3,2,1,0:T(8,128)(2,1)} %all-to-all-done.1), channel_id=1, source_target_pairs={{0,8},{1,9},{2,10},{3,11},{4,12},{5,13},{6,14},{7,15},{8,0},{9,1},... | collective-permute-start | bytes 786440 | tf_op jit(solution)/shard_map/ppermute | solution.py:318
  21.8 13.1 %collective-permute-start.2 = (bf16[8,2,64,128]{3,2,1,0:T(8,128)(2,1)}, bf16[8,2,64,128]{3,2,1,0:T(8,128)(2,1)S(1)}, u32[]{:S(2)}, u32[]{:S(2)}) collective-permute-start(bf16[8,2,64,128]{3,2,1,0:T(8,128)(2,1)} %all-to-all-done.1), channel_id=1, source_target_pairs={{0,4},{1,5},{2,6},{3,7},{4,0},{5,1},{6,2},{7,3},{8,12},{9,13},{10,... | collective-permute-start | bytes 786440 | tf_op jit(solution)/shard_map/ppermute | solution.py:318
  33.9 8.2 %collective-permute-start.1 = (bf16[8,2,64,128]{3,2,1,0:T(8,128)(2,1)}, bf16[8,2,64,128]{3,2,1,0:T(8,128)(2,1)S(1)}, u32[]{:S(2)}, u32[]{:S(2)}) collective-permute-start(bf16[8,2,64,128]{3,2,1,0:T(8,128)(2,1)} %collective-permute-done), channel_id=1, source_target_pairs={{0,4},{1,5},{2,6},{3,7},{4,0},{5,1},{6,2},{7,3},{8,12},{9,13},{10,... | collective-permute-start | bytes 786440 | tf_op jit(solution)/shard_map/ppermute | solution.py:318
  44.9 1.0 %copy-start.1 = (bf16[16,2,64,128]{3,2,1,0:T(8,128)(2,1)S(1)}, bf16[16,2,64,128]{3,2,1,0:T(8,128)(2,1)}, u32[]{:S(2)}) copy-start(bf16[16,2,64,128]{3,2,1,0:T(8,128)(2,1)} %maximum_select_fusion.kv) | copy-start | bytes 1572868
  49.4 14.2 %collective-permute-start.3 = (bf16[2,8,2,64,128]{4,3,2,1,0:T(8,128)(2,1)S(1)}, bf16[2,8,2,64,128]{4,3,2,1,0:T(8,128)(2,1)S(1)}, u32[]{:S(2)}, u32[]{:S(2)}) collective-permute-start(bf16[2,8,2,64,128]{4,3,2,1,0:T(8,128)(2,1)S(1)} %get-tuple-element.26), channel_id=1, source_target_pairs={{0,4},{1,5},{2,6},{3,7},{4,0},{5,1},{6,2},{7,3},{8,12},{9,13},{10,... | collective-permute-start | bytes 1572872 | tf_op jit(solution)/shard_map/ppermute | solution.py:318
  57.8 6.8 %copy-start.2 = (bf16[512,128]{1,0:T(8,128)(2,1)}, bf16[512,128]{1,0:T(8,128)(2,1)S(1)}, u32[]{:S(2)}) copy-start(bf16[512,128]{1,0:T(8,128)(2,1)S(1)} %get-tuple-element.37) | copy-start | bytes 393220
  57.8 6.8 %copy-start.3 = (bf16[512,128]{1,0:T(8,128)(2,1)}, bf16[512,128]{1,0:T(8,128)(2,1)S(1)}, u32[]{:S(2)}) copy-start(bf16[512,128]{1,0:T(8,128)(2,1)S(1)} %get-tuple-element.36) | copy-start | bytes 393220
  57.8 6.8 %copy-start.4 = (bf16[512,128]{1,0:T(8,128)(2,1)}, bf16[512,128]{1,0:T(8,128)(2,1)S(1)}, u32[]{:S(2)}) copy-start(bf16[512,128]{1,0:T(8,128)(2,1)S(1)} %get-tuple-element.35) | copy-start | bytes 393220
  57.8 6.8 %copy-start.5 = (bf16[512,128]{1,0:T(8,128)(2,1)}, bf16[512,128]{1,0:T(8,128)(2,1)S(1)}, u32[]{:S(2)}) copy-start(bf16[512,128]{1,0:T(8,128)(2,1)S(1)} %get-tuple-element.34) | copy-start | bytes 393220
  57.8 6.8 %copy-start.6 = (bf16[512,128]{1,0:T(8,128)(2,1)}, bf16[512,128]{1,0:T(8,128)(2,1)S(1)}, u32[]{:S(2)}) copy-start(bf16[512,128]{1,0:T(8,128)(2,1)S(1)} %get-tuple-element.33) | copy-start | bytes 393220
  57.9 6.8 %copy-start.7 = (bf16[512,128]{1,0:T(8,128)(2,1)}, bf16[512,128]{1,0:T(8,128)(2,1)S(1)}, u32[]{:S(2)}) copy-start(bf16[512,128]{1,0:T(8,128)(2,1)S(1)} %get-tuple-element.32) | copy-start | bytes 393220
  64.6 22.3 %all-to-all-start.2 = ((bf16[16,2,64,128]{3,2,1,0:T(8,128)(2,1)}), bf16[16,2,64,128]{3,2,1,0:T(8,128)(2,1)S(1)}, u32[]{:S(2)}, u32[]{:S(2)}) async-start(bf16[16,2,64,128]{3,2,1,0:T(8,128)(2,1)} %bitcast.25), calls=%async_computation.2 | async-start | bytes 1048576 | tf_op jit(solution)/shard_map/all_to_all | solution.py:375
  71.1 9.2 %collective-permute-start.4 = (bf16[512,128]{1,0:T(8,128)(2,1)}, bf16[512,128]{1,0:T(8,128)(2,1)S(1)}, u32[]{:S(2)}, u32[]{:S(2)}) collective-permute-start(bf16[512,128]{1,0:T(8,128)(2,1)} %copy-done.7), channel_id=1, source_target_pairs={{0,1},{1,0},{2,3},{3,2},{4,5},{5,4},{6,7},{7,6},{8,9},{9,8},{10,11... | collective-permute-start | bytes 393224 | tf_op jit(solution)/shard_map/ppermute | solution.py:280
  73.1 7.8 %collective-permute-start.5 = (bf16[512,128]{1,0:T(8,128)(2,1)}, bf16[512,128]{1,0:T(8,128)(2,1)S(1)}, u32[]{:S(2)}, u32[]{:S(2)}) collective-permute-start(bf16[512,128]{1,0:T(8,128)(2,1)} %copy-done.6), channel_id=1, source_target_pairs={{0,2},{1,3},{2,0},{3,1},{4,6},{5,7},{6,4},{7,5},{8,10},{9,11},{10,... | collective-permute-start | bytes 393224 | tf_op jit(solution)/shard_map/ppermute | solution.py:280
  74.5 13.4 %collective-permute-start.6 = (bf16[512,128]{1,0:T(8,128)(2,1)}, bf16[512,128]{1,0:T(8,128)(2,1)S(1)}, u32[]{:S(2)}, u32[]{:S(2)}) collective-permute-start(bf16[512,128]{1,0:T(8,128)(2,1)} %copy-done.5), channel_id=1, source_target_pairs={{0,3},{1,2},{2,1},{3,0},{4,7},{5,6},{6,5},{7,4},{8,11},{9,10},{10,... | collective-permute-start | bytes 393224 | tf_op jit(solution)/shard_map/ppermute | solution.py:280
  74.7 13.2 %collective-permute-start.7 = (bf16[512,128]{1,0:T(8,128)(2,1)}, bf16[512,128]{1,0:T(8,128)(2,1)S(1)}, u32[]{:S(2)}, u32[]{:S(2)}) collective-permute-start(bf16[512,128]{1,0:T(8,128)(2,1)} %copy-done.4), channel_id=1, source_target_pairs={{0,16},{1,17},{2,18},{3,19},{4,20},{5,21},{6,22},{7,23},{8,24},{9,... | collective-permute-start | bytes 393224 | tf_op jit(solution)/shard_map/ppermute | solution.py:280
  74.7 13.2 %collective-permute-start.8 = (bf16[512,128]{1,0:T(8,128)(2,1)}, bf16[512,128]{1,0:T(8,128)(2,1)S(1)}, u32[]{:S(2)}, u32[]{:S(2)}) collective-permute-start(bf16[512,128]{1,0:T(8,128)(2,1)} %copy-done.3), channel_id=1, source_target_pairs={{0,17},{1,16},{2,19},{3,18},{4,21},{5,20},{6,23},{7,22},{8,25},{9,... | collective-permute-start | bytes 393224 | tf_op jit(solution)/shard_map/ppermute | solution.py:280
  80.4 8.4 %collective-permute-start.9 = (bf16[512,128]{1,0:T(8,128)(2,1)}, bf16[512,128]{1,0:T(8,128)(2,1)S(1)}, u32[]{:S(2)}, u32[]{:S(2)}) collective-permute-start(bf16[512,128]{1,0:T(8,128)(2,1)} %copy-done.2), channel_id=1, source_target_pairs={{0,18},{1,19},{2,16},{3,17},{4,22},{5,23},{6,20},{7,21},{8,26},{9,... | collective-permute-start | bytes 393224 | tf_op jit(solution)/shard_map/ppermute | solution.py:280
  80.9 10.7 %collective-permute-start.10 = (bf16[512,128]{1,0:T(8,128)(2,1)S(1)}, bf16[512,128]{1,0:T(8,128)(2,1)S(1)}, u32[]{:S(2)}, u32[]{:S(2)}) collective-permute-start(bf16[512,128]{1,0:T(8,128)(2,1)S(1)} %get-tuple-element.38), channel_id=1, source_target_pairs={{0,19},{1,18},{2,17},{3,16},{4,23},{5,22},{6,21},{7,20},{8,27},{9,... | collective-permute-start | bytes 393224 | tf_op jit(solution)/shard_map/ppermute | solution.py:280

commit v5 on v4

--- a/solution.py
+++ b/solution.py
@@ -11,7 +11,7 @@
 LOG2E = 1.4426950408889634
 STAT_ROWS = 32
 LIMIT = 56 * 1024 * 1024
-PART_LIMIT = 24 * 1024 * 1024
+PART_LIMIT = 12 * 1024 * 1024
 SMALL_LIMIT = 6 * 1024 * 1024
 
 
@@ -30,13 +30,15 @@
     return lse * LOG2E, delta
 
 
-def block_pair(q, g, lse, delta, k, v, group, scale, masked):
+def block_pair(q, g, lse, delta, k, v, group, scale, mask):
     s = lax.dot_general(k, q, (((1,), (1,)), ((), ())), preferred_element_type=jnp.float32)
     p = jnp.exp2(s * (scale * LOG2E) - lse)
-    if masked:
+    if mask is True:
         key_at = lax.broadcasted_iota(jnp.int32, p.shape, 0)
         query_at = lax.broadcasted_iota(jnp.int32, p.shape, 1) // group
         p = jnp.where(query_at >= key_at, p, 0.0)
+    elif mask is not None:
+        p = jnp.where(mask, p, 0.0)
     dp = lax.dot_general(v, g, (((1,), (1,)), ((), ())), preferred_element_type=jnp.float32)
     ds = (p * (dp - delta)).astype(jnp.bfloat16)
     dv = jnp.dot(p.astype(jnp.bfloat16), g, preferred_element_type=jnp.float32)
@@ -62,7 +64,7 @@
         def step(j, masked):
             k = kv[pl.ds(sources * j, sources), 0].reshape(BLK, 128)
             v = kv[pl.ds(sources * j, sources), 1].reshape(BLK, 128)
-            dq_part, dk, dv = block_pair(q, g, lse, delta, k, v, rows // tok, scale, masked)
+            dq_part, dk, dv = block_pair(q, g, lse, delta, k, v, rows // tok, scale, masked or None)
             at = pl.ds(pl.multiple_of(j * BLK, BLK), BLK)
             dv_acc[at, :] += dv
             dk_acc[at, :] += dk
@@ -83,74 +85,135 @@
     dkv[:, 1] = dv_acc[...].astype(jnp.bfloat16).reshape(shards, tok, 128)
 
 
-def planes_kernel(meta, pkg, kv, *refs, rows, tok, q_blocks, scale, odd, planes):
-    halves = planes // 2
+def planes_kernel(meta, pkg, *refs, rows, tok, q_blocks, scale, distances, planes):
     team = pkg.shape[0]
-    if odd:
-        dq, grads, dk_acc, dv_acc, dq_acc = refs
-    else:
+    slots = team // 2
+    count = len(distances)
+    starts, ends = planes - 1 in distances, 0 in distances
+    near, refs = refs[:count], refs[count:]
+    if not starts:
         dq_before, refs = refs[0], refs[1:]
-        dq_out, (grads, dk_acc, dv_acc, dq_acc, dq, out_sems) = refs[:team], refs[team:]
+    outs = slots if ends else 1
+    dq_out, grads_out, refs = refs[:outs], refs[outs : outs + count], refs[outs + count :]
+    kv, grads, dk_acc, dv_acc, dq_acc, lse, delta, kv_sems, grad_sems = refs[:9]
+    if ends:
+        dq, out_sems = refs[9:]
     sources = BLK // tok
     wide = sources * rows
-    plane, place = meta[2 * q_blocks], meta[2 * q_blocks + 1]
-    team_blocks = team // 2 // sources
-    range_blocks = team_blocks * planes
+    group = rows // tok
+    plane, slot = meta[2 * q_blocks], meta[2 * q_blocks + 1]
+    range_blocks = 2 * planes
+    loads = [pltpu.make_async_copy(near[n], kv.at[n], kv_sems.at[n]) for n in range(count)]
+    for copy in loads:
+        copy.start()
     dk_acc[...] = jnp.zeros_like(dk_acc)
     dv_acc[...] = jnp.zeros_like(dv_acc)
-
-    def over_queries(i, _):
-        last, first = meta[i], meta[q_blocks + i]
-        mine = pl.ds(sources * i, sources)
-        q = pkg[mine, 0:rows, :].reshape(wide, 128)
-        g = pkg[mine, rows : 2 * rows, :].reshape(wide, 128)
-        lse, delta = stats_of(pkg[mine, 2 * rows :, :], sources, rows // 128)
-        if odd:
-            dq_acc[...] = jnp.zeros_like(dq_acc)
-        else:
-            dq_acc[...] = dq_before[i]
-
-        def step(j, half, masked):
-            within = lax.div(j, range_blocks) * team_blocks + lax.rem(j, team_blocks)
-            block = half * (2 * team_blocks) + within
-            at_shards = pl.ds(sources * block, sources)
-            k = kv[at_shards, 0].reshape(BLK, 128)
-            v = kv[at_shards, 1].reshape(BLK, 128)
-            dq_part, dk, dv = block_pair(q, g, lse, delta, k, v, rows // tok, scale, masked)
-            at = pl.ds(pl.multiple_of(block * BLK, BLK), BLK)
-            dv_acc[at, :] += dv
-            dk_acc[at, :] += dk
-            dq_acc[...] += dq_part
-
-        def inner(j, _):
-            key_plane = lax.div(lax.rem(j, range_blocks), team_blocks)
-
-            @pl.when((key_plane ^ plane) & 1 == odd)
+    for copy in loads:
+        copy.wait()
+
+    def over_range(r, _):
+        lasts = [meta[2 * r + x] for x in range(2)]
+        firsts = [meta[q_blocks + 2 * r + x] for x in range(2)]
+        for x in range(2):
+            stats = pkg[pl.ds(sources * (2 * r + x), sources), 2 * rows :, :]
+            lse[x], delta[x] = stats_of(stats, sources, rows // 128)
+            dq_acc[x] = jnp.zeros_like(dq_acc[x]) if starts else dq_before[2 * r + x]
+
+        def queries(x):
+            mine = pl.ds(sources * (2 * r + x), sources)
+            q = pkg[mine, 0:rows, :].reshape(wide, 128)
+            g = pkg[mine, rows : 2 * rows, :].reshape(wide, 128)
+            return q, g, lse[x], delta[x]
+
+        def keys(n, block, blocks):
+            at = pl.ds(sources * block, sources * blocks)
+            return kv[n, at, 0].reshape(blocks * BLK, 128), kv[n, at, 1].reshape(blocks * BLK, 128)
+
+        def add_keys(n, block, dk, dv):
+            at = pl.ds(pl.multiple_of(block * BLK, BLK), dk.shape[0])
+            dk_acc[n, at, :] += dk
+            dv_acc[n, at, :] += dv
+
+        def both(n, half):
+            k, v = keys(n, 2 * half, 2)
+            parts = [block_pair(*queries(x), k, v, group, scale, None) for x in range(2)]
+            for x in range(2):
+                dq_acc[x] += parts[x][0]
+            add_keys(n, 2 * half, parts[0][1] + parts[1][1], parts[0][2] + parts[1][2])
+
+        def one(x, n, block):
+            dq_part, dk, dv = block_pair(*queries(x), *keys(n, block, 1), group, scale, None)
+            dq_acc[x] += dq_part
+            add_keys(n, block, dk, dv)
+
+        def inner(t, _):
+            half, n = lax.div(t, count), lax.rem(t, count)
+            base = half * range_blocks + 2 * ((n + distances[0]) ^ plane)
+            seen = [
+                [(base + y >= firsts[x]) & (base + y <= lasts[x]) for y in range(2)] for x in range(2)
+            ]
+            every = seen[0][0] & seen[0][1] & seen[1][0] & seen[1][1]
+            if ends:
+                own = base == lasts[0]
+                every = every & jnp.logical_not(own)
+
+            @pl.when(every)
             def _():
-                step(j, key_plane // 2, False)
-
+                both(n, half)
+
+            for y in range(2):
+                some = [seen[x][y] & jnp.logical_not(every) for x in range(2)]
+                if ends:
+                    some = [z & jnp.logical_not(own) for z in some]
+
+                def single(x, _, y=y, some=some):
+                    @pl.when(jnp.where(x == 0, some[0], some[1]))
+                    def _():
+                        one(x, n, 2 * half + y)
+
+                    return 0
+
+                lax.fori_loop(0, 2, single, 0)
             return 0
 
-        lax.fori_loop(first, last, inner, 0)
-        if odd:
-            dq[i] = dq_acc[...]
-        else:
-            step(last, plane // 2, True)
-            dq[mine] = (dq_acc[...] * scale).astype(jnp.bfloat16).reshape(sources, rows, 128)
+        lax.fori_loop(0, (r + 1) * count, inner, 0)
+        if ends:
+            n = distances.index(0)
+            lower = [keys(n, 2 * r + y, 1) for y in range(2)]
+            first_dq, dk, dv = block_pair(*queries(0), *lower[0], group, scale, True)
+            cross = block_pair(*queries(1), *lower[0], group, scale, firsts[1] <= lasts[0])
+            last_dq, dk_1, dv_1 = block_pair(*queries(1), *lower[1], group, scale, True)
+            dq_acc[0] += first_dq
+            dq_acc[1] += cross[0] + last_dq
+            add_keys(n, 2 * r, dk + cross[1], dv + cross[2])
+            add_keys(n, 2 * r + 1, dk_1, dv_1)
+        for x in range(2):
+            if ends:
+                done = (dq_acc[x] * scale).astype(jnp.bfloat16).reshape(sources, rows, 128)
+                dq[pl.ds(sources * (2 * r + x), sources)] = done
+            else:
+                dq_out[0][2 * r + x] = dq_acc[x]
         return 0
 
-    lax.fori_loop(0, q_blocks, over_queries, 0)
-    if not odd:
-        stores = [pltpu.make_async_copy(dq.at[place ^ d], dq_out[d], out_sems.at[d]) for d in range(team)]
+    lax.fori_loop(0, 2, over_range, 0)
+    if ends:
+        stores = [
+            pltpu.make_async_copy(dq.at[b * slots + (slot ^ d)], dq_out[d].at[b], out_sems.at[b, d])
+            for b in range(2)
+            for d in range(slots)
+        ]
         for copy in stores:
             copy.start()
-    for half in range(halves):
-        at = pl.ds(half * team * tok, team * tok)
-        grads[half, :, 0] = (dk_acc[at, :] * scale).astype(jnp.bfloat16).reshape(team, tok, 128)
-        grads[half, :, 1] = dv_acc[at, :].astype(jnp.bfloat16).reshape(team, tok, 128)
-    if not odd:
+    grad_stores = [pltpu.make_async_copy(grads.at[n], grads_out[n], grad_sems.at[n]) for n in range(count)]
+    for n in reversed(range(count)):
+        grads[n, :, 0] = (dk_acc[n] * scale).astype(jnp.bfloat16).reshape(team, tok, 128)
+        grads[n, :, 1] = dv_acc[n].astype(jnp.bfloat16).reshape(team, tok, 128)
+        grad_stores[n].start()
+    if ends:
         for copy in stores:
             copy.wait()
+    for copy in grad_stores:
+        copy.wait()
 
 
 VMEM = pl.BlockSpec(memory_space=pltpu.VMEM)
@@ -183,60 +246,75 @@
     )(meta, pkg, kv)
 
 
-def attention_part(meta, pkg, kv, dq_before, rows, scale, planes):
-    shards, _, tok, head_dim = kv.shape
-    team = pkg.shape[0]
-    halves = planes // 2
+def attention_part(meta, pkg, kv, distances, dq_before, rows, scale, planes):
+    team, _, tok, head_dim = kv[0].shape
+    slots = team // 2
+    count = len(distances)
     q_blocks = team * tok // BLK
     wide = rows * (BLK // tok)
-    odd = dq_before is None
-    if odd:
+    scratch = [
+        pltpu.VMEM((count,) + kv[0].shape, jnp.bfloat16),
+        pltpu.VMEM((count,) + kv[0].shape, jnp.bfloat16),
+        pltpu.VMEM((count, team * tok, head_dim), jnp.float32),
+        pltpu.VMEM((count, team * tok, head_dim), jnp.float32),
+        pltpu.VMEM((2, wide, head_dim), jnp.float32),
+        pltpu.VMEM((2, 1, wide), jnp.float32),
+        pltpu.VMEM((2, 1, wide), jnp.float32),
+        pltpu.SemaphoreType.DMA((count,)),
+        pltpu.SemaphoreType.DMA((count,)),
+    ]
+    hbm = pl.BlockSpec(memory_space=pltpu.HBM)
+    ends = 0 in distances
+    if ends:
+        dq_shapes = (jax.ShapeDtypeStruct((2, rows, head_dim), jnp.bfloat16),) * slots
+        dq_specs = (hbm,) * slots
+        scratch += [pltpu.VMEM((team, rows, head_dim), jnp.bfloat16), pltpu.SemaphoreType.DMA((2, slots))]
+    else:
         dq_shapes = (jax.ShapeDtypeStruct((q_blocks, wide, head_dim), jnp.float32),)
-    else:
-        dq_shapes = (jax.ShapeDtypeStruct((rows, head_dim), jnp.bfloat16),) * team
-    pairs = 2 * q_blocks * halves
-    *dq, grads = pl.pallas_call(
+        dq_specs = (VMEM,)
+    before = [] if dq_before is None else [dq_before]
+    pairs = q_blocks * count
+    out = pl.pallas_call(
         functools.partial(
-            planes_kernel, rows=rows, tok=tok, q_blocks=q_blocks, scale=scale, odd=int(odd), planes=planes
+            planes_kernel, rows=rows, tok=tok, q_blocks=q_blocks, scale=scale, distances=distances, planes=planes
         ),
-        out_shape=dq_shapes + (jax.ShapeDtypeStruct((halves, team, 2, tok, head_dim), jnp.bfloat16),),
-        in_specs=[SMEM] + [VMEM] * (2 + (not odd)),
-        out_specs=((VMEM,) if odd else (pl.BlockSpec(memory_space=pl.ANY),) * team) + (VMEM,),
-        scratch_shapes=totals(shards, tok, wide, head_dim)
-        + (
-            []
-            if odd
-            else [pltpu.VMEM((team, rows, head_dim), jnp.bfloat16), pltpu.SemaphoreType.DMA((team,))]
-        ),
+        out_shape=dq_shapes + (jax.ShapeDtypeStruct(kv[0].shape, jnp.bfloat16),) * count,
+        in_specs=[SMEM, VMEM] + [hbm] * count + [VMEM] * len(before),
+        out_specs=dq_specs + (hbm,) * count,
+        scratch_shapes=scratch,
         compiler_params=pltpu.CompilerParams(vmem_limit_bytes=PART_LIMIT),
         cost_estimate=pl.CostEstimate(
             flops=pairs * 10 * BLK * wide * head_dim,
             bytes_accessed=4 * 1024 * 1024,
             transcendentals=pairs * BLK * wide,
         ),
-        name="attention_odd" if odd else "attention_even",
-    )(meta, pkg, kv, *([] if odd else [dq_before]))
-    return (dq[0] if odd else dq), grads
+        name="attention_" + "_".join(str(d) for d in distances),
+    )(meta, pkg, *kv, *before)
+    dq, grads = out[:-count], out[-count:]
+    return (dq if ends else dq[0]), grads
 
 
 def place_dq_kernel(place, *refs):
-    *arrived, out = refs
-    for d, block in enumerate(arrived):
-        out[:, place[0] ^ d] = block[...]
-
-
-def place_dq(place, arrived, tok):
-    rows, head_dim = arrived[0].shape
+    *arrived, swapped, out = refs
+    slots = len(arrived)
+    core, slot = place[0], place[1]
+    for d, blocks in enumerate(arrived):
+        out[:, core * slots + (slot ^ d)] = blocks[core]
+        out[:, (1 - core) * slots + (slot ^ d)] = swapped[d]
+
+
+def place_dq(place, arrived, swapped, tok):
+    slots, rows, head_dim = swapped.shape
     fan = rows // tok
     out = pl.pallas_call(
         place_dq_kernel,
-        out_shape=jax.ShapeDtypeStruct((tok, len(arrived), fan, head_dim), jnp.bfloat16),
-        in_specs=[SMEM] + [VMEM] * len(arrived),
+        out_shape=jax.ShapeDtypeStruct((tok, 2 * slots, fan, head_dim), jnp.bfloat16),
+        in_specs=[SMEM] + [VMEM] * (slots + 1),
         out_specs=VMEM,
         compiler_params=pltpu.CompilerParams(vmem_limit_bytes=SMALL_LIMIT),
         name="place_dq",
-    )(place, *[x.reshape(tok, fan, head_dim) for x in arrived])
-    return out.reshape(tok, len(arrived) * fan, head_dim)
+    )(place, *[x.reshape(2, tok, fan, head_dim) for x in arrived], swapped.reshape(slots, tok, fan, head_dim))
+    return out.reshape(tok, 2 * slots * fan, head_dim)
 
 
 def place_dkv_kernel(parts, dk, dv, wide):
@@ -250,7 +328,7 @@
 def place_dkv(parts):
     _, kv_heads, _, tok, head_dim = parts.shape
     shape = (tok, kv_heads, head_dim)
-    return pl.pallas_call(
+    dk, dv = pl.pallas_call(
         place_dkv_kernel,
         out_shape=(jax.ShapeDtypeStruct(shape, jnp.bfloat16),) * 2,
         in_specs=[VMEM],
@@ -259,6 +337,7 @@
         compiler_params=pltpu.CompilerParams(vmem_limit_bytes=SMALL_LIMIT),
         name="place_dkv",
     )(parts)
+    return dk, dv
 
 
 def pieces(x):
@@ -271,13 +350,6 @@
 
 def add(*terms):
     return sum(x.astype(jnp.float32) for x in terms).astype(jnp.bfloat16)
-
-
-def to_member(block, d, slots):
-    n_ctx, n_head = lax.axis_size("ctx"), lax.axis_size("head")
-    db, dr = divmod(d, slots)
-    moves = [(c * n_head + h, (c ^ db) * n_head + (h ^ dr)) for c in range(n_ctx) for h in range(n_head)]
-    return lax.ppermute(block, ("ctx", "head"), moves)
 
 
 def dq_by_token(dq, tok, fan):
@@ -311,22 +383,11 @@
         for c in range(n_ctx // 2)
     ]
 
-    by_plane = n_ctx == 2 and planes == 4
+    by_plane = n_ctx == 2 and planes == 4 and slots * tok == 2 * BLK
 
     def across(x, distance):
         step = distance * slots
         return lax.ppermute(x, "head", [(h, h ^ step) for h in range(n_head)])
-
-    alternate = [
-        [
-            (2 * c + b) * n_head + z * slots + r
-            for z in range(parity, planes, 2)
-            for b in range(2)
-            for r in range(slots)
-        ]
-        for c in range(n_ctx // 2)
-        for parity in range(2)
-    ]
 
     kv = jnp.stack([keys, values], axis=0).transpose(2, 0, 1, 3)
     if by_plane:
@@ -359,24 +420,30 @@
     first_block = jnp.sum(block_doc[None, :] < block_doc[at][:, None], axis=1, dtype=jnp.int32)
     ranges_before = 1 if n_ctx > 2 else 0
     base = (2 * pair - ranges_before) * range_blocks
-    place = lax.rem(ctx, 2) * slots + lax.rem(head, slots)
-    meta = jnp.concatenate([at - base, first_block - base, plane[None], place[None]]).astype(jnp.int32)
+    meta = jnp.concatenate([at - base, first_block - base, plane[None], lax.rem(head, slots)[None]]).astype(jnp.int32)
 
     if by_plane:
-        upper = plane // 2 == 1
-
-        def in_order(near, far):
-            return jnp.where(upper, jnp.concatenate([far, near]), jnp.concatenate([near, far]))
-
-        dq_before, odd_grads = attention_part(meta, pkg, in_order(kv[1], kv[3]), None, rows, scale, planes)
-        arrived = across(odd_grads, 1)
-        dq, even_grads = attention_part(meta, pkg, in_order(kv[0], kv[2]), dq_before, rows, scale, planes)
-        dkv = add(arrived, even_grads).reshape(planes // 2 * kv_heads, 2, tok, head_dim)
-        dkv = lax.all_to_all(dkv, both, 0, 0, axis_index_groups=alternate, tiled=True)
-        dq = [dq[0]] + [to_member(dq[d], d, slots) for d in range(1, kv_heads)]
-        dk, dv = place_dkv(dkv.reshape(planes // 2, kv_heads, 2, tok, head_dim))
-        dk, dv, *dq = lax.optimization_barrier((dk, dv, *dq))
-        return place_dq(place[None], dq, tok), dk, dv
+        def part(distances, dq_before):
+            return attention_part(
+                meta, pkg, [kv[d] for d in distances], distances, dq_before, rows, scale, planes
+            )
+
+        dq, (grads_3,) = part((3,), None)
+        relayed = across(grads_3, 1)
+        dq, (grads_0, grads_1, grads_2) = part((0, 1, 2), dq)
+        far = add(grads_2, relayed)
+        far, *dq = lax.optimization_barrier((far, *dq))
+        far = across(far, 2)
+        close = across(grads_1, 1)
+        dq = [lax.ppermute(x, "head", [(h, h ^ d) for h in range(n_head)]) if d else x for d, x in enumerate(dq)]
+        dkv = add(grads_0, close, far)
+        dkv, *dq = lax.optimization_barrier((dkv, *dq))
+        dkv = lax.all_to_all(dkv, both, 0, 0, axis_index_groups=teams, tiled=True)
+        other = jnp.where(ctx == 0, jnp.stack([x[1] for x in dq]), jnp.stack([x[0] for x in dq]))
+        swapped = lax.ppermute(other, "ctx", [(0, 1), (1, 0)])
+        dq = place_dq(jnp.stack([ctx, lax.rem(head, slots)]), dq, swapped, tok)
+        dkv, dq = lax.optimization_barrier((dkv, dq))
+        return (dq,) + place_dkv(dkv[None])
 
     if ranges_before:
         prior = lax.ppermute(kv[n_head:], "ctx", [(c, c + 2) for c in range(n_ctx - 2)])

time: 93 us -> 89.4 us (0.961)
  waiting for transfers between devices: 36.7 us -> 34.9 us
  starting transfers between devices: 30.1 us -> 31.5 us
  other arithmetic: 7.77 us -> 6.63 us
  local copies, waits for them, and re-layouts: 5.41 us -> 4.43 us
    ppermute x4 -> x6, starting transfers between devices: 5.87 us -> 15.6 us  [across(): return lax.ppermute(x, 'head', [(h, h ^ step) for h in range(n_head)])]
    ppermute x7 -> x4, waiting for transfers between devices: 7.56 us -> 0.44 us  [the longest x3 0.44 us: per_device(): lax.ppermute(x, 'head', [(h, h ^ d) for h in range(n_head)])]
    ppermute x7 -> x4, starting transfers between devices: 8.86 us -> 3.56 us  [the longest x3 3.49 us: per_device(): lax.ppermute(x, 'head', [(h, h ^ d) for h in range(n_head)])]
    all_to_all x1, starting transfers between devices: 6.49 us -> 3.42 us  [per_device(): dkv = lax.all_to_all(dkv, both, 0, 0, axis_index_groups=teams, tiled=True)]
    ppermute x4 -> x6, waiting for transfers between devices: 23.5 us -> 26.1 us  [across(): return lax.ppermute(x, 'head', [(h, h ^ step) for h in range(n_head)])]
    select_n x2 -> x1, other arithmetic: 2.18 us -> 0.12 us  [per_device(): jnp.where(ctx == 0, jnp.stack([x[1] for x in dq]), jnp.stack([x[0] for x...]
    all_to_all x1, waiting for transfers between devices: 2.98 us -> 4.61 us  [per_device(): dkv = lax.all_to_all(dkv, both, 0, 0, axis_index_groups=teams, tiled=True)]
    pallas_call x2, Pallas kernels: 9.81 us -> 8.42 us  [attention_part(): pl.pallas_call(functools.partial(planes_kernel, rows=rows, tok=tok, q_blo...]
  transfers between devices with their start and end apart: 14 -> 13, of which waited for: 11 -> 7; matrix products, arithmetic and copies ran while one was open for 10% -> 10% of each run, Pallas kernels for 8% -> 11%
where the time goes in v5:
time: 89.4 us; the launch traced here: 89.5 us
  waiting for transfers between devices  34.9 us (39%)
  starting transfers between devices  31.5 us (35%)
  Pallas kernels  11.2 us (13%)
  other arithmetic  6.63 us (7%)
  local copies, waits for them, and re-layouts  4.43 us (5%)
    ppermute x6, waiting for transfers between devices, across(): return lax.ppermute(x, 'head', [(h, h ^ step) for h in range(n_head)])  26.1 us
    ppermute x6, starting transfers between devices, across(): return lax.ppermute(x, 'head', [(h, h ^ step) for h in range(n_head)])  15.6 us
    pallas_call x2, Pallas kernels, attention_part(): pl.pallas_call(functools.partial(planes_kernel, rows=rows, tok=tok, q_blo...  8.42 us
    all_to_all x1, starting transfers between devices, per_device(): kv = lax.all_to_all(kv, both, 0, 0, axis_index_groups=teams, tiled=True)  5.17 us
    all_to_all x1, waiting for transfers between devices, per_device(): dkv = lax.all_to_all(dkv, both, 0, 0, axis_index_groups=teams, tiled=True)  4.61 us
    all_to_all x1, starting transfers between devices, per_device(): pkg = lax.all_to_all(pkg, both, 0, 0, axis_index_groups=teams, tiled=True)  3.78 us
    ppermute x3, starting transfers between devices, per_device(): lax.ppermute(x, 'head', [(h, h ^ d) for h in range(n_head)])  3.49 us
    all_to_all x1, starting transfers between devices, per_device(): dkv = lax.all_to_all(dkv, both, 0, 0, axis_index_groups=teams, tiled=True)  3.42 us
  transfers between devices with their start and end apart: 13, of which 7 were waited for; matrix products, arithmetic and copies ran while one was open for 10% of the time, Pallas kernels for 11%

profile of v5, /device:TPU:0, one launch (start us, length us, event | category | flops | bytes accessed | tf_op | source)
XLA Modules:
  0.0 89.5 jit_solution(9574072028649319965)
XLA Ops:
  0.6 0.0 copy-start
  0.6 0.0 copy-start.5
  0.7 1.2 %copy_bitcast_fusion.2 = (bf16[1,64,8,128]{3,1,0,2:T(8,128)(2,1)S(1)}, bf16[1,64,8,128]{3,1,0,2:T(8,128)(2,1)S(1)}) fusion(bf16[64,8,128]{2,1,0:T(8,128)(2,1)} %param.9, bf16[64,8,128]{2,1,0:T(8,128)(2,1)} %param.8), kind=kLoop, calls=%fused_computation.11 | loop fusion | bytes 524288 | tf_op jit(solution)/shard_map/stack | solution.py:392
  1.8 0.7 maximum_bitcast_fusion
  2.5 5.2 %all-to-all-start.1 = ((bf16[8,2,64,128]{3,2,1,0:T(8,128)(2,1)}), bf16[8,2,64,128]{3,2,1,0:T(8,128)(2,1)S(1)}, u32[]{:S(2)}, u32[]{:S(2)}) async-start(bf16[8,2,64,128]{3,2,1,0:T(8,128)(2,1)} %maximum_bitcast_fusion), calls=%async_computation.1 | async-start | bytes 524288 | tf_op jit(solution)/shard_map/all_to_all | solution.py:394
  7.7 0.8 copy.34
  8.6 0.0 copy-done.5
  8.6 1.8 %multiply_reduce_fusion = f32[64,64]{1,0:T(8,128)S(1)} fusion(bf16[64,64,128]{2,1,0:T(8,128)(2,1)} %param.10, bf16[64,64,128]{2,1,0:T(8,128)(2,1)S(1)} %copy-done.5), kind=kLoop, calls=%fused_computation.4 | loop fusion | flops 2093056 | bytes 2113536 | tf_op jit(solution)/shard_map/reduce_sum | solution.py:406
  10.4 0.1 copy.36
  10.6 0.4 copy.37
  11.0 0.8 reshape.264
  11.7 0.0 copy-done
  11.7 0.5 copy_bitcast_fusion
  12.2 1.5 %fusion.1 = bf16[8,1056,128]{2,1,0:T(8,128)(2,1)} fusion(bf16[8,24,128]{2,1,0:T(8,128)(2,1)S(1)} %reshape.264, bf16[8,512,128]{2,1,0:T(8,128)(2,1)S(1)} %get-tuple-element.59, bf16[8,512,128]{2,1,0:T(8,128)(2,1)S(1)} %get-tuple-element.60), kind=kLoop, calls=%fused_computation.3 | loop fusion | flops 8650752 | bytes 4308992 | tf_op jit(solution)/shard_map/concatenate | solution.py:411
  13.7 0.0 copy-start.4
  13.8 0.6 all-to-all-done.1.refs_0_
  14.3 0.0 copy-start.1
  14.3 3.8 %all-to-all-start = ((bf16[8,1056,128]{2,1,0:T(8,128)(2,1)}), bf16[8,1056,128]{2,1,0:T(8,128)(2,1)S(1)}, u32[]{:S(2)}, u32[]{:S(2)}) async-start(bf16[8,1056,128]{2,1,0:T(8,128)(2,1)} %fusion.1), calls=%async_computation | async-start | bytes 4325376 | tf_op jit(solution)/shard_map/all_to_all | solution.py:412
  18.1 2.6 %collective-permute-start.1 = (bf16[8,2,64,128]{3,2,1,0:T(8,128)(2,1)S(1)}, bf16[8,2,64,128]{3,2,1,0:T(8,128)(2,1)}, u32[]{:S(2)}, u32[]{:S(2)}) collective-permute-start(bf16[8,2,64,128]{3,2,1,0:T(8,128)(2,1)S(1)} %all-to-all-done.1.refs_0_), channel_id=1, source_target_pairs={{0,8},{1,9},{2,10},{3,11},{4,12},{5,13},{6,14},{7,15},{8,0},{9,1},... | collective-permute-start | bytes 786440 | tf_op jit(solution)/shard_map/ppermute | solution.py:390
  20.7 0.1 fusion.13
  20.8 0.0 copy-done.4
  20.8 0.6 gather_fusion
  21.4 0.2 convert_reduce_fusion
  21.6 0.0 copy-done.1
  21.6 1.6 %collective-permute-start = (bf16[8,2,64,128]{3,2,1,0:T(8,128)(2,1)S(1)}, bf16[8,2,64,128]{3,2,1,0:T(8,128)(2,1)}, u32[]{:S(2)}, u32[]{:S(2)}) collective-permute-start(bf16[8,2,64,128]{3,2,1,0:T(8,128)(2,1)S(1)} %all-to-all-done.1.refs_0_), channel_id=1, source_target_pairs={{0,4},{1,5},{2,6},{3,7},{4,0},{5,1},{6,2},{7,3},{8,12},{9,13},{10,... | collective-permute-start | bytes 786440 | tf_op jit(solution)/shard_map/ppermute | solution.py:390
  23.2 10.3 %collective-permute-done.1.refs_2_ = bf16[8,2,64,128]{3,2,1,0:T(8,128)(2,1)} collective-permute-done((bf16[8,2,64,128]{3,2,1,0:T(8,128)(2,1)S(1)}, bf16[8,2,64,128]{3,2,1,0:T(8,128)(2,1)}, u32[]{:S(2)}, u32[]{:S(2)}) %collective-permute-start.1) | collective-permute-done | bytes 262176 | tf_op jit(solution)/shard_map/ppermute | solution.py:390
  33.5 0.5 collective-permute-start.2
  34.1 0.1 add_subtract_fusion
  34.1 0.1 pad_add_fusion.meta
  34.2 7.5 %collective-permute-done.2.refs_0_ = bf16[8,2,64,128]{3,2,1,0:T(8,128)(2,1)} collective-permute-done((bf16[8,2,64,128]{3,2,1,0:T(8,128)(2,1)}, bf16[8,2,64,128]{3,2,1,0:T(8,128)(2,1)}, u32[]{:S(2)}, u32[]{:S(2)}) %collective-permute-start.2) | collective-permute-done | bytes 262176 | tf_op jit(solution)/shard_map/ppermute | solution.py:390
  41.7 3.2 %all-to-all-done.pkg = bf16[8,1056,128]{2,1,0:T(8,128)(2,1)S(1)} async-done(((bf16[8,1056,128]{2,1,0:T(8,128)(2,1)}), bf16[8,1056,128]{2,1,0:T(8,128)(2,1)S(1)}, u32[]{:S(2)}, u32[]{:S(2)}) %all-to-all-start) | async-done | bytes 2162720 | tf_op jit(solution)/shard_map/all_to_all | solution.py:412
  44.9 0.0 copy-start.2
  44.9 2.0 %attention_3.1 = (f32[4,1024,128]{2,1,0:T(8,128)S(1)}, bf16[8,2,64,128]{3,2,1,0:T(8,128)(2,1)S(1)}) custom-call(s32[10]{0:T(128)S(1)} %pad_add_fusion.meta, bf16[8,1056,128]{2,1,0:T(8,128)(2,1)S(1)} %all-to-all-done.pkg, bf16[8,2,64,128]{3,2,1,0:T(8,128)(2,1)} %collective-permute-done.2.refs_0_), custom_call_target="tpu_custom_call" | custom-call | flops 671088640 | bytes 4194304 | tf_op jit(solution)/shard_map/attention_3/pallas_call | solution.py:277
  46.9 1.6 %collective-permute-start.4 = (bf16[8,2,64,128]{3,2,1,0:T(8,128)(2,1)S(1)}, bf16[8,2,64,128]{3,2,1,0:T(8,128)(2,1)S(1)}, u32[]{:S(2)}, u32[]{:S(2)}) collective-permute-start(bf16[8,2,64,128]{3,2,1,0:T(8,128)(2,1)S(1)} %get-tuple-element.30), channel_id=1, source_target_pairs={{0,4},{1,5},{2,6},{3,7},{4,0},{5,1},{6,2},{7,3},{8,12},{9,13},{10,... | collective-permute-start | bytes 786440 | tf_op jit(solution)/shard_map/ppermute | solution.py:390
  48.6 0.0 collective-permute-done.refs_1_
  48.6 0.0 copy-done.2
  48.6 6.4 %attention_0_1_2.1 = (bf16[2,512,128]{2,1,0:T(8,128)(2,1)S(1)}, bf16[2,512,128]{2,1,0:T(8,128)(2,1)}, bf16[2,512,128]{2,1,0:T(8,128)(2,1)}, bf16[2,512,128]{2,1,...) custom-call(s32[10]{0:T(128)S(1)} %pad_add_fusion.meta, ...), custom_call_target="tpu_custom_call" | custom-call | flops 2013265920 | bytes 4194304 | tf_op jit(solution)/shard_map/attention_0_1_2/pallas_call | solution.py:277
  55.0 0.0 copy-start.3
  55.0 2.7 %collective-permute-start.3 = (bf16[8,2,64,128]{3,2,1,0:T(8,128)(2,1)}, bf16[8,2,64,128]{3,2,1,0:T(8,128)(2,1)S(1)}, u32[]{:S(2)}, u32[]{:S(2)}) collective-permute-start(bf16[8,2,64,128]{3,2,1,0:T(8,128)(2,1)} %get-tuple-element.28), channel_id=1, source_target_pairs={{0,4},{1,5},{2,6},{3,7},{4,0},{5,1},{6,2},{7,3},{8,12},{9,13},{10,... | collective-permute-start | bytes 786440 | tf_op jit(solution)/shard_map/ppermute | solution.py:390
  57.7 0.0 collective-permute-done.4
  57.7 0.1 add_convert_fusion.1
  57.8 6.5 %collective-permute-start.5 = (bf16[8,2,64,128]{3,2,1,0:T(8,128)(2,1)S(1)}, bf16[8,2,64,128]{3,2,1,0:T(8,128)(2,1)S(1)}, u32[]{:S(2)}, u32[]{:S(2)}) collective-permute-start(bf16[8,2,64,128]{3,2,1,0:T(8,128)(2,1)S(1)} %add_convert_fusion.1), channel_id=1, source_target_pairs={{0,8},{1,9},{2,10},{3,11},{4,12},{5,13},{6,14},{7,15},{8,0},{9,1},... | collective-permute-start | bytes 786440 | tf_op jit(solution)/shard_map/ppermute | solution.py:390
  64.3 1.0 %collective-permute-start.6 = (bf16[2,512,128]{2,1,0:T(8,128)(2,1)}, bf16[2,512,128]{2,1,0:T(8,128)(2,1)S(1)}, u32[]{:S(2)}, u32[]{:S(2)}) collective-permute-start(bf16[2,512,128]{2,1,0:T(8,128)(2,1)} %get-tuple-element.37), channel_id=1, source_target_pairs={{0,1},{1,0},{2,3},{3,2},{4,5},{5,4},{6,7},{7,6},{8,9},{9,8},{10,11... | collective-permute-start | bytes 786440 | tf_op jit(solution)/shard_map/ppermute | solution.py:438
  65.3 0.0 copy-done.3
  65.3 0.7 collective-permute-start.7
  65.9 1.8 %collective-permute-start.8 = (bf16[2,512,128]{2,1,0:T(8,128)(2,1)}, bf16[2,512,128]{2,1,0:T(8,128)(2,1)S(1)}, u32[]{:S(2)}, u32[]{:S(2)}) collective-permute-start(bf16[2,512,128]{2,1,0:T(8,128)(2,1)} %get-tuple-element.39), channel_id=1, source_target_pairs={{0,3},{1,2},{2,1},{3,0},{4,7},{5,6},{6,5},{7,4},{8,11},{9,10},{10,... | collective-permute-start | bytes 786440 | tf_op jit(solution)/shard_map/ppermute | solution.py:438
  67.8 0.0 collective-permute-done.3
  67.8 8.3 %collective-permute-done.5 = bf16[8,2,64,128]{3,2,1,0:T(8,128)(2,1)S(1)} collective-permute-done((bf16[8,2,64,128]{3,2,1,0:T(8,128)(2,1)S(1)}, bf16[8,2,64,128]{3,2,1,0:T(8,128)(2,1)S(1)}, u32[]{:S(2)}, u32[]{:S(2)}) %collective-permute-start.5) | collective-permute-done | bytes 262176 | tf_op jit(solution)/shard_map/ppermute | solution.py:390
  76.1 1.8 %add_convert_fusion = bf16[8,2,64,128]{3,2,1,0:T(8,128)(2,1)} fusion(bf16[8,2,64,128]{3,2,1,0:T(8,128)(2,1)S(1)} %collective-permute-done.5, bf16[8,2,64,128]{3,2,1,0:T(8,128)(2,1)S(1)} %collective-permute-done.3, bf16[8,2,64,128]{3,2,1,0:T(8,128)(2,1)} %copy-done.3), kind=kLoop, calls=%fused_computation.8 | loop fusion | flops 786432 | bytes 1048576 | tf_op jit(solution)/shard_map/convert_element_type | solution.py:352
  77.9 0.0 collective-permute-done.6
  77.9 0.4 collective-permute-done.7
  78.3 0.0 collective-permute-done.8
  78.4 0.1 maximum_select_fusion
  78.5 0.1 collective-permute-start.9
  78.6 3.4 %all-to-all-start.2 = ((bf16[8,2,64,128]{3,2,1,0:T(8,128)(2,1)}), bf16[8,2,64,128]{3,2,1,0:T(8,128)(2,1)S(1)}, u32[]{:S(2)}, u32[]{:S(2)}) async-start(bf16[8,2,64,128]{3,2,1,0:T(8,128)(2,1)} %add_convert_fusion), calls=%async_computation.2 | async-start | bytes 524288 | tf_op jit(solution)/shard_map/all_to_all | solution.py:441
  82.0 0.1 pad_add_fusion.1.place
  82.1 0.0 collective-permute-done.9
  82.1 1.8 %place_dq.1 = bf16[64,8,8,128]{3,2,1,0:T(8,128)(2,1)} custom-call(s32[2]{0:T(128)S(1)} %pad_add_fusion.1.place, bf16[2,64,8,128]{3,2,1,0:T(8,128)(2,1)S(1)} %bitcast.69, bf16[2,64,8,128]{3,2,1,0:T(8,128)(2,1)S(1)} %bitcast.70, bf16[2,64,8,128]{3,2,1,0:T(8,128)(2,1)S(1)} %bitcast.71, bf16[2,64,8,128]{3,2,1,0:T(8,128)(2,1)S(1)} %bitcast.72, ...), custom_call_target="tpu_custom_call" | custom-call | tf_op jit(solution)/shard_map/place_dq/pallas_call | solution.py:309
  83.9 4.6 %all-to-all-done.2 = bf16[8,2,64,128]{3,2,1,0:T(8,128)(2,1)S(1)} async-done(((bf16[8,2,64,128]{3,2,1,0:T(8,128)(2,1)}), bf16[8,2,64,128]{3,2,1,0:T(8,128)(2,1)S(1)}, u32[]{:S(2)}, u32[]{:S(2)}) %all-to-all-start.2) | async-done | bytes 262176 | tf_op jit(solution)/shard_map/all_to_all | solution.py:441
  88.5 1.0 %place_dkv.1 = (bf16[64,8,128]{2,1,0:T(8,128)(2,1)}, bf16[64,8,128]{2,1,0:T(8,128)(2,1)}) custom-call(bf16[1,8,2,64,128]{4,3,2,1,0:T(8,128)(2,1)S(1)} %bitcast.68), custom_call_target="tpu_custom_call" | custom-call | tf_op jit(solution)/shard_map/place_dkv/pallas_call | solution.py:331
  (11 shorter events, 0.2 us)
Async XLA Ops:
  0.6 11.1 %copy-start = (bf16[64,64,128]{2,1,0:T(8,128)(2,1)S(1)}, bf16[64,64,128]{2,1,0:T(8,128)(2,1)}, u32[]{:S(2)}) copy-start(bf16[64,64,128]{2,1,0:T(8,128)(2,1)} %param.7) | copy-start | bytes 3145732
  0.6 7.9 %copy-start.5 = (bf16[64,64,128]{2,1,0:T(8,128)(2,1)S(1)}, bf16[64,64,128]{2,1,0:T(8,128)(2,1)}, u32[]{:S(2)}) copy-start(bf16[64,64,128]{2,1,0:T(8,128)(2,1)} %param.11) | copy-start | bytes 3145732
  2.5 11.8 %all-to-all-start.1 = ((bf16[8,2,64,128]{3,2,1,0:T(8,128)(2,1)}), bf16[8,2,64,128]{3,2,1,0:T(8,128)(2,1)S(1)}, u32[]{:S(2)}, u32[]{:S(2)}) async-start(bf16[8,2,64,128]{3,2,1,0:T(8,128)(2,1)} %maximum_bitcast_fusion), calls=%async_computation.1 | async-start | bytes 524288 | tf_op jit(solution)/shard_map/all_to_all | solution.py:394
  13.7 7.0 %copy-start.4 = (s32[16]{0:T(128)S(1)}, s32[16]{0:T(128)}, u32[]{:S(2)}) copy-start(s32[16]{0:T(128)} %param.13) | copy-start | bytes 196
  14.3 7.3 %copy-start.1 = (bf16[8,2,64,128]{3,2,1,0:T(8,128)(2,1)}, bf16[8,2,64,128]{3,2,1,0:T(8,128)(2,1)S(1)}, u32[]{:S(2)}) copy-start(bf16[8,2,64,128]{3,2,1,0:T(8,128)(2,1)S(1)} %all-to-all-done.1.refs_0_) | copy-start | bytes 786436
  14.3 30.6 %all-to-all-start = ((bf16[8,1056,128]{2,1,0:T(8,128)(2,1)}), bf16[8,1056,128]{2,1,0:T(8,128)(2,1)S(1)}, u32[]{:S(2)}, u32[]{:S(2)}) async-start(bf16[8,1056,128]{2,1,0:T(8,128)(2,1)} %fusion.1), calls=%async_computation | async-start | bytes 4325376 | tf_op jit(solution)/shard_map/all_to_all | solution.py:412
  18.1 15.4 %collective-permute-start.1 = (bf16[8,2,64,128]{3,2,1,0:T(8,128)(2,1)S(1)}, bf16[8,2,64,128]{3,2,1,0:T(8,128)(2,1)}, u32[]{:S(2)}, u32[]{:S(2)}) collective-permute-start(bf16[8,2,64,128]{3,2,1,0:T(8,128)(2,1)S(1)} %all-to-all-done.1.refs_0_), channel_id=1, source_target_pairs={{0,8},{1,9},{2,10},{3,11},{4,12},{5,13},{6,14},{7,15},{8,0},{9,1},... | collective-permute-start | bytes 786440 | tf_op jit(solution)/shard_map/ppermute | solution.py:390
  21.6 27.0 %collective-permute-start = (bf16[8,2,64,128]{3,2,1,0:T(8,128)(2,1)S(1)}, bf16[8,2,64,128]{3,2,1,0:T(8,128)(2,1)}, u32[]{:S(2)}, u32[]{:S(2)}) collective-permute-start(bf16[8,2,64,128]{3,2,1,0:T(8,128)(2,1)S(1)} %all-to-all-done.1.refs_0_), channel_id=1, source_target_pairs={{0,4},{1,5},{2,6},{3,7},{4,0},{5,1},{6,2},{7,3},{8,12},{9,13},{10,... | collective-permute-start | bytes 786440 | tf_op jit(solution)/shard_map/ppermute | solution.py:390
  33.5 8.2 %collective-permute-start.2 = (bf16[8,2,64,128]{3,2,1,0:T(8,128)(2,1)}, bf16[8,2,64,128]{3,2,1,0:T(8,128)(2,1)}, u32[]{:S(2)}, u32[]{:S(2)}) collective-permute-start(bf16[8,2,64,128]{3,2,1,0:T(8,128)(2,1)} %collective-permute-done.1.refs_2_), channel_id=1, source_target_pairs={{0,4},{1,5},{2,6},{3,7},{4,0},{5,1},{6,2},{7,3},{8,12},{9,13},{10,... | collective-permute-start | bytes 786440 | tf_op jit(solution)/shard_map/ppermute | solution.py:390
  44.9 3.7 %copy-start.2 = (bf16[8,2,64,128]{3,2,1,0:T(8,128)(2,1)S(1)}, bf16[8,2,64,128]{3,2,1,0:T(8,128)(2,1)}, u32[]{:S(2)}) copy-start(bf16[8,2,64,128]{3,2,1,0:T(8,128)(2,1)} %copy-done.1) | copy-start | bytes 786436
  46.9 10.8 %collective-permute-start.4 = (bf16[8,2,64,128]{3,2,1,0:T(8,128)(2,1)S(1)}, bf16[8,2,64,128]{3,2,1,0:T(8,128)(2,1)S(1)}, u32[]{:S(2)}, u32[]{:S(2)}) collective-permute-start(bf16[8,2,64,128]{3,2,1,0:T(8,128)(2,1)S(1)} %get-tuple-element.30), channel_id=1, source_target_pairs={{0,4},{1,5},{2,6},{3,7},{4,0},{5,1},{6,2},{7,3},{8,12},{9,13},{10,... | collective-permute-start | bytes 786440 | tf_op jit(solution)/shard_map/ppermute | solution.py:390
  55.0 10.3 %copy-start.3 = (bf16[8,2,64,128]{3,2,1,0:T(8,128)(2,1)}, bf16[8,2,64,128]{3,2,1,0:T(8,128)(2,1)S(1)}, u32[]{:S(2)}) copy-start(bf16[8,2,64,128]{3,2,1,0:T(8,128)(2,1)S(1)} %get-tuple-element.27) | copy-start | bytes 786436
  55.0 12.8 %collective-permute-start.3 = (bf16[8,2,64,128]{3,2,1,0:T(8,128)(2,1)}, bf16[8,2,64,128]{3,2,1,0:T(8,128)(2,1)S(1)}, u32[]{:S(2)}, u32[]{:S(2)}) collective-permute-start(bf16[8,2,64,128]{3,2,1,0:T(8,128)(2,1)} %get-tuple-element.28), channel_id=1, source_target_pairs={{0,4},{1,5},{2,6},{3,7},{4,0},{5,1},{6,2},{7,3},{8,12},{9,13},{10,... | collective-permute-start | bytes 786440 | tf_op jit(solution)/shard_map/ppermute | solution.py:390
  57.8 18.3 %collective-permute-start.5 = (bf16[8,2,64,128]{3,2,1,0:T(8,128)(2,1)S(1)}, bf16[8,2,64,128]{3,2,1,0:T(8,128)(2,1)S(1)}, u32[]{:S(2)}, u32[]{:S(2)}) collective-permute-start(bf16[8,2,64,128]{3,2,1,0:T(8,128)(2,1)S(1)} %add_convert_fusion.1), channel_id=1, source_target_pairs={{0,8},{1,9},{2,10},{3,11},{4,12},{5,13},{6,14},{7,15},{8,0},{9,1},... | collective-permute-start | bytes 786440 | tf_op jit(solution)/shard_map/ppermute | solution.py:390
  64.3 13.6 %collective-permute-start.6 = (bf16[2,512,128]{2,1,0:T(8,128)(2,1)}, bf16[2,512,128]{2,1,0:T(8,128)(2,1)S(1)}, u32[]{:S(2)}, u32[]{:S(2)}) collective-permute-start(bf16[2,512,128]{2,1,0:T(8,128)(2,1)} %get-tuple-element.37), channel_id=1, source_target_pairs={{0,1},{1,0},{2,3},{3,2},{4,5},{5,4},{6,7},{7,6},{8,9},{9,8},{10,11... | collective-permute-start | bytes 786440 | tf_op jit(solution)/shard_map/ppermute | solution.py:438
  65.3 13.0 %collective-permute-start.7 = (bf16[2,512,128]{2,1,0:T(8,128)(2,1)}, bf16[2,512,128]{2,1,0:T(8,128)(2,1)S(1)}, u32[]{:S(2)}, u32[]{:S(2)}) collective-permute-start(bf16[2,512,128]{2,1,0:T(8,128)(2,1)} %get-tuple-element.38), channel_id=1, source_target_pairs={{0,2},{1,3},{2,0},{3,1},{4,6},{5,7},{6,4},{7,5},{8,10},{9,11},{10,... | collective-permute-start | bytes 786440 | tf_op jit(solution)/shard_map/ppermute | solution.py:438
  65.9 12.4 %collective-permute-start.8 = (bf16[2,512,128]{2,1,0:T(8,128)(2,1)}, bf16[2,512,128]{2,1,0:T(8,128)(2,1)S(1)}, u32[]{:S(2)}, u32[]{:S(2)}) collective-permute-start(bf16[2,512,128]{2,1,0:T(8,128)(2,1)} %get-tuple-element.39), channel_id=1, source_target_pairs={{0,3},{1,2},{2,1},{3,0},{4,7},{5,6},{6,5},{7,4},{8,11},{9,10},{10,... | collective-permute-start | bytes 786440 | tf_op jit(solution)/shard_map/ppermute | solution.py:438
  78.5 3.6 %collective-permute-start.9 = (bf16[4,512,128]{2,1,0:T(8,128)(2,1)S(1)}, bf16[4,512,128]{2,1,0:T(8,128)(2,1)S(1)}, u32[]{:S(2)}, u32[]{:S(2)}) collective-permute-start(bf16[4,512,128]{2,1,0:T(8,128)(2,1)S(1)} %maximum_select_fusion), channel_id=1, source_target_pairs={{0,16},{16,0},{1,17},{17,1},{2,18},{18,2},{3,19},{19,3},{4,20},{20... | collective-permute-start | bytes 1572872 | tf_op jit(solution)/shard_map/ppermute | solution.py:443
  78.6 9.9 %all-to-all-start.2 = ((bf16[8,2,64,128]{3,2,1,0:T(8,128)(2,1)}), bf16[8,2,64,128]{3,2,1,0:T(8,128)(2,1)S(1)}, u32[]{:S(2)}, u32[]{:S(2)}) async-start(bf16[8,2,64,128]{3,2,1,0:T(8,128)(2,1)} %add_convert_fusion), calls=%async_computation.2 | async-start | bytes 524288 | tf_op jit(solution)/shard_map/all_to_all | solution.py:441

commit v6 on v5

--- a/solution.py
+++ b/solution.py
@@ -33,12 +33,11 @@
 def block_pair(q, g, lse, delta, k, v, group, scale, mask):
     s = lax.dot_general(k, q, (((1,), (1,)), ((), ())), preferred_element_type=jnp.float32)
     p = jnp.exp2(s * (scale * LOG2E) - lse)
-    if mask is True:
+    if mask is not None:
+        lead, from_key = mask
         key_at = lax.broadcasted_iota(jnp.int32, p.shape, 0)
-        query_at = lax.broadcasted_iota(jnp.int32, p.shape, 1) // group
-        p = jnp.where(query_at >= key_at, p, 0.0)
-    elif mask is not None:
-        p = jnp.where(mask, p, 0.0)
+        query_at = lax.broadcasted_iota(jnp.int32, p.shape, 1) // group + lead
+        p = jnp.where((query_at >= key_at) & (key_at >= from_key), p, 0.0)
     dp = lax.dot_general(v, g, (((1,), (1,)), ((), ())), preferred_element_type=jnp.float32)
     ds = (p * (dp - delta)).astype(jnp.bfloat16)
     dv = jnp.dot(p.astype(jnp.bfloat16), g, preferred_element_type=jnp.float32)
@@ -64,7 +63,7 @@
         def step(j, masked):
             k = kv[pl.ds(sources * j, sources), 0].reshape(BLK, 128)
             v = kv[pl.ds(sources * j, sources), 1].reshape(BLK, 128)
-            dq_part, dk, dv = block_pair(q, g, lse, delta, k, v, rows // tok, scale, masked or None)
+            dq_part, dk, dv = block_pair(q, g, lse, delta, k, v, rows // tok, scale, (0, 0) if masked else None)
             at = pl.ds(pl.multiple_of(j * BLK, BLK), BLK)
             dv_acc[at, :] += dv
             dk_acc[at, :] += dk
@@ -103,13 +102,14 @@
     group = rows // tok
     plane, slot = meta[2 * q_blocks], meta[2 * q_blocks + 1]
     range_blocks = 2 * planes
-    loads = [pltpu.make_async_copy(near[n], kv.at[n], kv_sems.at[n]) for n in range(count)]
-    for copy in loads:
-        copy.start()
     dk_acc[...] = jnp.zeros_like(dk_acc)
     dv_acc[...] = jnp.zeros_like(dv_acc)
-    for copy in loads:
-        copy.wait()
+    if ends:
+        loads = [pltpu.make_async_copy(near[n], kv.at[n], kv_sems.at[n]) for n in range(count)]
+        for copy in loads:
+            copy.start()
+        for copy in loads:
+            copy.wait()
 
     def over_range(r, _):
         lasts = [meta[2 * r + x] for x in range(2)]
@@ -127,7 +127,8 @@
 
         def keys(n, block, blocks):
             at = pl.ds(sources * block, sources * blocks)
-            return kv[n, at, 0].reshape(blocks * BLK, 128), kv[n, at, 1].reshape(blocks * BLK, 128)
+            held = kv.at[n] if ends else near[0]
+            return held[at, 0].reshape(blocks * BLK, 128), held[at, 1].reshape(blocks * BLK, 128)
 
         def add_keys(n, block, dk, dv):
             at = pl.ds(pl.multiple_of(block * BLK, BLK), dk.shape[0])
@@ -179,14 +180,13 @@
         lax.fori_loop(0, (r + 1) * count, inner, 0)
         if ends:
             n = distances.index(0)
-            lower = [keys(n, 2 * r + y, 1) for y in range(2)]
-            first_dq, dk, dv = block_pair(*queries(0), *lower[0], group, scale, True)
-            cross = block_pair(*queries(1), *lower[0], group, scale, firsts[1] <= lasts[0])
-            last_dq, dk_1, dv_1 = block_pair(*queries(1), *lower[1], group, scale, True)
-            dq_acc[0] += first_dq
-            dq_acc[1] += cross[0] + last_dq
-            add_keys(n, 2 * r, dk + cross[1], dv + cross[2])
-            add_keys(n, 2 * r + 1, dk_1, dv_1)
+            from_key = jnp.where(firsts[1] <= lasts[0], 0, BLK)
+            dq_0, dk, dv = block_pair(*queries(0), *keys(n, 2 * r, 1), group, scale, (0, 0))
+            dq_1, dk_1, dv_1 = block_pair(*queries(1), *keys(n, 2 * r, 2), group, scale, (BLK, from_key))
+            dq_acc[0] += dq_0
+            dq_acc[1] += dq_1
+            add_keys(n, 2 * r, dk + dk_1[0:BLK], dv + dv_1[0:BLK])
+            add_keys(n, 2 * r + 1, dk_1[BLK:], dv_1[BLK:])
         for x in range(2):
             if ends:
                 done = (dq_acc[x] * scale).astype(jnp.bfloat16).reshape(sources, rows, 128)
@@ -204,15 +204,16 @@
         ]
         for copy in stores:
             copy.start()
+    if not ends:
+        grads_out[0][:, 0] = (dk_acc[0] * scale).astype(jnp.bfloat16).reshape(team, tok, 128)
+        grads_out[0][:, 1] = dv_acc[0].astype(jnp.bfloat16).reshape(team, tok, 128)
+        return
     grad_stores = [pltpu.make_async_copy(grads.at[n], grads_out[n], grad_sems.at[n]) for n in range(count)]
     for n in reversed(range(count)):
         grads[n, :, 0] = (dk_acc[n] * scale).astype(jnp.bfloat16).reshape(team, tok, 128)
         grads[n, :, 1] = dv_acc[n].astype(jnp.bfloat16).reshape(team, tok, 128)
         grad_stores[n].start()
-    if ends:
-        for copy in stores:
-            copy.wait()
-    for copy in grad_stores:
+    for copy in stores + grad_stores:
         copy.wait()
 
 
@@ -279,8 +280,8 @@
             planes_kernel, rows=rows, tok=tok, q_blocks=q_blocks, scale=scale, distances=distances, planes=planes
         ),
         out_shape=dq_shapes + (jax.ShapeDtypeStruct(kv[0].shape, jnp.bfloat16),) * count,
-        in_specs=[SMEM, VMEM] + [hbm] * count + [VMEM] * len(before),
-        out_specs=dq_specs + (hbm,) * count,
+        in_specs=[SMEM, VMEM] + [hbm if ends else VMEM] * count + [VMEM] * len(before),
+        out_specs=dq_specs + (hbm if ends else VMEM,) * count,
         scratch_shapes=scratch,
         compiler_params=pltpu.CompilerParams(vmem_limit_bytes=PART_LIMIT),
         cost_estimate=pl.CostEstimate(
@@ -292,6 +293,22 @@
     )(meta, pkg, *kv, *before)
     dq, grads = out[:-count], out[-count:]
     return (dq if ends else dq[0]), grads
+
+
+def sum_kernel(*refs):
+    *terms, out = refs
+    out[...] = sum(x[...].astype(jnp.float32) for x in terms)
+
+
+def sum_of(*terms):
+    return pl.pallas_call(
+        sum_kernel,
+        out_shape=jax.ShapeDtypeStruct(terms[0].shape, jnp.float32),
+        in_specs=[VMEM] * len(terms),
+        out_specs=VMEM,
+        compiler_params=pltpu.CompilerParams(vmem_limit_bytes=SMALL_LIMIT),
+        name="sum_dkv",
+    )(*terms)
 
 
 def place_dq_kernel(place, *refs):
@@ -436,7 +453,7 @@
         far = across(far, 2)
         close = across(grads_1, 1)
         dq = [lax.ppermute(x, "head", [(h, h ^ d) for h in range(n_head)]) if d else x for d, x in enumerate(dq)]
-        dkv = add(grads_0, close, far)
+        dkv = add(sum_of(grads_0, close), far)
         dkv, *dq = lax.optimization_barrier((dkv, *dq))
         dkv = lax.all_to_all(dkv, both, 0, 0, axis_index_groups=teams, tiled=True)
         other = jnp.where(ctx == 0, jnp.stack([x[1] for x in dq]), jnp.stack([x[0] for x in dq]))

time: 89.4 us -> 89 us (level); the launches traced: 89.5 us -> 88.1 us
  starting transfers between devices: 31.5 us -> 30.5 us
  other arithmetic: 6.63 us -> 5.64 us
  local copies, waits for them, and re-layouts: 4.43 us -> 5.38 us
    ppermute x6, starting transfers between devices: 15.6 us -> 14.5 us  [across(): return lax.ppermute(x, 'head', [(h, h ^ step) for h in range(n_head)])]
    convert_element_type x2, other arithmetic: 1.83 us -> 0.85 us  [add(): return sum((x.astype(jnp.float32) for x in terms)).astype(jnp.bfloat16)]
    ppermute x6, waiting for transfers between devices: 26.1 us -> 25.2 us  [across(): return lax.ppermute(x, 'head', [(h, h ^ step) for h in range(n_head)])]
    unnamed x13 -> x15, local copies, waits for them, and re-layouts: 0.86 us -> 1.81 us
    ppermute x3, waiting for transfers between devices: 0.44 us -> 1.38 us  [per_device(): lax.ppermute(x, 'head', [(h, h ^ d) for h in range(n_head)])]
  transfers between devices with their start and end apart: 13 -> 13, of which waited for: 7 -> 8; matrix products, arithmetic and copies ran while one was open for 10% -> 9% of each run, Pallas kernels for 11% -> 11%
where the time goes in v6:
time: 89 us; the launch traced here: 88.1 us
  waiting for transfers between devices  34.9 us (39%)
  starting transfers between devices  30.5 us (34%)
  Pallas kernels  10.9 us (12%)
  other arithmetic  5.64 us (6%)
  local copies, waits for them, and re-layouts  5.38 us (6%)
    ppermute x6, waiting for transfers between devices, across(): return lax.ppermute(x, 'head', [(h, h ^ step) for h in range(n_head)])  25.2 us
    ppermute x6, starting transfers between devices, across(): return lax.ppermute(x, 'head', [(h, h ^ step) for h in range(n_head)])  14.5 us
    pallas_call x2, Pallas kernels, attention_part(): pl.pallas_call(functools.partial(planes_kernel, rows=rows, tok=tok, q_blo...  8.07 us
    all_to_all x1, starting transfers between devices, per_device(): kv = lax.all_to_all(kv, both, 0, 0, axis_index_groups=teams, tiled=True)  5.17 us
    all_to_all x1, waiting for transfers between devices, per_device(): dkv = lax.all_to_all(dkv, both, 0, 0, axis_index_groups=teams, tiled=True)  4.61 us
    all_to_all x1, starting transfers between devices, per_device(): pkg = lax.all_to_all(pkg, both, 0, 0, axis_index_groups=teams, tiled=True)  3.78 us
    ppermute x3, starting transfers between devices, per_device(): lax.ppermute(x, 'head', [(h, h ^ d) for h in range(n_head)])  3.49 us
    all_to_all x1, starting transfers between devices, per_device(): dkv = lax.all_to_all(dkv, both, 0, 0, axis_index_groups=teams, tiled=True)  3.42 us
  transfers between devices with their start and end apart: 13, of which 8 were waited for; matrix products, arithmetic and copies ran while one was open for 9% of the time, Pallas kernels for 11%

profile of v6, /device:TPU:0, one launch (start us, length us, event | category | flops | bytes accessed | tf_op | source)
XLA Modules:
  0.0 88.1 jit_solution(9820769940880233366)
XLA Ops:
  0.6 0.0 copy-start
  0.6 0.0 copy-start.6
  0.7 1.2 %copy_bitcast_fusion.2 = (bf16[1,64,8,128]{3,1,0,2:T(8,128)(2,1)S(1)}, bf16[1,64,8,128]{3,1,0,2:T(8,128)(2,1)S(1)}) fusion(bf16[64,8,128]{2,1,0:T(8,128)(2,1)} %param.9, bf16[64,8,128]{2,1,0:T(8,128)(2,1)} %param.8), kind=kLoop, calls=%fused_computation.11 | loop fusion | bytes 524288 | tf_op jit(solution)/shard_map/stack | solution.py:409
  1.8 0.7 maximum_bitcast_fusion
  2.5 5.2 %all-to-all-start.1 = ((bf16[8,2,64,128]{3,2,1,0:T(8,128)(2,1)}), bf16[8,2,64,128]{3,2,1,0:T(8,128)(2,1)S(1)}, u32[]{:S(2)}, u32[]{:S(2)}) async-start(bf16[8,2,64,128]{3,2,1,0:T(8,128)(2,1)} %maximum_bitcast_fusion), calls=%async_computation.1 | async-start | bytes 524288 | tf_op jit(solution)/shard_map/all_to_all | solution.py:411
  7.7 0.8 copy.34
  8.6 0.0 copy-done.6
  8.6 1.8 %multiply_reduce_fusion = f32[64,64]{1,0:T(8,128)S(1)} fusion(bf16[64,64,128]{2,1,0:T(8,128)(2,1)} %param.10, bf16[64,64,128]{2,1,0:T(8,128)(2,1)S(1)} %copy-done.6), kind=kLoop, calls=%fused_computation.4 | loop fusion | flops 2093056 | bytes 2113536 | tf_op jit(solution)/shard_map/reduce_sum | solution.py:423
  10.4 0.1 copy.36
  10.6 0.4 copy.37
  11.0 0.8 reshape.264
  11.7 0.0 copy-done
  11.7 0.5 copy_bitcast_fusion
  12.2 1.5 %fusion.1 = bf16[8,1056,128]{2,1,0:T(8,128)(2,1)} fusion(bf16[8,24,128]{2,1,0:T(8,128)(2,1)S(1)} %reshape.264, bf16[8,512,128]{2,1,0:T(8,128)(2,1)S(1)} %get-tuple-element.59, bf16[8,512,128]{2,1,0:T(8,128)(2,1)S(1)} %get-tuple-element.60), kind=kLoop, calls=%fused_computation.3 | loop fusion | flops 8650752 | bytes 4308992 | tf_op jit(solution)/shard_map/concatenate | solution.py:428
  13.7 0.0 copy-start.5
  13.7 0.6 all-to-all-done.1.refs_0_
  14.3 0.0 copy-start.1
  14.3 3.8 %all-to-all-start = ((bf16[8,1056,128]{2,1,0:T(8,128)(2,1)}), bf16[8,1056,128]{2,1,0:T(8,128)(2,1)S(1)}, u32[]{:S(2)}, u32[]{:S(2)}) async-start(bf16[8,1056,128]{2,1,0:T(8,128)(2,1)} %fusion.1), calls=%async_computation | async-start | bytes 4325376 | tf_op jit(solution)/shard_map/all_to_all | solution.py:429
  18.1 2.6 %collective-permute-start.1 = (bf16[8,2,64,128]{3,2,1,0:T(8,128)(2,1)S(1)}, bf16[8,2,64,128]{3,2,1,0:T(8,128)(2,1)}, u32[]{:S(2)}, u32[]{:S(2)}) collective-permute-start(bf16[8,2,64,128]{3,2,1,0:T(8,128)(2,1)S(1)} %all-to-all-done.1.refs_0_), channel_id=1, source_target_pairs={{0,8},{1,9},{2,10},{3,11},{4,12},{5,13},{6,14},{7,15},{8,0},{9,1},... | collective-permute-start | bytes 786440 | tf_op jit(solution)/shard_map/ppermute | solution.py:407
  20.7 0.1 fusion.13
  20.8 0.0 copy-done.5
  20.8 0.6 gather_fusion
  21.4 0.2 convert_reduce_fusion
  21.6 0.0 copy-done.1
  21.6 1.6 %collective-permute-start = (bf16[8,2,64,128]{3,2,1,0:T(8,128)(2,1)S(1)}, bf16[8,2,64,128]{3,2,1,0:T(8,128)(2,1)}, u32[]{:S(2)}, u32[]{:S(2)}) collective-permute-start(bf16[8,2,64,128]{3,2,1,0:T(8,128)(2,1)S(1)} %all-to-all-done.1.refs_0_), channel_id=1, source_target_pairs={{0,4},{1,5},{2,6},{3,7},{4,0},{5,1},{6,2},{7,3},{8,12},{9,13},{10,... | collective-permute-start | bytes 786440 | tf_op jit(solution)/shard_map/ppermute | solution.py:407
  23.2 10.3 %collective-permute-done.1.refs_2_ = bf16[8,2,64,128]{3,2,1,0:T(8,128)(2,1)} collective-permute-done((bf16[8,2,64,128]{3,2,1,0:T(8,128)(2,1)S(1)}, bf16[8,2,64,128]{3,2,1,0:T(8,128)(2,1)}, u32[]{:S(2)}, u32[]{:S(2)}) %collective-permute-start.1) | collective-permute-done | bytes 262176 | tf_op jit(solution)/shard_map/ppermute | solution.py:407
  33.5 0.5 collective-permute-start.2
  34.1 0.1 add_subtract_fusion
  34.1 0.1 pad_add_fusion.meta
  34.2 7.5 %collective-permute-done.2.refs_0_ = bf16[8,2,64,128]{3,2,1,0:T(8,128)(2,1)} collective-permute-done((bf16[8,2,64,128]{3,2,1,0:T(8,128)(2,1)}, bf16[8,2,64,128]{3,2,1,0:T(8,128)(2,1)}, u32[]{:S(2)}, u32[]{:S(2)}) %collective-permute-start.2) | collective-permute-done | bytes 262176 | tf_op jit(solution)/shard_map/ppermute | solution.py:407
  41.7 3.2 %all-to-all-done.pkg = bf16[8,1056,128]{2,1,0:T(8,128)(2,1)S(1)} async-done(((bf16[8,1056,128]{2,1,0:T(8,128)(2,1)}), bf16[8,1056,128]{2,1,0:T(8,128)(2,1)S(1)}, u32[]{:S(2)}, u32[]{:S(2)}) %all-to-all-start) | async-done | bytes 2162720 | tf_op jit(solution)/shard_map/all_to_all | solution.py:429
  44.9 0.0 copy-start.2
  44.9 1.6 %attention_3.1 = (f32[4,1024,128]{2,1,0:T(8,128)S(1)}, bf16[8,2,64,128]{3,2,1,0:T(8,128)(2,1)S(1)}) custom-call(s32[10]{0:T(128)S(1)} %pad_add_fusion.meta, bf16[8,1056,128]{2,1,0:T(8,128)(2,1)S(1)} %all-to-all-done.pkg, bf16[8,2,64,128]{3,2,1,0:T(8,128)(2,1)} %collective-permute-done.2.refs_0_), custom_call_target="tpu_custom_call" | custom-call | flops 671088640 | bytes 4194304 | tf_op jit(solution)/shard_map/attention_3/pallas_call | solution.py:278
  46.5 1.6 %collective-permute-start.4 = (bf16[8,2,64,128]{3,2,1,0:T(8,128)(2,1)S(1)}, bf16[8,2,64,128]{3,2,1,0:T(8,128)(2,1)S(1)}, u32[]{:S(2)}, u32[]{:S(2)}) collective-permute-start(bf16[8,2,64,128]{3,2,1,0:T(8,128)(2,1)S(1)} %get-tuple-element.30), channel_id=1, source_target_pairs={{0,4},{1,5},{2,6},{3,7},{4,0},{5,1},{6,2},{7,3},{8,12},{9,13},{10,... | collective-permute-start | bytes 786440 | tf_op jit(solution)/shard_map/ppermute | solution.py:407
  48.1 0.0 collective-permute-done.refs_1_
  48.1 0.0 copy-done.2
  48.1 6.5 %attention_0_1_2.1 = (bf16[2,512,128]{2,1,0:T(8,128)(2,1)S(1)}, bf16[2,512,128]{2,1,0:T(8,128)(2,1)}, bf16[2,512,128]{2,1,0:T(8,128)(2,1)}, bf16[2,512,128]{2,1,...) custom-call(s32[10]{0:T(128)S(1)} %pad_add_fusion.meta, ...), custom_call_target="tpu_custom_call" | custom-call | flops 2013265920 | bytes 4194304 | tf_op jit(solution)/shard_map/attention_0_1_2/pallas_call | solution.py:278
  54.6 0.0 copy-start.3
  54.6 3.2 %collective-permute-start.3 = (bf16[8,2,64,128]{3,2,1,0:T(8,128)(2,1)}, bf16[8,2,64,128]{3,2,1,0:T(8,128)(2,1)S(1)}, u32[]{:S(2)}, u32[]{:S(2)}) collective-permute-start(bf16[8,2,64,128]{3,2,1,0:T(8,128)(2,1)} %get-tuple-element.28), channel_id=1, source_target_pairs={{0,4},{1,5},{2,6},{3,7},{4,0},{5,1},{6,2},{7,3},{8,12},{9,13},{10,... | collective-permute-start | bytes 786440 | tf_op jit(solution)/shard_map/ppermute | solution.py:407
  57.9 0.0 collective-permute-done.4
  57.9 0.1 add_convert_fusion.1
  57.9 4.9 %collective-permute-start.5 = (bf16[8,2,64,128]{3,2,1,0:T(8,128)(2,1)S(1)}, bf16[8,2,64,128]{3,2,1,0:T(8,128)(2,1)S(1)}, u32[]{:S(2)}, u32[]{:S(2)}) collective-permute-start(bf16[8,2,64,128]{3,2,1,0:T(8,128)(2,1)S(1)} %add_convert_fusion.1), channel_id=1, source_target_pairs={{0,8},{1,9},{2,10},{3,11},{4,12},{5,13},{6,14},{7,15},{8,0},{9,1},... | collective-permute-start | bytes 786440 | tf_op jit(solution)/shard_map/ppermute | solution.py:407
  62.9 1.0 %collective-permute-start.6 = (bf16[2,512,128]{2,1,0:T(8,128)(2,1)}, bf16[2,512,128]{2,1,0:T(8,128)(2,1)S(1)}, u32[]{:S(2)}, u32[]{:S(2)}) collective-permute-start(bf16[2,512,128]{2,1,0:T(8,128)(2,1)} %get-tuple-element.37), channel_id=1, source_target_pairs={{0,1},{1,0},{2,3},{3,2},{4,5},{5,4},{6,7},{7,6},{8,9},{9,8},{10,11... | collective-permute-start | bytes 786440 | tf_op jit(solution)/shard_map/ppermute | solution.py:455
  63.9 0.0 copy-done.3
  63.9 0.7 collective-permute-start.7
  64.5 1.8 %collective-permute-start.8 = (bf16[2,512,128]{2,1,0:T(8,128)(2,1)}, bf16[2,512,128]{2,1,0:T(8,128)(2,1)S(1)}, u32[]{:S(2)}, u32[]{:S(2)}) collective-permute-start(bf16[2,512,128]{2,1,0:T(8,128)(2,1)} %get-tuple-element.39), channel_id=1, source_target_pairs={{0,3},{1,2},{2,1},{3,0},{4,7},{5,6},{6,5},{7,4},{8,11},{9,10},{10,... | collective-permute-start | bytes 786440 | tf_op jit(solution)/shard_map/ppermute | solution.py:455
  66.4 3.6 %collective-permute-done.3.refs_1_ = bf16[8,2,64,128]{3,2,1,0:T(8,128)(2,1)S(1)} collective-permute-done((bf16[8,2,64,128]{3,2,1,0:T(8,128)(2,1)}, bf16[8,2,64,128]{3,2,1,0:T(8,128)(2,1)S(1)}, u32[]{:S(2)}, u32[]{:S(2)}) %collective-permute-start.3) | collective-permute-done | bytes 262176 | tf_op jit(solution)/shard_map/ppermute | solution.py:407
  70.0 0.0 copy-start.4
  70.0 0.9 %copy-done.4 = bf16[8,2,64,128]{3,2,1,0:T(8,128)(2,1)S(1)} copy-done((bf16[8,2,64,128]{3,2,1,0:T(8,128)(2,1)S(1)}, bf16[8,2,64,128]{3,2,1,0:T(8,128)(2,1)}, u32[]{:S(2)}) %copy-start.4) | copy-done | bytes 262168
  71.0 0.1 sum_dkv.1
  71.0 3.7 %collective-permute-done.5 = bf16[8,2,64,128]{3,2,1,0:T(8,128)(2,1)S(1)} collective-permute-done((bf16[8,2,64,128]{3,2,1,0:T(8,128)(2,1)S(1)}, bf16[8,2,64,128]{3,2,1,0:T(8,128)(2,1)S(1)}, u32[]{:S(2)}, u32[]{:S(2)}) %collective-permute-start.5) | collective-permute-done | bytes 262176 | tf_op jit(solution)/shard_map/ppermute | solution.py:407
  74.7 0.8 add_convert_fusion
  75.5 0.0 collective-permute-done.6
  75.5 1.4 %collective-permute-done.7 = bf16[2,512,128]{2,1,0:T(8,128)(2,1)S(1)} collective-permute-done((bf16[2,512,128]{2,1,0:T(8,128)(2,1)}, bf16[2,512,128]{2,1,0:T(8,128)(2,1)S(1)}, u32[]{:S(2)}, u32[]{:S(2)}) %collective-permute-start.7) | collective-permute-done | bytes 262176 | tf_op jit(solution)/shard_map/ppermute | solution.py:455
  76.9 0.0 collective-permute-done.8
  77.0 0.1 maximum_select_fusion
  77.1 0.1 collective-permute-start.9
  77.2 3.4 %all-to-all-start.2 = ((bf16[8,2,64,128]{3,2,1,0:T(8,128)(2,1)}), bf16[8,2,64,128]{3,2,1,0:T(8,128)(2,1)S(1)}, u32[]{:S(2)}, u32[]{:S(2)}) async-start(bf16[8,2,64,128]{3,2,1,0:T(8,128)(2,1)} %add_convert_fusion), calls=%async_computation.2 | async-start | bytes 524288 | tf_op jit(solution)/shard_map/all_to_all | solution.py:458
  80.7 0.1 pad_add_fusion.1.place
  80.7 0.0 collective-permute-done.9
  80.7 1.8 %place_dq.1 = bf16[64,8,8,128]{3,2,1,0:T(8,128)(2,1)} custom-call(s32[2]{0:T(128)S(1)} %pad_add_fusion.1.place, bf16[2,64,8,128]{3,2,1,0:T(8,128)(2,1)S(1)} %bitcast.69, bf16[2,64,8,128]{3,2,1,0:T(8,128)(2,1)S(1)} %bitcast.70, bf16[2,64,8,128]{3,2,1,0:T(8,128)(2,1)S(1)} %bitcast.71, bf16[2,64,8,128]{3,2,1,0:T(8,128)(2,1)S(1)} %bitcast.72, ...), custom_call_target="tpu_custom_call" | custom-call | tf_op jit(solution)/shard_map/place_dq/pallas_call | solution.py:326
  82.5 4.6 %all-to-all-done.2 = bf16[8,2,64,128]{3,2,1,0:T(8,128)(2,1)S(1)} async-done(((bf16[8,2,64,128]{3,2,1,0:T(8,128)(2,1)}), bf16[8,2,64,128]{3,2,1,0:T(8,128)(2,1)S(1)}, u32[]{:S(2)}, u32[]{:S(2)}) %all-to-all-start.2) | async-done | bytes 262176 | tf_op jit(solution)/shard_map/all_to_all | solution.py:458
  87.2 1.0 %place_dkv.1 = (bf16[64,8,128]{2,1,0:T(8,128)(2,1)}, bf16[64,8,128]{2,1,0:T(8,128)(2,1)}) custom-call(bf16[1,8,2,64,128]{4,3,2,1,0:T(8,128)(2,1)S(1)} %bitcast.68), custom_call_target="tpu_custom_call" | custom-call | tf_op jit(solution)/shard_map/place_dkv/pallas_call | solution.py:348
  (11 shorter events, 0.2 us)
Async XLA Ops:
  0.6 11.1 %copy-start = (bf16[64,64,128]{2,1,0:T(8,128)(2,1)S(1)}, bf16[64,64,128]{2,1,0:T(8,128)(2,1)}, u32[]{:S(2)}) copy-start(bf16[64,64,128]{2,1,0:T(8,128)(2,1)} %param.7) | copy-start | bytes 3145732
  0.6 7.9 %copy-start.6 = (bf16[64,64,128]{2,1,0:T(8,128)(2,1)S(1)}, bf16[64,64,128]{2,1,0:T(8,128)(2,1)}, u32[]{:S(2)}) copy-start(bf16[64,64,128]{2,1,0:T(8,128)(2,1)} %param.11) | copy-start | bytes 3145732
  2.5 11.8 %all-to-all-start.1 = ((bf16[8,2,64,128]{3,2,1,0:T(8,128)(2,1)}), bf16[8,2,64,128]{3,2,1,0:T(8,128)(2,1)S(1)}, u32[]{:S(2)}, u32[]{:S(2)}) async-start(bf16[8,2,64,128]{3,2,1,0:T(8,128)(2,1)} %maximum_bitcast_fusion), calls=%async_computation.1 | async-start | bytes 524288 | tf_op jit(solution)/shard_map/all_to_all | solution.py:411
  13.7 7.0 %copy-start.5 = (s32[16]{0:T(128)S(1)}, s32[16]{0:T(128)}, u32[]{:S(2)}) copy-start(s32[16]{0:T(128)} %param.13) | copy-start | bytes 196
  14.3 7.3 %copy-start.1 = (bf16[8,2,64,128]{3,2,1,0:T(8,128)(2,1)}, bf16[8,2,64,128]{3,2,1,0:T(8,128)(2,1)S(1)}, u32[]{:S(2)}) copy-start(bf16[8,2,64,128]{3,2,1,0:T(8,128)(2,1)S(1)} %all-to-all-done.1.refs_0_) | copy-start | bytes 786436
  14.3 30.6 %all-to-all-start = ((bf16[8,1056,128]{2,1,0:T(8,128)(2,1)}), bf16[8,1056,128]{2,1,0:T(8,128)(2,1)S(1)}, u32[]{:S(2)}, u32[]{:S(2)}) async-start(bf16[8,1056,128]{2,1,0:T(8,128)(2,1)} %fusion.1), calls=%async_computation | async-start | bytes 4325376 | tf_op jit(solution)/shard_map/all_to_all | solution.py:429
  18.1 15.4 %collective-permute-start.1 = (bf16[8,2,64,128]{3,2,1,0:T(8,128)(2,1)S(1)}, bf16[8,2,64,128]{3,2,1,0:T(8,128)(2,1)}, u32[]{:S(2)}, u32[]{:S(2)}) collective-permute-start(bf16[8,2,64,128]{3,2,1,0:T(8,128)(2,1)S(1)} %all-to-all-done.1.refs_0_), channel_id=1, source_target_pairs={{0,8},{1,9},{2,10},{3,11},{4,12},{5,13},{6,14},{7,15},{8,0},{9,1},... | collective-permute-start | bytes 786440 | tf_op jit(solution)/shard_map/ppermute | solution.py:407
  21.6 26.5 %collective-permute-start = (bf16[8,2,64,128]{3,2,1,0:T(8,128)(2,1)S(1)}, bf16[8,2,64,128]{3,2,1,0:T(8,128)(2,1)}, u32[]{:S(2)}, u32[]{:S(2)}) collective-permute-start(bf16[8,2,64,128]{3,2,1,0:T(8,128)(2,1)S(1)} %all-to-all-done.1.refs_0_), channel_id=1, source_target_pairs={{0,4},{1,5},{2,6},{3,7},{4,0},{5,1},{6,2},{7,3},{8,12},{9,13},{10,... | collective-permute-start | bytes 786440 | tf_op jit(solution)/shard_map/ppermute | solution.py:407
  33.5 8.2 %collective-permute-start.2 = (bf16[8,2,64,128]{3,2,1,0:T(8,128)(2,1)}, bf16[8,2,64,128]{3,2,1,0:T(8,128)(2,1)}, u32[]{:S(2)}, u32[]{:S(2)}) collective-permute-start(bf16[8,2,64,128]{3,2,1,0:T(8,128)(2,1)} %collective-permute-done.1.refs_2_), channel_id=1, source_target_pairs={{0,4},{1,5},{2,6},{3,7},{4,0},{5,1},{6,2},{7,3},{8,12},{9,13},{10,... | collective-permute-start | bytes 786440 | tf_op jit(solution)/shard_map/ppermute | solution.py:407
  44.9 3.2 %copy-start.2 = (bf16[8,2,64,128]{3,2,1,0:T(8,128)(2,1)S(1)}, bf16[8,2,64,128]{3,2,1,0:T(8,128)(2,1)}, u32[]{:S(2)}) copy-start(bf16[8,2,64,128]{3,2,1,0:T(8,128)(2,1)} %copy-done.1) | copy-start | bytes 786436
  46.5 11.4 %collective-permute-start.4 = (bf16[8,2,64,128]{3,2,1,0:T(8,128)(2,1)S(1)}, bf16[8,2,64,128]{3,2,1,0:T(8,128)(2,1)S(1)}, u32[]{:S(2)}, u32[]{:S(2)}) collective-permute-start(bf16[8,2,64,128]{3,2,1,0:T(8,128)(2,1)S(1)} %get-tuple-element.30), channel_id=1, source_target_pairs={{0,4},{1,5},{2,6},{3,7},{4,0},{5,1},{6,2},{7,3},{8,12},{9,13},{10,... | collective-permute-start | bytes 786440 | tf_op jit(solution)/shard_map/ppermute | solution.py:407
  54.6 9.2 %copy-start.3 = (bf16[8,2,64,128]{3,2,1,0:T(8,128)(2,1)}, bf16[8,2,64,128]{3,2,1,0:T(8,128)(2,1)S(1)}, u32[]{:S(2)}) copy-start(bf16[8,2,64,128]{3,2,1,0:T(8,128)(2,1)S(1)} %get-tuple-element.27.refs_0_) | copy-start | bytes 786436
  54.6 15.4 %collective-permute-start.3 = (bf16[8,2,64,128]{3,2,1,0:T(8,128)(2,1)}, bf16[8,2,64,128]{3,2,1,0:T(8,128)(2,1)S(1)}, u32[]{:S(2)}, u32[]{:S(2)}) collective-permute-start(bf16[8,2,64,128]{3,2,1,0:T(8,128)(2,1)} %get-tuple-element.28), channel_id=1, source_target_pairs={{0,4},{1,5},{2,6},{3,7},{4,0},{5,1},{6,2},{7,3},{8,12},{9,13},{10,... | collective-permute-start | bytes 786440 | tf_op jit(solution)/shard_map/ppermute | solution.py:407
  57.9 16.8 %collective-permute-start.5 = (bf16[8,2,64,128]{3,2,1,0:T(8,128)(2,1)S(1)}, bf16[8,2,64,128]{3,2,1,0:T(8,128)(2,1)S(1)}, u32[]{:S(2)}, u32[]{:S(2)}) collective-permute-start(bf16[8,2,64,128]{3,2,1,0:T(8,128)(2,1)S(1)} %add_convert_fusion.1), channel_id=1, source_target_pairs={{0,8},{1,9},{2,10},{3,11},{4,12},{5,13},{6,14},{7,15},{8,0},{9,1},... | collective-permute-start | bytes 786440 | tf_op jit(solution)/shard_map/ppermute | solution.py:407
  62.9 12.7 %collective-permute-start.6 = (bf16[2,512,128]{2,1,0:T(8,128)(2,1)}, bf16[2,512,128]{2,1,0:T(8,128)(2,1)S(1)}, u32[]{:S(2)}, u32[]{:S(2)}) collective-permute-start(bf16[2,512,128]{2,1,0:T(8,128)(2,1)} %get-tuple-element.37), channel_id=1, source_target_pairs={{0,1},{1,0},{2,3},{3,2},{4,5},{5,4},{6,7},{7,6},{8,9},{9,8},{10,11... | collective-permute-start | bytes 786440 | tf_op jit(solution)/shard_map/ppermute | solution.py:455
  63.9 13.0 %collective-permute-start.7 = (bf16[2,512,128]{2,1,0:T(8,128)(2,1)}, bf16[2,512,128]{2,1,0:T(8,128)(2,1)S(1)}, u32[]{:S(2)}, u32[]{:S(2)}) collective-permute-start(bf16[2,512,128]{2,1,0:T(8,128)(2,1)} %get-tuple-element.38), channel_id=1, source_target_pairs={{0,2},{1,3},{2,0},{3,1},{4,6},{5,7},{6,4},{7,5},{8,10},{9,11},{10,... | collective-permute-start | bytes 786440 | tf_op jit(solution)/shard_map/ppermute | solution.py:455
  64.5 12.4 %collective-permute-start.8 = (bf16[2,512,128]{2,1,0:T(8,128)(2,1)}, bf16[2,512,128]{2,1,0:T(8,128)(2,1)S(1)}, u32[]{:S(2)}, u32[]{:S(2)}) collective-permute-start(bf16[2,512,128]{2,1,0:T(8,128)(2,1)} %get-tuple-element.39), channel_id=1, source_target_pairs={{0,3},{1,2},{2,1},{3,0},{4,7},{5,6},{6,5},{7,4},{8,11},{9,10},{10,... | collective-permute-start | bytes 786440 | tf_op jit(solution)/shard_map/ppermute | solution.py:455
  70.0 1.0 %copy-start.4 = (bf16[8,2,64,128]{3,2,1,0:T(8,128)(2,1)S(1)}, bf16[8,2,64,128]{3,2,1,0:T(8,128)(2,1)}, u32[]{:S(2)}) copy-start(bf16[8,2,64,128]{3,2,1,0:T(8,128)(2,1)} %copy-done.3) | copy-start | bytes 786436
  77.1 3.6 %collective-permute-start.9 = (bf16[4,512,128]{2,1,0:T(8,128)(2,1)S(1)}, bf16[4,512,128]{2,1,0:T(8,128)(2,1)S(1)}, u32[]{:S(2)}, u32[]{:S(2)}) collective-permute-start(bf16[4,512,128]{2,1,0:T(8,128)(2,1)S(1)} %maximum_select_fusion), channel_id=1, source_target_pairs={{0,16},{16,0},{1,17},{17,1},{2,18},{18,2},{3,19},{19,3},{4,20},{20... | collective-permute-start | bytes 1572872 | tf_op jit(solution)/shard_map/ppermute | solution.py:460
  77.2 9.9 %all-to-all-start.2 = ((bf16[8,2,64,128]{3,2,1,0:T(8,128)(2,1)}), bf16[8,2,64,128]{3,2,1,0:T(8,128)(2,1)S(1)}, u32[]{:S(2)}, u32[]{:S(2)}) async-start(bf16[8,2,64,128]{3,2,1,0:T(8,128)(2,1)} %add_convert_fusion), calls=%async_computation.2 | async-start | bytes 524288 | tf_op jit(solution)/shard_map/all_to_all | solution.py:458

commit v7 on v6

--- a/solution.py
+++ b/solution.py
@@ -9,7 +9,6 @@
 
 BLK = 128
 LOG2E = 1.4426950408889634
-STAT_ROWS = 32
 LIMIT = 56 * 1024 * 1024
 PART_LIMIT = 12 * 1024 * 1024
 SMALL_LIMIT = 6 * 1024 * 1024
@@ -18,10 +17,8 @@
 def stats_of(stats, sources, chunks):
     stats = stats.astype(jnp.float32)
     sums = (
-        stats[:, base : base + chunks]
-        + stats[:, base + chunks : base + 2 * chunks]
-        + stats[:, base + 2 * chunks : base + 3 * chunks]
-        for base in (0, 3 * chunks)
+        stats[:, base : base + chunks] + stats[:, base + chunks : base + 2 * chunks]
+        for base in (0, 2 * chunks)
     )
     lse, delta = (
         jnp.concatenate([x[s, c : c + 1, :] for s in range(sources) for c in range(chunks)], axis=1)
@@ -162,19 +159,25 @@
             def _():
                 both(n, half)
 
-            for y in range(2):
-                some = [seen[x][y] & jnp.logical_not(every) for x in range(2)]
-                if ends:
-                    some = [z & jnp.logical_not(own) for z in some]
-
-                def single(x, _, y=y, some=some):
-                    @pl.when(jnp.where(x == 0, some[0], some[1]))
+            some = seen[0][0] | seen[0][1] | seen[1][0] | seen[1][1]
+            some = some & jnp.logical_not(every)
+            if ends:
+                some = some & jnp.logical_not(own)
+
+            @pl.when(some)
+            def _():
+                def single(at, _):
+                    x, y = at // 2, at % 2
+                    last, first = meta[2 * r + x], meta[q_blocks + 2 * r + x]
+
+                    @pl.when((base + y >= first) & (base + y <= last))
                     def _():
                         one(x, n, 2 * half + y)
 
                     return 0
 
-                lax.fori_loop(0, 2, single, 0)
+                lax.fori_loop(0, 4, single, 0)
+
             return 0
 
         lax.fori_loop(0, (r + 1) * count, inner, 0)
@@ -359,10 +362,7 @@
 
 def pieces(x):
     high = lax.reduce_precision(x, 8, 7)
-    rest = x - high
-    mid = lax.reduce_precision(rest, 8, 7)
-    low = rest - mid
-    return [part.astype(jnp.bfloat16) for part in (high, mid, low)]
+    return [part.astype(jnp.bfloat16) for part in (high, x - high)]
 
 
 def add(*terms):
@@ -422,9 +422,8 @@
 
     deltas = jnp.sum(out_grads.astype(jnp.float32) * outputs.astype(jnp.float32), axis=-1)
     stats = jnp.stack(pieces(log_norms) + pieces(deltas), axis=0)
-    stats = stats.reshape(6, tok, kv_heads, fan).transpose(2, 0, 1, 3)
-    stats = stats.reshape(kv_heads, 6 * rows // 128, 128)
-    stats = jnp.pad(stats, ((0, 0), (0, STAT_ROWS - stats.shape[1]), (0, 0)))
+    stats = stats.reshape(4, tok, kv_heads, fan).transpose(2, 0, 1, 3)
+    stats = stats.reshape(kv_heads, 4 * rows // 128, 128)
     pkg = jnp.concatenate([by_group(queries), by_group(out_grads), stats], axis=1)
     pkg = lax.all_to_all(pkg, both, 0, 0, axis_index_groups=teams, tiled=True)
 
@@ -449,7 +448,7 @@
         relayed = across(grads_3, 1)
         dq, (grads_0, grads_1, grads_2) = part((0, 1, 2), dq)
         far = add(grads_2, relayed)
-        far, *dq = lax.optimization_barrier((far, *dq))
+        far, grads_1, *dq = lax.optimization_barrier((far, grads_1, *dq))
         far = across(far, 2)
         close = across(grads_1, 1)
         dq = [lax.ppermute(x, "head", [(h, h ^ d) for h in range(n_head)]) if d else x for d, x in enumerate(dq)]

time: 89 us -> 87.5 us (0.983)
  starting transfers between devices: 30.5 us -> 24.9 us
  Pallas kernels: 10.9 us -> 13.2 us
  waiting for transfers between devices: 34.9 us -> 36.8 us
  local copies, waits for them, and re-layouts: 5.38 us -> 4.26 us
    ppermute x6, starting transfers between devices: 14.5 us -> 9.14 us  [across(): return lax.ppermute(x, 'head', [(h, h ^ step) for h in range(n_head)])]
    pallas_call x2, Pallas kernels: 8.07 us -> 10.4 us  [attention_part(): pl.pallas_call(functools.partial(planes_kernel, rows=rows, tok=tok, q_blo...]
    ppermute x6, waiting for transfers between devices: 25.2 us -> 27.5 us  [across(): return lax.ppermute(x, 'head', [(h, h ^ step) for h in range(n_head)])]
    ppermute x3, waiting for transfers between devices: 1.38 us -> 0.01 us  [per_device(): lax.ppermute(x, 'head', [(h, h ^ d) for h in range(n_head)])]
    all_to_all x1, waiting for transfers between devices: 0.56 us -> 1.71 us  [per_device(): kv = lax.all_to_all(kv, both, 0, 0, axis_index_groups=teams, tiled=True)]
    unnamed x15 -> x17, local copies, waits for them, and re-layouts: 1.81 us -> 1.06 us
  transfers between devices with their start and end apart: 13 -> 13, of which waited for: 8 -> 8; matrix products, arithmetic and copies ran while one was open for 9% -> 8% of each run, Pallas kernels for 11% -> 14%
where the time goes in v7:
time: 87.5 us; the launch traced here: 85.7 us
  waiting for transfers between devices  36.8 us (42%)
  starting transfers between devices  24.9 us (28%)
  Pallas kernels  13.2 us (15%)
  other arithmetic  5.64 us (6%)
  local copies, waits for them, and re-layouts  4.26 us (5%)
    ppermute x6, waiting for transfers between devices, across(): return lax.ppermute(x, 'head', [(h, h ^ step) for h in range(n_head)])  27.5 us
    pallas_call x2, Pallas kernels, attention_part(): pl.pallas_call(functools.partial(planes_kernel, rows=rows, tok=tok, q_blo...  10.4 us
    ppermute x6, starting transfers between devices, across(): return lax.ppermute(x, 'head', [(h, h ^ step) for h in range(n_head)])  9.14 us
    all_to_all x1, starting transfers between devices, per_device(): kv = lax.all_to_all(kv, both, 0, 0, axis_index_groups=teams, tiled=True)  5.17 us
    all_to_all x1, waiting for transfers between devices, per_device(): dkv = lax.all_to_all(dkv, both, 0, 0, axis_index_groups=teams, tiled=True)  4.61 us
    all_to_all x1, starting transfers between devices, per_device(): pkg = lax.all_to_all(pkg, both, 0, 0, axis_index_groups=teams, tiled=True)  3.61 us
    ppermute x3, starting transfers between devices, per_device(): lax.ppermute(x, 'head', [(h, h ^ d) for h in range(n_head)])  3.49 us
    all_to_all x1, starting transfers between devices, per_device(): dkv = lax.all_to_all(dkv, both, 0, 0, axis_index_groups=teams, tiled=True)  3.42 us
  transfers between devices with their start and end apart: 13, of which 8 were waited for; matrix products, arithmetic and copies ran while one was open for 8% of the time, Pallas kernels for 14%

profile of v7, /device:TPU:0, one launch (start us, length us, event | category | flops | bytes accessed | tf_op | source)
XLA Modules:
  0.0 85.7 jit_solution(13204891569277181897)
XLA Ops:
  0.6 0.0 copy-start
  0.6 0.0 copy-start.6
  0.7 0.0 copy-start.7
  0.7 1.2 %copy_bitcast_fusion.2 = (bf16[1,64,8,128]{3,1,0,2:T(8,128)(2,1)S(1)}, bf16[1,64,8,128]{3,1,0,2:T(8,128)(2,1)S(1)}) fusion(bf16[64,8,128]{2,1,0:T(8,128)(2,1)} %param.9, bf16[64,8,128]{2,1,0:T(8,128)(2,1)} %param.8), kind=kLoop, calls=%fused_computation.9 | loop fusion | bytes 524288 | tf_op jit(solution)/shard_map/stack | solution.py:409
  1.8 0.7 maximum_bitcast_fusion
  2.6 5.2 %all-to-all-start.1 = ((bf16[8,2,64,128]{3,2,1,0:T(8,128)(2,1)}), bf16[8,2,64,128]{3,2,1,0:T(8,128)(2,1)S(1)}, u32[]{:S(2)}, u32[]{:S(2)}) async-start(bf16[8,2,64,128]{3,2,1,0:T(8,128)(2,1)} %maximum_bitcast_fusion), calls=%async_computation.1 | async-start | bytes 524288 | tf_op jit(solution)/shard_map/all_to_all | solution.py:411
  7.7 0.0 copy-done.6
  7.7 1.8 %multiply_reduce_fusion = f32[64,64]{1,0:T(8,128)S(1)} fusion(bf16[64,64,128]{2,1,0:T(8,128)(2,1)} %param.10, bf16[64,64,128]{2,1,0:T(8,128)(2,1)S(1)} %copy-done.6), kind=kLoop, calls=%fused_computation.2 | loop fusion | flops 2093056 | bytes 2113536 | tf_op jit(solution)/shard_map/reduce_sum | solution.py:423
  9.6 0.1 copy.35
  9.7 0.0 copy-done.7
  9.7 0.1 copy.33
  9.8 0.3 copy.36
  10.1 0.5 reshape.244
  10.6 0.0 copy-done
  10.6 0.5 copy_bitcast_fusion
  11.1 1.5 %pad_maximum_fusion = bf16[8,1040,128]{2,1,0:T(8,128)(2,1)} fusion(bf16[8,16,128]{2,1,0:T(8,128)(2,1)S(1)} %reshape.244, bf16[8,512,128]{2,1,0:T(8,128)(2,1)S(1)} %get-tuple-element.65, bf16[8,512,128]{2,1,0:T(8,128)(2,1)S(1)} %get-tuple-element.66), kind=kLoop, calls=%fused_computation.1 | loop fusion | flops 6389760 | bytes 4259840 | tf_op jit(solution)/shard_map/concatenate | solution.py:427
  12.6 0.0 copy-start.5
  12.6 1.7 %all-to-all-done.1.refs_0_ = bf16[8,2,64,128]{3,2,1,0:T(8,128)(2,1)S(1)} async-done(((bf16[8,2,64,128]{3,2,1,0:T(8,128)(2,1)}), bf16[8,2,64,128]{3,2,1,0:T(8,128)(2,1)S(1)}, u32[]{:S(2)}, u32[]{:S(2)}) %all-to-all-start.1) | async-done | bytes 262176 | tf_op jit(solution)/shard_map/all_to_all | solution.py:411
  14.3 0.0 copy-start.1
  14.3 3.6 %all-to-all-start = ((bf16[8,1040,128]{2,1,0:T(8,128)(2,1)}), bf16[8,1040,128]{2,1,0:T(8,128)(2,1)S(1)}, u32[]{:S(2)}, u32[]{:S(2)}) async-start(bf16[8,1040,128]{2,1,0:T(8,128)(2,1)} %pad_maximum_fusion), calls=%async_computation | async-start | bytes 4259840 | tf_op jit(solution)/shard_map/all_to_all | solution.py:428
  17.9 2.7 %collective-permute-start.1 = (bf16[8,2,64,128]{3,2,1,0:T(8,128)(2,1)S(1)}, bf16[8,2,64,128]{3,2,1,0:T(8,128)(2,1)}, u32[]{:S(2)}, u32[]{:S(2)}) collective-permute-start(bf16[8,2,64,128]{3,2,1,0:T(8,128)(2,1)S(1)} %all-to-all-done.1.refs_0_), channel_id=1, source_target_pairs={{0,8},{1,9},{2,10},{3,11},{4,12},{5,13},{6,14},{7,15},{8,0},{9,1},... | collective-permute-start | bytes 786440 | tf_op jit(solution)/shard_map/ppermute | solution.py:407
  20.6 0.1 fusion.4
  20.7 0.0 copy-done.5
  20.7 0.6 gather_fusion
  21.3 0.2 convert_reduce_fusion
  21.5 0.0 copy-done.1
  21.5 1.6 %collective-permute-start = (bf16[8,2,64,128]{3,2,1,0:T(8,128)(2,1)S(1)}, bf16[8,2,64,128]{3,2,1,0:T(8,128)(2,1)}, u32[]{:S(2)}, u32[]{:S(2)}) collective-permute-start(bf16[8,2,64,128]{3,2,1,0:T(8,128)(2,1)S(1)} %all-to-all-done.1.refs_0_), channel_id=1, source_target_pairs={{0,4},{1,5},{2,6},{3,7},{4,0},{5,1},{6,2},{7,3},{8,12},{9,13},{10,... | collective-permute-start | bytes 786440 | tf_op jit(solution)/shard_map/ppermute | solution.py:407
  23.2 10.1 %collective-permute-done.1.refs_2_ = bf16[8,2,64,128]{3,2,1,0:T(8,128)(2,1)} collective-permute-done((bf16[8,2,64,128]{3,2,1,0:T(8,128)(2,1)S(1)}, bf16[8,2,64,128]{3,2,1,0:T(8,128)(2,1)}, u32[]{:S(2)}, u32[]{:S(2)}) %collective-permute-start.1) | collective-permute-done | bytes 262176 | tf_op jit(solution)/shard_map/ppermute | solution.py:407
  33.3 0.5 collective-permute-start.2
  33.8 0.1 add_subtract_fusion
  33.9 0.1 pad_add_fusion.meta
  34.0 7.3 %collective-permute-done.2.refs_0_ = bf16[8,2,64,128]{3,2,1,0:T(8,128)(2,1)} collective-permute-done((bf16[8,2,64,128]{3,2,1,0:T(8,128)(2,1)}, bf16[8,2,64,128]{3,2,1,0:T(8,128)(2,1)}, u32[]{:S(2)}, u32[]{:S(2)}) %collective-permute-start.2) | collective-permute-done | bytes 262176 | tf_op jit(solution)/shard_map/ppermute | solution.py:407
  41.3 3.0 %all-to-all-done.pkg = bf16[8,1040,128]{2,1,0:T(8,128)(2,1)S(1)} async-done(((bf16[8,1040,128]{2,1,0:T(8,128)(2,1)}), bf16[8,1040,128]{2,1,0:T(8,128)(2,1)S(1)}, u32[]{:S(2)}, u32[]{:S(2)}) %all-to-all-start) | async-done | bytes 2129952 | tf_op jit(solution)/shard_map/all_to_all | solution.py:428
  44.3 0.0 copy-start.2
  44.3 3.1 %attention_3.1 = (f32[4,1024,128]{2,1,0:T(8,128)S(1)}, bf16[8,2,64,128]{3,2,1,0:T(8,128)(2,1)S(1)}) custom-call(s32[10]{0:T(128)S(1)} %pad_add_fusion.meta, bf16[8,1040,128]{2,1,0:T(8,128)(2,1)S(1)} %all-to-all-done.pkg, bf16[8,2,64,128]{3,2,1,0:T(8,128)(2,1)} %collective-permute-done.2.refs_0_), custom_call_target="tpu_custom_call" | custom-call | flops 671088640 | bytes 4194304 | tf_op jit(solution)/shard_map/attention_3/pallas_call | solution.py:281
  47.4 1.1 %collective-permute-start.3 = (bf16[8,2,64,128]{3,2,1,0:T(8,128)(2,1)S(1)}, bf16[8,2,64,128]{3,2,1,0:T(8,128)(2,1)S(1)}, u32[]{:S(2)}, u32[]{:S(2)}) collective-permute-start(bf16[8,2,64,128]{3,2,1,0:T(8,128)(2,1)S(1)} %get-tuple-element.30), channel_id=1, source_target_pairs={{0,4},{1,5},{2,6},{3,7},{4,0},{5,1},{6,2},{7,3},{8,12},{9,13},{10,... | collective-permute-start | bytes 786440 | tf_op jit(solution)/shard_map/ppermute | solution.py:407
  48.5 0.0 collective-permute-done.refs_1_
  48.5 0.0 copy-done.2
  48.5 7.3 %attention_0_1_2.1 = (bf16[2,512,128]{2,1,0:T(8,128)(2,1)S(1)}, bf16[2,512,128]{2,1,0:T(8,128)(2,1)}, bf16[2,512,128]{2,1,0:T(8,128)(2,1)}, bf16[2,512,128]{2,1,...) custom-call(s32[10]{0:T(128)S(1)} %pad_add_fusion.meta, ...), custom_call_target="tpu_custom_call" | custom-call | flops 2013265920 | bytes 4194304 | tf_op jit(solution)/shard_map/attention_0_1_2/pallas_call | solution.py:281
  55.9 0.0 copy-start.3
  55.9 0.1 collective-permute-done.3
  56.0 0.1 add_convert_fusion.1
  56.1 3.1 %collective-permute-start.4 = (bf16[8,2,64,128]{3,2,1,0:T(8,128)(2,1)}, bf16[8,2,64,128]{3,2,1,0:T(8,128)(2,1)S(1)}, u32[]{:S(2)}, u32[]{:S(2)}) collective-permute-start(bf16[8,2,64,128]{3,2,1,0:T(8,128)(2,1)} %get-tuple-element.36), channel_id=1, source_target_pairs={{0,4},{1,5},{2,6},{3,7},{4,0},{5,1},{6,2},{7,3},{8,12},{9,13},{10,... | collective-permute-start | bytes 786440 | tf_op jit(solution)/shard_map/ppermute | solution.py:407
  59.2 0.1 collective-permute-start.5
  59.3 1.0 %collective-permute-start.6 = (bf16[2,512,128]{2,1,0:T(8,128)(2,1)}, bf16[2,512,128]{2,1,0:T(8,128)(2,1)S(1)}, u32[]{:S(2)}, u32[]{:S(2)}) collective-permute-start(bf16[2,512,128]{2,1,0:T(8,128)(2,1)} %get-tuple-element.39), channel_id=1, source_target_pairs={{0,1},{1,0},{2,3},{3,2},{4,5},{5,4},{6,7},{7,6},{8,9},{9,8},{10,11... | collective-permute-start | bytes 786440 | tf_op jit(solution)/shard_map/ppermute | solution.py:454
  60.3 0.0 copy-done.3
  60.3 0.7 collective-permute-start.7
  60.9 1.9 %collective-permute-start.8 = (bf16[2,512,128]{2,1,0:T(8,128)(2,1)}, bf16[2,512,128]{2,1,0:T(8,128)(2,1)S(1)}, u32[]{:S(2)}, u32[]{:S(2)}) collective-permute-start(bf16[2,512,128]{2,1,0:T(8,128)(2,1)} %get-tuple-element.41), channel_id=1, source_target_pairs={{0,3},{1,2},{2,1},{3,0},{4,7},{5,6},{6,5},{7,4},{8,11},{9,10},{10,... | collective-permute-start | bytes 786440 | tf_op jit(solution)/shard_map/ppermute | solution.py:454
  62.8 7.8 %collective-permute-done.4.refs_1_ = bf16[8,2,64,128]{3,2,1,0:T(8,128)(2,1)S(1)} collective-permute-done((bf16[8,2,64,128]{3,2,1,0:T(8,128)(2,1)}, bf16[8,2,64,128]{3,2,1,0:T(8,128)(2,1)S(1)}, u32[]{:S(2)}, u32[]{:S(2)}) %collective-permute-start.4) | collective-permute-done | bytes 262176 | tf_op jit(solution)/shard_map/ppermute | solution.py:407
  70.6 0.9 %copy-done.4 = bf16[8,2,64,128]{3,2,1,0:T(8,128)(2,1)S(1)} copy-done((bf16[8,2,64,128]{3,2,1,0:T(8,128)(2,1)S(1)}, bf16[8,2,64,128]{3,2,1,0:T(8,128)(2,1)}, u32[]{:S(2)}) %copy-start.4) | copy-done | bytes 262168
  71.6 0.1 sum_dkv.1
  71.6 2.1 %collective-permute-done.5 = bf16[8,2,64,128]{3,2,1,0:T(8,128)(2,1)S(1)} collective-permute-done((bf16[8,2,64,128]{3,2,1,0:T(8,128)(2,1)S(1)}, bf16[8,2,64,128]{3,2,1,0:T(8,128)(2,1)S(1)}, u32[]{:S(2)}, u32[]{:S(2)}) %collective-permute-start.5) | collective-permute-done | bytes 262176 | tf_op jit(solution)/shard_map/ppermute | solution.py:407
  73.7 0.8 add_convert_fusion
  74.5 0.0 collective-permute-done.6
  74.5 0.0 collective-permute-done.7
  74.5 0.0 collective-permute-done.8
  74.6 0.1 maximum_select_fusion
  74.8 0.1 collective-permute-start.9
  74.8 3.4 %all-to-all-start.2 = ((bf16[8,2,64,128]{3,2,1,0:T(8,128)(2,1)}), bf16[8,2,64,128]{3,2,1,0:T(8,128)(2,1)S(1)}, u32[]{:S(2)}, u32[]{:S(2)}) async-start(bf16[8,2,64,128]{3,2,1,0:T(8,128)(2,1)} %add_convert_fusion), calls=%async_computation.2 | async-start | bytes 524288 | tf_op jit(solution)/shard_map/all_to_all | solution.py:457
  78.3 0.1 pad_add_fusion.1.place
  78.3 0.0 collective-permute-done.9
  78.3 1.8 %place_dq.1 = bf16[64,8,8,128]{3,2,1,0:T(8,128)(2,1)} custom-call(s32[2]{0:T(128)S(1)} %pad_add_fusion.1.place, bf16[2,64,8,128]{3,2,1,0:T(8,128)(2,1)S(1)} %bitcast.52, bf16[2,64,8,128]{3,2,1,0:T(8,128)(2,1)S(1)} %bitcast.53, bf16[2,64,8,128]{3,2,1,0:T(8,128)(2,1)S(1)} %bitcast.54, bf16[2,64,8,128]{3,2,1,0:T(8,128)(2,1)S(1)} %bitcast.55, ...), custom_call_target="tpu_custom_call" | custom-call | tf_op jit(solution)/shard_map/place_dq/pallas_call | solution.py:329
  80.2 4.6 %all-to-all-done.2 = bf16[8,2,64,128]{3,2,1,0:T(8,128)(2,1)S(1)} async-done(((bf16[8,2,64,128]{3,2,1,0:T(8,128)(2,1)}), bf16[8,2,64,128]{3,2,1,0:T(8,128)(2,1)S(1)}, u32[]{:S(2)}, u32[]{:S(2)}) %all-to-all-start.2) | async-done | bytes 262176 | tf_op jit(solution)/shard_map/all_to_all | solution.py:457
  84.8 1.0 %place_dkv.1 = (bf16[64,8,128]{2,1,0:T(8,128)(2,1)}, bf16[64,8,128]{2,1,0:T(8,128)(2,1)}) custom-call(bf16[1,8,2,64,128]{4,3,2,1,0:T(8,128)(2,1)S(1)} %bitcast.51), custom_call_target="tpu_custom_call" | custom-call | tf_op jit(solution)/shard_map/place_dkv/pallas_call | solution.py:351
  (9 shorter events, 0.1 us)
Async XLA Ops:
  0.6 10.0 %copy-start = (bf16[64,64,128]{2,1,0:T(8,128)(2,1)S(1)}, bf16[64,64,128]{2,1,0:T(8,128)(2,1)}, u32[]{:S(2)}) copy-start(bf16[64,64,128]{2,1,0:T(8,128)(2,1)} %param.7) | copy-start | bytes 3145732
  0.6 7.1 %copy-start.6 = (bf16[64,64,128]{2,1,0:T(8,128)(2,1)S(1)}, bf16[64,64,128]{2,1,0:T(8,128)(2,1)}, u32[]{:S(2)}) copy-start(bf16[64,64,128]{2,1,0:T(8,128)(2,1)} %param.11) | copy-start | bytes 3145732
  0.7 9.0 %copy-start.7 = (f32[64,64]{1,0:T(8,128)S(1)}, f32[64,64]{1,0:T(8,128)}, u32[]{:S(2)}) copy-start(f32[64,64]{1,0:T(8,128)} %param.12) | copy-start | bytes 49156
  2.6 11.8 %all-to-all-start.1 = ((bf16[8,2,64,128]{3,2,1,0:T(8,128)(2,1)}), bf16[8,2,64,128]{3,2,1,0:T(8,128)(2,1)S(1)}, u32[]{:S(2)}, u32[]{:S(2)}) async-start(bf16[8,2,64,128]{3,2,1,0:T(8,128)(2,1)} %maximum_bitcast_fusion), calls=%async_computation.1 | async-start | bytes 524288 | tf_op jit(solution)/shard_map/all_to_all | solution.py:411
  12.6 8.1 %copy-start.5 = (s32[16]{0:T(128)S(1)}, s32[16]{0:T(128)}, u32[]{:S(2)}) copy-start(s32[16]{0:T(128)} %param.13) | copy-start | bytes 196
  14.3 7.2 %copy-start.1 = (bf16[8,2,64,128]{3,2,1,0:T(8,128)(2,1)}, bf16[8,2,64,128]{3,2,1,0:T(8,128)(2,1)S(1)}, u32[]{:S(2)}) copy-start(bf16[8,2,64,128]{3,2,1,0:T(8,128)(2,1)S(1)} %all-to-all-done.1.refs_0_) | copy-start | bytes 786436
  14.3 30.0 %all-to-all-start = ((bf16[8,1040,128]{2,1,0:T(8,128)(2,1)}), bf16[8,1040,128]{2,1,0:T(8,128)(2,1)S(1)}, u32[]{:S(2)}, u32[]{:S(2)}) async-start(bf16[8,1040,128]{2,1,0:T(8,128)(2,1)} %pad_maximum_fusion), calls=%async_computation | async-start | bytes 4259840 | tf_op jit(solution)/shard_map/all_to_all | solution.py:428
  17.9 15.3 %collective-permute-start.1 = (bf16[8,2,64,128]{3,2,1,0:T(8,128)(2,1)S(1)}, bf16[8,2,64,128]{3,2,1,0:T(8,128)(2,1)}, u32[]{:S(2)}, u32[]{:S(2)}) collective-permute-start(bf16[8,2,64,128]{3,2,1,0:T(8,128)(2,1)S(1)} %all-to-all-done.1.refs_0_), channel_id=1, source_target_pairs={{0,8},{1,9},{2,10},{3,11},{4,12},{5,13},{6,14},{7,15},{8,0},{9,1},... | collective-permute-start | bytes 786440 | tf_op jit(solution)/shard_map/ppermute | solution.py:407
  21.5 27.0 %collective-permute-start = (bf16[8,2,64,128]{3,2,1,0:T(8,128)(2,1)S(1)}, bf16[8,2,64,128]{3,2,1,0:T(8,128)(2,1)}, u32[]{:S(2)}, u32[]{:S(2)}) collective-permute-start(bf16[8,2,64,128]{3,2,1,0:T(8,128)(2,1)S(1)} %all-to-all-done.1.refs_0_), channel_id=1, source_target_pairs={{0,4},{1,5},{2,6},{3,7},{4,0},{5,1},{6,2},{7,3},{8,12},{9,13},{10,... | collective-permute-start | bytes 786440 | tf_op jit(solution)/shard_map/ppermute | solution.py:407
  33.3 8.0 %collective-permute-start.2 = (bf16[8,2,64,128]{3,2,1,0:T(8,128)(2,1)}, bf16[8,2,64,128]{3,2,1,0:T(8,128)(2,1)}, u32[]{:S(2)}, u32[]{:S(2)}) collective-permute-start(bf16[8,2,64,128]{3,2,1,0:T(8,128)(2,1)} %collective-permute-done.1.refs_2_), channel_id=1, source_target_pairs={{0,4},{1,5},{2,6},{3,7},{4,0},{5,1},{6,2},{7,3},{8,12},{9,13},{10,... | collective-permute-start | bytes 786440 | tf_op jit(solution)/shard_map/ppermute | solution.py:407
  44.3 4.2 %copy-start.2 = (bf16[8,2,64,128]{3,2,1,0:T(8,128)(2,1)S(1)}, bf16[8,2,64,128]{3,2,1,0:T(8,128)(2,1)}, u32[]{:S(2)}) copy-start(bf16[8,2,64,128]{3,2,1,0:T(8,128)(2,1)} %copy-done.1) | copy-start | bytes 786436
  47.4 8.6 %collective-permute-start.3 = (bf16[8,2,64,128]{3,2,1,0:T(8,128)(2,1)S(1)}, bf16[8,2,64,128]{3,2,1,0:T(8,128)(2,1)S(1)}, u32[]{:S(2)}, u32[]{:S(2)}) collective-permute-start(bf16[8,2,64,128]{3,2,1,0:T(8,128)(2,1)S(1)} %get-tuple-element.30), channel_id=1, source_target_pairs={{0,4},{1,5},{2,6},{3,7},{4,0},{5,1},{6,2},{7,3},{8,12},{9,13},{10,... | collective-permute-start | bytes 786440 | tf_op jit(solution)/shard_map/ppermute | solution.py:407
  55.9 4.4 %copy-start.3 = (bf16[8,2,64,128]{3,2,1,0:T(8,128)(2,1)}, bf16[8,2,64,128]{3,2,1,0:T(8,128)(2,1)S(1)}, u32[]{:S(2)}) copy-start(bf16[8,2,64,128]{3,2,1,0:T(8,128)(2,1)S(1)} %get-tuple-element.28.refs_0_) | copy-start | bytes 786436
  56.1 14.5 %collective-permute-start.4 = (bf16[8,2,64,128]{3,2,1,0:T(8,128)(2,1)}, bf16[8,2,64,128]{3,2,1,0:T(8,128)(2,1)S(1)}, u32[]{:S(2)}, u32[]{:S(2)}) collective-permute-start(bf16[8,2,64,128]{3,2,1,0:T(8,128)(2,1)} %get-tuple-element.36), channel_id=1, source_target_pairs={{0,4},{1,5},{2,6},{3,7},{4,0},{5,1},{6,2},{7,3},{8,12},{9,13},{10,... | collective-permute-start | bytes 786440 | tf_op jit(solution)/shard_map/ppermute | solution.py:407
  59.2 14.5 %collective-permute-start.5 = (bf16[8,2,64,128]{3,2,1,0:T(8,128)(2,1)S(1)}, bf16[8,2,64,128]{3,2,1,0:T(8,128)(2,1)S(1)}, u32[]{:S(2)}, u32[]{:S(2)}) collective-permute-start(bf16[8,2,64,128]{3,2,1,0:T(8,128)(2,1)S(1)} %add_convert_fusion.1), channel_id=1, source_target_pairs={{0,8},{1,9},{2,10},{3,11},{4,12},{5,13},{6,14},{7,15},{8,0},{9,1},... | collective-permute-start | bytes 786440 | tf_op jit(solution)/shard_map/ppermute | solution.py:407
  59.3 15.2 %collective-permute-start.6 = (bf16[2,512,128]{2,1,0:T(8,128)(2,1)}, bf16[2,512,128]{2,1,0:T(8,128)(2,1)S(1)}, u32[]{:S(2)}, u32[]{:S(2)}) collective-permute-start(bf16[2,512,128]{2,1,0:T(8,128)(2,1)} %get-tuple-element.39), channel_id=1, source_target_pairs={{0,1},{1,0},{2,3},{3,2},{4,5},{5,4},{6,7},{7,6},{8,9},{9,8},{10,11... | collective-permute-start | bytes 786440 | tf_op jit(solution)/shard_map/ppermute | solution.py:454
  60.3 14.2 %collective-permute-start.7 = (bf16[2,512,128]{2,1,0:T(8,128)(2,1)}, bf16[2,512,128]{2,1,0:T(8,128)(2,1)S(1)}, u32[]{:S(2)}, u32[]{:S(2)}) collective-permute-start(bf16[2,512,128]{2,1,0:T(8,128)(2,1)} %get-tuple-element.40), channel_id=1, source_target_pairs={{0,2},{1,3},{2,0},{3,1},{4,6},{5,7},{6,4},{7,5},{8,10},{9,11},{10,... | collective-permute-start | bytes 786440 | tf_op jit(solution)/shard_map/ppermute | solution.py:454
  60.9 13.6 %collective-permute-start.8 = (bf16[2,512,128]{2,1,0:T(8,128)(2,1)}, bf16[2,512,128]{2,1,0:T(8,128)(2,1)S(1)}, u32[]{:S(2)}, u32[]{:S(2)}) collective-permute-start(bf16[2,512,128]{2,1,0:T(8,128)(2,1)} %get-tuple-element.41), channel_id=1, source_target_pairs={{0,3},{1,2},{2,1},{3,0},{4,7},{5,6},{6,5},{7,4},{8,11},{9,10},{10,... | collective-permute-start | bytes 786440 | tf_op jit(solution)/shard_map/ppermute | solution.py:454
  70.6 1.0 %copy-start.4 = (bf16[8,2,64,128]{3,2,1,0:T(8,128)(2,1)S(1)}, bf16[8,2,64,128]{3,2,1,0:T(8,128)(2,1)}, u32[]{:S(2)}) copy-start(bf16[8,2,64,128]{3,2,1,0:T(8,128)(2,1)} %copy-done.3) | copy-start | bytes 786436
  74.8 3.6 %collective-permute-start.9 = (bf16[4,512,128]{2,1,0:T(8,128)(2,1)S(1)}, bf16[4,512,128]{2,1,0:T(8,128)(2,1)S(1)}, u32[]{:S(2)}, u32[]{:S(2)}) collective-permute-start(bf16[4,512,128]{2,1,0:T(8,128)(2,1)S(1)} %maximum_select_fusion), channel_id=1, source_target_pairs={{0,16},{16,0},{1,17},{17,1},{2,18},{18,2},{3,19},{19,3},{4,20},{20... | collective-permute-start | bytes 1572872 | tf_op jit(solution)/shard_map/ppermute | solution.py:459
  74.8 9.9 %all-to-all-start.2 = ((bf16[8,2,64,128]{3,2,1,0:T(8,128)(2,1)}), bf16[8,2,64,128]{3,2,1,0:T(8,128)(2,1)S(1)}, u32[]{:S(2)}, u32[]{:S(2)}) async-start(bf16[8,2,64,128]{3,2,1,0:T(8,128)(2,1)} %add_convert_fusion), calls=%async_computation.2 | async-start | bytes 524288 | tf_op jit(solution)/shard_map/all_to_all | solution.py:457

commit v8 on v7

--- a/solution.py
+++ b/solution.py
@@ -448,12 +448,14 @@
         relayed = across(grads_3, 1)
         dq, (grads_0, grads_1, grads_2) = part((0, 1, 2), dq)
         far = add(grads_2, relayed)
-        far, grads_1, *dq = lax.optimization_barrier((far, grads_1, *dq))
+        far, *dq = lax.optimization_barrier((far, *dq))
         far = across(far, 2)
         close = across(grads_1, 1)
         dq = [lax.ppermute(x, "head", [(h, h ^ d) for h in range(n_head)]) if d else x for d, x in enumerate(dq)]
-        dkv = add(sum_of(grads_0, close), far)
+        dkv = sum_of(grads_0, far)
         dkv, *dq = lax.optimization_barrier((dkv, *dq))
+        dkv, close = lax.optimization_barrier((dkv, close))
+        dkv = add(dkv, close)
         dkv = lax.all_to_all(dkv, both, 0, 0, axis_index_groups=teams, tiled=True)
         other = jnp.where(ctx == 0, jnp.stack([x[1] for x in dq]), jnp.stack([x[0] for x in dq]))
         swapped = lax.ppermute(other, "ctx", [(0, 1), (1, 0)])

time: 87.5 us -> 86.6 us (0.990); the launches traced: 85.7 us -> 86.8 us
  waiting for transfers between devices: 36.8 us -> 39.7 us
  Pallas kernels: 13.2 us -> 12 us
    ppermute x6, waiting for transfers between devices: 27.5 us -> 29.3 us  [across(): return lax.ppermute(x, 'head', [(h, h ^ step) for h in range(n_head)])]
    pallas_call x2, Pallas kernels: 10.4 us -> 9.19 us  [attention_part(): pl.pallas_call(functools.partial(planes_kernel, rows=rows, tok=tok, q_blo...]
    ppermute x3, waiting for transfers between devices: 0.01 us -> 1.07 us  [per_device(): lax.ppermute(x, 'head', [(h, h ^ d) for h in range(n_head)])]
  transfers between devices with their start and end apart: 13 -> 13, of which waited for: 8 -> 9; matrix products, arithmetic and copies ran while one was open for 8% -> 8% of each run, Pallas kernels for 14% -> 13%
where the time goes in v8:
time: 86.6 us; the launch traced here: 86.8 us
  waiting for transfers between devices  39.7 us (46%)
  starting transfers between devices  24.3 us (28%)
  Pallas kernels  12 us (14%)
  other arithmetic  5.6 us (6%)
  local copies, waits for them, and re-layouts  4.27 us (5%)
  between operations  0.9 us (1%)
    ppermute x6, waiting for transfers between devices, across(): return lax.ppermute(x, 'head', [(h, h ^ step) for h in range(n_head)])  29.3 us
    pallas_call x2, Pallas kernels, attention_part(): pl.pallas_call(functools.partial(planes_kernel, rows=rows, tok=tok, q_blo...  9.19 us
    ppermute x6, starting transfers between devices, across(): return lax.ppermute(x, 'head', [(h, h ^ step) for h in range(n_head)])  8.52 us
    all_to_all x1, starting transfers between devices, per_device(): kv = lax.all_to_all(kv, both, 0, 0, axis_index_groups=teams, tiled=True)  5.17 us
    all_to_all x1, waiting for transfers between devices, per_device(): dkv = lax.all_to_all(dkv, both, 0, 0, axis_index_groups=teams, tiled=True)  4.61 us
    all_to_all x1, starting transfers between devices, per_device(): pkg = lax.all_to_all(pkg, both, 0, 0, axis_index_groups=teams, tiled=True)  3.61 us
    ppermute x3, starting transfers between devices, per_device(): lax.ppermute(x, 'head', [(h, h ^ d) for h in range(n_head)])  3.49 us
    all_to_all x1, starting transfers between devices, per_device(): dkv = lax.all_to_all(dkv, both, 0, 0, axis_index_groups=teams, tiled=True)  3.41 us
  transfers between devices with their start and end apart: 13, of which 9 were waited for; matrix products, arithmetic and copies ran while one was open for 8% of the time, Pallas kernels for 13%

profile of v8, /device:TPU:0, one launch (start us, length us, event | category | flops | bytes accessed | tf_op | source)
XLA Modules:
  0.0 86.8 jit_solution(8304483688329397347)
XLA Ops:
  0.6 0.0 copy-start
  0.6 0.0 copy-start.7
  0.7 0.0 copy-start.8
  0.7 1.2 %copy_bitcast_fusion.2 = (bf16[1,64,8,128]{3,1,0,2:T(8,128)(2,1)S(1)}, bf16[1,64,8,128]{3,1,0,2:T(8,128)(2,1)S(1)}) fusion(bf16[64,8,128]{2,1,0:T(8,128)(2,1)} %param.9, bf16[64,8,128]{2,1,0:T(8,128)(2,1)} %param.8), kind=kLoop, calls=%fused_computation.9 | loop fusion | bytes 524288 | tf_op jit(solution)/shard_map/stack | solution.py:409
  1.8 0.7 maximum_bitcast_fusion
  2.6 5.2 %all-to-all-start.1 = ((bf16[8,2,64,128]{3,2,1,0:T(8,128)(2,1)}), bf16[8,2,64,128]{3,2,1,0:T(8,128)(2,1)S(1)}, u32[]{:S(2)}, u32[]{:S(2)}) async-start(bf16[8,2,64,128]{3,2,1,0:T(8,128)(2,1)} %maximum_bitcast_fusion), calls=%async_computation.1 | async-start | bytes 524288 | tf_op jit(solution)/shard_map/all_to_all | solution.py:411
  7.7 0.0 copy-done.7
  7.7 1.8 %multiply_reduce_fusion = f32[64,64]{1,0:T(8,128)S(1)} fusion(bf16[64,64,128]{2,1,0:T(8,128)(2,1)} %param.10, bf16[64,64,128]{2,1,0:T(8,128)(2,1)S(1)} %copy-done.7), kind=kLoop, calls=%fused_computation.2 | loop fusion | flops 2093056 | bytes 2113536 | tf_op jit(solution)/shard_map/reduce_sum | solution.py:423
  9.6 0.1 copy.35
  9.7 0.0 copy-done.8
  9.7 0.1 copy.33
  9.8 0.3 copy.36
  10.1 0.5 reshape.244
  10.6 0.0 copy-done
  10.6 0.5 copy_bitcast_fusion
  11.1 1.5 %pad_maximum_fusion = bf16[8,1040,128]{2,1,0:T(8,128)(2,1)} fusion(bf16[8,16,128]{2,1,0:T(8,128)(2,1)S(1)} %reshape.244, bf16[8,512,128]{2,1,0:T(8,128)(2,1)S(1)} %get-tuple-element.67, bf16[8,512,128]{2,1,0:T(8,128)(2,1)S(1)} %get-tuple-element.68), kind=kLoop, calls=%fused_computation.1 | loop fusion | flops 6389760 | bytes 4259840 | tf_op jit(solution)/shard_map/concatenate | solution.py:427
  12.6 0.0 copy-start.6
  12.6 1.7 %all-to-all-done.1.refs_0_ = bf16[8,2,64,128]{3,2,1,0:T(8,128)(2,1)S(1)} async-done(((bf16[8,2,64,128]{3,2,1,0:T(8,128)(2,1)}), bf16[8,2,64,128]{3,2,1,0:T(8,128)(2,1)S(1)}, u32[]{:S(2)}, u32[]{:S(2)}) %all-to-all-start.1) | async-done | bytes 262176 | tf_op jit(solution)/shard_map/all_to_all | solution.py:411
  14.3 3.6 %all-to-all-start = ((bf16[8,1040,128]{2,1,0:T(8,128)(2,1)}), bf16[8,1040,128]{2,1,0:T(8,128)(2,1)S(1)}, u32[]{:S(2)}, u32[]{:S(2)}) async-start(bf16[8,1040,128]{2,1,0:T(8,128)(2,1)} %pad_maximum_fusion), calls=%async_computation | async-start | bytes 4259840 | tf_op jit(solution)/shard_map/all_to_all | solution.py:428
  17.9 2.7 %collective-permute-start.1 = (bf16[8,2,64,128]{3,2,1,0:T(8,128)(2,1)S(1)}, bf16[8,2,64,128]{3,2,1,0:T(8,128)(2,1)}, u32[]{:S(2)}, u32[]{:S(2)}) collective-permute-start(bf16[8,2,64,128]{3,2,1,0:T(8,128)(2,1)S(1)} %all-to-all-done.1.refs_0_), channel_id=1, source_target_pairs={{0,8},{1,9},{2,10},{3,11},{4,12},{5,13},{6,14},{7,15},{8,0},{9,1},... | collective-permute-start | bytes 786440 | tf_op jit(solution)/shard_map/ppermute | solution.py:407
  20.6 0.1 fusion.4
  20.7 0.0 copy-done.6
  20.7 0.6 gather_fusion
  21.3 0.2 convert_reduce_fusion
  21.5 0.0 copy-done.1
  21.5 1.6 %collective-permute-start = (bf16[8,2,64,128]{3,2,1,0:T(8,128)(2,1)S(1)}, bf16[8,2,64,128]{3,2,1,0:T(8,128)(2,1)}, u32[]{:S(2)}, u32[]{:S(2)}) collective-permute-start(bf16[8,2,64,128]{3,2,1,0:T(8,128)(2,1)S(1)} %all-to-all-done.1.refs_0_), channel_id=1, source_target_pairs={{0,4},{1,5},{2,6},{3,7},{4,0},{5,1},{6,2},{7,3},{8,12},{9,13},{10,... | collective-permute-start | bytes 786440 | tf_op jit(solution)/shard_map/ppermute | solution.py:407
  23.2 10.1 %collective-permute-done.1.refs_2_ = bf16[8,2,64,128]{3,2,1,0:T(8,128)(2,1)} collective-permute-done((bf16[8,2,64,128]{3,2,1,0:T(8,128)(2,1)S(1)}, bf16[8,2,64,128]{3,2,1,0:T(8,128)(2,1)}, u32[]{:S(2)}, u32[]{:S(2)}) %collective-permute-start.1) | collective-permute-done | bytes 262176 | tf_op jit(solution)/shard_map/ppermute | solution.py:407
  33.3 0.5 collective-permute-start.2
  33.8 0.1 add_subtract_fusion
  33.9 0.1 pad_add_fusion.meta
  34.0 7.3 %collective-permute-done.2.refs_0_ = bf16[8,2,64,128]{3,2,1,0:T(8,128)(2,1)} collective-permute-done((bf16[8,2,64,128]{3,2,1,0:T(8,128)(2,1)}, bf16[8,2,64,128]{3,2,1,0:T(8,128)(2,1)}, u32[]{:S(2)}, u32[]{:S(2)}) %collective-permute-start.2) | collective-permute-done | bytes 262176 | tf_op jit(solution)/shard_map/ppermute | solution.py:407
  41.3 3.0 %all-to-all-done.pkg = bf16[8,1040,128]{2,1,0:T(8,128)(2,1)S(1)} async-done(((bf16[8,1040,128]{2,1,0:T(8,128)(2,1)}), bf16[8,1040,128]{2,1,0:T(8,128)(2,1)S(1)}, u32[]{:S(2)}, u32[]{:S(2)}) %all-to-all-start) | async-done | bytes 2129952 | tf_op jit(solution)/shard_map/all_to_all | solution.py:428
  44.3 3.1 %attention_3.1 = (f32[4,1024,128]{2,1,0:T(8,128)S(1)}, bf16[8,2,64,128]{3,2,1,0:T(8,128)(2,1)S(1)}) custom-call(s32[10]{0:T(128)S(1)} %pad_add_fusion.meta, bf16[8,1040,128]{2,1,0:T(8,128)(2,1)S(1)} %all-to-all-done.pkg, bf16[8,2,64,128]{3,2,1,0:T(8,128)(2,1)} %collective-permute-done.2.refs_0_), custom_call_target="tpu_custom_call" | custom-call | flops 671088640 | bytes 4194304 | tf_op jit(solution)/shard_map/attention_3/pallas_call | solution.py:281
  47.4 0.1 collective-permute-start.3
  47.5 0.0 collective-permute-done.refs_1_
  47.5 0.0 copy-done.2
  47.5 6.1 %attention_0_1_2.1 = (bf16[2,512,128]{2,1,0:T(8,128)(2,1)S(1)}, bf16[2,512,128]{2,1,0:T(8,128)(2,1)}, bf16[2,512,128]{2,1,0:T(8,128)(2,1)}, bf16[2,512,128]{2,1,...) custom-call(s32[10]{0:T(128)S(1)} %pad_add_fusion.meta, ...), custom_call_target="tpu_custom_call" | custom-call | flops 2013265920 | bytes 4194304 | tf_op jit(solution)/shard_map/attention_0_1_2/pallas_call | solution.py:281
  53.6 0.0 copy-start.3
  53.6 0.0 copy-start.5
  53.6 2.4 %collective-permute-done.3 = bf16[8,2,64,128]{3,2,1,0:T(8,128)(2,1)S(1)} collective-permute-done((bf16[8,2,64,128]{3,2,1,0:T(8,128)(2,1)S(1)}, bf16[8,2,64,128]{3,2,1,0:T(8,128)(2,1)S(1)}, u32[]{:S(2)}, u32[]{:S(2)}) %collective-permute-start.3) | collective-permute-done | bytes 262176 | tf_op jit(solution)/shard_map/ppermute | solution.py:407
  56.0 0.1 add_convert_fusion.1
  56.1 3.6 %collective-permute-start.4 = (bf16[8,2,64,128]{3,2,1,0:T(8,128)(2,1)S(1)}, bf16[8,2,64,128]{3,2,1,0:T(8,128)(2,1)S(1)}, u32[]{:S(2)}, u32[]{:S(2)}) collective-permute-start(bf16[8,2,64,128]{3,2,1,0:T(8,128)(2,1)S(1)} %add_convert_fusion.1), channel_id=1, source_target_pairs={{0,8},{1,9},{2,10},{3,11},{4,12},{5,13},{6,14},{7,15},{8,0},{9,1},... | collective-permute-start | bytes 786440 | tf_op jit(solution)/shard_map/ppermute | solution.py:407
  59.7 1.0 %collective-permute-start.5 = (bf16[2,512,128]{2,1,0:T(8,128)(2,1)}, bf16[2,512,128]{2,1,0:T(8,128)(2,1)S(1)}, u32[]{:S(2)}, u32[]{:S(2)}) collective-permute-start(bf16[2,512,128]{2,1,0:T(8,128)(2,1)} %get-tuple-element.38), channel_id=1, source_target_pairs={{0,1},{1,0},{2,3},{3,2},{4,5},{5,4},{6,7},{7,6},{8,9},{9,8},{10,11... | collective-permute-start | bytes 786440 | tf_op jit(solution)/shard_map/ppermute | solution.py:454
  60.7 0.0 copy-done.3
  60.7 0.7 collective-permute-start.6
  61.3 0.0 copy-done.5
  61.3 1.9 %collective-permute-start.7 = (bf16[2,512,128]{2,1,0:T(8,128)(2,1)}, bf16[2,512,128]{2,1,0:T(8,128)(2,1)S(1)}, u32[]{:S(2)}, u32[]{:S(2)}) collective-permute-start(bf16[2,512,128]{2,1,0:T(8,128)(2,1)} %get-tuple-element.40), channel_id=1, source_target_pairs={{0,3},{1,2},{2,1},{3,0},{4,7},{5,6},{6,5},{7,4},{8,11},{9,10},{10,... | collective-permute-start | bytes 786440 | tf_op jit(solution)/shard_map/ppermute | solution.py:454
  63.2 0.0 collective-permute-start.8
  63.2 9.0 %collective-permute-done.4.refs_1_ = bf16[8,2,64,128]{3,2,1,0:T(8,128)(2,1)S(1)} collective-permute-done((bf16[8,2,64,128]{3,2,1,0:T(8,128)(2,1)S(1)}, bf16[8,2,64,128]{3,2,1,0:T(8,128)(2,1)S(1)}, u32[]{:S(2)}, u32[]{:S(2)}) %collective-permute-start.4) | collective-permute-done | bytes 262176 | tf_op jit(solution)/shard_map/ppermute | solution.py:407
  72.2 0.9 %copy-done.4 = bf16[8,2,64,128]{3,2,1,0:T(8,128)(2,1)S(1)} copy-done((bf16[8,2,64,128]{3,2,1,0:T(8,128)(2,1)S(1)}, bf16[8,2,64,128]{3,2,1,0:T(8,128)(2,1)}, u32[]{:S(2)}) %copy-start.4) | copy-done | bytes 262168
  73.1 0.1 sum_dkv.1
  73.2 0.0 collective-permute-done.5
  73.2 1.1 %collective-permute-done.6 = bf16[2,512,128]{2,1,0:T(8,128)(2,1)S(1)} collective-permute-done((bf16[2,512,128]{2,1,0:T(8,128)(2,1)}, bf16[2,512,128]{2,1,0:T(8,128)(2,1)S(1)}, u32[]{:S(2)}, u32[]{:S(2)}) %collective-permute-start.6) | collective-permute-done | bytes 262176 | tf_op jit(solution)/shard_map/ppermute | solution.py:454
  74.3 0.0 collective-permute-done.7
  74.4 0.1 maximum_select_fusion
  74.5 0.1 collective-permute-start.9
  74.6 0.5 collective-permute-done.8
  75.1 0.8 add_convert_fusion
  75.9 3.4 %all-to-all-start.2 = ((bf16[8,2,64,128]{3,2,1,0:T(8,128)(2,1)}), bf16[8,2,64,128]{3,2,1,0:T(8,128)(2,1)S(1)}, u32[]{:S(2)}, u32[]{:S(2)}) async-start(bf16[8,2,64,128]{3,2,1,0:T(8,128)(2,1)} %add_convert_fusion), calls=%async_computation.2 | async-start | bytes 524288 | tf_op jit(solution)/shard_map/all_to_all | solution.py:459
  79.3 0.1 pad_add_fusion.1.place
  79.4 0.0 collective-permute-done.9
  79.4 1.8 %place_dq.1 = bf16[64,8,8,128]{3,2,1,0:T(8,128)(2,1)} custom-call(s32[2]{0:T(128)S(1)} %pad_add_fusion.1.place, bf16[2,64,8,128]{3,2,1,0:T(8,128)(2,1)S(1)} %bitcast.52, bf16[2,64,8,128]{3,2,1,0:T(8,128)(2,1)S(1)} %bitcast.53, bf16[2,64,8,128]{3,2,1,0:T(8,128)(2,1)S(1)} %bitcast.54, bf16[2,64,8,128]{3,2,1,0:T(8,128)(2,1)S(1)} %bitcast.55, ...), custom_call_target="tpu_custom_call" | custom-call | tf_op jit(solution)/shard_map/place_dq/pallas_call | solution.py:329
  81.2 4.6 %all-to-all-done.2 = bf16[8,2,64,128]{3,2,1,0:T(8,128)(2,1)S(1)} async-done(((bf16[8,2,64,128]{3,2,1,0:T(8,128)(2,1)}), bf16[8,2,64,128]{3,2,1,0:T(8,128)(2,1)S(1)}, u32[]{:S(2)}, u32[]{:S(2)}) %all-to-all-start.2) | async-done | bytes 262176 | tf_op jit(solution)/shard_map/all_to_all | solution.py:459
  85.8 1.0 %place_dkv.1 = (bf16[64,8,128]{2,1,0:T(8,128)(2,1)}, bf16[64,8,128]{2,1,0:T(8,128)(2,1)}) custom-call(bf16[1,8,2,64,128]{4,3,2,1,0:T(8,128)(2,1)S(1)} %bitcast.51), custom_call_target="tpu_custom_call" | custom-call | tf_op jit(solution)/shard_map/place_dkv/pallas_call | solution.py:351
  (11 shorter events, 0.1 us)
Async XLA Ops:
  0.6 10.0 %copy-start = (bf16[64,64,128]{2,1,0:T(8,128)(2,1)S(1)}, bf16[64,64,128]{2,1,0:T(8,128)(2,1)}, u32[]{:S(2)}) copy-start(bf16[64,64,128]{2,1,0:T(8,128)(2,1)} %param.7) | copy-start | bytes 3145732
  0.6 7.1 %copy-start.7 = (bf16[64,64,128]{2,1,0:T(8,128)(2,1)S(1)}, bf16[64,64,128]{2,1,0:T(8,128)(2,1)}, u32[]{:S(2)}) copy-start(bf16[64,64,128]{2,1,0:T(8,128)(2,1)} %param.11) | copy-start | bytes 3145732
  0.7 9.0 %copy-start.8 = (f32[64,64]{1,0:T(8,128)S(1)}, f32[64,64]{1,0:T(8,128)}, u32[]{:S(2)}) copy-start(f32[64,64]{1,0:T(8,128)} %param.12) | copy-start | bytes 49156
  2.6 11.8 %all-to-all-start.1 = ((bf16[8,2,64,128]{3,2,1,0:T(8,128)(2,1)}), bf16[8,2,64,128]{3,2,1,0:T(8,128)(2,1)S(1)}, u32[]{:S(2)}, u32[]{:S(2)}) async-start(bf16[8,2,64,128]{3,2,1,0:T(8,128)(2,1)} %maximum_bitcast_fusion), calls=%async_computation.1 | async-start | bytes 524288 | tf_op jit(solution)/shard_map/all_to_all | solution.py:411
  12.6 8.1 %copy-start.6 = (s32[16]{0:T(128)S(1)}, s32[16]{0:T(128)}, u32[]{:S(2)}) copy-start(s32[16]{0:T(128)} %param.13) | copy-start | bytes 196
  14.3 7.2 %copy-start.1 = (bf16[8,2,64,128]{3,2,1,0:T(8,128)(2,1)}, bf16[8,2,64,128]{3,2,1,0:T(8,128)(2,1)S(1)}, u32[]{:S(2)}) copy-start(bf16[8,2,64,128]{3,2,1,0:T(8,128)(2,1)S(1)} %all-to-all-done.1.refs_0_) | copy-start | bytes 786436
  14.3 30.0 %all-to-all-start = ((bf16[8,1040,128]{2,1,0:T(8,128)(2,1)}), bf16[8,1040,128]{2,1,0:T(8,128)(2,1)S(1)}, u32[]{:S(2)}, u32[]{:S(2)}) async-start(bf16[8,1040,128]{2,1,0:T(8,128)(2,1)} %pad_maximum_fusion), calls=%async_computation | async-start | bytes 4259840 | tf_op jit(solution)/shard_map/all_to_all | solution.py:428
  17.9 15.3 %collective-permute-start.1 = (bf16[8,2,64,128]{3,2,1,0:T(8,128)(2,1)S(1)}, bf16[8,2,64,128]{3,2,1,0:T(8,128)(2,1)}, u32[]{:S(2)}, u32[]{:S(2)}) collective-permute-start(bf16[8,2,64,128]{3,2,1,0:T(8,128)(2,1)S(1)} %all-to-all-done.1.refs_0_), channel_id=1, source_target_pairs={{0,8},{1,9},{2,10},{3,11},{4,12},{5,13},{6,14},{7,15},{8,0},{9,1},... | collective-permute-start | bytes 786440 | tf_op jit(solution)/shard_map/ppermute | solution.py:407
  21.5 26.0 %collective-permute-start = (bf16[8,2,64,128]{3,2,1,0:T(8,128)(2,1)S(1)}, bf16[8,2,64,128]{3,2,1,0:T(8,128)(2,1)}, u32[]{:S(2)}, u32[]{:S(2)}) collective-permute-start(bf16[8,2,64,128]{3,2,1,0:T(8,128)(2,1)S(1)} %all-to-all-done.1.refs_0_), channel_id=1, source_target_pairs={{0,4},{1,5},{2,6},{3,7},{4,0},{5,1},{6,2},{7,3},{8,12},{9,13},{10,... | collective-permute-start | bytes 786440 | tf_op jit(solution)/shard_map/ppermute | solution.py:407
  33.3 8.0 %collective-permute-start.2 = (bf16[8,2,64,128]{3,2,1,0:T(8,128)(2,1)}, bf16[8,2,64,128]{3,2,1,0:T(8,128)(2,1)}, u32[]{:S(2)}, u32[]{:S(2)}) collective-permute-start(bf16[8,2,64,128]{3,2,1,0:T(8,128)(2,1)} %collective-permute-done.1.refs_2_), channel_id=1, source_target_pairs={{0,4},{1,5},{2,6},{3,7},{4,0},{5,1},{6,2},{7,3},{8,12},{9,13},{10,... | collective-permute-start | bytes 786440 | tf_op jit(solution)/shard_map/ppermute | solution.py:407
  44.3 3.2 %copy-start.2 = (bf16[8,2,64,128]{3,2,1,0:T(8,128)(2,1)S(1)}, bf16[8,2,64,128]{3,2,1,0:T(8,128)(2,1)}, u32[]{:S(2)}) copy-start(bf16[8,2,64,128]{3,2,1,0:T(8,128)(2,1)} %copy-done.1) | copy-start | bytes 786436
  47.4 8.6 %collective-permute-start.3 = (bf16[8,2,64,128]{3,2,1,0:T(8,128)(2,1)S(1)}, bf16[8,2,64,128]{3,2,1,0:T(8,128)(2,1)S(1)}, u32[]{:S(2)}, u32[]{:S(2)}) collective-permute-start(bf16[8,2,64,128]{3,2,1,0:T(8,128)(2,1)S(1)} %get-tuple-element.31), channel_id=1, source_target_pairs={{0,4},{1,5},{2,6},{3,7},{4,0},{5,1},{6,2},{7,3},{8,12},{9,13},{10,... | collective-permute-start | bytes 786440 | tf_op jit(solution)/shard_map/ppermute | solution.py:407
  53.6 7.1 %copy-start.3 = (bf16[8,2,64,128]{3,2,1,0:T(8,128)(2,1)}, bf16[8,2,64,128]{3,2,1,0:T(8,128)(2,1)S(1)}, u32[]{:S(2)}) copy-start(bf16[8,2,64,128]{3,2,1,0:T(8,128)(2,1)S(1)} %get-tuple-element.29.refs_0_) | copy-start | bytes 786436
  53.6 7.7 %copy-start.5 = (bf16[8,2,64,128]{3,2,1,0:T(8,128)(2,1)}, bf16[8,2,64,128]{3,2,1,0:T(8,128)(2,1)S(1)}, u32[]{:S(2)}) copy-start(bf16[8,2,64,128]{3,2,1,0:T(8,128)(2,1)S(1)} %get-tuple-element.42) | copy-start | bytes 786436
  56.1 16.1 %collective-permute-start.4 = (bf16[8,2,64,128]{3,2,1,0:T(8,128)(2,1)S(1)}, bf16[8,2,64,128]{3,2,1,0:T(8,128)(2,1)S(1)}, u32[]{:S(2)}, u32[]{:S(2)}) collective-permute-start(bf16[8,2,64,128]{3,2,1,0:T(8,128)(2,1)S(1)} %add_convert_fusion.1), channel_id=1, source_target_pairs={{0,8},{1,9},{2,10},{3,11},{4,12},{5,13},{6,14},{7,15},{8,0},{9,1},... | collective-permute-start | bytes 786440 | tf_op jit(solution)/shard_map/ppermute | solution.py:407
  59.7 13.5 %collective-permute-start.5 = (bf16[2,512,128]{2,1,0:T(8,128)(2,1)}, bf16[2,512,128]{2,1,0:T(8,128)(2,1)S(1)}, u32[]{:S(2)}, u32[]{:S(2)}) collective-permute-start(bf16[2,512,128]{2,1,0:T(8,128)(2,1)} %get-tuple-element.38), channel_id=1, source_target_pairs={{0,1},{1,0},{2,3},{3,2},{4,5},{5,4},{6,7},{7,6},{8,9},{9,8},{10,11... | collective-permute-start | bytes 786440 | tf_op jit(solution)/shard_map/ppermute | solution.py:454
  60.7 13.6 %collective-permute-start.6 = (bf16[2,512,128]{2,1,0:T(8,128)(2,1)}, bf16[2,512,128]{2,1,0:T(8,128)(2,1)S(1)}, u32[]{:S(2)}, u32[]{:S(2)}) collective-permute-start(bf16[2,512,128]{2,1,0:T(8,128)(2,1)} %get-tuple-element.39), channel_id=1, source_target_pairs={{0,2},{1,3},{2,0},{3,1},{4,6},{5,7},{6,4},{7,5},{8,10},{9,11},{10,... | collective-permute-start | bytes 786440 | tf_op jit(solution)/shard_map/ppermute | solution.py:454
  61.3 12.9 %collective-permute-start.7 = (bf16[2,512,128]{2,1,0:T(8,128)(2,1)}, bf16[2,512,128]{2,1,0:T(8,128)(2,1)S(1)}, u32[]{:S(2)}, u32[]{:S(2)}) collective-permute-start(bf16[2,512,128]{2,1,0:T(8,128)(2,1)} %get-tuple-element.40), channel_id=1, source_target_pairs={{0,3},{1,2},{2,1},{3,0},{4,7},{5,6},{6,5},{7,4},{8,11},{9,10},{10,... | collective-permute-start | bytes 786440 | tf_op jit(solution)/shard_map/ppermute | solution.py:454
  63.2 11.9 %collective-permute-start.8 = (bf16[8,2,64,128]{3,2,1,0:T(8,128)(2,1)}, bf16[8,2,64,128]{3,2,1,0:T(8,128)(2,1)S(1)}, u32[]{:S(2)}, u32[]{:S(2)}) collective-permute-start(bf16[8,2,64,128]{3,2,1,0:T(8,128)(2,1)} %copy-done.5), channel_id=1, source_target_pairs={{0,4},{1,5},{2,6},{3,7},{4,0},{5,1},{6,2},{7,3},{8,12},{9,13},{10,... | collective-permute-start | bytes 786440 | tf_op jit(solution)/shard_map/ppermute | solution.py:407
  72.2 1.0 %copy-start.4 = (bf16[8,2,64,128]{3,2,1,0:T(8,128)(2,1)S(1)}, bf16[8,2,64,128]{3,2,1,0:T(8,128)(2,1)}, u32[]{:S(2)}) copy-start(bf16[8,2,64,128]{3,2,1,0:T(8,128)(2,1)} %copy-done.3) | copy-start | bytes 786436
  74.5 4.9 %collective-permute-start.9 = (bf16[4,512,128]{2,1,0:T(8,128)(2,1)S(1)}, bf16[4,512,128]{2,1,0:T(8,128)(2,1)S(1)}, u32[]{:S(2)}, u32[]{:S(2)}) collective-permute-start(bf16[4,512,128]{2,1,0:T(8,128)(2,1)S(1)} %maximum_select_fusion), channel_id=1, source_target_pairs={{0,16},{16,0},{1,17},{17,1},{2,18},{18,2},{3,19},{19,3},{4,20},{20... | collective-permute-start | bytes 1572872 | tf_op jit(solution)/shard_map/ppermute | solution.py:461
  75.9 9.9 %all-to-all-start.2 = ((bf16[8,2,64,128]{3,2,1,0:T(8,128)(2,1)}), bf16[8,2,64,128]{3,2,1,0:T(8,128)(2,1)S(1)}, u32[]{:S(2)}, u32[]{:S(2)}) async-start(bf16[8,2,64,128]{3,2,1,0:T(8,128)(2,1)} %add_convert_fusion), calls=%async_computation.2 | async-start | bytes 524288 | tf_op jit(solution)/shard_map/all_to_all | solution.py:459

commit v9 on v8

--- a/solution.py
+++ b/solution.py
@@ -10,7 +10,7 @@
 BLK = 128
 LOG2E = 1.4426950408889634
 LIMIT = 56 * 1024 * 1024
-PART_LIMIT = 12 * 1024 * 1024
+PART_LIMIT = 20 * 1024 * 1024
 SMALL_LIMIT = 6 * 1024 * 1024
 
 
@@ -108,6 +108,9 @@
         for copy in loads:
             copy.wait()
 
+    def dq_store(b, d):
+        return pltpu.make_async_copy(dq.at[b * slots + (slot ^ d)], dq_out[d].at[b], out_sems.at[b, d])
+
     def over_range(r, _):
         lasts = [meta[2 * r + x] for x in range(2)]
         firsts = [meta[q_blocks + 2 * r + x] for x in range(2)]
@@ -196,17 +199,13 @@
                 dq[pl.ds(sources * (2 * r + x), sources)] = done
             else:
                 dq_out[0][2 * r + x] = dq_acc[x]
+        if ends:
+            for d in range(slots):
+                dq_store(r, d).start()
         return 0
 
     lax.fori_loop(0, 2, over_range, 0)
-    if ends:
-        stores = [
-            pltpu.make_async_copy(dq.at[b * slots + (slot ^ d)], dq_out[d].at[b], out_sems.at[b, d])
-            for b in range(2)
-            for d in range(slots)
-        ]
-        for copy in stores:
-            copy.start()
+    stores = [dq_store(b, d) for b in range(2) for d in range(slots)] if ends else []
     if not ends:
         grads_out[0][:, 0] = (dk_acc[0] * scale).astype(jnp.bfloat16).reshape(team, tok, 128)
         grads_out[0][:, 1] = dv_acc[0].astype(jnp.bfloat16).reshape(team, tok, 128)
@@ -298,22 +297,6 @@
     return (dq if ends else dq[0]), grads
 
 
-def sum_kernel(*refs):
-    *terms, out = refs
-    out[...] = sum(x[...].astype(jnp.float32) for x in terms)
-
-
-def sum_of(*terms):
-    return pl.pallas_call(
-        sum_kernel,
-        out_shape=jax.ShapeDtypeStruct(terms[0].shape, jnp.float32),
-        in_specs=[VMEM] * len(terms),
-        out_specs=VMEM,
-        compiler_params=pltpu.CompilerParams(vmem_limit_bytes=SMALL_LIMIT),
-        name="sum_dkv",
-    )(*terms)
-
-
 def place_dq_kernel(place, *refs):
     *arrived, swapped, out = refs
     slots = len(arrived)
@@ -452,7 +435,7 @@
         far = across(far, 2)
         close = across(grads_1, 1)
         dq = [lax.ppermute(x, "head", [(h, h ^ d) for h in range(n_head)]) if d else x for d, x in enumerate(dq)]
-        dkv = sum_of(grads_0, far)
+        dkv = grads_0.astype(jnp.float32) + far.astype(jnp.float32)
         dkv, *dq = lax.optimization_barrier((dkv, *dq))
         dkv, close = lax.optimization_barrier((dkv, close))
         dkv = add(dkv, close)

time: 86.6 us -> 86.9 us (level)
  waiting for transfers between devices: 39.7 us -> 34.3 us
  Pallas kernels: 12 us -> 15.3 us
  starting transfers between devices: 24.3 us -> 26.4 us
  other arithmetic: 5.6 us -> 6.62 us
  local copies, waits for them, and re-layouts: 4.27 us -> 3.32 us
    ppermute x6, waiting for transfers between devices: 29.3 us -> 24.8 us  [across(): return lax.ppermute(x, 'head', [(h, h ^ step) for h in range(n_head)])]
    pallas_call x2, Pallas kernels: 9.19 us -> 12.5 us  [attention_part(): pl.pallas_call(functools.partial(planes_kernel, rows=rows, tok=tok, q_blo...]
    ppermute x6, starting transfers between devices: 8.52 us -> 10.7 us  [across(): return lax.ppermute(x, 'head', [(h, h ^ step) for h in range(n_head)])]
    add x0 -> x1, other arithmetic: none -> 1.01 us  [per_device(): dkv = grads_0.astype(jnp.float32) + far.astype(jnp.float32)]
    unnamed x19 -> x17, local copies, waits for them, and re-layouts: 1.06 us -> 0.11 us
    ppermute x3, waiting for transfers between devices: 1.07 us -> 0.15 us  [per_device(): lax.ppermute(x, 'head', [(h, h ^ d) for h in range(n_head)])]
  transfers between devices with their start and end apart: 13 -> 13, of which waited for: 9 -> 8; matrix products, arithmetic and copies ran while one was open for 8% -> 9% of each run, Pallas kernels for 13% -> 16%
where the time goes in v9:
time: 86.9 us; the launch traced here: 86.8 us
  waiting for transfers between devices  34.3 us (39%)
  starting transfers between devices  26.4 us (30%)
  Pallas kernels  15.3 us (18%)
  other arithmetic  6.62 us (8%)
  local copies, waits for them, and re-layouts  3.32 us (4%)
  between operations  0.91 us (1%)
    ppermute x6, waiting for transfers between devices, across(): return lax.ppermute(x, 'head', [(h, h ^ step) for h in range(n_head)])  24.8 us
    pallas_call x2, Pallas kernels, attention_part(): pl.pallas_call(functools.partial(planes_kernel, rows=rows, tok=tok, q_blo...  12.5 us
    ppermute x6, starting transfers between devices, across(): return lax.ppermute(x, 'head', [(h, h ^ step) for h in range(n_head)])  10.7 us
    all_to_all x1, starting transfers between devices, per_device(): kv = lax.all_to_all(kv, both, 0, 0, axis_index_groups=teams, tiled=True)  5.17 us
    all_to_all x1, waiting for transfers between devices, per_device(): dkv = lax.all_to_all(dkv, both, 0, 0, axis_index_groups=teams, tiled=True)  4.61 us
    all_to_all x1, starting transfers between devices, per_device(): pkg = lax.all_to_all(pkg, both, 0, 0, axis_index_groups=teams, tiled=True)  3.61 us
    ppermute x3, starting transfers between devices, per_device(): lax.ppermute(x, 'head', [(h, h ^ d) for h in range(n_head)])  3.49 us
    all_to_all x1, starting transfers between devices, per_device(): dkv = lax.all_to_all(dkv, both, 0, 0, axis_index_groups=teams, tiled=True)  3.41 us
  transfers between devices with their start and end apart: 13, of which 8 were waited for; matrix products, arithmetic and copies ran while one was open for 9% of the time, Pallas kernels for 16%

profile of v9, /device:TPU:0, one launch (start us, length us, event | category | flops | bytes accessed | tf_op | source)
XLA Modules:
  0.0 86.8 jit_solution(2881044033208783147)
XLA Ops:
  0.6 0.0 copy-start
  0.6 0.0 copy-start.6
  0.7 0.0 copy-start.7
  0.7 1.2 %copy_bitcast_fusion.2 = (bf16[1,64,8,128]{3,1,0,2:T(8,128)(2,1)S(1)}, bf16[1,64,8,128]{3,1,0,2:T(8,128)(2,1)S(1)}) fusion(bf16[64,8,128]{2,1,0:T(8,128)(2,1)} %param.9, bf16[64,8,128]{2,1,0:T(8,128)(2,1)} %param.8), kind=kLoop, calls=%fused_computation.10 | loop fusion | bytes 524288 | tf_op jit(solution)/shard_map/stack | solution.py:392
  1.8 0.7 maximum_bitcast_fusion
  2.6 5.2 %all-to-all-start.1 = ((bf16[8,2,64,128]{3,2,1,0:T(8,128)(2,1)}), bf16[8,2,64,128]{3,2,1,0:T(8,128)(2,1)S(1)}, u32[]{:S(2)}, u32[]{:S(2)}) async-start(bf16[8,2,64,128]{3,2,1,0:T(8,128)(2,1)} %maximum_bitcast_fusion), calls=%async_computation.1 | async-start | bytes 524288 | tf_op jit(solution)/shard_map/all_to_all | solution.py:394
  7.7 0.0 copy-done.6
  7.7 1.8 %multiply_reduce_fusion = f32[64,64]{1,0:T(8,128)S(1)} fusion(bf16[64,64,128]{2,1,0:T(8,128)(2,1)} %param.10, bf16[64,64,128]{2,1,0:T(8,128)(2,1)S(1)} %copy-done.6), kind=kLoop, calls=%fused_computation.2 | loop fusion | flops 2093056 | bytes 2113536 | tf_op jit(solution)/shard_map/reduce_sum | solution.py:406
  9.6 0.1 copy.35
  9.7 0.0 copy-done.7
  9.7 0.1 copy.33
  9.8 0.3 copy.36
  10.1 0.5 reshape.244
  10.6 0.0 copy-done
  10.6 0.5 copy_bitcast_fusion
  11.1 1.5 %pad_maximum_fusion = bf16[8,1040,128]{2,1,0:T(8,128)(2,1)} fusion(bf16[8,16,128]{2,1,0:T(8,128)(2,1)S(1)} %reshape.244, bf16[8,512,128]{2,1,0:T(8,128)(2,1)S(1)} %get-tuple-element.67, bf16[8,512,128]{2,1,0:T(8,128)(2,1)S(1)} %get-tuple-element.68), kind=kLoop, calls=%fused_computation.1 | loop fusion | flops 6389760 | bytes 4259840 | tf_op jit(solution)/shard_map/concatenate | solution.py:410
  12.6 0.0 copy-start.5
  12.6 1.7 %all-to-all-done.1.refs_0_ = bf16[8,2,64,128]{3,2,1,0:T(8,128)(2,1)S(1)} async-done(((bf16[8,2,64,128]{3,2,1,0:T(8,128)(2,1)}), bf16[8,2,64,128]{3,2,1,0:T(8,128)(2,1)S(1)}, u32[]{:S(2)}, u32[]{:S(2)}) %all-to-all-start.1) | async-done | bytes 262176 | tf_op jit(solution)/shard_map/all_to_all | solution.py:394
  14.3 0.0 copy-start.1
  14.3 3.6 %all-to-all-start = ((bf16[8,1040,128]{2,1,0:T(8,128)(2,1)}), bf16[8,1040,128]{2,1,0:T(8,128)(2,1)S(1)}, u32[]{:S(2)}, u32[]{:S(2)}) async-start(bf16[8,1040,128]{2,1,0:T(8,128)(2,1)} %pad_maximum_fusion), calls=%async_computation | async-start | bytes 4259840 | tf_op jit(solution)/shard_map/all_to_all | solution.py:411
  17.9 2.7 %collective-permute-start.1 = (bf16[8,2,64,128]{3,2,1,0:T(8,128)(2,1)S(1)}, bf16[8,2,64,128]{3,2,1,0:T(8,128)(2,1)}, u32[]{:S(2)}, u32[]{:S(2)}) collective-permute-start(bf16[8,2,64,128]{3,2,1,0:T(8,128)(2,1)S(1)} %all-to-all-done.1.refs_0_), channel_id=1, source_target_pairs={{0,8},{1,9},{2,10},{3,11},{4,12},{5,13},{6,14},{7,15},{8,0},{9,1},... | collective-permute-start | bytes 786440 | tf_op jit(solution)/shard_map/ppermute | solution.py:390
  20.6 0.1 fusion.4
  20.7 0.0 copy-done.5
  20.7 0.6 gather_fusion
  21.3 0.2 convert_reduce_fusion
  21.5 0.0 copy-done.1
  21.5 1.6 %collective-permute-start = (bf16[8,2,64,128]{3,2,1,0:T(8,128)(2,1)S(1)}, bf16[8,2,64,128]{3,2,1,0:T(8,128)(2,1)}, u32[]{:S(2)}, u32[]{:S(2)}) collective-permute-start(bf16[8,2,64,128]{3,2,1,0:T(8,128)(2,1)S(1)} %all-to-all-done.1.refs_0_), channel_id=1, source_target_pairs={{0,4},{1,5},{2,6},{3,7},{4,0},{5,1},{6,2},{7,3},{8,12},{9,13},{10,... | collective-permute-start | bytes 786440 | tf_op jit(solution)/shard_map/ppermute | solution.py:390
  23.2 10.1 %collective-permute-done.1.refs_2_ = bf16[8,2,64,128]{3,2,1,0:T(8,128)(2,1)} collective-permute-done((bf16[8,2,64,128]{3,2,1,0:T(8,128)(2,1)S(1)}, bf16[8,2,64,128]{3,2,1,0:T(8,128)(2,1)}, u32[]{:S(2)}, u32[]{:S(2)}) %collective-permute-start.1) | collective-permute-done | bytes 262176 | tf_op jit(solution)/shard_map/ppermute | solution.py:390
  33.3 0.5 collective-permute-start.2
  33.8 0.1 add_subtract_fusion
  33.9 0.1 pad_add_fusion.meta
  34.0 7.3 %collective-permute-done.2.refs_0_ = bf16[8,2,64,128]{3,2,1,0:T(8,128)(2,1)} collective-permute-done((bf16[8,2,64,128]{3,2,1,0:T(8,128)(2,1)}, bf16[8,2,64,128]{3,2,1,0:T(8,128)(2,1)}, u32[]{:S(2)}, u32[]{:S(2)}) %collective-permute-start.2) | collective-permute-done | bytes 262176 | tf_op jit(solution)/shard_map/ppermute | solution.py:390
  41.3 3.0 %all-to-all-done.pkg = bf16[8,1040,128]{2,1,0:T(8,128)(2,1)S(1)} async-done(((bf16[8,1040,128]{2,1,0:T(8,128)(2,1)}), bf16[8,1040,128]{2,1,0:T(8,128)(2,1)S(1)}, u32[]{:S(2)}, u32[]{:S(2)}) %all-to-all-start) | async-done | bytes 2129952 | tf_op jit(solution)/shard_map/all_to_all | solution.py:411
  44.3 3.1 %attention_3.1 = (f32[4,1024,128]{2,1,0:T(8,128)S(1)}, bf16[8,2,64,128]{3,2,1,0:T(8,128)(2,1)S(1)}) custom-call(s32[10]{0:T(128)S(1)} %pad_add_fusion.meta, bf16[8,1040,128]{2,1,0:T(8,128)(2,1)S(1)} %all-to-all-done.pkg, bf16[8,2,64,128]{3,2,1,0:T(8,128)(2,1)} %collective-permute-done.2.refs_0_), custom_call_target="tpu_custom_call" | custom-call | flops 671088640 | bytes 4194304 | tf_op jit(solution)/shard_map/attention_3/pallas_call | solution.py:280
  47.4 0.1 collective-permute-start.3
  47.5 0.0 collective-permute-done.refs_1_
  47.5 0.0 copy-done.2
  47.5 9.4 %attention_0_1_2.1 = (bf16[2,512,128]{2,1,0:T(8,128)(2,1)S(1)}, bf16[2,512,128]{2,1,0:T(8,128)(2,1)}, bf16[2,512,128]{2,1,0:T(8,128)(2,1)}, bf16[2,512,128]{2,1,...) custom-call(s32[10]{0:T(128)S(1)} %pad_add_fusion.meta, ...), custom_call_target="tpu_custom_call" | custom-call | flops 2013265920 | bytes 4194304 | tf_op jit(solution)/shard_map/attention_0_1_2/pallas_call | solution.py:280
  56.9 0.0 copy-start.3
  56.9 0.0 copy-start.4
  57.0 0.0 collective-permute-done.3
  57.0 0.1 add_convert_fusion.1
  57.0 2.8 %collective-permute-start.4 = (bf16[8,2,64,128]{3,2,1,0:T(8,128)(2,1)S(1)}, bf16[8,2,64,128]{3,2,1,0:T(8,128)(2,1)S(1)}, u32[]{:S(2)}, u32[]{:S(2)}) collective-permute-start(bf16[8,2,64,128]{3,2,1,0:T(8,128)(2,1)S(1)} %add_convert_fusion.1), channel_id=1, source_target_pairs={{0,8},{1,9},{2,10},{3,11},{4,12},{5,13},{6,14},{7,15},{8,0},{9,1},... | collective-permute-start | bytes 786440 | tf_op jit(solution)/shard_map/ppermute | solution.py:390
  59.9 0.8 collective-permute-start.5
  60.7 0.0 copy-done.3
  60.7 0.4 collective-permute-start.6
  61.0 0.0 copy-done.4
  61.0 2.3 %collective-permute-start.7 = (bf16[2,512,128]{2,1,0:T(8,128)(2,1)}, bf16[2,512,128]{2,1,0:T(8,128)(2,1)S(1)}, u32[]{:S(2)}, u32[]{:S(2)}) collective-permute-start(bf16[2,512,128]{2,1,0:T(8,128)(2,1)} %get-tuple-element.40), channel_id=1, source_target_pairs={{0,3},{1,2},{2,1},{3,0},{4,7},{5,6},{6,5},{7,4},{8,11},{9,10},{10,... | collective-permute-start | bytes 786440 | tf_op jit(solution)/shard_map/ppermute | solution.py:437
  63.3 3.0 %collective-permute-start.8 = (bf16[8,2,64,128]{3,2,1,0:T(8,128)(2,1)}, bf16[8,2,64,128]{3,2,1,0:T(8,128)(2,1)S(1)}, u32[]{:S(2)}, u32[]{:S(2)}) collective-permute-start(bf16[8,2,64,128]{3,2,1,0:T(8,128)(2,1)} %copy-done.4), channel_id=1, source_target_pairs={{0,4},{1,5},{2,6},{3,7},{4,0},{5,1},{6,2},{7,3},{8,12},{9,13},{10,... | collective-permute-start | bytes 786440 | tf_op jit(solution)/shard_map/ppermute | solution.py:390
  66.3 5.9 %collective-permute-done.4 = bf16[8,2,64,128]{3,2,1,0:T(8,128)(2,1)S(1)} collective-permute-done((bf16[8,2,64,128]{3,2,1,0:T(8,128)(2,1)S(1)}, bf16[8,2,64,128]{3,2,1,0:T(8,128)(2,1)S(1)}, u32[]{:S(2)}, u32[]{:S(2)}) %collective-permute-start.4) | collective-permute-done | bytes 262176 | tf_op jit(solution)/shard_map/ppermute | solution.py:390
  72.2 1.0 %convert_add_fusion = f32[8,2,64,128]{3,2,1,0:T(8,128)S(1)} fusion(bf16[8,2,64,128]{3,2,1,0:T(8,128)(2,1)S(1)} %collective-permute-done.4, bf16[8,2,64,128]{3,2,1,0:T(8,128)(2,1)} %copy-done.3), kind=kLoop, calls=%fused_computation.7 | loop fusion | flops 393216 | bytes 1048576 | tf_op jit(solution)/shard_map/add | solution.py:438
  73.3 0.0 collective-permute-done.5
  73.3 0.1 collective-permute-done.6
  73.4 0.0 collective-permute-done.7
  73.5 0.1 maximum_select_fusion
  73.6 0.1 collective-permute-start.9
  73.7 1.4 %collective-permute-done.8 = bf16[8,2,64,128]{3,2,1,0:T(8,128)(2,1)S(1)} collective-permute-done((bf16[8,2,64,128]{3,2,1,0:T(8,128)(2,1)}, bf16[8,2,64,128]{3,2,1,0:T(8,128)(2,1)S(1)}, u32[]{:S(2)}, u32[]{:S(2)}) %collective-permute-start.8) | collective-permute-done | bytes 262176 | tf_op jit(solution)/shard_map/ppermute | solution.py:390
  75.2 0.8 add_convert_fusion
  75.9 3.4 %all-to-all-start.2 = ((bf16[8,2,64,128]{3,2,1,0:T(8,128)(2,1)}), bf16[8,2,64,128]{3,2,1,0:T(8,128)(2,1)S(1)}, u32[]{:S(2)}, u32[]{:S(2)}) async-start(bf16[8,2,64,128]{3,2,1,0:T(8,128)(2,1)} %add_convert_fusion), calls=%async_computation.2 | async-start | bytes 524288 | tf_op jit(solution)/shard_map/all_to_all | solution.py:442
  79.4 0.1 pad_add_fusion.1.place
  79.4 0.0 collective-permute-done.9
  79.4 1.8 %place_dq.1 = bf16[64,8,8,128]{3,2,1,0:T(8,128)(2,1)} custom-call(s32[2]{0:T(128)S(1)} %pad_add_fusion.1.place, bf16[2,64,8,128]{3,2,1,0:T(8,128)(2,1)S(1)} %bitcast.52, bf16[2,64,8,128]{3,2,1,0:T(8,128)(2,1)S(1)} %bitcast.53, bf16[2,64,8,128]{3,2,1,0:T(8,128)(2,1)S(1)} %bitcast.54, bf16[2,64,8,128]{3,2,1,0:T(8,128)(2,1)S(1)} %bitcast.55, ...), custom_call_target="tpu_custom_call" | custom-call | tf_op jit(solution)/shard_map/place_dq/pallas_call | solution.py:312
  81.3 4.6 %all-to-all-done.2 = bf16[8,2,64,128]{3,2,1,0:T(8,128)(2,1)S(1)} async-done(((bf16[8,2,64,128]{3,2,1,0:T(8,128)(2,1)}), bf16[8,2,64,128]{3,2,1,0:T(8,128)(2,1)S(1)}, u32[]{:S(2)}, u32[]{:S(2)}) %all-to-all-start.2) | async-done | bytes 262176 | tf_op jit(solution)/shard_map/all_to_all | solution.py:442
  85.9 1.0 %place_dkv.1 = (bf16[64,8,128]{2,1,0:T(8,128)(2,1)}, bf16[64,8,128]{2,1,0:T(8,128)(2,1)}) custom-call(bf16[1,8,2,64,128]{4,3,2,1,0:T(8,128)(2,1)S(1)} %bitcast.51), custom_call_target="tpu_custom_call" | custom-call | tf_op jit(solution)/shard_map/place_dkv/pallas_call | solution.py:334
  (9 shorter events, 0.1 us)
Async XLA Ops:
  0.6 10.0 %copy-start = (bf16[64,64,128]{2,1,0:T(8,128)(2,1)S(1)}, bf16[64,64,128]{2,1,0:T(8,128)(2,1)}, u32[]{:S(2)}) copy-start(bf16[64,64,128]{2,1,0:T(8,128)(2,1)} %param.7) | copy-start | bytes 3145732
  0.6 7.1 %copy-start.6 = (bf16[64,64,128]{2,1,0:T(8,128)(2,1)S(1)}, bf16[64,64,128]{2,1,0:T(8,128)(2,1)}, u32[]{:S(2)}) copy-start(bf16[64,64,128]{2,1,0:T(8,128)(2,1)} %param.11) | copy-start | bytes 3145732
  0.7 9.0 %copy-start.7 = (f32[64,64]{1,0:T(8,128)S(1)}, f32[64,64]{1,0:T(8,128)}, u32[]{:S(2)}) copy-start(f32[64,64]{1,0:T(8,128)} %param.12) | copy-start | bytes 49156
  2.6 11.8 %all-to-all-start.1 = ((bf16[8,2,64,128]{3,2,1,0:T(8,128)(2,1)}), bf16[8,2,64,128]{3,2,1,0:T(8,128)(2,1)S(1)}, u32[]{:S(2)}, u32[]{:S(2)}) async-start(bf16[8,2,64,128]{3,2,1,0:T(8,128)(2,1)} %maximum_bitcast_fusion), calls=%async_computation.1 | async-start | bytes 524288 | tf_op jit(solution)/shard_map/all_to_all | solution.py:394
  12.6 8.1 %copy-start.5 = (s32[16]{0:T(128)S(1)}, s32[16]{0:T(128)}, u32[]{:S(2)}) copy-start(s32[16]{0:T(128)} %param.13) | copy-start | bytes 196
  14.3 7.2 %copy-start.1 = (bf16[8,2,64,128]{3,2,1,0:T(8,128)(2,1)}, bf16[8,2,64,128]{3,2,1,0:T(8,128)(2,1)S(1)}, u32[]{:S(2)}) copy-start(bf16[8,2,64,128]{3,2,1,0:T(8,128)(2,1)S(1)} %all-to-all-done.1.refs_0_) | copy-start | bytes 786436
  14.3 30.0 %all-to-all-start = ((bf16[8,1040,128]{2,1,0:T(8,128)(2,1)}), bf16[8,1040,128]{2,1,0:T(8,128)(2,1)S(1)}, u32[]{:S(2)}, u32[]{:S(2)}) async-start(bf16[8,1040,128]{2,1,0:T(8,128)(2,1)} %pad_maximum_fusion), calls=%async_computation | async-start | bytes 4259840 | tf_op jit(solution)/shard_map/all_to_all | solution.py:411
  17.9 15.3 %collective-permute-start.1 = (bf16[8,2,64,128]{3,2,1,0:T(8,128)(2,1)S(1)}, bf16[8,2,64,128]{3,2,1,0:T(8,128)(2,1)}, u32[]{:S(2)}, u32[]{:S(2)}) collective-permute-start(bf16[8,2,64,128]{3,2,1,0:T(8,128)(2,1)S(1)} %all-to-all-done.1.refs_0_), channel_id=1, source_target_pairs={{0,8},{1,9},{2,10},{3,11},{4,12},{5,13},{6,14},{7,15},{8,0},{9,1},... | collective-permute-start | bytes 786440 | tf_op jit(solution)/shard_map/ppermute | solution.py:390
  21.5 26.0 %collective-permute-start = (bf16[8,2,64,128]{3,2,1,0:T(8,128)(2,1)S(1)}, bf16[8,2,64,128]{3,2,1,0:T(8,128)(2,1)}, u32[]{:S(2)}, u32[]{:S(2)}) collective-permute-start(bf16[8,2,64,128]{3,2,1,0:T(8,128)(2,1)S(1)} %all-to-all-done.1.refs_0_), channel_id=1, source_target_pairs={{0,4},{1,5},{2,6},{3,7},{4,0},{5,1},{6,2},{7,3},{8,12},{9,13},{10,... | collective-permute-start | bytes 786440 | tf_op jit(solution)/shard_map/ppermute | solution.py:390
  33.3 8.0 %collective-permute-start.2 = (bf16[8,2,64,128]{3,2,1,0:T(8,128)(2,1)}, bf16[8,2,64,128]{3,2,1,0:T(8,128)(2,1)}, u32[]{:S(2)}, u32[]{:S(2)}) collective-permute-start(bf16[8,2,64,128]{3,2,1,0:T(8,128)(2,1)} %collective-permute-done.1.refs_2_), channel_id=1, source_target_pairs={{0,4},{1,5},{2,6},{3,7},{4,0},{5,1},{6,2},{7,3},{8,12},{9,13},{10,... | collective-permute-start | bytes 786440 | tf_op jit(solution)/shard_map/ppermute | solution.py:390
  44.3 3.2 %copy-start.2 = (bf16[8,2,64,128]{3,2,1,0:T(8,128)(2,1)S(1)}, bf16[8,2,64,128]{3,2,1,0:T(8,128)(2,1)}, u32[]{:S(2)}) copy-start(bf16[8,2,64,128]{3,2,1,0:T(8,128)(2,1)} %copy-done.1) | copy-start | bytes 786436
  47.4 9.5 %collective-permute-start.3 = (bf16[8,2,64,128]{3,2,1,0:T(8,128)(2,1)S(1)}, bf16[8,2,64,128]{3,2,1,0:T(8,128)(2,1)S(1)}, u32[]{:S(2)}, u32[]{:S(2)}) collective-permute-start(bf16[8,2,64,128]{3,2,1,0:T(8,128)(2,1)S(1)} %get-tuple-element.31), channel_id=1, source_target_pairs={{0,4},{1,5},{2,6},{3,7},{4,0},{5,1},{6,2},{7,3},{8,12},{9,13},{10,... | collective-permute-start | bytes 786440 | tf_op jit(solution)/shard_map/ppermute | solution.py:390
  56.9 3.7 %copy-start.3 = (bf16[8,2,64,128]{3,2,1,0:T(8,128)(2,1)}, bf16[8,2,64,128]{3,2,1,0:T(8,128)(2,1)S(1)}, u32[]{:S(2)}) copy-start(bf16[8,2,64,128]{3,2,1,0:T(8,128)(2,1)S(1)} %get-tuple-element.29) | copy-start | bytes 786436
  56.9 4.1 %copy-start.4 = (bf16[8,2,64,128]{3,2,1,0:T(8,128)(2,1)}, bf16[8,2,64,128]{3,2,1,0:T(8,128)(2,1)S(1)}, u32[]{:S(2)}) copy-start(bf16[8,2,64,128]{3,2,1,0:T(8,128)(2,1)S(1)} %get-tuple-element.42) | copy-start | bytes 786436
  57.0 15.2 %collective-permute-start.4 = (bf16[8,2,64,128]{3,2,1,0:T(8,128)(2,1)S(1)}, bf16[8,2,64,128]{3,2,1,0:T(8,128)(2,1)S(1)}, u32[]{:S(2)}, u32[]{:S(2)}) collective-permute-start(bf16[8,2,64,128]{3,2,1,0:T(8,128)(2,1)S(1)} %add_convert_fusion.1), channel_id=1, source_target_pairs={{0,8},{1,9},{2,10},{3,11},{4,12},{5,13},{6,14},{7,15},{8,0},{9,1},... | collective-permute-start | bytes 786440 | tf_op jit(solution)/shard_map/ppermute | solution.py:390
  59.9 13.4 %collective-permute-start.5 = (bf16[2,512,128]{2,1,0:T(8,128)(2,1)}, bf16[2,512,128]{2,1,0:T(8,128)(2,1)S(1)}, u32[]{:S(2)}, u32[]{:S(2)}) collective-permute-start(bf16[2,512,128]{2,1,0:T(8,128)(2,1)} %get-tuple-element.38), channel_id=1, source_target_pairs={{0,1},{1,0},{2,3},{3,2},{4,5},{5,4},{6,7},{7,6},{8,9},{9,8},{10,11... | collective-permute-start | bytes 786440 | tf_op jit(solution)/shard_map/ppermute | solution.py:437
  60.7 12.8 %collective-permute-start.6 = (bf16[2,512,128]{2,1,0:T(8,128)(2,1)}, bf16[2,512,128]{2,1,0:T(8,128)(2,1)S(1)}, u32[]{:S(2)}, u32[]{:S(2)}) collective-permute-start(bf16[2,512,128]{2,1,0:T(8,128)(2,1)} %get-tuple-element.39), channel_id=1, source_target_pairs={{0,2},{1,3},{2,0},{3,1},{4,6},{5,7},{6,4},{7,5},{8,10},{9,11},{10,... | collective-permute-start | bytes 786440 | tf_op jit(solution)/shard_map/ppermute | solution.py:437
  61.0 12.4 %collective-permute-start.7 = (bf16[2,512,128]{2,1,0:T(8,128)(2,1)}, bf16[2,512,128]{2,1,0:T(8,128)(2,1)S(1)}, u32[]{:S(2)}, u32[]{:S(2)}) collective-permute-start(bf16[2,512,128]{2,1,0:T(8,128)(2,1)} %get-tuple-element.40), channel_id=1, source_target_pairs={{0,3},{1,2},{2,1},{3,0},{4,7},{5,6},{6,5},{7,4},{8,11},{9,10},{10,... | collective-permute-start | bytes 786440 | tf_op jit(solution)/shard_map/ppermute | solution.py:437
  63.3 11.8 %collective-permute-start.8 = (bf16[8,2,64,128]{3,2,1,0:T(8,128)(2,1)}, bf16[8,2,64,128]{3,2,1,0:T(8,128)(2,1)S(1)}, u32[]{:S(2)}, u32[]{:S(2)}) collective-permute-start(bf16[8,2,64,128]{3,2,1,0:T(8,128)(2,1)} %copy-done.4), channel_id=1, source_target_pairs={{0,4},{1,5},{2,6},{3,7},{4,0},{5,1},{6,2},{7,3},{8,12},{9,13},{10,... | collective-permute-start | bytes 786440 | tf_op jit(solution)/shard_map/ppermute | solution.py:390
  73.6 5.8 %collective-permute-start.9 = (bf16[4,512,128]{2,1,0:T(8,128)(2,1)S(1)}, bf16[4,512,128]{2,1,0:T(8,128)(2,1)S(1)}, u32[]{:S(2)}, u32[]{:S(2)}) collective-permute-start(bf16[4,512,128]{2,1,0:T(8,128)(2,1)S(1)} %maximum_select_fusion), channel_id=1, source_target_pairs={{0,16},{16,0},{1,17},{17,1},{2,18},{18,2},{3,19},{19,3},{4,20},{20... | collective-permute-start | bytes 1572872 | tf_op jit(solution)/shard_map/ppermute | solution.py:444
  75.9 9.9 %all-to-all-start.2 = ((bf16[8,2,64,128]{3,2,1,0:T(8,128)(2,1)}), bf16[8,2,64,128]{3,2,1,0:T(8,128)(2,1)S(1)}, u32[]{:S(2)}, u32[]{:S(2)}) async-start(bf16[8,2,64,128]{3,2,1,0:T(8,128)(2,1)} %add_convert_fusion), calls=%async_computation.2 | async-start | bytes 524288 | tf_op jit(solution)/shard_map/all_to_all | solution.py:442

commit v10 on v9

--- a/solution.py
+++ b/solution.py
@@ -105,8 +105,7 @@
         loads = [pltpu.make_async_copy(near[n], kv.at[n], kv_sems.at[n]) for n in range(count)]
         for copy in loads:
             copy.start()
-        for copy in loads:
-            copy.wait()
+        loads[distances.index(0)].wait()
 
     def dq_store(b, d):
         return pltpu.make_async_copy(dq.at[b * slots + (slot ^ d)], dq_out[d].at[b], out_sems.at[b, d])
@@ -183,7 +182,6 @@
 
             return 0
 
-        lax.fori_loop(0, (r + 1) * count, inner, 0)
         if ends:
             n = distances.index(0)
             from_key = jnp.where(firsts[1] <= lasts[0], 0, BLK)
@@ -193,6 +191,15 @@
             dq_acc[1] += dq_1
             add_keys(n, 2 * r, dk + dk_1[0:BLK], dv + dv_1[0:BLK])
             add_keys(n, 2 * r + 1, dk_1[BLK:], dv_1[BLK:])
+        if ends:
+
+            @pl.when(r == 0)
+            def _():
+                for n, copy in enumerate(loads):
+                    if distances[n] != 0:
+                        copy.wait()
+
+        lax.fori_loop(0, (r + 1) * count, inner, 0)
         for x in range(2):
             if ends:
                 done = (dq_acc[x] * scale).astype(jnp.bfloat16).reshape(sources, rows, 128)

time: 86.9 us -> 85.4 us (0.983)
  Pallas kernels: 15.3 us -> 14.3 us
    pallas_call x2, Pallas kernels: 12.5 us -> 11.5 us  [attention_part(): pl.pallas_call(functools.partial(planes_kernel, rows=rows, tok=tok, q_blo...]
  transfers between devices with their start and end apart: 13 -> 13, of which waited for: 8 -> 9; matrix products, arithmetic and copies ran while one was open for 9% -> 9% of each run, Pallas kernels for 16% -> 15%
where the time goes in v10:
time: 85.4 us; the launch traced here: 85.8 us
  waiting for transfers between devices  34.9 us (41%)
  starting transfers between devices  25.8 us (30%)
  Pallas kernels  14.3 us (17%)
  other arithmetic  6.62 us (8%)
  local copies, waits for them, and re-layouts  3.32 us (4%)
  between operations  0.9 us (1%)
    ppermute x6, waiting for transfers between devices, across(): return lax.ppermute(x, 'head', [(h, h ^ step) for h in range(n_head)])  25.5 us
    pallas_call x2, Pallas kernels, attention_part(): pl.pallas_call(functools.partial(planes_kernel, rows=rows, tok=tok, q_blo...  11.5 us
    ppermute x6, starting transfers between devices, across(): return lax.ppermute(x, 'head', [(h, h ^ step) for h in range(n_head)])  10.1 us
    all_to_all x1, starting transfers between devices, per_device(): kv = lax.all_to_all(kv, both, 0, 0, axis_index_groups=teams, tiled=True)  5.17 us
    all_to_all x1, waiting for transfers between devices, per_device(): dkv = lax.all_to_all(dkv, both, 0, 0, axis_index_groups=teams, tiled=True)  4.61 us
    all_to_all x1, starting transfers between devices, per_device(): pkg = lax.all_to_all(pkg, both, 0, 0, axis_index_groups=teams, tiled=True)  3.61 us
    ppermute x3, starting transfers between devices, per_device(): lax.ppermute(x, 'head', [(h, h ^ d) for h in range(n_head)])  3.49 us
    all_to_all x1, starting transfers between devices, per_device(): dkv = lax.all_to_all(dkv, both, 0, 0, axis_index_groups=teams, tiled=True)  3.41 us
  transfers between devices with their start and end apart: 13, of which 9 were waited for; matrix products, arithmetic and copies ran while one was open for 9% of the time, Pallas kernels for 15%

profile of v10, /device:TPU:0, one launch (start us, length us, event | category | flops | bytes accessed | tf_op | source)
XLA Modules:
  0.0 85.8 jit_solution(13121722439651044103)
XLA Ops:
  0.6 0.0 copy-start
  0.6 0.0 copy-start.6
  0.7 0.0 copy-start.7
  0.7 1.2 %copy_bitcast_fusion.2 = (bf16[1,64,8,128]{3,1,0,2:T(8,128)(2,1)S(1)}, bf16[1,64,8,128]{3,1,0,2:T(8,128)(2,1)S(1)}) fusion(bf16[64,8,128]{2,1,0:T(8,128)(2,1)} %param.9, bf16[64,8,128]{2,1,0:T(8,128)(2,1)} %param.8), kind=kLoop, calls=%fused_computation.10 | loop fusion | bytes 524288 | tf_op jit(solution)/shard_map/stack | solution.py:399
  1.8 0.7 maximum_bitcast_fusion
  2.6 5.2 %all-to-all-start.1 = ((bf16[8,2,64,128]{3,2,1,0:T(8,128)(2,1)}), bf16[8,2,64,128]{3,2,1,0:T(8,128)(2,1)S(1)}, u32[]{:S(2)}, u32[]{:S(2)}) async-start(bf16[8,2,64,128]{3,2,1,0:T(8,128)(2,1)} %maximum_bitcast_fusion), calls=%async_computation.1 | async-start | bytes 524288 | tf_op jit(solution)/shard_map/all_to_all | solution.py:401
  7.7 0.0 copy-done.6
  7.7 1.8 %multiply_reduce_fusion = f32[64,64]{1,0:T(8,128)S(1)} fusion(bf16[64,64,128]{2,1,0:T(8,128)(2,1)} %param.10, bf16[64,64,128]{2,1,0:T(8,128)(2,1)S(1)} %copy-done.6), kind=kLoop, calls=%fused_computation.2 | loop fusion | flops 2093056 | bytes 2113536 | tf_op jit(solution)/shard_map/reduce_sum | solution.py:413
  9.6 0.1 copy.35
  9.7 0.0 copy-done.7
  9.7 0.1 copy.33
  9.8 0.3 copy.36
  10.1 0.5 reshape.244
  10.6 0.0 copy-done
  10.6 0.5 copy_bitcast_fusion
  11.1 1.5 %pad_maximum_fusion = bf16[8,1040,128]{2,1,0:T(8,128)(2,1)} fusion(bf16[8,16,128]{2,1,0:T(8,128)(2,1)S(1)} %reshape.244, bf16[8,512,128]{2,1,0:T(8,128)(2,1)S(1)} %get-tuple-element.67, bf16[8,512,128]{2,1,0:T(8,128)(2,1)S(1)} %get-tuple-element.68), kind=kLoop, calls=%fused_computation.1 | loop fusion | flops 6389760 | bytes 4259840 | tf_op jit(solution)/shard_map/concatenate | solution.py:417
  12.6 0.0 copy-start.5
  12.6 1.7 %all-to-all-done.1.refs_0_ = bf16[8,2,64,128]{3,2,1,0:T(8,128)(2,1)S(1)} async-done(((bf16[8,2,64,128]{3,2,1,0:T(8,128)(2,1)}), bf16[8,2,64,128]{3,2,1,0:T(8,128)(2,1)S(1)}, u32[]{:S(2)}, u32[]{:S(2)}) %all-to-all-start.1) | async-done | bytes 262176 | tf_op jit(solution)/shard_map/all_to_all | solution.py:401
  14.3 0.0 copy-start.1
  14.3 3.6 %all-to-all-start = ((bf16[8,1040,128]{2,1,0:T(8,128)(2,1)}), bf16[8,1040,128]{2,1,0:T(8,128)(2,1)S(1)}, u32[]{:S(2)}, u32[]{:S(2)}) async-start(bf16[8,1040,128]{2,1,0:T(8,128)(2,1)} %pad_maximum_fusion), calls=%async_computation | async-start | bytes 4259840 | tf_op jit(solution)/shard_map/all_to_all | solution.py:418
  17.9 2.7 %collective-permute-start.1 = (bf16[8,2,64,128]{3,2,1,0:T(8,128)(2,1)S(1)}, bf16[8,2,64,128]{3,2,1,0:T(8,128)(2,1)}, u32[]{:S(2)}, u32[]{:S(2)}) collective-permute-start(bf16[8,2,64,128]{3,2,1,0:T(8,128)(2,1)S(1)} %all-to-all-done.1.refs_0_), channel_id=1, source_target_pairs={{0,8},{1,9},{2,10},{3,11},{4,12},{5,13},{6,14},{7,15},{8,0},{9,1},... | collective-permute-start | bytes 786440 | tf_op jit(solution)/shard_map/ppermute | solution.py:397
  20.6 0.1 fusion.4
  20.7 0.0 copy-done.5
  20.7 0.6 gather_fusion
  21.3 0.2 convert_reduce_fusion
  21.5 0.0 copy-done.1
  21.5 1.6 %collective-permute-start = (bf16[8,2,64,128]{3,2,1,0:T(8,128)(2,1)S(1)}, bf16[8,2,64,128]{3,2,1,0:T(8,128)(2,1)}, u32[]{:S(2)}, u32[]{:S(2)}) collective-permute-start(bf16[8,2,64,128]{3,2,1,0:T(8,128)(2,1)S(1)} %all-to-all-done.1.refs_0_), channel_id=1, source_target_pairs={{0,4},{1,5},{2,6},{3,7},{4,0},{5,1},{6,2},{7,3},{8,12},{9,13},{10,... | collective-permute-start | bytes 786440 | tf_op jit(solution)/shard_map/ppermute | solution.py:397
  23.2 10.1 %collective-permute-done.1.refs_2_ = bf16[8,2,64,128]{3,2,1,0:T(8,128)(2,1)} collective-permute-done((bf16[8,2,64,128]{3,2,1,0:T(8,128)(2,1)S(1)}, bf16[8,2,64,128]{3,2,1,0:T(8,128)(2,1)}, u32[]{:S(2)}, u32[]{:S(2)}) %collective-permute-start.1) | collective-permute-done | bytes 262176 | tf_op jit(solution)/shard_map/ppermute | solution.py:397
  33.3 0.5 collective-permute-start.2
  33.8 0.1 add_subtract_fusion
  33.9 0.1 pad_add_fusion.meta
  34.0 7.3 %collective-permute-done.2.refs_0_ = bf16[8,2,64,128]{3,2,1,0:T(8,128)(2,1)} collective-permute-done((bf16[8,2,64,128]{3,2,1,0:T(8,128)(2,1)}, bf16[8,2,64,128]{3,2,1,0:T(8,128)(2,1)}, u32[]{:S(2)}, u32[]{:S(2)}) %collective-permute-start.2) | collective-permute-done | bytes 262176 | tf_op jit(solution)/shard_map/ppermute | solution.py:397
  41.3 3.0 %all-to-all-done.pkg = bf16[8,1040,128]{2,1,0:T(8,128)(2,1)S(1)} async-done(((bf16[8,1040,128]{2,1,0:T(8,128)(2,1)}), bf16[8,1040,128]{2,1,0:T(8,128)(2,1)S(1)}, u32[]{:S(2)}, u32[]{:S(2)}) %all-to-all-start) | async-done | bytes 2129952 | tf_op jit(solution)/shard_map/all_to_all | solution.py:418
  44.3 3.1 %attention_3.1 = (f32[4,1024,128]{2,1,0:T(8,128)S(1)}, bf16[8,2,64,128]{3,2,1,0:T(8,128)(2,1)S(1)}) custom-call(s32[10]{0:T(128)S(1)} %pad_add_fusion.meta, bf16[8,1040,128]{2,1,0:T(8,128)(2,1)S(1)} %all-to-all-done.pkg, bf16[8,2,64,128]{3,2,1,0:T(8,128)(2,1)} %collective-permute-done.2.refs_0_), custom_call_target="tpu_custom_call" | custom-call | flops 671088640 | bytes 4194304 | tf_op jit(solution)/shard_map/attention_3/pallas_call | solution.py:287
  47.4 0.1 collective-permute-start.3
  47.5 0.0 collective-permute-done.refs_1_
  47.5 0.0 copy-done.2
  47.5 8.4 %attention_0_1_2.1 = (bf16[2,512,128]{2,1,0:T(8,128)(2,1)S(1)}, bf16[2,512,128]{2,1,0:T(8,128)(2,1)}, bf16[2,512,128]{2,1,0:T(8,128)(2,1)}, bf16[2,512,128]{2,1,...) custom-call(s32[10]{0:T(128)S(1)} %pad_add_fusion.meta, ...), custom_call_target="tpu_custom_call" | custom-call | flops 2013265920 | bytes 4194304 | tf_op jit(solution)/shard_map/attention_0_1_2/pallas_call | solution.py:287
  55.9 0.0 copy-start.3
  55.9 0.0 copy-start.4
  55.9 0.1 collective-permute-done.3
  56.0 0.1 add_convert_fusion.1
  56.1 2.7 %collective-permute-start.4 = (bf16[8,2,64,128]{3,2,1,0:T(8,128)(2,1)S(1)}, bf16[8,2,64,128]{3,2,1,0:T(8,128)(2,1)S(1)}, u32[]{:S(2)}, u32[]{:S(2)}) collective-permute-start(bf16[8,2,64,128]{3,2,1,0:T(8,128)(2,1)S(1)} %add_convert_fusion.1), channel_id=1, source_target_pairs={{0,8},{1,9},{2,10},{3,11},{4,12},{5,13},{6,14},{7,15},{8,0},{9,1},... | collective-permute-start | bytes 786440 | tf_op jit(solution)/shard_map/ppermute | solution.py:397
  58.7 0.8 collective-permute-start.5
  59.5 0.0 copy-done.3
  59.5 0.4 collective-permute-start.6
  59.9 0.0 copy-done.4
  59.9 2.3 %collective-permute-start.7 = (bf16[2,512,128]{2,1,0:T(8,128)(2,1)}, bf16[2,512,128]{2,1,0:T(8,128)(2,1)S(1)}, u32[]{:S(2)}, u32[]{:S(2)}) collective-permute-start(bf16[2,512,128]{2,1,0:T(8,128)(2,1)} %get-tuple-element.40), channel_id=1, source_target_pairs={{0,3},{1,2},{2,1},{3,0},{4,7},{5,6},{6,5},{7,4},{8,11},{9,10},{10,... | collective-permute-start | bytes 786440 | tf_op jit(solution)/shard_map/ppermute | solution.py:444
  62.2 2.5 %collective-permute-start.8 = (bf16[8,2,64,128]{3,2,1,0:T(8,128)(2,1)}, bf16[8,2,64,128]{3,2,1,0:T(8,128)(2,1)S(1)}, u32[]{:S(2)}, u32[]{:S(2)}) collective-permute-start(bf16[8,2,64,128]{3,2,1,0:T(8,128)(2,1)} %copy-done.4), channel_id=1, source_target_pairs={{0,4},{1,5},{2,6},{3,7},{4,0},{5,1},{6,2},{7,3},{8,12},{9,13},{10,... | collective-permute-start | bytes 786440 | tf_op jit(solution)/shard_map/ppermute | solution.py:397
  64.8 6.4 %collective-permute-done.4 = bf16[8,2,64,128]{3,2,1,0:T(8,128)(2,1)S(1)} collective-permute-done((bf16[8,2,64,128]{3,2,1,0:T(8,128)(2,1)S(1)}, bf16[8,2,64,128]{3,2,1,0:T(8,128)(2,1)S(1)}, u32[]{:S(2)}, u32[]{:S(2)}) %collective-permute-start.4) | collective-permute-done | bytes 262176 | tf_op jit(solution)/shard_map/ppermute | solution.py:397
  71.2 1.0 %convert_add_fusion = f32[8,2,64,128]{3,2,1,0:T(8,128)S(1)} fusion(bf16[8,2,64,128]{3,2,1,0:T(8,128)(2,1)S(1)} %collective-permute-done.4, bf16[8,2,64,128]{3,2,1,0:T(8,128)(2,1)} %copy-done.3), kind=kLoop, calls=%fused_computation.7 | loop fusion | flops 393216 | bytes 1048576 | tf_op jit(solution)/shard_map/add | solution.py:445
  72.2 0.0 collective-permute-done.5
  72.2 0.1 collective-permute-done.6
  72.3 0.0 collective-permute-done.7
  72.4 0.1 maximum_select_fusion
  72.5 0.1 collective-permute-start.9
  72.6 1.5 %collective-permute-done.8 = bf16[8,2,64,128]{3,2,1,0:T(8,128)(2,1)S(1)} collective-permute-done((bf16[8,2,64,128]{3,2,1,0:T(8,128)(2,1)}, bf16[8,2,64,128]{3,2,1,0:T(8,128)(2,1)S(1)}, u32[]{:S(2)}, u32[]{:S(2)}) %collective-permute-start.8) | collective-permute-done | bytes 262176 | tf_op jit(solution)/shard_map/ppermute | solution.py:397
  74.2 0.8 add_convert_fusion
  74.9 3.4 %all-to-all-start.2 = ((bf16[8,2,64,128]{3,2,1,0:T(8,128)(2,1)}), bf16[8,2,64,128]{3,2,1,0:T(8,128)(2,1)S(1)}, u32[]{:S(2)}, u32[]{:S(2)}) async-start(bf16[8,2,64,128]{3,2,1,0:T(8,128)(2,1)} %add_convert_fusion), calls=%async_computation.2 | async-start | bytes 524288 | tf_op jit(solution)/shard_map/all_to_all | solution.py:449
  78.3 0.1 pad_add_fusion.1.place
  78.4 0.0 collective-permute-done.9
  78.4 1.8 %place_dq.1 = bf16[64,8,8,128]{3,2,1,0:T(8,128)(2,1)} custom-call(s32[2]{0:T(128)S(1)} %pad_add_fusion.1.place, bf16[2,64,8,128]{3,2,1,0:T(8,128)(2,1)S(1)} %bitcast.52, bf16[2,64,8,128]{3,2,1,0:T(8,128)(2,1)S(1)} %bitcast.53, bf16[2,64,8,128]{3,2,1,0:T(8,128)(2,1)S(1)} %bitcast.54, bf16[2,64,8,128]{3,2,1,0:T(8,128)(2,1)S(1)} %bitcast.55, ...), custom_call_target="tpu_custom_call" | custom-call | tf_op jit(solution)/shard_map/place_dq/pallas_call | solution.py:319
  80.2 4.6 %all-to-all-done.2 = bf16[8,2,64,128]{3,2,1,0:T(8,128)(2,1)S(1)} async-done(((bf16[8,2,64,128]{3,2,1,0:T(8,128)(2,1)}), bf16[8,2,64,128]{3,2,1,0:T(8,128)(2,1)S(1)}, u32[]{:S(2)}, u32[]{:S(2)}) %all-to-all-start.2) | async-done | bytes 262176 | tf_op jit(solution)/shard_map/all_to_all | solution.py:449
  84.8 1.0 %place_dkv.1 = (bf16[64,8,128]{2,1,0:T(8,128)(2,1)}, bf16[64,8,128]{2,1,0:T(8,128)(2,1)}) custom-call(bf16[1,8,2,64,128]{4,3,2,1,0:T(8,128)(2,1)S(1)} %bitcast.51), custom_call_target="tpu_custom_call" | custom-call | tf_op jit(solution)/shard_map/place_dkv/pallas_call | solution.py:341
  (9 shorter events, 0.1 us)
Async XLA Ops:
  0.6 10.0 %copy-start = (bf16[64,64,128]{2,1,0:T(8,128)(2,1)S(1)}, bf16[64,64,128]{2,1,0:T(8,128)(2,1)}, u32[]{:S(2)}) copy-start(bf16[64,64,128]{2,1,0:T(8,128)(2,1)} %param.7) | copy-start | bytes 3145732
  0.6 7.1 %copy-start.6 = (bf16[64,64,128]{2,1,0:T(8,128)(2,1)S(1)}, bf16[64,64,128]{2,1,0:T(8,128)(2,1)}, u32[]{:S(2)}) copy-start(bf16[64,64,128]{2,1,0:T(8,128)(2,1)} %param.11) | copy-start | bytes 3145732
  0.7 9.0 %copy-start.7 = (f32[64,64]{1,0:T(8,128)S(1)}, f32[64,64]{1,0:T(8,128)}, u32[]{:S(2)}) copy-start(f32[64,64]{1,0:T(8,128)} %param.12) | copy-start | bytes 49156
  2.6 11.8 %all-to-all-start.1 = ((bf16[8,2,64,128]{3,2,1,0:T(8,128)(2,1)}), bf16[8,2,64,128]{3,2,1,0:T(8,128)(2,1)S(1)}, u32[]{:S(2)}, u32[]{:S(2)}) async-start(bf16[8,2,64,128]{3,2,1,0:T(8,128)(2,1)} %maximum_bitcast_fusion), calls=%async_computation.1 | async-start | bytes 524288 | tf_op jit(solution)/shard_map/all_to_all | solution.py:401
  12.6 8.1 %copy-start.5 = (s32[16]{0:T(128)S(1)}, s32[16]{0:T(128)}, u32[]{:S(2)}) copy-start(s32[16]{0:T(128)} %param.13) | copy-start | bytes 196
  14.3 7.2 %copy-start.1 = (bf16[8,2,64,128]{3,2,1,0:T(8,128)(2,1)}, bf16[8,2,64,128]{3,2,1,0:T(8,128)(2,1)S(1)}, u32[]{:S(2)}) copy-start(bf16[8,2,64,128]{3,2,1,0:T(8,128)(2,1)S(1)} %all-to-all-done.1.refs_0_) | copy-start | bytes 786436
  14.3 30.0 %all-to-all-start = ((bf16[8,1040,128]{2,1,0:T(8,128)(2,1)}), bf16[8,1040,128]{2,1,0:T(8,128)(2,1)S(1)}, u32[]{:S(2)}, u32[]{:S(2)}) async-start(bf16[8,1040,128]{2,1,0:T(8,128)(2,1)} %pad_maximum_fusion), calls=%async_computation | async-start | bytes 4259840 | tf_op jit(solution)/shard_map/all_to_all | solution.py:418
  17.9 15.3 %collective-permute-start.1 = (bf16[8,2,64,128]{3,2,1,0:T(8,128)(2,1)S(1)}, bf16[8,2,64,128]{3,2,1,0:T(8,128)(2,1)}, u32[]{:S(2)}, u32[]{:S(2)}) collective-permute-start(bf16[8,2,64,128]{3,2,1,0:T(8,128)(2,1)S(1)} %all-to-all-done.1.refs_0_), channel_id=1, source_target_pairs={{0,8},{1,9},{2,10},{3,11},{4,12},{5,13},{6,14},{7,15},{8,0},{9,1},... | collective-permute-start | bytes 786440 | tf_op jit(solution)/shard_map/ppermute | solution.py:397
  21.5 26.0 %collective-permute-start = (bf16[8,2,64,128]{3,2,1,0:T(8,128)(2,1)S(1)}, bf16[8,2,64,128]{3,2,1,0:T(8,128)(2,1)}, u32[]{:S(2)}, u32[]{:S(2)}) collective-permute-start(bf16[8,2,64,128]{3,2,1,0:T(8,128)(2,1)S(1)} %all-to-all-done.1.refs_0_), channel_id=1, source_target_pairs={{0,4},{1,5},{2,6},{3,7},{4,0},{5,1},{6,2},{7,3},{8,12},{9,13},{10,... | collective-permute-start | bytes 786440 | tf_op jit(solution)/shard_map/ppermute | solution.py:397
  33.3 8.0 %collective-permute-start.2 = (bf16[8,2,64,128]{3,2,1,0:T(8,128)(2,1)}, bf16[8,2,64,128]{3,2,1,0:T(8,128)(2,1)}, u32[]{:S(2)}, u32[]{:S(2)}) collective-permute-start(bf16[8,2,64,128]{3,2,1,0:T(8,128)(2,1)} %collective-permute-done.1.refs_2_), channel_id=1, source_target_pairs={{0,4},{1,5},{2,6},{3,7},{4,0},{5,1},{6,2},{7,3},{8,12},{9,13},{10,... | collective-permute-start | bytes 786440 | tf_op jit(solution)/shard_map/ppermute | solution.py:397
  44.3 3.2 %copy-start.2 = (bf16[8,2,64,128]{3,2,1,0:T(8,128)(2,1)S(1)}, bf16[8,2,64,128]{3,2,1,0:T(8,128)(2,1)}, u32[]{:S(2)}) copy-start(bf16[8,2,64,128]{3,2,1,0:T(8,128)(2,1)} %copy-done.1) | copy-start | bytes 786436
  47.4 8.6 %collective-permute-start.3 = (bf16[8,2,64,128]{3,2,1,0:T(8,128)(2,1)S(1)}, bf16[8,2,64,128]{3,2,1,0:T(8,128)(2,1)S(1)}, u32[]{:S(2)}, u32[]{:S(2)}) collective-permute-start(bf16[8,2,64,128]{3,2,1,0:T(8,128)(2,1)S(1)} %get-tuple-element.31), channel_id=1, source_target_pairs={{0,4},{1,5},{2,6},{3,7},{4,0},{5,1},{6,2},{7,3},{8,12},{9,13},{10,... | collective-permute-start | bytes 786440 | tf_op jit(solution)/shard_map/ppermute | solution.py:397
  55.9 3.6 %copy-start.3 = (bf16[8,2,64,128]{3,2,1,0:T(8,128)(2,1)}, bf16[8,2,64,128]{3,2,1,0:T(8,128)(2,1)S(1)}, u32[]{:S(2)}) copy-start(bf16[8,2,64,128]{3,2,1,0:T(8,128)(2,1)S(1)} %get-tuple-element.29) | copy-start | bytes 786436
  55.9 4.0 %copy-start.4 = (bf16[8,2,64,128]{3,2,1,0:T(8,128)(2,1)}, bf16[8,2,64,128]{3,2,1,0:T(8,128)(2,1)S(1)}, u32[]{:S(2)}) copy-start(bf16[8,2,64,128]{3,2,1,0:T(8,128)(2,1)S(1)} %get-tuple-element.42) | copy-start | bytes 786436
  56.1 15.1 %collective-permute-start.4 = (bf16[8,2,64,128]{3,2,1,0:T(8,128)(2,1)S(1)}, bf16[8,2,64,128]{3,2,1,0:T(8,128)(2,1)S(1)}, u32[]{:S(2)}, u32[]{:S(2)}) collective-permute-start(bf16[8,2,64,128]{3,2,1,0:T(8,128)(2,1)S(1)} %add_convert_fusion.1), channel_id=1, source_target_pairs={{0,8},{1,9},{2,10},{3,11},{4,12},{5,13},{6,14},{7,15},{8,0},{9,1},... | collective-permute-start | bytes 786440 | tf_op jit(solution)/shard_map/ppermute | solution.py:397
  58.7 13.5 %collective-permute-start.5 = (bf16[2,512,128]{2,1,0:T(8,128)(2,1)}, bf16[2,512,128]{2,1,0:T(8,128)(2,1)S(1)}, u32[]{:S(2)}, u32[]{:S(2)}) collective-permute-start(bf16[2,512,128]{2,1,0:T(8,128)(2,1)} %get-tuple-element.38), channel_id=1, source_target_pairs={{0,1},{1,0},{2,3},{3,2},{4,5},{5,4},{6,7},{7,6},{8,9},{9,8},{10,11... | collective-permute-start | bytes 786440 | tf_op jit(solution)/shard_map/ppermute | solution.py:444
  59.5 12.8 %collective-permute-start.6 = (bf16[2,512,128]{2,1,0:T(8,128)(2,1)}, bf16[2,512,128]{2,1,0:T(8,128)(2,1)S(1)}, u32[]{:S(2)}, u32[]{:S(2)}) collective-permute-start(bf16[2,512,128]{2,1,0:T(8,128)(2,1)} %get-tuple-element.39), channel_id=1, source_target_pairs={{0,2},{1,3},{2,0},{3,1},{4,6},{5,7},{6,4},{7,5},{8,10},{9,11},{10,... | collective-permute-start | bytes 786440 | tf_op jit(solution)/shard_map/ppermute | solution.py:444
  59.9 12.4 %collective-permute-start.7 = (bf16[2,512,128]{2,1,0:T(8,128)(2,1)}, bf16[2,512,128]{2,1,0:T(8,128)(2,1)S(1)}, u32[]{:S(2)}, u32[]{:S(2)}) collective-permute-start(bf16[2,512,128]{2,1,0:T(8,128)(2,1)} %get-tuple-element.40), channel_id=1, source_target_pairs={{0,3},{1,2},{2,1},{3,0},{4,7},{5,6},{6,5},{7,4},{8,11},{9,10},{10,... | collective-permute-start | bytes 786440 | tf_op jit(solution)/shard_map/ppermute | solution.py:444
  62.2 11.9 %collective-permute-start.8 = (bf16[8,2,64,128]{3,2,1,0:T(8,128)(2,1)}, bf16[8,2,64,128]{3,2,1,0:T(8,128)(2,1)S(1)}, u32[]{:S(2)}, u32[]{:S(2)}) collective-permute-start(bf16[8,2,64,128]{3,2,1,0:T(8,128)(2,1)} %copy-done.4), channel_id=1, source_target_pairs={{0,4},{1,5},{2,6},{3,7},{4,0},{5,1},{6,2},{7,3},{8,12},{9,13},{10,... | collective-permute-start | bytes 786440 | tf_op jit(solution)/shard_map/ppermute | solution.py:397
  72.5 5.9 %collective-permute-start.9 = (bf16[4,512,128]{2,1,0:T(8,128)(2,1)S(1)}, bf16[4,512,128]{2,1,0:T(8,128)(2,1)S(1)}, u32[]{:S(2)}, u32[]{:S(2)}) collective-permute-start(bf16[4,512,128]{2,1,0:T(8,128)(2,1)S(1)} %maximum_select_fusion), channel_id=1, source_target_pairs={{0,16},{16,0},{1,17},{17,1},{2,18},{18,2},{3,19},{19,3},{4,20},{20... | collective-permute-start | bytes 1572872 | tf_op jit(solution)/shard_map/ppermute | solution.py:451
  74.9 9.9 %all-to-all-start.2 = ((bf16[8,2,64,128]{3,2,1,0:T(8,128)(2,1)}), bf16[8,2,64,128]{3,2,1,0:T(8,128)(2,1)S(1)}, u32[]{:S(2)}, u32[]{:S(2)}) async-start(bf16[8,2,64,128]{3,2,1,0:T(8,128)(2,1)} %add_convert_fusion), calls=%async_computation.2 | async-start | bytes 524288 | tf_op jit(solution)/shard_map/all_to_all | solution.py:449
